TPU v7x, 32 devices: a whole 2x2x4 slice. The times are simulated.
32 devices in a mesh: section: 2 (over y), dp: 16 (over z, x, core).
Axes of the slice: x: 2, y: 2, z: 4, core: 2. Of those that a mesh axis runs over, the one named last changes fastest.
Arguments:
- fresh_acts: bfloat16 [3, 128, 8192], P(None, None, 'dp'), may hold values from -36 to 36
- carried: bfloat16 [2, 128, 8192], P('section', None, 'dp'), may hold values from -36 to 36
- norm_gain: float32 [2, 8192], P('section'), may hold values from 0.1 to 1.9
- w_in: bfloat16 [2, 3, 4096, 8192], P('section', None, 'dp'), may hold values from -0.0625 to 0.0625
- short_filter: float32 [2, 3, 4096, 3], P('section', None, 'dp'), may hold values from -3 to 3
- filter_taps: float32 [2, 4096, 128], P('section', 'dp'), may hold values from -0.9 to 0.9
- decay_rate: float32 [2, 4096], P('section', 'dp'), may hold values from 0.01 to 0.12
- w_out: bfloat16 [2, 4096, 8192], P('section', None, 'dp'), may hold values from -0.09375 to 0.09375
Outputs:
- section_outputs: bfloat16 [2, 3, 128, 8192], P('section', None, None, 'dp')
All inputs are finite; a program needn't handle non-finite values.
Results may differ from a plain program's by a relative error of at most 0.011.
Values may be sent and summed in bfloat16 or wider, within the bound.
No kernel may reach another device: no remote copies, remote signals or barrier semaphores. Data moves between devices by JAX's collectives and lax.ppermute only.
A program may use at most 128 MiB of HBM per device.

v0:
```python
import jax
import jax.numpy as jnp
from jax import lax
from jax.sharding import PartitionSpec as P

EPS = 1e-06


def shifted(value, axis, steps):
    count = lax.axis_size(axis)
    pairs = [(source, (source + steps) % count) for source in range(count)]
    return lax.ppermute(value, axis, pairs)


def build_toeplitz(tap_values, decay_rate, tok_len):
    tap_count = tap_values.shape[1]
    lag_grid = jnp.arange(tok_len)[:, None] - jnp.arange(tok_len)[None, :]
    onehot = (lag_grid[:, :, None] == jnp.arange(tap_count)[None, None, :]).astype(jnp.float32)
    filter_vals = tap_values * jnp.exp(
        -decay_rate[:, None] * jnp.arange(tap_count, dtype=jnp.float32)[None, :]
    )
    return jnp.einsum("cj,tsj->cts", filter_vals, onehot, precision=lax.Precision.HIGHEST)


def mixing(u_proj, short_taps, toeplitz):
    tok_len = u_proj.shape[0]
    tap_count = short_taps.shape[2]
    padded = jnp.pad(u_proj, ((tap_count - 1, 0), (0, 0), (0, 0)))
    mixed_out = short_taps[:, :, 0] * u_proj
    for j in range(1, tap_count):
        mixed_out = (
            mixed_out
            + short_taps[:, :, j] * padded[tap_count - 1 - j : tap_count - 1 - j + tok_len]
        )
    query_part = mixed_out[:, 0]
    product = mixed_out[:, 1] * mixed_out[:, 2]
    long_conv = jnp.einsum("cts,sc->tc", toeplitz, product, precision=lax.Precision.HIGHEST)
    return (query_part * long_conv).astype(jnp.bfloat16)


def contract_rows(normed, weight_rows):
    return lax.dot_general(
        normed, weight_rows, (((1,), (1,)), ((), ())), preferred_element_type=jnp.float32
    )


def body(fresh_acts, carried, norm_gain, w_in, short_filter, filter_taps, decay_rate, w_out):
    section_idx = lax.axis_index("section")
    section_count = lax.axis_size("section")
    is_first = section_idx == 0
    tick_count = fresh_acts.shape[0]
    tok_len = fresh_acts.shape[1]
    feat_dev = fresh_acts.shape[2]
    model_width = norm_gain.shape[1]
    chan_dev = w_in.shape[2]
    gain_row = norm_gain[0]
    w_in_flat = w_in[0].reshape(3 * chan_dev, model_width)
    w_out_local = w_out[0]
    short_taps = short_filter[0]
    toeplitz = build_toeplitz(filter_taps[0], decay_rate[0], tok_len)
    own_start = lax.axis_index("dp") * feat_dev
    start_slice = jnp.where(is_first, fresh_acts[0], carried[0])
    results = []
    is_last = section_idx == section_count - 1
    full_rows = lax.all_gather(start_slice, "dp", axis=1, tiled=True)
    for k in range(tick_count):
        widened = full_rows.astype(jnp.float32)
        normed = (widened * gain_row).astype(jnp.bfloat16)
        from_proj_acc = contract_rows(normed, w_in_flat)
        from_sum_sq = jnp.sum(widened * widened, axis=1)
        from_own_slice = lax.dynamic_slice_in_dim(full_rows, own_start, feat_dev, 1)
        factor = lax.rsqrt(from_sum_sq / model_width + EPS)
        u_proj = (from_proj_acc * factor[:, None]).reshape(tok_len, 3, chan_dev)
        y_local = mixing(u_proj, short_taps, toeplitz)
        out_acc = jnp.dot(
            lax.all_gather(y_local, "dp", axis=1, tiled=True),
            w_out_local,
            preferred_element_type=jnp.float32,
        )
        produced = (from_own_slice.astype(jnp.float32) + out_acc).astype(jnp.bfloat16)
        results.append(produced)
        if k + 1 < tick_count:
            source = jnp.where(is_last, fresh_acts[k + 1], produced)
            gathered = lax.all_gather(source, "dp", axis=1, tiled=True)
            full_rows = shifted(gathered, "section", 1)
    return jnp.stack(results)[None]


def solution(mesh):
    return jax.shard_map(
        body,
        mesh=mesh,
        in_specs=(
            P(None, None, "dp"),
            P("section", None, "dp"),
            P("section", None),
            P("section", None, "dp", None),
            P("section", None, "dp", None),
            P("section", "dp", None),
            P("section", "dp"),
            P("section", None, "dp"),
        ),
        out_specs=P("section", None, None, "dp"),
        check_vma=False,
    )
```

profile of v0, /device:TPU:0, one launch (start us, length us, event | category | flops | bytes accessed | tf_op | source)
XLA Modules:
  0.0 444.3 jit_solution(10954909282627055905)
XLA Ops:
  6.5 1.6 slice_select_fusion
  9.6 10.8 %fusion = f32[256,128,128]{2,0,1:T(8,128)} fusion(s32[128,128]{1,0:T(8,128)S(1)} %iota_subtract_fusion, f32[1,256,128]{2,1,0:T(8,128)} %param.13, f32[256]{0:T(256)S(1)} %bitcast.138), kind=kOutput, calls=%fused_computation.1 | convolution fusion | flops 6444613632 | bytes 16974848 | tf_op jit(solution)/shard_map/cj,tsj->cts/dot_general | solution.py:22
  20.4 17.6 %copy.13 = f32[256,128,128]{1,2,0:T(8,128)} copy(f32[256,128,128]{2,0,1:T(8,128)} %fusion) | data formatting | bytes 33554432 | tf_op jit(solution)/shard_map/cj,tsj->cts/dot_general | solution.py:22
  38.0 15.5 %all-gather.18.cloned.1.call-done = bf16[1,128,8192]{2,1,0:T(8,128)(2,1)} async-done(((bf16[1,128,512]{2,1,0:T(8,128)(2,1)}), bf16[1,128,8192]{2,1,0:T(8,128)(2,1)}) %all-gather.18.cloned.1.call-update) | async-done | bytes 2097168 | tf_op jit(solution)/shard_map/all_gather | solution.py:65
  53.4 2.1 fusion.6
  55.5 9.5 %fusion.30 = f32[128,768]{1,0:T(8,128)S(1)} fusion(bf16[768,8192]{1,0:T(8,128)(2,1)} %bitcast.117, bf16[1,128,8192]{2,1,0:T(8,128)(2,1)} %all-gather.18.cloned.1.call-done, f32[8192]{0:T(1024)S(1)} %bitcast.131, f32[128]{0:T(128)S(1)} %add_rsqrt_fusion.2), kind=kOutput, calls=%fused_computation.30 | convolution fusion | flops 1613856768 | bytes 15106560 | tf_op jit(solution)/shard_map/dot_general | solution.py:42
  65.8 16.6 %fusion.66 = f32[256,1,128]{2,1,0:T(1,128)S(1)} fusion(f32[128,256,1]{0,2,1:T(1,128)S(1)} %bitcast.124, f32[256,128,128]{1,2,0:T(8,128)} %copy.13), kind=kOutput, calls=%fused_computation.85 | convolution fusion | flops 50331648 | bytes 17039360 | tf_op jit(solution)/shard_map/cts,sc->tc/dot_general | solution.py:37
  83.2 37.0 %all-gather.8.cloned.1.call-done = bf16[128,4096]{0,1:T(8,128)(2,1)} async-done(((bf16[128,256]{0,1:T(8,128)(2,1)}), bf16[128,4096]{0,1:T(8,128)(2,1)}) %all-gather.8.cloned.1.call-update) | async-done | bytes 1048592 | tf_op jit(solution)/shard_map/all_gather | solution.py:76
  120.1 3.9 bitcast_select_fusion.1
  124.3 40.0 %all-gather.10.cloned.1.call-done = bf16[128,8192]{1,0:T(8,128)(2,1)} async-done(((bf16[128,512]{1,0:T(8,128)(2,1)}), bf16[128,8192]{1,0:T(8,128)(2,1)}) %all-gather.10.cloned.1.call-update) | async-done | bytes 2097168 | tf_op jit(solution)/shard_map/all_gather | solution.py:84
  164.4 1.5 collective-permute-start
  165.9 46.5 %collective-permute-done = bf16[128,8192]{1,0:T(8,128)(2,1)S(1)} collective-permute-done((bf16[128,8192]{1,0:T(8,128)(2,1)}, bf16[128,8192]{1,0:T(8,128)(2,1)S(1)}, u32[]{:S(2)}, u32[]{:S(2)}) %collective-permute-start) | collective-permute-done | bytes 2097184 | tf_op jit(solution)/shard_map/ppermute | solution.py:12
  212.9 8.8 %fusion.24 = f32[128,768]{1,0:T(8,128)S(1)} fusion(bf16[768,8192]{1,0:T(8,128)(2,1)} %bitcast.118, bf16[128,8192]{1,0:T(8,128)(2,1)S(1)} %collective-permute-done, f32[8192]{0:T(1024)S(1)} %bitcast.132, f32[128]{0:T(128)S(1)} %add_rsqrt_fusion.1), kind=kOutput, calls=%fused_computation.28 | convolution fusion | flops 1613856768 | bytes 15106560 | tf_op jit(solution)/shard_map/dot_general | solution.py:42
  222.5 16.6 %fusion.67 = f32[256,1,128]{2,1,0:T(1,128)S(1)} fusion(f32[128,256,1]{0,2,1:T(1,128)S(1)} %bitcast.125, f32[256,128,128]{1,2,0:T(8,128)} %copy.13), kind=kOutput, calls=%fused_computation.86 | convolution fusion | flops 50331648 | bytes 17039360 | tf_op jit(solution)/shard_map/cts,sc->tc/dot_general | solution.py:37
  239.8 37.0 %all-gather.12.cloned.1.call-done = bf16[128,4096]{0,1:T(8,128)(2,1)} async-done(((bf16[128,256]{0,1:T(8,128)(2,1)}), bf16[128,4096]{0,1:T(8,128)(2,1)}) %all-gather.12.cloned.1.call-update) | async-done | bytes 1048592 | tf_op jit(solution)/shard_map/all_gather | solution.py:76
  276.8 3.9 bitcast_select_fusion
  281.0 40.0 %all-gather.14.cloned.1.call-done = bf16[128,8192]{1,0:T(8,128)(2,1)} async-done(((bf16[128,512]{1,0:T(8,128)(2,1)}), bf16[128,8192]{1,0:T(8,128)(2,1)}) %all-gather.14.cloned.1.call-update) | async-done | bytes 2097168 | tf_op jit(solution)/shard_map/all_gather | solution.py:84
  321.0 1.5 collective-permute-start.1
  322.5 46.5 %collective-permute-done.1 = bf16[128,8192]{1,0:T(8,128)(2,1)S(1)} collective-permute-done((bf16[128,8192]{1,0:T(8,128)(2,1)}, bf16[128,8192]{1,0:T(8,128)(2,1)S(1)}, u32[]{:S(2)}, u32[]{:S(2)}) %collective-permute-start.1) | collective-permute-done | bytes 2097184 | tf_op jit(solution)/shard_map/ppermute | solution.py:12
  369.5 8.8 %fusion.27 = f32[128,768]{1,0:T(8,128)S(1)} fusion(bf16[768,8192]{1,0:T(8,128)(2,1)} %bitcast.119, bf16[128,8192]{1,0:T(8,128)(2,1)S(1)} %collective-permute-done.1, f32[8192]{0:T(1024)S(1)} %bitcast.133, f32[128]{0:T(128)S(1)} %add_rsqrt_fusion), kind=kOutput, calls=%fused_computation.29 | convolution fusion | flops 1613856768 | bytes 15106560 | tf_op jit(solution)/shard_map/dot_general | solution.py:42
  379.1 16.6 %fusion.68 = f32[256,1,128]{2,1,0:T(1,128)S(1)} fusion(f32[128,256,1]{0,2,1:T(1,128)S(1)} %bitcast.123, f32[256,128,128]{1,2,0:T(8,128)} %copy.13), kind=kOutput, calls=%fused_computation.87 | convolution fusion | flops 50331648 | bytes 17039360 | tf_op jit(solution)/shard_map/cts,sc->tc/dot_general | solution.py:37
  396.4 37.0 %all-gather.16.cloned.1.call-done = bf16[128,4096]{0,1:T(8,128)(2,1)} async-done(((bf16[128,256]{0,1:T(8,128)(2,1)}), bf16[128,4096]{0,1:T(8,128)(2,1)}) %all-gather.16.cloned.1.call-update) | async-done | bytes 1048592 | tf_op jit(solution)/shard_map/all_gather | solution.py:76
  433.4 3.3 fusion.51
  436.7 0.8 maximum_bitcast_fusion
  (41 shorter events, 7.3 us)
Async XLA Ops:
  6.5 46.9 %all-gather.18.cloned.1.call-start = ((), (), s32[]{:S(2)}) async-start(), calls=%async_computation.5 | async-start | bytes 2228224 | tf_op jit(solution)/shard_map/all_gather | solution.py:65
  8.1 112.0 %all-gather.8.cloned.1.call-start = ((), (), s32[]{:S(2)}) async-start(), calls=%async_computation | async-start | bytes 1114112 | tf_op jit(solution)/shard_map/all_gather | solution.py:76
  20.4 35.2 %copy-start.1 = (f32[1,8192]{1,0:T(1,128)S(1)}, f32[1,8192]{1,0:T(1,128)}, u32[]{:S(2)}) copy-start(f32[1,8192]{1,0:T(1,128)} %param.10) | copy-start | bytes 98308
  65.8 54.4 %copy-start = (bf16[3,128,512]{2,1,0:T(8,128)(2,1)S(1)}, bf16[3,128,512]{2,1,0:T(8,128)(2,1)}, u32[]{:S(2)}) copy-start(bf16[3,128,512]{2,1,0:T(8,128)(2,1)} %param.8) | copy-start | bytes 1179652
  83.1 81.2 %all-gather.10.cloned.1.call-start = ((), (), s32[]{:S(2)}) async-start(), calls=%async_computation.1 | async-start | bytes 2228224 | tf_op jit(solution)/shard_map/all_gather | solution.py:84
  124.1 152.7 %all-gather.12.cloned.1.call-start = ((), (), s32[]{:S(2)}) async-start(), calls=%async_computation.2 | async-start | bytes 1114112 | tf_op jit(solution)/shard_map/all_gather | solution.py:76
  164.4 48.0 %collective-permute-start = (bf16[128,8192]{1,0:T(8,128)(2,1)}, bf16[128,8192]{1,0:T(8,128)(2,1)S(1)}, u32[]{:S(2)}, u32[]{:S(2)}) collective-permute-start(bf16[128,8192]{1,0:T(8,128)(2,1)} %all-gather.10.cloned.1.call-done), channel_id=1, source_target_pairs={{0,16},{16,0},{1,17},{17,1},{2,18},{18,2},{3,19},{19,3},{4,20},{20... | collective-permute-start | bytes 6291464 | tf_op jit(solution)/shard_map/ppermute | solution.py:12
  239.1 130.4 %copy-start.2 = (f32[1,8192]{1,0:T(1,128)S(1)}, f32[1,8192]{1,0:T(1,128)}, u32[]{:S(2)}) copy-start(f32[1,8192]{1,0:T(1,128)} %param.10) | copy-start | bytes 98308
  239.7 81.2 %all-gather.14.cloned.1.call-start = ((), (), s32[]{:S(2)}) async-start(), calls=%async_computation.3 | async-start | bytes 2228224 | tf_op jit(solution)/shard_map/all_gather | solution.py:84
  280.7 152.7 %all-gather.16.cloned.1.call-start = ((), (), s32[]{:S(2)}) async-start(), calls=%async_computation.4 | async-start | bytes 1114112 | tf_op jit(solution)/shard_map/all_gather | solution.py:76
  321.0 48.0 %collective-permute-start.1 = (bf16[128,8192]{1,0:T(8,128)(2,1)}, bf16[128,8192]{1,0:T(8,128)(2,1)S(1)}, u32[]{:S(2)}, u32[]{:S(2)}) collective-permute-start(bf16[128,8192]{1,0:T(8,128)(2,1)} %all-gather.14.cloned.1.call-done), channel_id=1, source_target_pairs={{0,16},{16,0},{1,17},{17,1},{2,18},{18,2},{3,19},{19,3},{4,20},{20... | collective-permute-start | bytes 6291464 | tf_op jit(solution)/shard_map/ppermute | solution.py:12
Sparse Core Ops, SparseCore 0:
  9.5 43.8 all-gather.17
  83.2 36.8 all-gather.7
  124.2 40.1 all-gather.9
  239.9 36.8 all-gather.11
  280.9 40.0 all-gather.13
  396.5 36.8 all-gather.15
where the time goes:
time: 445 us; the launch traced here: 444 us
  waiting for transfers between devices  299 us (67%)
  matrix products  98.9 us (22%)
  local copies, waits for them, and re-layouts  18.8 us (4%)
  between operations  13.6 us (3%)
  other arithmetic  9.86 us (2%)
    all_gather x3, waiting for transfers between devices, body(): lax.all_gather(y_local, 'dp', axis=1, tiled=True)  111 us
    ppermute x2, waiting for transfers between devices, shifted(): return lax.ppermute(value, axis, pairs)  93 us
    all_gather x2, waiting for transfers between devices, body(): gathered = lax.all_gather(source, 'dp', axis=1, tiled=True)  80 us
    dot_general x3, matrix products, mixing(): jnp.einsum('cts,sc->tc', toeplitz, product, precision=lax.Precision.HIGHEST)  49.8 us
    dot_general x3, matrix products, contract_rows(): lax.dot_general(normed, weight_rows, (((1,), (1,)), ((), ())), preferred_...  27.2 us
    dot_general x1, local copies, waits for them, and re-layouts, build_toeplitz(): jnp.einsum('cj,tsj->cts', filter_vals, onehot, precision=lax.Precision.HI...  17.6 us
    all_gather x1, waiting for transfers between devices, body(): full_rows = lax.all_gather(start_slice, 'dp', axis=1, tiled=True)  15.5 us
    dot_general x3, matrix products, body(): jnp.dot(lax.all_gather(y_local, 'dp', axis=1, tiled=True), w_out_local, p...  11.1 us
  transfers between devices with their start and end apart: 8, of which 8 were waited for; matrix products, arithmetic and copies ran while one was open for 7% of the time, Pallas kernels for 0%

commit v1 on v0

v1 whole, which is shorter than its diff:
```python
import functools

import jax
import jax.numpy as jnp
from jax import lax
from jax.experimental import pallas as pl
from jax.experimental.pallas import tpu as pltpu
from jax.sharding import PartitionSpec as P

EPS = 1e-06
VMEM_LIMIT = 48 * 1024 * 1024
PAD = 8


def plan(section_count, tick_count):
    wave_count = min(section_count, tick_count)
    waves = [[[] for _ in range(section_count)] for _ in range(wave_count)]
    where = {}
    for k in range(tick_count):
        for s in range(section_count):
            first = where[s - 1, k - 1][0] + 1 if s > 0 and k > 0 else 0
            last = wave_count - 1 - min(section_count - 1 - s, tick_count - 1 - k)
            best = min(range(first, last + 1), key=lambda w: (len(waves[w][s]), w))
            where[s, k] = (best, len(waves[best][s]))
            waves[best][s].append(k)
    return waves, where


def split_dp(dp_count):
    core = 2 if dp_count % 2 == 0 else 1
    chips = dp_count // core
    near = 1
    while near * near * 4 <= chips:
        near *= 2
    return chips // near, near, core


def pick(section_idx, options):
    distinct = []
    for s, value in enumerate(options):
        if value is None:
            continue
        for held, members in distinct:
            if held is value:
                members.append(s)
                break
        else:
            distinct.append((value, [s]))
    result = distinct[0][0]
    for value, members in distinct[1:]:
        mine = functools.reduce(jnp.logical_or, [section_idx == s for s in members])
        result = jnp.where(mine, value, result)
    return result


def mix_kernel(group, tok_len, model_width, rank_ref, *refs):
    pieces = refs[:group]
    w_ref, gain_ref, short_ref, long_ref, y_ref = refs[group : group + 5]
    norm_ref, acc_ref, sq_ref, pad_ref = refs[group + 5 :]
    step = pl.program_id(0)
    feat = pieces[0].shape[2]
    rows = pieces[0].shape[1]
    chan = w_ref.shape[1]
    low = lax.rem(rank_ref[0], group)

    @pl.when(step == 0)
    def _():
        acc_ref[...] = jnp.zeros_like(acc_ref)
        sq_ref[...] = jnp.zeros_like(sq_ref)

    for q in range(group):
        start = pl.multiple_of((low ^ q) * feat, feat)
        wide = pieces[q][0].astype(jnp.float32)
        norm_ref[:, pl.ds(start, feat)] = (wide * gain_ref[:, pl.ds(start, feat)]).astype(jnp.bfloat16)
        squares = wide * wide
        lanes = min(feat, 128)
        part = squares[:, :lanes]
        for j in range(1, feat // lanes):
            part = part + squares[:, j * lanes : (j + 1) * lanes]
        sq_ref[...] += part
    for i in range(3):
        acc_ref[i] += lax.dot_general(
            norm_ref[...], w_ref[i], (((1,), (1,)), ((), ())), preferred_element_type=jnp.float32
        )

    @pl.when(step == pl.num_programs(0) - 1)
    def _():
        pad_ref[0:PAD, :] = jnp.zeros((PAD, chan), jnp.float32)
        taps = short_ref.shape[0] // 3
        for slot in range(rows // tok_len):
            low_row = slot * tok_len
            here = slice(low_row, low_row + tok_len)
            total = jnp.sum(sq_ref[here, :], axis=1, keepdims=True)
            factor = lax.rsqrt(total / model_width + EPS)

            def branch(i):
                u = acc_ref[i, here, :] * factor
                pad_ref[PAD : PAD + tok_len, :] = u
                z = short_ref[i * taps : i * taps + 1, :] * u
                for j in range(1, taps):
                    z = z + short_ref[i * taps + j : i * taps + j + 1, :] * pad_ref[PAD - j : PAD - j + tok_len, :]
                return z

            key = branch(1)
            product = key * branch(2)
            query = branch(0)
            acc_ref[0, here, :] = query
            pad_ref[PAD : PAD + tok_len, :] = product
            width = min(chan, 128)
            for c in range(0, chan, width):
                cols = slice(c, c + width)
                conv = [None] * (tok_len // 8)
                for b in range(8):
                    moved = [pad_ref[PAD - b + 8 * i : PAD - b + 8 * i + 8, cols] for i in range(tok_len // 8)]
                    for a in range(long_ref.shape[0] // 8):
                        tap = long_ref[8 * a + b : 8 * a + b + 1, cols]
                        for i in range(a, tok_len // 8):
                            term = tap * moved[i - a]
                            conv[i] = term if conv[i] is None else conv[i] + term
                for i in range(tok_len // 8):
                    at = low_row + 8 * i
                    acc_ref[1, at : at + 8, cols] = conv[i]
            y_ref[here, :] = (acc_ref[0, here, :] * acc_ref[1, here, :]).astype(jnp.bfloat16)


def mix(pieces, w_in, gain, short_rows, long_rows, rank, tok_len):
    group = len(pieces)
    far, rows, feat = pieces[0].shape
    branches, chan, model_width = w_in.shape
    wide = group * feat
    kernel = functools.partial(mix_kernel, group, tok_len, model_width)
    return pl.pallas_call(
        kernel,
        grid_spec=pltpu.PrefetchScalarGridSpec(
            num_scalar_prefetch=1,
            grid=(far,),
            in_specs=[pl.BlockSpec((1, rows, feat), lambda d, r: (d, 0, 0))] * group
            + [
                pl.BlockSpec((branches, chan, wide), lambda d, r: (0, 0, (r[0] // group) ^ d)),
                pl.BlockSpec((1, wide), lambda d, r: (0, (r[0] // group) ^ d)),
                pl.BlockSpec(short_rows.shape, lambda d, r: (0, 0)),
                pl.BlockSpec(long_rows.shape, lambda d, r: (0, 0)),
            ],
            out_specs=pl.BlockSpec((rows, chan), lambda d, r: (0, 0)),
            scratch_shapes=[
                pltpu.VMEM((rows, wide), jnp.bfloat16),
                pltpu.VMEM((branches, rows, chan), jnp.float32),
                pltpu.VMEM((rows, min(feat, 128)), jnp.float32),
                pltpu.VMEM((PAD + tok_len, chan), jnp.float32),
            ],
        ),
        out_shape=jax.ShapeDtypeStruct((rows, chan), jnp.bfloat16),
        compiler_params=pltpu.CompilerParams(
            dimension_semantics=("arbitrary",), vmem_limit_bytes=VMEM_LIMIT
        ),
        cost_estimate=pl.CostEstimate(
            flops=2 * rows * branches * chan * model_width,
            bytes_accessed=2 * branches * chan * model_width + 2 * rows * model_width,
            transcendentals=0,
        ),
        name="norm_project_mix",
    )(rank, *pieces, w_in, gain, short_rows, long_rows)


def out_kernel(group, rank_ref, *refs):
    pieces = refs[:group]
    w_ref, own_ref, result_ref, cat_ref, acc_ref = refs[group:]
    step = pl.program_id(0)
    chan = pieces[0].shape[2]
    low = lax.rem(rank_ref[0], group)

    @pl.when(step == 0)
    def _():
        acc_ref[...] = own_ref[...].astype(jnp.float32)

    if chan % 128 == 0:
        for q in range(group):
            start = pl.multiple_of((low ^ q) * chan, chan)
            cat_ref[:, pl.ds(start, chan)] = pieces[q][0]
        acc_ref[...] += jnp.dot(cat_ref[...], w_ref[...], preferred_element_type=jnp.float32)
    else:
        for q in range(group):
            start = pl.multiple_of((low ^ q) * chan, chan)
            acc_ref[...] += jnp.dot(
                pieces[q][0], w_ref[pl.ds(start, chan), :], preferred_element_type=jnp.float32
            )

    @pl.when(step == pl.num_programs(0) - 1)
    def _():
        result_ref[...] = acc_ref[...].astype(jnp.bfloat16)


def project_out(pieces, w_out, own, rank):
    group = len(pieces)
    far, rows, chan = pieces[0].shape
    feat = w_out.shape[1]
    wide = group * chan
    return pl.pallas_call(
        functools.partial(out_kernel, group),
        grid_spec=pltpu.PrefetchScalarGridSpec(
            num_scalar_prefetch=1,
            grid=(far,),
            in_specs=[pl.BlockSpec((1, rows, chan), lambda d, r: (d, 0, 0))] * group
            + [
                pl.BlockSpec((wide, feat), lambda d, r: ((r[0] // group) ^ d, 0)),
                pl.BlockSpec((rows, feat), lambda d, r: (0, 0)),
            ],
            out_specs=pl.BlockSpec((rows, feat), lambda d, r: (0, 0)),
            scratch_shapes=[
                pltpu.VMEM((rows, wide), jnp.bfloat16),
                pltpu.VMEM((rows, feat), jnp.float32),
            ],
        ),
        out_shape=jax.ShapeDtypeStruct((rows, feat), jnp.bfloat16),
        compiler_params=pltpu.CompilerParams(
            dimension_semantics=("arbitrary",), vmem_limit_bytes=VMEM_LIMIT
        ),
        cost_estimate=pl.CostEstimate(
            flops=2 * rows * w_out.shape[0] * feat,
            bytes_accessed=2 * w_out.shape[0] * feat + 2 * rows * w_out.shape[0],
            transcendentals=0,
        ),
        name="project_out",
    )(rank, *pieces, w_out, own)


def body(section_count, dp_count, fresh_acts, carried, norm_gain, w_in, short_filter, filter_taps, decay_rate, w_out):
    tick_count, tok_len, _ = fresh_acts.shape
    far, near, core = split_dp(dp_count)
    group = near * core
    waves, where = plan(section_count, tick_count)
    section_idx = lax.axis_index("section")
    rank_idx = lax.axis_index("dp")
    rank = rank_idx.astype(jnp.int32).reshape(1)

    def swap(value, offset):
        return lax.ppermute(value, "dp", [(r, r ^ offset) for r in range(dp_count)])

    def onward(value, offset):
        pairs = [
            (s * dp_count + r, (s + 1) % section_count * dp_count + (r ^ offset))
            for s in range(section_count)
            for r in range(dp_count)
        ]
        return lax.ppermute(value, ("section", "dp"), pairs)

    def spread(line):
        pieces = []
        for x in range(near):
            piece = line if x == 0 else swap(line, x * core)
            pieces.append(piece)
            for c in range(1, core):
                pieces.append(swap(piece, c))
        return pieces

    lags = jnp.arange(filter_taps.shape[2], dtype=jnp.float32)
    long_rows = (filter_taps[0] * jnp.exp(-decay_rate[0][:, None] * lags[None, :])).T
    short_rows = short_filter[0].transpose(0, 2, 1).reshape(-1, short_filter.shape[2])

    waiting = carried[0]
    results = {}
    for w, slots in enumerate(waves):
        slot_count = max(len(ticks) for ticks in slots)
        sources = []
        for i in range(slot_count):
            options = []
            for s in range(section_count):
                if w == 0:
                    ticks = slots[s]
                    if i >= len(ticks):
                        options.append(None)
                    elif s == 0:
                        options.append(fresh_acts[ticks[i]])
                    else:
                        options.append(waiting)
                else:
                    ticks = slots[(s + 1) % section_count]
                    if i >= len(ticks):
                        options.append(None)
                    elif s + 1 == section_count:
                        options.append(fresh_acts[ticks[i]])
                    else:
                        options.append(results[s, ticks[i] - 1])
            sources.append(pick(section_idx, options))
        source = jnp.concatenate(sources, axis=0)
        if w == 0:
            blocks = [source] + [swap(source, d * group) for d in range(1, far)]
        else:
            blocks = [onward(source, d * group) for d in range(far)]
        y = mix(spread(jnp.stack(blocks)), w_in[0], norm_gain, short_rows, long_rows, rank, tok_len)
        y_blocks = [y] + [swap(y, d * group) for d in range(1, far)]
        produced = project_out(spread(jnp.stack(y_blocks)), w_out[0], blocks[0], rank)
        made = [produced[i * tok_len : (i + 1) * tok_len] for i in range(slot_count)]
        for s in range(section_count):
            for i, k in enumerate(slots[s]):
                results[s, k] = made[i]
    outputs = []
    for k in range(tick_count):
        outputs.append(pick(section_idx, [results[s, k] for s in range(section_count)]))
    return jnp.stack(outputs)[None]


def solution(mesh):
    run = functools.partial(body, mesh.shape["section"], mesh.shape["dp"])
    return jax.shard_map(
        run,
        mesh=mesh,
        in_specs=(
            P(None, None, "dp"),
            P("section", None, "dp"),
            P("section", None),
            P("section", None, "dp", None),
            P("section", None, "dp", None),
            P("section", "dp", None),
            P("section", "dp"),
            P("section", None, "dp"),
        ),
        out_specs=P("section", None, None, "dp"),
        check_vma=False,
    )
```

time: 445 us -> 206 us (0.46)
  waiting for transfers between devices: 299 us -> 137 us
  matrix products: 98.9 us -> 0 us
  Pallas kernels: 0 us -> 32.7 us
  starting transfers between devices: 3.66 us -> 27.7 us
  local copies, waits for them, and re-layouts: 18.8 us -> 2.47 us
  between operations: 13.6 us -> 0.14 us
  other arithmetic: 9.86 us -> 5.18 us
    all_gather x6 -> x0, waiting for transfers between devices: 206 us -> none  [the longest x3 111 us: body(): lax.all_gather(y_local, 'dp', axis=1, tiled=True)]
    dot_general x10 -> x0, matrix products: 98.9 us -> none  [the longest x3 49.8 us: mixing(): jnp.einsum('cts,sc->tc', toeplitz, product, precision=lax.Precision.HIGHEST)]
    ppermute x2 -> x25, waiting for transfers between devices: 93 us -> 137 us  [the longest x21 116 us: swap(): return lax.ppermute(value, 'dp', [(r, r ^ offset) for r in range(dp_count)])]
    pallas_call x0 -> x4, Pallas kernels: none -> 32.7 us  [the longest x2 24.5 us: mix(): pl.pallas_call(kernel, grid_spec=pltpu.PrefetchScalarGridSpec(num_scalar_...]
    ppermute x2 -> x25, starting transfers between devices: 3.04 us -> 27.7 us  [the longest x21 20.9 us: swap(): return lax.ppermute(value, 'dp', [(r, r ^ offset) for r in range(dp_count)])]
    dot_general x1 -> x0, local copies, waits for them, and re-layouts: 17.6 us -> none  [build_toeplitz(): jnp.einsum('cj,tsj->cts', filter_vals, onehot, precision=lax.Precision.HI...]
  transfers between devices with their start and end apart: 8 -> 25, of which waited for: 8 -> 15; matrix products, arithmetic and copies ran while one was open for 7% -> 2% of each run, Pallas kernels for 0% -> 0%
where the time goes in v1:
time: 206 us; the launch traced here: 205 us
  waiting for transfers between devices  137 us (67%)
  Pallas kernels  32.7 us (16%)
  starting transfers between devices  27.7 us (13%)
  other arithmetic  5.18 us (3%)
  local copies, waits for them, and re-layouts  2.47 us (1%)
    ppermute x21, waiting for transfers between devices, swap(): return lax.ppermute(value, 'dp', [(r, r ^ offset) for r in range(dp_count)])  116 us
    pallas_call x2, Pallas kernels, mix(): pl.pallas_call(kernel, grid_spec=pltpu.PrefetchScalarGridSpec(num_scalar_...  24.5 us
    ppermute x4, waiting for transfers between devices, onward(): return lax.ppermute(value, ('section', 'dp'), pairs)  21.2 us
    ppermute x21, starting transfers between devices, swap(): return lax.ppermute(value, 'dp', [(r, r ^ offset) for r in range(dp_count)])  20.9 us
    pallas_call x2, Pallas kernels, project_out(): pl.pallas_call(functools.partial(out_kernel, group), grid_spec=pltpu.Pref...  8.19 us
    ppermute x4, starting transfers between devices, onward(): return lax.ppermute(value, ('section', 'dp'), pairs)  6.81 us
  transfers between devices with their start and end apart: 25, of which 15 were waited for; matrix products, arithmetic and copies ran while one was open for 2% of the time, Pallas kernels for 0%

profile of v1, /device:TPU:0, one launch (start us, length us, event | category | flops | bytes accessed | tf_op | source)
XLA Modules:
  0.0 205.3 jit_solution(657563675574887884)
XLA Ops:
  1.0 5.1 %collective-permute-start.2 = (bf16[256,512]{1,0:T(8,128)(2,1)S(1)}, bf16[256,512]{1,0:T(8,128)(2,1)S(1)}, u32[]{:S(2)}, u32[]{:S(2)}) collective-permute-start(bf16[256,512]{1,0:T(8,128)(2,1)S(1)} %get-tuple-element.13.refs_5_), channel_id=1, source_target_pairs={{0,12},{1,13},{2,14},{3,15},{4,8},{5,9},{6,10},{7,11},{8,4},{9,5},... | collective-permute-start | bytes 786440 | tf_op jit(solution)/shard_map/ppermute | solution.py:237
  6.8 6.6 %collective-permute-done.2 = bf16[256,512]{1,0:T(8,128)(2,1)S(1)} collective-permute-done((bf16[256,512]{1,0:T(8,128)(2,1)S(1)}, bf16[256,512]{1,0:T(8,128)(2,1)S(1)}, u32[]{:S(2)}, u32[]{:S(2)}) %collective-permute-start.2) | collective-permute-done | bytes 262176 | tf_op jit(solution)/shard_map/ppermute | solution.py:237
  13.4 15.0 %collective-permute-done.1 = bf16[256,512]{1,0:T(8,128)(2,1)S(1)} collective-permute-done((bf16[256,512]{1,0:T(8,128)(2,1)S(1)}, bf16[256,512]{1,0:T(8,128)(2,1)S(1)}, u32[]{:S(2)}, u32[]{:S(2)}) %collective-permute-start.1) | collective-permute-done | bytes 262176 | tf_op jit(solution)/shard_map/ppermute | solution.py:237
  30.2 22.7 %collective-permute-done.4.refs_2_ = bf16[4,256,512]{2,1,0:T(8,128)(2,1)S(1)} collective-permute-done((bf16[4,256,512]{2,1,0:T(8,128)(2,1)S(1)}, bf16[4,256,512]{2,1,0:T(8,128)(2,1)S(1)}, u32[]{:S(2)}, u32[]{:S(2)}) %collective-permute-start.4) | collective-permute-done | bytes 1048608 | tf_op jit(solution)/shard_map/ppermute | solution.py:237
  57.4 12.3 %norm_project_mix.2 = bf16[256,256]{1,0:T(8,128)(2,1)S(1)} custom-call(s32[1]{0:T(128)} %bitcast.rank_ref, bf16[4,256,512]{2,1,0:T(8,128)(2,1)S(1)} %pad_maximum_fusion.refs_0_, bf16[4,256,512]{2,1,0:T(8,128)(2,1)S(1)} %collective-permute-done.3.refs_1_, bf16[4,256,512]{2,1,0:T(8,128)(2,1)S(1)} %collective-permute-done.4.refs_2_, ...), custom_call_target="tpu_custom_call" | custom-call | flops 3221225472 | bytes 16777216 | tf_op jit(solution)/shard_map/norm_project_mix/pallas_call | solution.py:132
  69.7 2.4 %collective-permute-start.8 = (bf16[256,256]{1,0:T(8,128)(2,1)S(1)}, bf16[256,256]{1,0:T(8,128)(2,1)S(1)}, u32[]{:S(2)}, u32[]{:S(2)}) collective-permute-start(bf16[256,256]{1,0:T(8,128)(2,1)S(1)} %norm_project_mix.2), channel_id=1, source_target_pairs={{0,12},{1,13},{2,14},{3,15},{4,8},{5,9},{6,10},{7,11},{8,4},{9,5},... | collective-permute-start | bytes 393224 | tf_op jit(solution)/shard_map/ppermute | solution.py:237
  72.1 2.1 %collective-permute-start.6 = (bf16[256,256]{1,0:T(8,128)(2,1)S(1)}, bf16[256,256]{1,0:T(8,128)(2,1)S(1)}, u32[]{:S(2)}, u32[]{:S(2)}) collective-permute-start(bf16[256,256]{1,0:T(8,128)(2,1)S(1)} %norm_project_mix.2), channel_id=1, source_target_pairs={{0,4},{1,5},{2,6},{3,7},{4,0},{5,1},{6,2},{7,3},{8,12},{9,13},{10,... | collective-permute-start | bytes 393224 | tf_op jit(solution)/shard_map/ppermute | solution.py:237
  74.2 3.8 %collective-permute-done.8 = bf16[256,256]{1,0:T(8,128)(2,1)S(1)} collective-permute-done((bf16[256,256]{1,0:T(8,128)(2,1)S(1)}, bf16[256,256]{1,0:T(8,128)(2,1)S(1)}, u32[]{:S(2)}, u32[]{:S(2)}) %collective-permute-start.8) | collective-permute-done | bytes 131104 | tf_op jit(solution)/shard_map/ppermute | solution.py:237
  78.0 5.1 %collective-permute-done.7 = bf16[256,256]{1,0:T(8,128)(2,1)S(1)} collective-permute-done((bf16[256,256]{1,0:T(8,128)(2,1)S(1)}, bf16[256,256]{1,0:T(8,128)(2,1)S(1)}, u32[]{:S(2)}, u32[]{:S(2)}) %collective-permute-start.7) | collective-permute-done | bytes 131104 | tf_op jit(solution)/shard_map/ppermute | solution.py:237
  84.8 12.4 %collective-permute-done.10.refs_2_ = bf16[4,256,256]{2,1,0:T(8,128)(2,1)S(1)} collective-permute-done((bf16[4,256,256]{2,1,0:T(8,128)(2,1)S(1)}, bf16[4,256,256]{2,1,0:T(8,128)(2,1)S(1)}, u32[]{:S(2)}, u32[]{:S(2)}) %collective-permute-start.10) | collective-permute-done | bytes 524320 | tf_op jit(solution)/shard_map/ppermute | solution.py:237
  99.1 4.1 %project_out.2 = bf16[256,512]{1,0:T(8,128)(2,1)S(1)} custom-call(s32[1]{0:T(128)} %bitcast.rank_ref, bf16[4,256,256]{2,1,0:T(8,128)(2,1)S(1)} %pad_maximum_fusion.2.refs_0_, bf16[4,256,256]{2,1,0:T(8,128)(2,1)S(1)} %collective-permute-done.9.refs_1_, bf16[4,256,256]{2,1,0:T(8,128)(2,1)S(1)} %collective-permute-done.10.refs_2_, ...), custom_call_target="tpu_custom_call" | custom-call | flops 1073741824 | bytes 6291456 | tf_op jit(solution)/shard_map/project_out/pallas_call | solution.py:198
  104.2 3.4 %collective-permute-start.15 = (bf16[256,512]{1,0:T(8,128)(2,1)S(1)}, bf16[256,512]{1,0:T(8,128)(2,1)S(1)}, u32[]{:S(2)}, u32[]{:S(2)}) collective-permute-start(bf16[256,512]{1,0:T(8,128)(2,1)S(1)} %pad_maximum_fusion.5), channel_id=1, source_target_pairs={{0,28},{1,29},{2,30},{3,31},{4,24},{5,25},{6,26},{7,27},{8,20},{9,... | collective-permute-start | bytes 786440 | tf_op jit(solution)/shard_map/ppermute | solution.py:245
  107.5 3.0 %collective-permute-start.13 = (bf16[256,512]{1,0:T(8,128)(2,1)S(1)}, bf16[256,512]{1,0:T(8,128)(2,1)S(1)}, u32[]{:S(2)}, u32[]{:S(2)}) collective-permute-start(bf16[256,512]{1,0:T(8,128)(2,1)S(1)} %pad_maximum_fusion.5), channel_id=1, source_target_pairs={{0,20},{1,21},{2,22},{3,23},{4,16},{5,17},{6,18},{7,19},{8,28},{9,... | collective-permute-start | bytes 786440 | tf_op jit(solution)/shard_map/ppermute | solution.py:245
  111.0 5.3 %collective-permute-done.15 = bf16[256,512]{1,0:T(8,128)(2,1)S(1)} collective-permute-done((bf16[256,512]{1,0:T(8,128)(2,1)S(1)}, bf16[256,512]{1,0:T(8,128)(2,1)S(1)}, u32[]{:S(2)}, u32[]{:S(2)}) %collective-permute-start.15) | collective-permute-done | bytes 262176 | tf_op jit(solution)/shard_map/ppermute | solution.py:245
  116.3 15.9 %collective-permute-done.14 = bf16[256,512]{1,0:T(8,128)(2,1)S(1)} collective-permute-done((bf16[256,512]{1,0:T(8,128)(2,1)S(1)}, bf16[256,512]{1,0:T(8,128)(2,1)S(1)}, u32[]{:S(2)}, u32[]{:S(2)}) %collective-permute-start.14) | collective-permute-done | bytes 262176 | tf_op jit(solution)/shard_map/ppermute | solution.py:245
  133.9 22.8 %collective-permute-done.17.refs_2_ = bf16[4,256,512]{2,1,0:T(8,128)(2,1)S(1)} collective-permute-done((bf16[4,256,512]{2,1,0:T(8,128)(2,1)S(1)}, bf16[4,256,512]{2,1,0:T(8,128)(2,1)S(1)}, u32[]{:S(2)}, u32[]{:S(2)}) %collective-permute-start.17) | collective-permute-done | bytes 1048608 | tf_op jit(solution)/shard_map/ppermute | solution.py:237
  156.7 2.7 %collective-permute-done.18.refs_3_ = bf16[4,256,512]{2,1,0:T(8,128)(2,1)S(1)} collective-permute-done((bf16[4,256,512]{2,1,0:T(8,128)(2,1)S(1)}, bf16[4,256,512]{2,1,0:T(8,128)(2,1)S(1)}, u32[]{:S(2)}, u32[]{:S(2)}) %collective-permute-start.18) | collective-permute-done | bytes 1048608 | tf_op jit(solution)/shard_map/ppermute | solution.py:237
  159.3 12.1 %norm_project_mix.3 = bf16[256,256]{1,0:T(8,128)(2,1)S(1)} custom-call(s32[1]{0:T(128)} %bitcast.rank_ref, bf16[4,256,512]{2,1,0:T(8,128)(2,1)S(1)} %pad_maximum_fusion.1.refs_0_, bf16[4,256,512]{2,1,0:T(8,128)(2,1)S(1)} %collective-permute-done.16.refs_1_, bf16[4,256,512]{2,1,0:T(8,128)(2,1)S(1)} %collective-permute-done.17.refs_2_, ...), custom_call_target="tpu_custom_call" | custom-call | flops 3221225472 | bytes 16777216 | tf_op jit(solution)/shard_map/norm_project_mix/pallas_call | solution.py:132
  171.5 3.2 %collective-permute-start.21 = (bf16[256,256]{1,0:T(8,128)(2,1)S(1)}, bf16[256,256]{1,0:T(8,128)(2,1)S(1)}, u32[]{:S(2)}, u32[]{:S(2)}) collective-permute-start(bf16[256,256]{1,0:T(8,128)(2,1)S(1)} %norm_project_mix.3), channel_id=1, source_target_pairs={{0,12},{1,13},{2,14},{3,15},{4,8},{5,9},{6,10},{7,11},{8,4},{9,5},... | collective-permute-start | bytes 393224 | tf_op jit(solution)/shard_map/ppermute | solution.py:237
  175.9 3.9 %collective-permute-done.21 = bf16[256,256]{1,0:T(8,128)(2,1)S(1)} collective-permute-done((bf16[256,256]{1,0:T(8,128)(2,1)S(1)}, bf16[256,256]{1,0:T(8,128)(2,1)S(1)}, u32[]{:S(2)}, u32[]{:S(2)}) %collective-permute-start.21) | collective-permute-done | bytes 131104 | tf_op jit(solution)/shard_map/ppermute | solution.py:237
  179.8 4.7 %collective-permute-done.20 = bf16[256,256]{1,0:T(8,128)(2,1)S(1)} collective-permute-done((bf16[256,256]{1,0:T(8,128)(2,1)S(1)}, bf16[256,256]{1,0:T(8,128)(2,1)S(1)}, u32[]{:S(2)}, u32[]{:S(2)}) %collective-permute-start.20) | collective-permute-done | bytes 131104 | tf_op jit(solution)/shard_map/ppermute | solution.py:237
  186.2 12.3 %collective-permute-done.23.refs_2_ = bf16[4,256,256]{2,1,0:T(8,128)(2,1)S(1)} collective-permute-done((bf16[4,256,256]{2,1,0:T(8,128)(2,1)S(1)}, bf16[4,256,256]{2,1,0:T(8,128)(2,1)S(1)}, u32[]{:S(2)}, u32[]{:S(2)}) %collective-permute-start.23) | collective-permute-done | bytes 524320 | tf_op jit(solution)/shard_map/ppermute | solution.py:237
  198.5 1.9 collective-permute-done.24.refs_3_
  200.4 4.1 %project_out.3 = bf16[256,512]{1,0:T(8,128)(2,1)S(1)} custom-call(s32[1]{0:T(128)} %bitcast.rank_ref, bf16[4,256,256]{2,1,0:T(8,128)(2,1)S(1)} %pad_maximum_fusion.3.refs_0_, bf16[4,256,256]{2,1,0:T(8,128)(2,1)S(1)} %collective-permute-done.22.refs_1_, bf16[4,256,256]{2,1,0:T(8,128)(2,1)S(1)} %collective-permute-done.23.refs_2_, ...), custom_call_target="tpu_custom_call" | custom-call | flops 1073741824 | bytes 6291456 | tf_op jit(solution)/shard_map/project_out/pallas_call | solution.py:198
  (49 shorter events, 18.2 us)
Async XLA Ops:
  1.0 12.4 %collective-permute-start.2 = (bf16[256,512]{1,0:T(8,128)(2,1)S(1)}, bf16[256,512]{1,0:T(8,128)(2,1)S(1)}, u32[]{:S(2)}, u32[]{:S(2)}) collective-permute-start(bf16[256,512]{1,0:T(8,128)(2,1)S(1)} %get-tuple-element.13.refs_5_), channel_id=1, source_target_pairs={{0,12},{1,13},{2,14},{3,15},{4,8},{5,9},{6,10},{7,11},{8,4},{9,5},... | collective-permute-start | bytes 786440 | tf_op jit(solution)/shard_map/ppermute | solution.py:237
  6.2 22.3 %collective-permute-start.1 = (bf16[256,512]{1,0:T(8,128)(2,1)S(1)}, bf16[256,512]{1,0:T(8,128)(2,1)S(1)}, u32[]{:S(2)}, u32[]{:S(2)}) collective-permute-start(bf16[256,512]{1,0:T(8,128)(2,1)S(1)} %get-tuple-element.13.refs_5_), channel_id=1, source_target_pairs={{0,8},{1,9},{2,10},{3,11},{4,12},{5,13},{6,14},{7,15},{8,0},{9,1},... | collective-permute-start | bytes 786440 | tf_op jit(solution)/shard_map/ppermute | solution.py:237
  6.2 22.3 %collective-permute-start = (bf16[256,512]{1,0:T(8,128)(2,1)S(1)}, bf16[256,512]{1,0:T(8,128)(2,1)S(1)}, u32[]{:S(2)}, u32[]{:S(2)}) collective-permute-start(bf16[256,512]{1,0:T(8,128)(2,1)S(1)} %get-tuple-element.13.refs_5_), channel_id=1, source_target_pairs={{0,4},{1,5},{2,6},{3,7},{4,0},{5,1},{6,2},{7,3},{8,12},{9,13},{10,... | collective-permute-start | bytes 786440 | tf_op jit(solution)/shard_map/ppermute | solution.py:237
  28.6 24.3 %collective-permute-start.4 = (bf16[4,256,512]{2,1,0:T(8,128)(2,1)S(1)}, bf16[4,256,512]{2,1,0:T(8,128)(2,1)S(1)}, u32[]{:S(2)}, u32[]{:S(2)}) collective-permute-start(bf16[4,256,512]{2,1,0:T(8,128)(2,1)S(1)} %pad_maximum_fusion.refs_0_), channel_id=1, source_target_pairs={{0,2},{1,3},{2,0},{3,1},{4,6},{5,7},{6,4},{7,5},{8,10},{9,11},{10,... | collective-permute-start | bytes 3145736 | tf_op jit(solution)/shard_map/ppermute | solution.py:237
  30.2 26.4 %collective-permute-start.3 = (bf16[4,256,512]{2,1,0:T(8,128)(2,1)S(1)}, bf16[4,256,512]{2,1,0:T(8,128)(2,1)S(1)}, u32[]{:S(2)}, u32[]{:S(2)}) collective-permute-start(bf16[4,256,512]{2,1,0:T(8,128)(2,1)S(1)} %pad_maximum_fusion.refs_0_), channel_id=1, source_target_pairs={{0,1},{1,0},{2,3},{3,2},{4,5},{5,4},{6,7},{7,6},{8,9},{9,8},{10,11... | collective-permute-start | bytes 3145736 | tf_op jit(solution)/shard_map/ppermute | solution.py:237
  52.9 3.7 %collective-permute-start.5 = (bf16[4,256,512]{2,1,0:T(8,128)(2,1)S(1)}, bf16[4,256,512]{2,1,0:T(8,128)(2,1)}, u32[]{:S(2)}, u32[]{:S(2)}) collective-permute-start(bf16[4,256,512]{2,1,0:T(8,128)(2,1)S(1)} %collective-permute-done.4.refs_2_), channel_id=1, source_target_pairs={{0,1},{1,0},{2,3},{3,2},{4,5},{5,4},{6,7},{7,6},{8,9},{9,8},{10,11... | collective-permute-start | bytes 3145736 | tf_op jit(solution)/shard_map/ppermute | solution.py:237
  69.7 8.3 %collective-permute-start.8 = (bf16[256,256]{1,0:T(8,128)(2,1)S(1)}, bf16[256,256]{1,0:T(8,128)(2,1)S(1)}, u32[]{:S(2)}, u32[]{:S(2)}) collective-permute-start(bf16[256,256]{1,0:T(8,128)(2,1)S(1)} %norm_project_mix.2), channel_id=1, source_target_pairs={{0,12},{1,13},{2,14},{3,15},{4,8},{5,9},{6,10},{7,11},{8,4},{9,5},... | collective-permute-start | bytes 393224 | tf_op jit(solution)/shard_map/ppermute | solution.py:237
  72.1 11.1 %collective-permute-start.7 = (bf16[256,256]{1,0:T(8,128)(2,1)S(1)}, bf16[256,256]{1,0:T(8,128)(2,1)S(1)}, u32[]{:S(2)}, u32[]{:S(2)}) collective-permute-start(bf16[256,256]{1,0:T(8,128)(2,1)S(1)} %norm_project_mix.2), channel_id=1, source_target_pairs={{0,8},{1,9},{2,10},{3,11},{4,12},{5,13},{6,14},{7,15},{8,0},{9,1},... | collective-permute-start | bytes 393224 | tf_op jit(solution)/shard_map/ppermute | solution.py:237
  72.1 11.1 %collective-permute-start.6 = (bf16[256,256]{1,0:T(8,128)(2,1)S(1)}, bf16[256,256]{1,0:T(8,128)(2,1)S(1)}, u32[]{:S(2)}, u32[]{:S(2)}) collective-permute-start(bf16[256,256]{1,0:T(8,128)(2,1)S(1)} %norm_project_mix.2), channel_id=1, source_target_pairs={{0,4},{1,5},{2,6},{3,7},{4,0},{5,1},{6,2},{7,3},{8,12},{9,13},{10,... | collective-permute-start | bytes 393224 | tf_op jit(solution)/shard_map/ppermute | solution.py:237
  83.2 13.9 %collective-permute-start.10 = (bf16[4,256,256]{2,1,0:T(8,128)(2,1)S(1)}, bf16[4,256,256]{2,1,0:T(8,128)(2,1)S(1)}, u32[]{:S(2)}, u32[]{:S(2)}) collective-permute-start(bf16[4,256,256]{2,1,0:T(8,128)(2,1)S(1)} %pad_maximum_fusion.2.refs_0_), channel_id=1, source_target_pairs={{0,2},{1,3},{2,0},{3,1},{4,6},{5,7},{6,4},{7,5},{8,10},{9,11},{10,... | collective-permute-start | bytes 1572872 | tf_op jit(solution)/shard_map/ppermute | solution.py:237
  84.8 12.4 %collective-permute-start.9 = (bf16[4,256,256]{2,1,0:T(8,128)(2,1)S(1)}, bf16[4,256,256]{2,1,0:T(8,128)(2,1)S(1)}, u32[]{:S(2)}, u32[]{:S(2)}) collective-permute-start(bf16[4,256,256]{2,1,0:T(8,128)(2,1)S(1)} %pad_maximum_fusion.2.refs_0_), channel_id=1, source_target_pairs={{0,1},{1,0},{2,3},{3,2},{4,5},{5,4},{6,7},{7,6},{8,9},{9,8},{10,11... | collective-permute-start | bytes 1572872 | tf_op jit(solution)/shard_map/ppermute | solution.py:237
  104.2 12.1 %collective-permute-start.15 = (bf16[256,512]{1,0:T(8,128)(2,1)S(1)}, bf16[256,512]{1,0:T(8,128)(2,1)S(1)}, u32[]{:S(2)}, u32[]{:S(2)}) collective-permute-start(bf16[256,512]{1,0:T(8,128)(2,1)S(1)} %pad_maximum_fusion.5), channel_id=1, source_target_pairs={{0,28},{1,29},{2,30},{3,31},{4,24},{5,25},{6,26},{7,27},{8,20},{9,... | collective-permute-start | bytes 786440 | tf_op jit(solution)/shard_map/ppermute | solution.py:245
  107.5 24.7 %collective-permute-start.14 = (bf16[256,512]{1,0:T(8,128)(2,1)S(1)}, bf16[256,512]{1,0:T(8,128)(2,1)S(1)}, u32[]{:S(2)}, u32[]{:S(2)}) collective-permute-start(bf16[256,512]{1,0:T(8,128)(2,1)S(1)} %pad_maximum_fusion.5), channel_id=1, source_target_pairs={{0,24},{1,25},{2,26},{3,27},{4,28},{5,29},{6,30},{7,31},{8,16},{9,... | collective-permute-start | bytes 786440 | tf_op jit(solution)/shard_map/ppermute | solution.py:245
  107.5 24.7 %collective-permute-start.13 = (bf16[256,512]{1,0:T(8,128)(2,1)S(1)}, bf16[256,512]{1,0:T(8,128)(2,1)S(1)}, u32[]{:S(2)}, u32[]{:S(2)}) collective-permute-start(bf16[256,512]{1,0:T(8,128)(2,1)S(1)} %pad_maximum_fusion.5), channel_id=1, source_target_pairs={{0,20},{1,21},{2,22},{3,23},{4,16},{5,17},{6,18},{7,19},{8,28},{9,... | collective-permute-start | bytes 786440 | tf_op jit(solution)/shard_map/ppermute | solution.py:245
  110.5 21.7 %collective-permute-start.12 = (bf16[256,512]{1,0:T(8,128)(2,1)S(1)}, bf16[256,512]{1,0:T(8,128)(2,1)S(1)}, u32[]{:S(2)}, u32[]{:S(2)}) collective-permute-start(bf16[256,512]{1,0:T(8,128)(2,1)S(1)} %pad_maximum_fusion.5), channel_id=1, source_target_pairs={{0,16},{1,17},{2,18},{3,19},{4,20},{5,21},{6,22},{7,23},{8,24},{9,... | collective-permute-start | bytes 786440 | tf_op jit(solution)/shard_map/ppermute | solution.py:245
  132.4 24.3 %collective-permute-start.17 = (bf16[4,256,512]{2,1,0:T(8,128)(2,1)S(1)}, bf16[4,256,512]{2,1,0:T(8,128)(2,1)S(1)}, u32[]{:S(2)}, u32[]{:S(2)}) collective-permute-start(bf16[4,256,512]{2,1,0:T(8,128)(2,1)S(1)} %pad_maximum_fusion.1.refs_0_), channel_id=1, source_target_pairs={{0,2},{1,3},{2,0},{3,1},{4,6},{5,7},{6,4},{7,5},{8,10},{9,11},{10,... | collective-permute-start | bytes 3145736 | tf_op jit(solution)/shard_map/ppermute | solution.py:237
  133.9 22.8 %collective-permute-start.16 = (bf16[4,256,512]{2,1,0:T(8,128)(2,1)S(1)}, bf16[4,256,512]{2,1,0:T(8,128)(2,1)S(1)}, u32[]{:S(2)}, u32[]{:S(2)}) collective-permute-start(bf16[4,256,512]{2,1,0:T(8,128)(2,1)S(1)} %pad_maximum_fusion.1.refs_0_), channel_id=1, source_target_pairs={{0,1},{1,0},{2,3},{3,2},{4,5},{5,4},{6,7},{7,6},{8,9},{9,8},{10,11... | collective-permute-start | bytes 3145736 | tf_op jit(solution)/shard_map/ppermute | solution.py:237
  156.7 2.7 %collective-permute-start.18 = (bf16[4,256,512]{2,1,0:T(8,128)(2,1)S(1)}, bf16[4,256,512]{2,1,0:T(8,128)(2,1)S(1)}, u32[]{:S(2)}, u32[]{:S(2)}) collective-permute-start(bf16[4,256,512]{2,1,0:T(8,128)(2,1)S(1)} %collective-permute-done.17.refs_2_), channel_id=1, source_target_pairs={{0,1},{1,0},{2,3},{3,2},{4,5},{5,4},{6,7},{7,6},{8,9},{9,8},{10,11... | collective-permute-start | bytes 3145736 | tf_op jit(solution)/shard_map/ppermute | solution.py:237
  171.5 8.3 %collective-permute-start.21 = (bf16[256,256]{1,0:T(8,128)(2,1)S(1)}, bf16[256,256]{1,0:T(8,128)(2,1)S(1)}, u32[]{:S(2)}, u32[]{:S(2)}) collective-permute-start(bf16[256,256]{1,0:T(8,128)(2,1)S(1)} %norm_project_mix.3), channel_id=1, source_target_pairs={{0,12},{1,13},{2,14},{3,15},{4,8},{5,9},{6,10},{7,11},{8,4},{9,5},... | collective-permute-start | bytes 393224 | tf_op jit(solution)/shard_map/ppermute | solution.py:237
  174.7 9.9 %collective-permute-start.20 = (bf16[256,256]{1,0:T(8,128)(2,1)S(1)}, bf16[256,256]{1,0:T(8,128)(2,1)S(1)}, u32[]{:S(2)}, u32[]{:S(2)}) collective-permute-start(bf16[256,256]{1,0:T(8,128)(2,1)S(1)} %norm_project_mix.3), channel_id=1, source_target_pairs={{0,8},{1,9},{2,10},{3,11},{4,12},{5,13},{6,14},{7,15},{8,0},{9,1},... | collective-permute-start | bytes 393224 | tf_op jit(solution)/shard_map/ppermute | solution.py:237
  174.7 9.9 %collective-permute-start.19 = (bf16[256,256]{1,0:T(8,128)(2,1)S(1)}, bf16[256,256]{1,0:T(8,128)(2,1)S(1)}, u32[]{:S(2)}, u32[]{:S(2)}) collective-permute-start(bf16[256,256]{1,0:T(8,128)(2,1)S(1)} %norm_project_mix.3), channel_id=1, source_target_pairs={{0,4},{1,5},{2,6},{3,7},{4,0},{5,1},{6,2},{7,3},{8,12},{9,13},{10,... | collective-permute-start | bytes 393224 | tf_op jit(solution)/shard_map/ppermute | solution.py:237
  184.6 13.9 %collective-permute-start.23 = (bf16[4,256,256]{2,1,0:T(8,128)(2,1)S(1)}, bf16[4,256,256]{2,1,0:T(8,128)(2,1)S(1)}, u32[]{:S(2)}, u32[]{:S(2)}) collective-permute-start(bf16[4,256,256]{2,1,0:T(8,128)(2,1)S(1)} %pad_maximum_fusion.3.refs_0_), channel_id=1, source_target_pairs={{0,2},{1,3},{2,0},{3,1},{4,6},{5,7},{6,4},{7,5},{8,10},{9,11},{10,... | collective-permute-start | bytes 1572872 | tf_op jit(solution)/shard_map/ppermute | solution.py:237
  186.2 12.3 %collective-permute-start.22 = (bf16[4,256,256]{2,1,0:T(8,128)(2,1)S(1)}, bf16[4,256,256]{2,1,0:T(8,128)(2,1)S(1)}, u32[]{:S(2)}, u32[]{:S(2)}) collective-permute-start(bf16[4,256,256]{2,1,0:T(8,128)(2,1)S(1)} %pad_maximum_fusion.3.refs_0_), channel_id=1, source_target_pairs={{0,1},{1,0},{2,3},{3,2},{4,5},{5,4},{6,7},{7,6},{8,9},{9,8},{10,11... | collective-permute-start | bytes 1572872 | tf_op jit(solution)/shard_map/ppermute | solution.py:237
  198.5 1.9 collective-permute-start.24
  (3 other events, 104.7 us)

commit v2 on v1

--- a/solution.py
+++ b/solution.py
@@ -1,4 +1,6 @@
 import functools
+import itertools
+import math
 
 import jax
 import jax.numpy as jnp
@@ -23,16 +25,15 @@
             best = min(range(first, last + 1), key=lambda w: (len(waves[w][s]), w))
             where[s, k] = (best, len(waves[best][s]))
             waves[best][s].append(k)
-    return waves, where
-
-
-def split_dp(dp_count):
-    core = 2 if dp_count % 2 == 0 else 1
-    chips = dp_count // core
-    near = 1
-    while near * near * 4 <= chips:
-        near *= 2
-    return chips // near, near, core
+    return waves
+
+
+def core_count(dp_count):
+    return 2 if dp_count % 2 == 0 else 1
+
+
+def step_count(chips):
+    return math.gcd(chips, 4)
 
 
 def pick(section_idx, options):
@@ -58,8 +59,7 @@
     w_ref, gain_ref, short_ref, long_ref, y_ref = refs[group : group + 5]
     norm_ref, acc_ref, sq_ref, pad_ref = refs[group + 5 :]
     step = pl.program_id(0)
-    feat = pieces[0].shape[2]
-    rows = pieces[0].shape[1]
+    chips, rows, feat = pieces[0].shape
     chan = w_ref.shape[1]
     low = lax.rem(rank_ref[0], group)
 
@@ -68,15 +68,15 @@
         acc_ref[...] = jnp.zeros_like(acc_ref)
         sq_ref[...] = jnp.zeros_like(sq_ref)
 
-    for q in range(group):
-        start = pl.multiple_of((low ^ q) * feat, feat)
-        wide = pieces[q][0].astype(jnp.float32)
+    for j, q in itertools.product(range(chips), range(group)):
+        start = pl.multiple_of((j * group + (low ^ q)) * feat, feat)
+        wide = pieces[q][j].astype(jnp.float32)
         norm_ref[:, pl.ds(start, feat)] = (wide * gain_ref[:, pl.ds(start, feat)]).astype(jnp.bfloat16)
         squares = wide * wide
         lanes = min(feat, 128)
         part = squares[:, :lanes]
-        for j in range(1, feat // lanes):
-            part = part + squares[:, j * lanes : (j + 1) * lanes]
+        for n in range(1, feat // lanes):
+            part = part + squares[:, n * lanes : (n + 1) * lanes]
         sq_ref[...] += part
     for i in range(3):
         acc_ref[i] += lax.dot_general(
@@ -125,19 +125,20 @@
 
 def mix(pieces, w_in, gain, short_rows, long_rows, rank, tok_len):
     group = len(pieces)
-    far, rows, feat = pieces[0].shape
+    chips, rows, feat = pieces[0].shape
     branches, chan, model_width = w_in.shape
-    wide = group * feat
+    steps = step_count(chips)
+    wide = model_width // steps
     kernel = functools.partial(mix_kernel, group, tok_len, model_width)
     return pl.pallas_call(
         kernel,
         grid_spec=pltpu.PrefetchScalarGridSpec(
             num_scalar_prefetch=1,
-            grid=(far,),
-            in_specs=[pl.BlockSpec((1, rows, feat), lambda d, r: (d, 0, 0))] * group
+            grid=(steps,),
+            in_specs=[pl.BlockSpec((chips // steps, rows, feat), lambda d, r: (d, 0, 0))] * group
             + [
-                pl.BlockSpec((branches, chan, wide), lambda d, r: (0, 0, (r[0] // group) ^ d)),
-                pl.BlockSpec((1, wide), lambda d, r: (0, (r[0] // group) ^ d)),
+                pl.BlockSpec((branches, chan, wide), lambda d, r: (0, 0, d)),
+                pl.BlockSpec((1, wide), lambda d, r: (0, d)),
                 pl.BlockSpec(short_rows.shape, lambda d, r: (0, 0)),
                 pl.BlockSpec(long_rows.shape, lambda d, r: (0, 0)),
             ],
@@ -166,7 +167,7 @@
     pieces = refs[:group]
     w_ref, own_ref, result_ref, cat_ref, acc_ref = refs[group:]
     step = pl.program_id(0)
-    chan = pieces[0].shape[2]
+    chips, _, chan = pieces[0].shape
     low = lax.rem(rank_ref[0], group)
 
     @pl.when(step == 0)
@@ -174,15 +175,15 @@
         acc_ref[...] = own_ref[...].astype(jnp.float32)
 
     if chan % 128 == 0:
-        for q in range(group):
-            start = pl.multiple_of((low ^ q) * chan, chan)
-            cat_ref[:, pl.ds(start, chan)] = pieces[q][0]
+        for j, q in itertools.product(range(chips), range(group)):
+            start = pl.multiple_of((j * group + (low ^ q)) * chan, chan)
+            cat_ref[:, pl.ds(start, chan)] = pieces[q][j]
         acc_ref[...] += jnp.dot(cat_ref[...], w_ref[...], preferred_element_type=jnp.float32)
     else:
-        for q in range(group):
-            start = pl.multiple_of((low ^ q) * chan, chan)
+        for j, q in itertools.product(range(chips), range(group)):
+            start = pl.multiple_of((j * group + (low ^ q)) * chan, chan)
             acc_ref[...] += jnp.dot(
-                pieces[q][0], w_ref[pl.ds(start, chan), :], preferred_element_type=jnp.float32
+                pieces[q][j], w_ref[pl.ds(start, chan), :], preferred_element_type=jnp.float32
             )
 
     @pl.when(step == pl.num_programs(0) - 1)
@@ -192,17 +193,18 @@
 
 def project_out(pieces, w_out, own, rank):
     group = len(pieces)
-    far, rows, chan = pieces[0].shape
+    chips, rows, chan = pieces[0].shape
     feat = w_out.shape[1]
-    wide = group * chan
+    steps = step_count(chips)
+    wide = w_out.shape[0] // steps
     return pl.pallas_call(
         functools.partial(out_kernel, group),
         grid_spec=pltpu.PrefetchScalarGridSpec(
             num_scalar_prefetch=1,
-            grid=(far,),
-            in_specs=[pl.BlockSpec((1, rows, chan), lambda d, r: (d, 0, 0))] * group
+            grid=(steps,),
+            in_specs=[pl.BlockSpec((chips // steps, rows, chan), lambda d, r: (d, 0, 0))] * group
             + [
-                pl.BlockSpec((wide, feat), lambda d, r: ((r[0] // group) ^ d, 0)),
+                pl.BlockSpec((wide, feat), lambda d, r: (d, 0)),
                 pl.BlockSpec((rows, feat), lambda d, r: (0, 0)),
             ],
             out_specs=pl.BlockSpec((rows, feat), lambda d, r: (0, 0)),
@@ -226,31 +228,17 @@
 
 def body(section_count, dp_count, fresh_acts, carried, norm_gain, w_in, short_filter, filter_taps, decay_rate, w_out):
     tick_count, tok_len, _ = fresh_acts.shape
-    far, near, core = split_dp(dp_count)
-    group = near * core
-    waves, where = plan(section_count, tick_count)
+    core = core_count(dp_count)
+    same_core = [list(range(c, dp_count, core)) for c in range(core)]
+    waves = plan(section_count, tick_count)
     section_idx = lax.axis_index("section")
-    rank_idx = lax.axis_index("dp")
-    rank = rank_idx.astype(jnp.int32).reshape(1)
-
-    def swap(value, offset):
-        return lax.ppermute(value, "dp", [(r, r ^ offset) for r in range(dp_count)])
-
-    def onward(value, offset):
-        pairs = [
-            (s * dp_count + r, (s + 1) % section_count * dp_count + (r ^ offset))
-            for s in range(section_count)
-            for r in range(dp_count)
-        ]
-        return lax.ppermute(value, ("section", "dp"), pairs)
-
-    def spread(line):
-        pieces = []
-        for x in range(near):
-            piece = line if x == 0 else swap(line, x * core)
-            pieces.append(piece)
-            for c in range(1, core):
-                pieces.append(swap(piece, c))
+    rank = lax.axis_index("dp").astype(jnp.int32).reshape(1)
+
+    def spread(own):
+        line = lax.all_gather(own, "dp", axis=0, axis_index_groups=same_core)
+        pieces = [line]
+        for c in range(1, core):
+            pieces.append(lax.ppermute(line, "dp", [(r, r ^ c) for r in range(dp_count)]))
         return pieces
 
     lags = jnp.arange(filter_taps.shape[2], dtype=jnp.float32)
@@ -282,15 +270,13 @@
                     else:
                         options.append(results[s, ticks[i] - 1])
             sources.append(pick(section_idx, options))
-        source = jnp.concatenate(sources, axis=0)
-        if w == 0:
-            blocks = [source] + [swap(source, d * group) for d in range(1, far)]
-        else:
-            blocks = [onward(source, d * group) for d in range(far)]
-        y = mix(spread(jnp.stack(blocks)), w_in[0], norm_gain, short_rows, long_rows, rank, tok_len)
-        y_blocks = [y] + [swap(y, d * group) for d in range(1, far)]
-        produced = project_out(spread(jnp.stack(y_blocks)), w_out[0], blocks[0], rank)
-        made = [produced[i * tok_len : (i + 1) * tok_len] for i in range(slot_count)]
+        if w > 0:
+            shift = [(s, (s + 1) % section_count) for s in range(section_count)]
+            sources = [lax.ppermute(source, "section", shift) for source in sources]
+        made = []
+        for own in sources:
+            y = mix(spread(own), w_in[0], norm_gain, short_rows, long_rows, rank, tok_len)
+            made.append(project_out(spread(y), w_out[0], own, rank))
         for s in range(section_count):
             for i, k in enumerate(slots[s]):
                 results[s, k] = made[i]

time: 206 us -> 301 us (1.46)
  blocking collectives: 0 us -> 127 us
  waiting for transfers between devices: 137 us -> 96.2 us
  starting transfers between devices: 27.7 us -> 4.28 us
  between operations: 0.14 us -> 13.3 us
  Pallas kernels: 32.7 us -> 45.6 us
  local copies, waits for them, and re-layouts: 2.47 us -> 9.96 us
    all_gather x0 -> x4, blocking collectives: none -> 127 us  [spread(): line = lax.all_gather(own, 'dp', axis=0, axis_index_groups=same_core)]
    ppermute x25 -> x10, waiting for transfers between devices: 137 us -> 12.7 us  [the longest x2 7.8 us: body(): sources = [lax.ppermute(source, 'section', shift) for source in sources]]
    all_gather x0 -> x4, waiting for transfers between devices: none -> 82.7 us  [spread(): line = lax.all_gather(own, 'dp', axis=0, axis_index_groups=same_core)]
    ppermute x25 -> x10, starting transfers between devices: 27.7 us -> 4.15 us  [the longest x2 3.56 us: body(): sources = [lax.ppermute(source, 'section', shift) for source in sources]]
    pallas_call x2 -> x4, Pallas kernels: 24.5 us -> 40.1 us  [mix(): pl.pallas_call(kernel, grid_spec=pltpu.PrefetchScalarGridSpec(num_scalar_...]
    unnamed x6 -> x30, local copies, waits for them, and re-layouts: 2.46 us -> 9.95 us
    pallas_call x2 -> x4, Pallas kernels: 8.19 us -> 5.54 us  [project_out(): pl.pallas_call(functools.partial(out_kernel, group), grid_spec=pltpu.Pref...]
  transfers between devices with their start and end apart: 25 -> 14, of which waited for: 15 -> 8; matrix products, arithmetic and copies ran while one was open for 2% -> 1% of each run, Pallas kernels for 0% -> 15%
where the time goes in v2:
time: 301 us; the launch traced here: 300 us
  blocking collectives  127 us (42%)
  waiting for transfers between devices  96.2 us (32%)
  Pallas kernels  45.6 us (15%)
  between operations  13.3 us (4%)
  local copies, waits for them, and re-layouts  9.96 us (3%)
  starting transfers between devices  4.28 us (1%)
  other arithmetic  4.17 us (1%)
    all_gather x4, blocking collectives, spread(): line = lax.all_gather(own, 'dp', axis=0, axis_index_groups=same_core)  127 us
    all_gather x4, waiting for transfers between devices, spread(): line = lax.all_gather(own, 'dp', axis=0, axis_index_groups=same_core)  82.7 us
    pallas_call x4, Pallas kernels, mix(): pl.pallas_call(kernel, grid_spec=pltpu.PrefetchScalarGridSpec(num_scalar_...  40.1 us
    unnamed x30, local copies, waits for them, and re-layouts  9.95 us
    ppermute x2, waiting for transfers between devices, body(): sources = [lax.ppermute(source, 'section', shift) for source in sources]  7.8 us
  transfers between devices with their start and end apart: 14, of which 8 were waited for; matrix products, arithmetic and copies ran while one was open for 1% of the time, Pallas kernels for 15%

profile of v2, /device:TPU:0, one launch (start us, length us, event | category | flops | bytes accessed | tf_op | source)
XLA Modules:
  0.0 300.4 jit_solution(9762776562869184595)
XLA Ops:
  6.5 1.7 slice_select_fusion
  9.1 43.3 %all-gather.13.cloned.1.call-done.refs_0_ = bf16[8,128,512]{2,1,0:T(8,128)(2,1)} async-done(((bf16[1,128,512]{2,1,0:T(8,128)(2,1)}), bf16[8,128,512]{2,1,0:T(8,128)(2,1)}) %all-gather.13.cloned.1.call-update) | async-done | bytes 1048592 | tf_op jit(solution)/shard_map/all_gather | solution.py:238
  57.2 9.9 %norm_project_mix.6 = bf16[128,256]{1,0:T(8,128)(2,1)S(1)} custom-call(s32[1]{0:T(128)} %bitcast.rank_ref, bf16[8,128,512]{2,1,0:T(8,128)(2,1)S(1)} %copy-done.6, bf16[8,128,512]{2,1,0:T(8,128)(2,1)S(1)} %collective-permute-done.5.refs_1_, bf16[3,256,8192]{2,1,0:T(8,128)(2,1)} %bitcast.51, f32[1,8192]{1,0:T(1,128)S(1)} %copy-done.8, ...), custom_call_target="tpu_custom_call" | custom-call | flops 1610612736 | bytes 14680064 | tf_op jit(solution)/shard_map/norm_project_mix/pallas_call | solution.py:133
  67.2 32.0 %all-gather.3 = bf16[1024,256]{1,0:T(8,128)(2,1)S(1)} all-gather(bf16[128,256]{1,0:T(8,128)(2,1)S(1)} %norm_project_mix.6), channel_id=5, replica_groups={{0,2,4,6,8,10,12,14},{1,3,5,7,9,11,13,15},{16,18,20,22,24,26,28,30},{17..., dimensions={0}, use_global_device_ids=true | all-gather | bytes 589824 | tf_op jit(solution)/shard_map/all_gather | solution.py:238
  99.7 2.1 collective-permute-done.6.refs_1_
  101.8 2.2 copy-done
  103.9 1.4 project_out.6
  105.3 1.6 collective-permute-start.7
  106.9 4.0 %collective-permute-done.7.refs_3_ = bf16[128,512]{1,0:T(8,128)(2,1)S(1)} collective-permute-done((bf16[128,512]{1,0:T(8,128)(2,1)S(1)}, bf16[128,512]{1,0:T(8,128)(2,1)S(1)}, u32[]{:S(2)}, u32[]{:S(2)}) %collective-permute-start.7) | collective-permute-done | bytes 131104 | tf_op jit(solution)/shard_map/ppermute | solution.py:275
  111.7 1.4 copy-done.4
  113.1 10.1 %norm_project_mix.4 = bf16[128,256]{1,0:T(8,128)(2,1)S(1)} custom-call(s32[1]{0:T(128)} %bitcast.rank_ref, bf16[8,128,512]{2,1,0:T(8,128)(2,1)S(1)} %copy-done.4, bf16[8,128,512]{2,1,0:T(8,128)(2,1)S(1)} %collective-permute-done.refs_1_, bf16[3,256,8192]{2,1,0:T(8,128)(2,1)} %bitcast.52, f32[1,8192]{1,0:T(1,128)S(1)} %copy-done.9, ...), custom_call_target="tpu_custom_call" | custom-call | flops 1610612736 | bytes 14680064 | tf_op jit(solution)/shard_map/norm_project_mix/pallas_call | solution.py:133
  123.2 31.7 %all-gather = bf16[1024,256]{1,0:T(8,128)(2,1)S(1)} all-gather(bf16[128,256]{1,0:T(8,128)(2,1)S(1)} %norm_project_mix.4), channel_id=2, replica_groups={{0,2,4,6,8,10,12,14},{1,3,5,7,9,11,13,15},{16,18,20,22,24,26,28,30},{17..., dimensions={0}, use_global_device_ids=true | all-gather | bytes 589824 | tf_op jit(solution)/shard_map/all_gather | solution.py:238
  154.9 1.9 collective-permute-done.1.refs_1_
  156.8 1.4 project_out.4
  159.1 2.0 collective-permute-start.2
  161.1 3.8 %collective-permute-done.2.refs_3_ = bf16[128,512]{1,0:T(8,128)(2,1)S(1)} collective-permute-done((bf16[128,512]{1,0:T(8,128)(2,1)S(1)}, bf16[128,512]{1,0:T(8,128)(2,1)S(1)}, u32[]{:S(2)}, u32[]{:S(2)}) %collective-permute-start.2) | collective-permute-done | bytes 131104 | tf_op jit(solution)/shard_map/ppermute | solution.py:275
  165.7 39.4 %all-gather.15.cloned.1.call-done = bf16[1024,512]{1,0:T(8,128)(2,1)} async-done(((bf16[128,512]{1,0:T(8,128)(2,1)}), bf16[1024,512]{1,0:T(8,128)(2,1)}) %all-gather.15.cloned.1.call-update) | async-done | bytes 1048592 | tf_op jit(solution)/shard_map/all_gather | solution.py:238
  205.1 1.4 copy-done.5
  206.5 10.1 %norm_project_mix.7 = bf16[128,256]{1,0:T(8,128)(2,1)S(1)} custom-call(s32[1]{0:T(128)} %bitcast.rank_ref, bf16[8,128,512]{2,1,0:T(8,128)(2,1)S(1)} %bitcast.48, bf16[8,128,512]{2,1,0:T(8,128)(2,1)S(1)} %collective-permute-done.8.refs_1_, bf16[3,256,8192]{2,1,0:T(8,128)(2,1)} %bitcast.53, f32[1,8192]{1,0:T(1,128)S(1)} %copy-done.9, ...), custom_call_target="tpu_custom_call" | custom-call | flops 1610612736 | bytes 14680064 | tf_op jit(solution)/shard_map/norm_project_mix/pallas_call | solution.py:133
  216.7 31.6 %all-gather.5 = bf16[1024,256]{1,0:T(8,128)(2,1)S(1)} all-gather(bf16[128,256]{1,0:T(8,128)(2,1)S(1)} %norm_project_mix.7), channel_id=7, replica_groups={{0,2,4,6,8,10,12,14},{1,3,5,7,9,11,13,15},{16,18,20,22,24,26,28,30},{17..., dimensions={0}, use_global_device_ids=true | all-gather | bytes 589824 | tf_op jit(solution)/shard_map/all_gather | solution.py:238
  248.3 9.9 %norm_project_mix.5 = bf16[128,256]{1,0:T(8,128)(2,1)S(1)} custom-call(s32[1]{0:T(128)} %bitcast.rank_ref, bf16[8,128,512]{2,1,0:T(8,128)(2,1)S(1)} %bitcast.50, bf16[8,128,512]{2,1,0:T(8,128)(2,1)S(1)} %collective-permute-done.3.refs_1_, bf16[3,256,8192]{2,1,0:T(8,128)(2,1)} %bitcast.54, f32[1,8192]{1,0:T(1,128)S(1)} %copy-done.9, ...), custom_call_target="tpu_custom_call" | custom-call | flops 1610612736 | bytes 14680064 | tf_op jit(solution)/shard_map/norm_project_mix/pallas_call | solution.py:133
  258.2 31.5 %all-gather.2 = bf16[1024,256]{1,0:T(8,128)(2,1)S(1)} all-gather(bf16[128,256]{1,0:T(8,128)(2,1)S(1)} %norm_project_mix.5), channel_id=4, replica_groups={{0,2,4,6,8,10,12,14},{1,3,5,7,9,11,13,15},{16,18,20,22,24,26,28,30},{17..., dimensions={0}, use_global_device_ids=true | all-gather | bytes 589824 | tf_op jit(solution)/shard_map/all_gather | solution.py:238
  289.8 1.4 project_out.7
  291.7 1.4 project_out.5
  (57 shorter events, 9.9 us)
Async XLA Ops:
  6.5 105.1 %copy-start.9 = (f32[1,8192]{1,0:T(1,128)S(1)}, f32[1,8192]{1,0:T(1,128)}, u32[]{:S(2)}) copy-start(f32[1,8192]{1,0:T(1,128)} %refs_3_.7) | copy-start | bytes 98308
  6.5 45.8 %all-gather.13.cloned.1.call-start = ((), (), s32[]{:S(2)}) async-start(), calls=%async_computation.1 | async-start | bytes 1179648 | tf_op jit(solution)/shard_map/all_gather | solution.py:238
  8.3 90.9 %all-gather.11.cloned.1.call-start = ((), (), s32[]{:S(2)}) async-start(), calls=%async_computation | async-start | bytes 1179648 | tf_op jit(solution)/shard_map/all_gather | solution.py:238
  9.0 156.6 %all-gather.17.cloned.1.call-start = ((), (), s32[]{:S(2)}) async-start(), calls=%async_computation.3 | async-start | bytes 1179648 | tf_op jit(solution)/shard_map/all_gather | solution.py:238
  52.4 2.9 collective-permute-start.5
  67.1 89.7 %copy-start.3 = (bf16[1,128,512]{2,1,0:T(8,128)(2,1)S(1)}, bf16[1,128,512]{2,1,0:T(8,128)(2,1)}, u32[]{:S(2)}) copy-start(bf16[1,128,512]{2,1,0:T(8,128)(2,1)} %get-tuple-element.5) | copy-start | bytes 393220
  99.2 2.6 collective-permute-start.6
  99.2 12.5 %collective-permute-start = (bf16[8,128,512]{2,1,0:T(8,128)(2,1)}, bf16[8,128,512]{2,1,0:T(8,128)(2,1)S(1)}, u32[]{:S(2)}, u32[]{:S(2)}) collective-permute-start(bf16[8,128,512]{2,1,0:T(8,128)(2,1)} %all-gather.11.cloned.1.call-done.refs_0_), channel_id=1, source_target_pairs={{0,1},{1,0},{2,3},{3,2},{4,5},{5,4},{6,7},{7,6},{8,9},{9,8},{10,11... | collective-permute-start | bytes 3145736 | tf_op jit(solution)/shard_map/ppermute | solution.py:241
  101.8 2.2 copy-start
  105.3 5.6 %collective-permute-start.7 = (bf16[128,512]{1,0:T(8,128)(2,1)S(1)}, bf16[128,512]{1,0:T(8,128)(2,1)S(1)}, u32[]{:S(2)}, u32[]{:S(2)}) collective-permute-start(bf16[128,512]{1,0:T(8,128)(2,1)S(1)} %project_out.6), channel_id=1, source_target_pairs={{0,16},{16,0},{1,17},{17,1},{2,18},{18,2},{3,19},{19,3},{4,20},{20... | collective-permute-start | bytes 393224 | tf_op jit(solution)/shard_map/ppermute | solution.py:275
  111.6 93.5 %all-gather.15.cloned.1.call-start = ((), (), s32[]{:S(2)}) async-start(), calls=%async_computation.2 | async-start | bytes 1179648 | tf_op jit(solution)/shard_map/all_gather | solution.py:238
  111.7 45.2 %copy-start.1 = (bf16[1,4096,512]{2,1,0:T(8,128)(2,1)S(1)}, bf16[1,4096,512]{2,1,0:T(8,128)(2,1)}, u32[]{:S(2)}) copy-start(bf16[1,4096,512]{2,1,0:T(8,128)(2,1)} %param.15) | copy-start | bytes 12582916
  111.7 1.4 copy-start.4
  154.9 1.9 collective-permute-start.1
  159.1 5.8 %collective-permute-start.2 = (bf16[128,512]{1,0:T(8,128)(2,1)S(1)}, bf16[128,512]{1,0:T(8,128)(2,1)S(1)}, u32[]{:S(2)}, u32[]{:S(2)}) collective-permute-start(bf16[128,512]{1,0:T(8,128)(2,1)S(1)} %bitcast_select_fusion), channel_id=1, source_target_pairs={{0,16},{16,0},{1,17},{17,1},{2,18},{18,2},{3,19},{19,3},{4,20},{20... | collective-permute-start | bytes 393224 | tf_op jit(solution)/shard_map/ppermute | solution.py:275
  165.6 39.5 %collective-permute-start.8 = (bf16[8,128,512]{2,1,0:T(8,128)(2,1)}, bf16[8,128,512]{2,1,0:T(8,128)(2,1)S(1)}, u32[]{:S(2)}, u32[]{:S(2)}) collective-permute-start(bf16[8,128,512]{2,1,0:T(8,128)(2,1)} %bitcast.47), channel_id=1, source_target_pairs={{0,1},{1,0},{2,3},{3,2},{4,5},{5,4},{6,7},{7,6},{8,9},{9,8},{10,11... | collective-permute-start | bytes 3145736 | tf_op jit(solution)/shard_map/ppermute | solution.py:241
  205.1 84.6 %copy-start.2 = (bf16[1,4096,512]{2,1,0:T(8,128)(2,1)S(1)}, bf16[1,4096,512]{2,1,0:T(8,128)(2,1)}, u32[]{:S(2)}) copy-start(bf16[1,4096,512]{2,1,0:T(8,128)(2,1)} %param.15) | copy-start | bytes 12582916
  205.1 43.2 %collective-permute-start.3 = (bf16[8,128,512]{2,1,0:T(8,128)(2,1)}, bf16[8,128,512]{2,1,0:T(8,128)(2,1)S(1)}, u32[]{:S(2)}, u32[]{:S(2)}) collective-permute-start(bf16[8,128,512]{2,1,0:T(8,128)(2,1)} %bitcast.49), channel_id=1, source_target_pairs={{0,1},{1,0},{2,3},{3,2},{4,5},{5,4},{6,7},{7,6},{8,9},{9,8},{10,11... | collective-permute-start | bytes 3145736 | tf_op jit(solution)/shard_map/ppermute | solution.py:241
  205.1 1.4 copy-start.5
  206.5 41.8 %copy-start.7 = (bf16[1024,512]{1,0:T(8,128)(2,1)S(1)}, bf16[1024,512]{1,0:T(8,128)(2,1)}, u32[]{:S(2)}) copy-start(bf16[1024,512]{1,0:T(8,128)(2,1)} %all-gather.15.cloned.1.call-done) | copy-start | bytes 3145732
  206.5 83.2 %copy-start.11 = (bf16[128,512]{1,0:T(8,128)(2,1)S(1)}, bf16[128,512]{1,0:T(8,128)(2,1)}, u32[]{:S(2)}) copy-start(bf16[128,512]{1,0:T(8,128)(2,1)} %copy-done.10) | copy-start | bytes 393220
  216.7 75.0 %copy-start.13 = (bf16[128,512]{1,0:T(8,128)(2,1)S(1)}, bf16[128,512]{1,0:T(8,128)(2,1)}, u32[]{:S(2)}) copy-start(bf16[128,512]{1,0:T(8,128)(2,1)} %copy-done.12) | copy-start | bytes 393220
  248.3 41.5 %collective-permute-start.9 = (bf16[8,128,256]{2,1,0:T(8,128)(2,1)S(1)}, bf16[8,128,256]{2,1,0:T(8,128)(2,1)S(1)}, u32[]{:S(2)}, u32[]{:S(2)}) collective-permute-start(bf16[8,128,256]{2,1,0:T(8,128)(2,1)S(1)} %bitcast.37), channel_id=1, source_target_pairs={{0,1},{1,0},{2,3},{3,2},{4,5},{5,4},{6,7},{7,6},{8,9},{9,8},{10,11... | collective-permute-start | bytes 1572872 | tf_op jit(solution)/shard_map/ppermute | solution.py:241
  289.7 1.9 collective-permute-start.4
  (4 other events, 3.3 us)
Sparse Core Ops, SparseCore 0:
  9.5 42.8 all-gather.12
  54.5 41.8 all-gather.10
  111.7 41.9 all-gather.16
  165.7 39.3 all-gather.14

commit v3 on v0

v3 whole, which is shorter than its diff:
```python
import functools

import jax
import jax.numpy as jnp
from jax import lax
from jax.experimental import pallas as pl
from jax.experimental.pallas import tpu as pltpu
from jax.sharding import PartitionSpec as P

EPS = 1e-06
VMEM_LIMIT = 12 * 1024 * 1024
PAD = 8


def plan(section_count, tick_count):
    wave_count = min(section_count, tick_count)
    waves = [[[] for _ in range(section_count)] for _ in range(wave_count)]
    where = {}
    for k in range(tick_count):
        for s in range(section_count):
            first = where[s - 1, k - 1][0] + 1 if s > 0 and k > 0 else 0
            last = wave_count - 1 - min(section_count - 1 - s, tick_count - 1 - k)
            best = min(range(first, last + 1), key=lambda w: (len(waves[w][s]), w))
            where[s, k] = (best, len(waves[best][s]))
            waves[best][s].append(k)
    return waves


def split_dp(dp_count):
    core = 2 if dp_count % 2 == 0 else 1
    chips = dp_count // core
    near = 1
    while near * near * 4 <= chips:
        near *= 2
    return chips // near, near, core


def pick(section_idx, options):
    distinct = []
    for s, value in enumerate(options):
        if value is None:
            continue
        for held, members in distinct:
            if held is value:
                members.append(s)
                break
        else:
            distinct.append((value, [s]))
    result = distinct[0][0]
    for value, members in distinct[1:]:
        mine = functools.reduce(jnp.logical_or, [section_idx == s for s in members])
        result = jnp.where(mine, value, result)
    return result


def project_cells(cells, sides, rank_ref, w_ref, gain_ref, acc_ref, sq_ref, ready=None):
    feat = sides[0].shape[2]
    core = len(sides)
    lanes = sq_ref.shape[1]
    chip, side = lax.div(rank_ref[0], core), lax.rem(rank_ref[0], core)
    for n, cell in enumerate(cells):
        normed, columns = [], []
        for c in range(core):
            values = sides[c][n].astype(jnp.float32)
            columns.append(pl.ds(pl.multiple_of(((chip ^ cell) * core + (side ^ c)) * feat, feat), feat))
            normed.append((values * gain_ref[:, columns[c]]).astype(jnp.bfloat16))
            squares = values * values
            part = squares[:, :lanes]
            for m in range(1, feat // lanes):
                part = part + squares[:, m * lanes : (m + 1) * lanes]
            sq_ref[...] = part if n == 0 and c == 0 else sq_ref[...] + part
        if ready is not None:
            ready(n)
        for i in range(w_ref.shape[0]):
            terms = [
                lax.dot_general(
                    normed[c],
                    w_ref[i, :, columns[c]],
                    (((1,), (1,)), ((), ())),
                    preferred_element_type=jnp.float32,
                )
                for c in range(core)
            ]
            term = functools.reduce(jnp.add, terms)
            acc_ref[i] = term if n == 0 else acc_ref[i] + term


def early_kernel(cells, core, rank_ref, *refs):
    sides = refs[:core]
    w_ref, gain_ref, acc_ref, sq_ref = refs[core : core + 4]
    project_cells(cells, sides, rank_ref, w_ref, gain_ref, acc_ref, sq_ref)


def first_kernel(cells, later, core, rank_ref, *refs):
    sides = refs[:core]
    w_far, gain_ref, taps_ref, decay_ref, acc_ref, sq_ref, w_ref, gain_here, long_ref = refs[core : core + 9]
    sems = refs[-1]
    wide = core * sides[0].shape[2]
    chip = lax.div(rank_ref[0], core)
    copies = []
    for n, cell in enumerate(cells + later):
        columns = pl.ds(pl.multiple_of((chip ^ cell) * wide, wide), wide)
        copies.append(
            [
                pltpu.make_async_copy(w_far.at[i, :, columns], w_ref.at[i, :, columns], sems.at[n, i])
                for i in range(w_far.shape[0])
            ]
        )
    for group in copies:
        for copy in group:
            copy.start()

    gain_here[...] = gain_ref[...]
    lags = lax.broadcasted_iota(jnp.int32, long_ref.shape, 0).astype(jnp.float32)
    long_ref[...] = taps_ref[...].T * jnp.exp(-decay_ref[...] * lags)

    def ready(n):
        for copy in copies[n]:
            copy.wait()

    project_cells(cells, sides, rank_ref, w_ref, gain_ref, acc_ref, sq_ref, ready)
    for n in range(len(cells), len(copies)):
        ready(n)


def mix_kernel(cells, core, rank_ref, *refs):
    sides = refs[:core]
    w_ref, gain_ref, acc_in, sq_in, short_ref, long_ref, y_ref = refs[core : core + 7]
    acc_ref, sq_ref, pad_ref, query_ref = refs[core + 7 :]
    branches, chan, model_width = w_ref.shape
    tok_len = y_ref.shape[0]
    project_cells(cells, sides, rank_ref, w_ref, gain_ref, acc_ref, sq_ref)

    total = jnp.sum(sq_in[...] + sq_ref[...], axis=1, keepdims=True)
    factor = lax.rsqrt(total / model_width + EPS)
    taps = short_ref.shape[0] // branches
    pad_ref[0:PAD, :] = jnp.zeros((PAD, chan), jnp.float32)

    def branch(i):
        u = (acc_in[i] + acc_ref[i]) * factor
        pad_ref[PAD : PAD + tok_len, :] = u
        z = short_ref[i * taps : i * taps + 1, :] * u
        for j in range(1, taps):
            z = z + short_ref[i * taps + j : i * taps + j + 1, :] * pad_ref[PAD - j : PAD - j + tok_len, :]
        return z

    query_ref[...] = branch(1)
    product = query_ref[...] * branch(2)
    query_ref[...] = branch(0)
    pad_ref[PAD : PAD + tok_len, :] = product
    width = min(chan, 128)
    tiles = tok_len // 8
    for c in range(0, chan, width):
        cols = slice(c, c + width)
        conv = [None] * tiles
        for b in range(8):
            moved = [pad_ref[PAD - b + 8 * i : PAD - b + 8 * i + 8, cols] for i in range(tiles)]
            for a in range(long_ref.shape[0] // 8):
                tap = long_ref[8 * a + b : 8 * a + b + 1, cols]
                for i in range(a, tiles):
                    term = tap * moved[i - a]
                    conv[i] = term if conv[i] is None else conv[i] + term
        for i in range(0, tiles, 2):
            at = slice(8 * i, 8 * i + 16)
            both = jnp.concatenate(conv[i : i + 2], axis=0)
            y_ref[at, cols] = (query_ref[at, cols] * both).astype(jnp.bfloat16)


def out_kernel(parts, core, rank_ref, *refs):
    w_ref, own_ref, result_ref, acc_ref = refs[-4:]
    chan = refs[0].shape[2]
    chip, side = lax.div(rank_ref[0], core), lax.rem(rank_ref[0], core)
    acc_ref[...] = own_ref[...].astype(jnp.float32)
    for p, cells in enumerate(parts):
        sides = refs[p * core : (p + 1) * core]
        for n, cell in enumerate(cells):
            terms = []
            for c in range(core):
                at = pl.multiple_of(((chip ^ cell) * core + (side ^ c)) * chan, chan)
                terms.append(
                    jnp.dot(sides[c][n], w_ref[pl.ds(at, chan), :], preferred_element_type=jnp.float32)
                )
            acc_ref[...] += functools.reduce(jnp.add, terms)
    result_ref[...] = acc_ref[...].astype(jnp.bfloat16)


def in_vmem(count):
    return [pl.BlockSpec(memory_space=pltpu.VMEM)] * count


def call(kernel, operands, outs, scratch, flops, name, far_operands=(), moved=0):
    specs = [pl.BlockSpec(memory_space=pltpu.SMEM)] + in_vmem(len(operands) - 1)
    for n in far_operands:
        specs[n] = pl.BlockSpec(memory_space=pltpu.HBM)
    return pl.pallas_call(
        kernel,
        in_specs=specs,
        out_specs=in_vmem(len(outs)),
        out_shape=outs,
        scratch_shapes=scratch,
        compiler_params=pltpu.CompilerParams(vmem_limit_bytes=VMEM_LIMIT),
        cost_estimate=pl.CostEstimate(flops=flops, bytes_accessed=flops // 1024 + moved, transcendentals=0),
        name=name,
    )(*operands)


def project_early(part, later, w_in, gain, rank, taps=None, decay=None):
    cells, sides = part
    core = len(sides)
    rows, feat = sides[0].shape[1:]
    branches, chan, model_width = w_in.shape
    outs = [
        jax.ShapeDtypeStruct((branches, rows, chan), jnp.float32),
        jax.ShapeDtypeStruct((rows, min(feat, 128)), jnp.float32),
    ]
    scratch = []
    flops = 2 * rows * branches * chan * feat * core * len(cells)
    operands = [rank, *sides, w_in, gain]
    if taps is not None:
        operands += [taps, decay]
        operands[1 + core] = pltpu.with_memory_space_constraint(w_in, pltpu.HBM)
        outs.append(pltpu.VMEM(w_in.shape, w_in.dtype))
        outs.append(pltpu.VMEM(gain.shape, gain.dtype))
        outs.append(pltpu.VMEM(taps.shape[::-1], taps.dtype))
        scratch.append(pltpu.SemaphoreType.DMA((len(cells) + len(later), branches)))
        kernel = functools.partial(first_kernel, cells, later, core)
        return call(kernel, operands, outs, scratch, flops, "load_project", (1 + core,), 4 * w_in.size)
    return call(functools.partial(early_kernel, cells, core), operands, outs, scratch, flops, "project_early")


def mix(part, w_in, gain, acc, sq, short_rows, long_rows, rank):
    cells, sides = part
    core = len(sides)
    rows, feat = sides[0].shape[1:]
    branches, chan, _ = w_in.shape
    scratch = [
        pltpu.VMEM(acc.shape, jnp.float32),
        pltpu.VMEM(sq.shape, jnp.float32),
        pltpu.VMEM((PAD + rows, chan), jnp.float32),
        pltpu.VMEM((rows, chan), jnp.float32),
    ]
    return call(
        functools.partial(mix_kernel, cells, core),
        [rank, *sides, w_in, gain, acc, sq, short_rows, long_rows],
        [jax.ShapeDtypeStruct((rows, chan), jnp.bfloat16)],
        scratch,
        2 * rows * branches * chan * feat * core * len(cells),
        "project_mix",
    )[0]


def project_out(parts, w_out, own, rank):
    core = len(parts[0][1])
    rows, feat = own.shape
    arrays = [side for _, sides in parts for side in sides]
    return call(
        functools.partial(out_kernel, [cells for cells, _ in parts], core),
        [rank, *arrays, w_out, own],
        [jax.ShapeDtypeStruct((rows, feat), jnp.bfloat16)],
        [pltpu.VMEM((rows, feat), jnp.float32)],
        2 * rows * w_out.shape[0] * feat,
        "project_out",
    )[0]


def body(section_count, dp_count, fresh_acts, carried, norm_gain, w_in, short_filter, filter_taps, decay_rate, w_out):
    tick_count, tok_len, _ = fresh_acts.shape
    far, near, core = split_dp(dp_count)
    group = near * core
    waves = plan(section_count, tick_count)
    section_idx = lax.axis_index("section")
    rank_idx = lax.axis_index("dp")
    rank = rank_idx.astype(jnp.int32).reshape(1)

    def swap(value, offset):
        return lax.ppermute(value, "dp", [(r, r ^ offset) for r in range(dp_count)])

    def onward(value, offset):
        pairs = [
            (s * dp_count + r, (s + 1) % section_count * dp_count + (r ^ offset))
            for s in range(section_count)
            for r in range(dp_count)
        ]
        return lax.ppermute(value, ("section", "dp"), pairs)

    def after(value, earlier):
        return value if earlier is None else lax.optimization_barrier((value, earlier))[0]

    def gather(source, cross, order):
        source = after(source, order.get("near"))
        blocks = [onward(source, 0) if cross else source]
        blocks += [(onward if cross else swap)(source, d * group) for d in range(1, far)]
        blocks = after(blocks, order.get("early"))
        line = jnp.stack(blocks)
        cells = [d * near for d in range(far)]
        leaving = after(line, order.get("rest"))
        rest = [swap(leaving, d * core) for d in range(1, near)]
        rest = rest[0] if near == 2 else jnp.concatenate(rest)
        more = [cell ^ d for d in range(1, near) for cell in cells]
        early = both_cores(cells, line)
        order["near"], order["rest"] = early[1][-1], rest
        return early, (more, rest), blocks[0]

    def both_cores(cells, line):
        return cells, [line] + [swap(line, c) for c in range(1, core)]

    short_rows = short_filter[0].transpose(0, 2, 1).reshape(-1, short_filter.shape[2])
    w_in_here, gain, loaded = w_in[0], norm_gain, (filter_taps[0], decay_rate)
    waiting = carried[0]
    results = {}
    for w, slots in enumerate(waves):
        slot_count = max(len(ticks) for ticks in slots)
        sources = []
        for i in range(slot_count):
            options = []
            for s in range(section_count):
                if w == 0:
                    ticks = slots[s]
                    if i >= len(ticks):
                        options.append(None)
                    elif s == 0:
                        options.append(fresh_acts[ticks[i]])
                    else:
                        options.append(waiting)
                else:
                    ticks = slots[(s + 1) % section_count]
                    if i >= len(ticks):
                        options.append(None)
                    elif s + 1 == section_count:
                        options.append(fresh_acts[ticks[i]])
                    else:
                        options.append(results[s, ticks[i] - 1])
            sources.append(pick(section_idx, options))
        made = []
        order, y_order = {}, {}
        for source in sources:
            early, (cells, rest), own = gather(source, w > 0, order)
            acc, sq, *loads = project_early(early, cells, w_in_here, gain, rank, *loaded)
            if loads:
                w_in_here, gain, long_rows = [pltpu.with_memory_space_constraint(x, pltpu.VMEM) for x in loads]
                loaded = ()
            order["early"] = acc
            late = both_cores(cells, after(rest, acc))
            acc = after(acc, y_order.get("near"))
            y = mix(late, w_in_here, gain, acc, sq, short_rows, long_rows, rank)
            y_order["near"] = y_order.get("rest")
            early, late, _ = gather(y, False, y_order)
            made.append(project_out([early, both_cores(*late)], w_out[0], own, rank))
        for s in range(section_count):
            for i, k in enumerate(slots[s]):
                results[s, k] = made[i]
    outputs = []
    for k in range(tick_count):
        outputs.append(pick(section_idx, [results[s, k] for s in range(section_count)]))
    return jnp.stack(outputs)[None]


def solution(mesh):
    run = functools.partial(body, mesh.shape["section"], mesh.shape["dp"])
    return jax.shard_map(
        run,
        mesh=mesh,
        in_specs=(
            P(None, None, "dp"),
            P("section", None, "dp"),
            P("section", None),
            P("section", None, "dp", None),
            P("section", None, "dp", None),
            P("section", "dp", None),
            P("section", "dp"),
            P("section", None, "dp"),
        ),
        out_specs=P("section", None, None, "dp"),
        check_vma=False,
    )
```

time: 445 us -> 180 us (0.40)
  waiting for transfers between devices: 299 us -> 81.5 us
  matrix products: 98.9 us -> 0 us
  starting transfers between devices: 3.66 us -> 51.5 us
  Pallas kernels: 0 us -> 31.7 us
  between operations: 13.6 us -> 0.28 us
  local copies, waits for them, and re-layouts: 18.8 us -> 11.5 us
  other arithmetic: 9.86 us -> 3.15 us
    all_gather x6 -> x0, waiting for transfers between devices: 206 us -> none  [the longest x3 111 us: body(): lax.all_gather(y_local, 'dp', axis=1, tiled=True)]
    dot_general x10 -> x0, matrix products: 98.9 us -> none  [the longest x3 49.8 us: mixing(): jnp.einsum('cts,sc->tc', toeplitz, product, precision=lax.Precision.HIGHEST)]
    ppermute x2 -> x50, starting transfers between devices: 3.04 us -> 51.5 us  [the longest x42 37.7 us: swap(): return lax.ppermute(value, 'dp', [(r, r ^ offset) for r in range(dp_count)])]
    pallas_call x0 -> x12, Pallas kernels: none -> 31.7 us  [call(): pl.pallas_call(kernel, in_specs=specs, out_specs=in_vmem(len(outs)), out_...]
    dot_general x1 -> x0, local copies, waits for them, and re-layouts: 17.6 us -> none  [build_toeplitz(): jnp.einsum('cj,tsj->cts', filter_vals, onehot, precision=lax.Precision.HI...]
    ppermute x2 -> x50, waiting for transfers between devices: 93 us -> 81.5 us  [the longest x42 65.8 us: swap(): return lax.ppermute(value, 'dp', [(r, r ^ offset) for r in range(dp_count)])]
    unnamed x9 -> x17, local copies, waits for them, and re-layouts: 0.72 us -> 11.5 us
  transfers between devices with their start and end apart: 8 -> 50, of which waited for: 8 -> 26; matrix products, arithmetic and copies ran while one was open for 7% -> 1% of each run, Pallas kernels for 0% -> 15%
where the time goes in v3:
time: 180 us
  waiting for transfers between devices  81.5 us (45%)
  starting transfers between devices  51.5 us (29%)
  Pallas kernels  31.7 us (18%)
  local copies, waits for them, and re-layouts  11.5 us (6%)
  other arithmetic  3.15 us (2%)
    ppermute x42, waiting for transfers between devices, swap(): return lax.ppermute(value, 'dp', [(r, r ^ offset) for r in range(dp_count)])  65.8 us
    ppermute x42, starting transfers between devices, swap(): return lax.ppermute(value, 'dp', [(r, r ^ offset) for r in range(dp_count)])  37.7 us
    pallas_call x12, Pallas kernels, call(): pl.pallas_call(kernel, in_specs=specs, out_specs=in_vmem(len(outs)), out_...  31.7 us
    ppermute x8, waiting for transfers between devices, onward(): return lax.ppermute(value, ('section', 'dp'), pairs)  15.7 us
    ppermute x8, starting transfers between devices, onward(): return lax.ppermute(value, ('section', 'dp'), pairs)  13.9 us
    unnamed x17, local copies, waits for them, and re-layouts  11.5 us
  transfers between devices with their start and end apart: 50, of which 26 were waited for; matrix products, arithmetic and copies ran while one was open for 1% of the time, Pallas kernels for 15%

profile of v3, /device:TPU:0, one launch (start us, length us, event | category | flops | bytes accessed | tf_op | source)
XLA Modules:
  0.0 179.7 jit_solution(13104764161237684418)
XLA Ops:
  1.0 3.1 %collective-permute-start = (bf16[128,512]{1,0:T(8,128)(2,1)S(1)}, bf16[128,512]{1,0:T(8,128)(2,1)S(1)}, u32[]{:S(2)}, u32[]{:S(2)}) collective-permute-start(bf16[128,512]{1,0:T(8,128)(2,1)S(1)} %bitcast.58), channel_id=1, source_target_pairs={{0,4},{1,5},{2,6},{3,7},{4,0},{5,1},{6,2},{7,3},{8,12},{9,13},{10,... | collective-permute-start | bytes 393224 | tf_op jit(solution)/shard_map/ppermute | solution.py:276
  4.1 2.6 %collective-permute-start.1 = (bf16[128,512]{1,0:T(8,128)(2,1)S(1)}, bf16[128,512]{1,0:T(8,128)(2,1)S(1)}, u32[]{:S(2)}, u32[]{:S(2)}) collective-permute-start(bf16[128,512]{1,0:T(8,128)(2,1)S(1)} %bitcast.59), channel_id=1, source_target_pairs={{0,8},{1,9},{2,10},{3,11},{4,12},{5,13},{6,14},{7,15},{8,0},{9,1},... | collective-permute-start | bytes 393224 | tf_op jit(solution)/shard_map/ppermute | solution.py:276
  9.1 7.9 %collective-permute-done.1 = bf16[128,512]{1,0:T(8,128)(2,1)S(1)} collective-permute-done((bf16[128,512]{1,0:T(8,128)(2,1)S(1)}, bf16[128,512]{1,0:T(8,128)(2,1)S(1)}, u32[]{:S(2)}, u32[]{:S(2)}) %collective-permute-start.1) | collective-permute-done | bytes 131104 | tf_op jit(solution)/shard_map/ppermute | solution.py:276
  21.4 5.0 %load_project.1 = (f32[3,128,256]{2,1,0:T(8,128)S(1)}, f32[128,128]{1,0:T(8,128)S(1)}, bf16[3,256,8192]{2,1,0:T(8,128)(2,1)S(1)}, f32[1,8192]{1,0:T(1,128)S(1)}, f32[128,256]{1,0:T(8,128)S(1)}) custom-call(s32[1]{0:T(128)} %bitcast.rank_ref, bf16[4,128,512]{2,1,0:T(8,128)(2,1)S(1)} %pad_maximum_fusion.refs_0_, ...), custom_call_target="tpu_custom_call" | custom-call | flops 805306368 | bytes 25952256 | tf_op jit(solution)/shard_map/load_project/pallas_call | solution.py:195
  26.4 4.6 %copy-done = bf16[3,256,8192]{2,1,0:T(8,128)(2,1)} copy-done((bf16[3,256,8192]{2,1,0:T(8,128)(2,1)}, bf16[3,256,8192]{2,1,0:T(8,128)(2,1)S(1)}, u32[]{:S(2)}) %copy-start) | copy-done | bytes 12582936
  36.0 4.0 %collective-permute-done.25 = bf16[128,512]{1,0:T(8,128)(2,1)S(1)} collective-permute-done((bf16[128,512]{1,0:T(8,128)(2,1)S(1)}, bf16[128,512]{1,0:T(8,128)(2,1)S(1)}, u32[]{:S(2)}, u32[]{:S(2)}) %collective-permute-start.25) | collective-permute-done | bytes 131104 | tf_op jit(solution)/shard_map/ppermute | solution.py:276
  39.9 6.5 %collective-permute-done.26 = bf16[128,512]{1,0:T(8,128)(2,1)S(1)} collective-permute-done((bf16[128,512]{1,0:T(8,128)(2,1)S(1)}, bf16[128,512]{1,0:T(8,128)(2,1)S(1)}, u32[]{:S(2)}, u32[]{:S(2)}) %collective-permute-start.26) | collective-permute-done | bytes 131104 | tf_op jit(solution)/shard_map/ppermute | solution.py:276
  48.1 4.6 %copy-done.1 = bf16[3,256,8192]{2,1,0:T(8,128)(2,1)S(1)} copy-done((bf16[3,256,8192]{2,1,0:T(8,128)(2,1)S(1)}, bf16[3,256,8192]{2,1,0:T(8,128)(2,1)}, u32[]{:S(2)}) %copy-start.1) | copy-done | bytes 12582936
  52.7 4.2 %project_mix.4 = bf16[128,256]{1,0:T(8,128)(2,1)S(1)} custom-call(s32[1]{0:T(128)} %bitcast.rank_ref, bf16[4,128,512]{2,1,0:T(8,128)(2,1)S(1)} %collective-permute-done.3.refs_0_, bf16[4,128,512]{2,1,0:T(8,128)(2,1)S(1)} %collective-permute-done.5.refs_1_, bf16[3,256,8192]{2,1,0:T(8,128)(2,1)S(1)} %copy-done.1, f32[1,8192]{1,0:T(1,128)S(1)} %get-tuple-element.41.refs_3_, ...), custom_call_target="tpu_custom_call" | custom-call | flops 805306368 | bytes 786432 | tf_op jit(solution)/shard_map/project_mix/pallas_call | solution.py:195
  56.9 3.7 %collective-permute-start.7 = (bf16[128,256]{1,0:T(8,128)(2,1)S(1)}, bf16[128,256]{1,0:T(8,128)(2,1)S(1)}, u32[]{:S(2)}, u32[]{:S(2)}) collective-permute-start(bf16[128,256]{1,0:T(8,128)(2,1)S(1)} %project_mix.4), channel_id=1, source_target_pairs={{0,8},{1,9},{2,10},{3,11},{4,12},{5,13},{6,14},{7,15},{8,0},{9,1},... | collective-permute-start | bytes 196616 | tf_op jit(solution)/shard_map/ppermute | solution.py:276
  62.0 2.9 %collective-permute-done.7 = bf16[128,256]{1,0:T(8,128)(2,1)S(1)} collective-permute-done((bf16[128,256]{1,0:T(8,128)(2,1)S(1)}, bf16[128,256]{1,0:T(8,128)(2,1)S(1)}, u32[]{:S(2)}, u32[]{:S(2)}) %collective-permute-start.7) | collective-permute-done | bytes 65568 | tf_op jit(solution)/shard_map/ppermute | solution.py:276
  70.8 3.7 %collective-permute-done.10.refs_2_ = bf16[4,128,256]{2,1,0:T(8,128)(2,1)S(1)} collective-permute-done((bf16[4,128,256]{2,1,0:T(8,128)(2,1)S(1)}, bf16[4,128,256]{2,1,0:T(8,128)(2,1)S(1)}, u32[]{:S(2)}, u32[]{:S(2)}) %collective-permute-start.10) | collective-permute-done | bytes 262176 | tf_op jit(solution)/shard_map/ppermute | solution.py:276
  76.8 4.4 %project_mix.6 = bf16[128,256]{1,0:T(8,128)(2,1)S(1)} custom-call(s32[1]{0:T(128)} %bitcast.rank_ref, bf16[4,128,512]{2,1,0:T(8,128)(2,1)S(1)} %collective-permute-done.28.refs_0_, bf16[4,128,512]{2,1,0:T(8,128)(2,1)S(1)} %collective-permute-done.30.refs_1_, bf16[3,256,8192]{2,1,0:T(8,128)(2,1)S(1)} %copy-done.2, f32[1,8192]{1,0:T(1,128)S(1)} %get-tuple-element.41.refs_3_, ...), custom_call_target="tpu_custom_call" | custom-call | flops 805306368 | bytes 786432 | tf_op jit(solution)/shard_map/project_mix/pallas_call | solution.py:195
  88.2 4.1 %collective-permute-start.14 = (bf16[128,512]{1,0:T(8,128)(2,1)S(1)}, bf16[128,512]{1,0:T(8,128)(2,1)S(1)}, u32[]{:S(2)}, u32[]{:S(2)}) collective-permute-start(bf16[128,512]{1,0:T(8,128)(2,1)S(1)} %bitcast_select_fusion), channel_id=1, source_target_pairs={{0,24},{1,25},{2,26},{3,27},{4,28},{5,29},{6,30},{7,31},{8,16},{9,... | collective-permute-start | bytes 393224 | tf_op jit(solution)/shard_map/ppermute | solution.py:284
  96.2 5.8 %collective-permute-done.14 = bf16[128,512]{1,0:T(8,128)(2,1)S(1)} collective-permute-done((bf16[128,512]{1,0:T(8,128)(2,1)S(1)}, bf16[128,512]{1,0:T(8,128)(2,1)S(1)}, u32[]{:S(2)}, u32[]{:S(2)}) %collective-permute-start.14) | collective-permute-done | bytes 131104 | tf_op jit(solution)/shard_map/ppermute | solution.py:284
  106.4 2.7 %collective-permute-start.38 = (bf16[128,512]{1,0:T(8,128)(2,1)S(1)}, bf16[128,512]{1,0:T(8,128)(2,1)S(1)}, u32[]{:S(2)}, u32[]{:S(2)}) collective-permute-start(bf16[128,512]{1,0:T(8,128)(2,1)S(1)} %project_out.6), channel_id=1, source_target_pairs={{0,20},{1,21},{2,22},{3,23},{4,16},{5,17},{6,18},{7,19},{8,28},{9,... | collective-permute-start | bytes 393224 | tf_op jit(solution)/shard_map/ppermute | solution.py:284
  115.6 6.9 %collective-permute-done.39 = bf16[128,512]{1,0:T(8,128)(2,1)S(1)} collective-permute-done((bf16[128,512]{1,0:T(8,128)(2,1)S(1)}, bf16[128,512]{1,0:T(8,128)(2,1)S(1)}, u32[]{:S(2)}, u32[]{:S(2)}) %collective-permute-start.39) | collective-permute-done | bytes 131104 | tf_op jit(solution)/shard_map/ppermute | solution.py:284
  126.9 10.2 %collective-permute-done.41.refs_0_ = bf16[4,128,512]{2,1,0:T(8,128)(2,1)S(1)} collective-permute-done((bf16[4,128,512]{2,1,0:T(8,128)(2,1)S(1)}, bf16[4,128,512]{2,1,0:T(8,128)(2,1)S(1)}, u32[]{:S(2)}, u32[]{:S(2)}) %collective-permute-start.41) | collective-permute-done | bytes 524320 | tf_op jit(solution)/shard_map/ppermute | solution.py:276
  137.1 4.2 %project_mix.5 = bf16[128,256]{1,0:T(8,128)(2,1)S(1)} custom-call(s32[1]{0:T(128)} %bitcast.rank_ref, bf16[4,128,512]{2,1,0:T(8,128)(2,1)S(1)} %collective-permute-done.16.refs_0_, bf16[4,128,512]{2,1,0:T(8,128)(2,1)S(1)} %collective-permute-done.18.refs_1_, bf16[3,256,8192]{2,1,0:T(8,128)(2,1)S(1)} %copy-done.2, f32[1,8192]{1,0:T(1,128)S(1)} %get-tuple-element.41.refs_3_, ...), custom_call_target="tpu_custom_call" | custom-call | flops 805306368 | bytes 786432 | tf_op jit(solution)/shard_map/project_mix/pallas_call | solution.py:195
  146.3 5.8 %collective-permute-done.20 = bf16[128,256]{1,0:T(8,128)(2,1)S(1)} collective-permute-done((bf16[128,256]{1,0:T(8,128)(2,1)S(1)}, bf16[128,256]{1,0:T(8,128)(2,1)S(1)}, u32[]{:S(2)}, u32[]{:S(2)}) %collective-permute-start.20) | collective-permute-done | bytes 65568 | tf_op jit(solution)/shard_map/ppermute | solution.py:276
  153.7 4.4 %project_mix.7 = bf16[128,256]{1,0:T(8,128)(2,1)S(1)} custom-call(s32[1]{0:T(128)} %bitcast.rank_ref, bf16[4,128,512]{2,1,0:T(8,128)(2,1)S(1)} %collective-permute-done.41.refs_0_, bf16[4,128,512]{2,1,0:T(8,128)(2,1)S(1)} %collective-permute-done.43.refs_1_, bf16[3,256,8192]{2,1,0:T(8,128)(2,1)S(1)} %copy-done.2, f32[1,8192]{1,0:T(1,128)S(1)} %get-tuple-element.41.refs_3_, ...), custom_call_target="tpu_custom_call" | custom-call | flops 805306368 | bytes 786432 | tf_op jit(solution)/shard_map/project_mix/pallas_call | solution.py:195
  158.1 2.8 %collective-permute-done.23.refs_2_ = bf16[4,128,256]{2,1,0:T(8,128)(2,1)S(1)} collective-permute-done((bf16[4,128,256]{2,1,0:T(8,128)(2,1)S(1)}, bf16[4,128,256]{2,1,0:T(8,128)(2,1)S(1)}, u32[]{:S(2)}, u32[]{:S(2)}) %collective-permute-start.23) | collective-permute-done | bytes 262176 | tf_op jit(solution)/shard_map/ppermute | solution.py:276
  165.3 4.8 %collective-permute-done.45 = bf16[128,256]{1,0:T(8,128)(2,1)S(1)} collective-permute-done((bf16[128,256]{1,0:T(8,128)(2,1)S(1)}, bf16[128,256]{1,0:T(8,128)(2,1)S(1)}, u32[]{:S(2)}, u32[]{:S(2)}) %collective-permute-start.45) | collective-permute-done | bytes 65568 | tf_op jit(solution)/shard_map/ppermute | solution.py:276
  171.3 5.3 %collective-permute-done.48.refs_2_ = bf16[4,128,256]{2,1,0:T(8,128)(2,1)S(1)} collective-permute-done((bf16[4,128,256]{2,1,0:T(8,128)(2,1)S(1)}, bf16[4,128,256]{2,1,0:T(8,128)(2,1)S(1)}, u32[]{:S(2)}, u32[]{:S(2)}) %collective-permute-start.48) | collective-permute-done | bytes 262176 | tf_op jit(solution)/shard_map/ppermute | solution.py:276
  (118 shorter events, 65.5 us)
Async XLA Ops:
  4.1 12.9 %collective-permute-start.1 = (bf16[128,512]{1,0:T(8,128)(2,1)S(1)}, bf16[128,512]{1,0:T(8,128)(2,1)S(1)}, u32[]{:S(2)}, u32[]{:S(2)}) collective-permute-start(bf16[128,512]{1,0:T(8,128)(2,1)S(1)} %bitcast.59), channel_id=1, source_target_pairs={{0,8},{1,9},{2,10},{3,11},{4,12},{5,13},{6,14},{7,15},{8,0},{9,1},... | collective-permute-start | bytes 393224 | tf_op jit(solution)/shard_map/ppermute | solution.py:276
  6.7 10.3 %collective-permute-start.2 = (bf16[128,512]{1,0:T(8,128)(2,1)S(1)}, bf16[128,512]{1,0:T(8,128)(2,1)S(1)}, u32[]{:S(2)}, u32[]{:S(2)}) collective-permute-start(bf16[128,512]{1,0:T(8,128)(2,1)S(1)} %bitcast.60), channel_id=1, source_target_pairs={{0,12},{1,13},{2,14},{3,15},{4,8},{5,9},{6,10},{7,11},{8,4},{9,5},... | collective-permute-start | bytes 393224 | tf_op jit(solution)/shard_map/ppermute | solution.py:276
  17.2 14.3 %collective-permute-start.3 = (bf16[4,128,512]{2,1,0:T(8,128)(2,1)S(1)}, bf16[4,128,512]{2,1,0:T(8,128)(2,1)S(1)}, u32[]{:S(2)}, u32[]{:S(2)}) collective-permute-start(bf16[4,128,512]{2,1,0:T(8,128)(2,1)S(1)} %pad_maximum_fusion.refs_0_), channel_id=1, source_target_pairs={{0,2},{1,3},{2,0},{3,1},{4,6},{5,7},{6,4},{7,5},{8,10},{9,11},{10,... | collective-permute-start | bytes 1572872 | tf_op jit(solution)/shard_map/ppermute | solution.py:276
  31.5 16.6 %collective-permute-start.5 = (bf16[4,128,512]{2,1,0:T(8,128)(2,1)S(1)}, bf16[4,128,512]{2,1,0:T(8,128)(2,1)S(1)}, u32[]{:S(2)}, u32[]{:S(2)}) collective-permute-start(bf16[4,128,512]{2,1,0:T(8,128)(2,1)S(1)} %collective-permute-done.3.refs_0_), channel_id=1, source_target_pairs={{0,1},{1,0},{2,3},{3,2},{4,5},{5,4},{6,7},{7,6},{8,9},{9,8},{10,11... | collective-permute-start | bytes 1572872 | tf_op jit(solution)/shard_map/ppermute | solution.py:276
  33.5 12.9 %collective-permute-start.26 = (bf16[128,512]{1,0:T(8,128)(2,1)S(1)}, bf16[128,512]{1,0:T(8,128)(2,1)S(1)}, u32[]{:S(2)}, u32[]{:S(2)}) collective-permute-start(bf16[128,512]{1,0:T(8,128)(2,1)S(1)} %get-tuple-element.48.refs_5_), channel_id=1, source_target_pairs={{0,8},{1,9},{2,10},{3,11},{4,12},{5,13},{6,14},{7,15},{8,0},{9,1},... | collective-permute-start | bytes 393224 | tf_op jit(solution)/shard_map/ppermute | solution.py:276
  34.5 11.9 %collective-permute-start.27 = (bf16[128,512]{1,0:T(8,128)(2,1)S(1)}, bf16[128,512]{1,0:T(8,128)(2,1)S(1)}, u32[]{:S(2)}, u32[]{:S(2)}) collective-permute-start(bf16[128,512]{1,0:T(8,128)(2,1)S(1)} %get-tuple-element.48.refs_5_), channel_id=1, source_target_pairs={{0,12},{1,13},{2,14},{3,15},{4,8},{5,9},{6,10},{7,11},{8,4},{9,5},... | collective-permute-start | bytes 393224 | tf_op jit(solution)/shard_map/ppermute | solution.py:276
  46.5 21.5 %collective-permute-start.29 = (bf16[4,128,512]{2,1,0:T(8,128)(2,1)S(1)}, bf16[4,128,512]{2,1,0:T(8,128)(2,1)S(1)}, u32[]{:S(2)}, u32[]{:S(2)}) collective-permute-start(bf16[4,128,512]{2,1,0:T(8,128)(2,1)S(1)} %pad_maximum_fusion.2.refs_0_), channel_id=1, source_target_pairs={{0,1},{1,0},{2,3},{3,2},{4,5},{5,4},{6,7},{7,6},{8,9},{9,8},{10,11... | collective-permute-start | bytes 1572872 | tf_op jit(solution)/shard_map/ppermute | solution.py:276
  46.5 23.7 %collective-permute-start.28 = (bf16[4,128,512]{2,1,0:T(8,128)(2,1)S(1)}, bf16[4,128,512]{2,1,0:T(8,128)(2,1)S(1)}, u32[]{:S(2)}, u32[]{:S(2)}) collective-permute-start(bf16[4,128,512]{2,1,0:T(8,128)(2,1)S(1)} %pad_maximum_fusion.2.refs_0_), channel_id=1, source_target_pairs={{0,2},{1,3},{2,0},{3,1},{4,6},{5,7},{6,4},{7,5},{8,10},{9,11},{10,... | collective-permute-start | bytes 1572872 | tf_op jit(solution)/shard_map/ppermute | solution.py:276
  82.2 10.1 %collective-permute-start.32 = (bf16[128,256]{1,0:T(8,128)(2,1)S(1)}, bf16[128,256]{1,0:T(8,128)(2,1)S(1)}, u32[]{:S(2)}, u32[]{:S(2)}) collective-permute-start(bf16[128,256]{1,0:T(8,128)(2,1)S(1)} %project_mix.6), channel_id=1, source_target_pairs={{0,8},{1,9},{2,10},{3,11},{4,12},{5,13},{6,14},{7,15},{8,0},{9,1},... | collective-permute-start | bytes 196616 | tf_op jit(solution)/shard_map/ppermute | solution.py:276
  84.4 9.2 %collective-permute-start.33 = (bf16[128,256]{1,0:T(8,128)(2,1)S(1)}, bf16[128,256]{1,0:T(8,128)(2,1)S(1)}, u32[]{:S(2)}, u32[]{:S(2)}) collective-permute-start(bf16[128,256]{1,0:T(8,128)(2,1)S(1)} %project_mix.6), channel_id=1, source_target_pairs={{0,12},{1,13},{2,14},{3,15},{4,8},{5,9},{6,10},{7,11},{8,4},{9,5},... | collective-permute-start | bytes 196616 | tf_op jit(solution)/shard_map/ppermute | solution.py:276
  86.5 9.7 %collective-permute-start.12 = (bf16[128,512]{1,0:T(8,128)(2,1)S(1)}, bf16[128,512]{1,0:T(8,128)(2,1)S(1)}, u32[]{:S(2)}, u32[]{:S(2)}) collective-permute-start(bf16[128,512]{1,0:T(8,128)(2,1)S(1)} %bitcast_select_fusion), channel_id=1, source_target_pairs={{0,16},{1,17},{2,18},{3,19},{4,20},{5,21},{6,22},{7,23},{8,24},{9,... | collective-permute-start | bytes 393224 | tf_op jit(solution)/shard_map/ppermute | solution.py:284
  88.2 13.8 %collective-permute-start.14 = (bf16[128,512]{1,0:T(8,128)(2,1)S(1)}, bf16[128,512]{1,0:T(8,128)(2,1)S(1)}, u32[]{:S(2)}, u32[]{:S(2)}) collective-permute-start(bf16[128,512]{1,0:T(8,128)(2,1)S(1)} %bitcast_select_fusion), channel_id=1, source_target_pairs={{0,24},{1,25},{2,26},{3,27},{4,28},{5,29},{6,30},{7,31},{8,16},{9,... | collective-permute-start | bytes 393224 | tf_op jit(solution)/shard_map/ppermute | solution.py:284
  92.3 9.7 %collective-permute-start.15 = (bf16[128,512]{1,0:T(8,128)(2,1)S(1)}, bf16[128,512]{1,0:T(8,128)(2,1)S(1)}, u32[]{:S(2)}, u32[]{:S(2)}) collective-permute-start(bf16[128,512]{1,0:T(8,128)(2,1)S(1)} %bitcast_select_fusion), channel_id=1, source_target_pairs={{0,28},{1,29},{2,30},{3,31},{4,24},{5,25},{6,26},{7,27},{8,20},{9,... | collective-permute-start | bytes 393224 | tf_op jit(solution)/shard_map/ppermute | solution.py:284
  93.6 9.0 %collective-permute-start.35 = (bf16[4,128,256]{2,1,0:T(8,128)(2,1)S(1)}, bf16[4,128,256]{2,1,0:T(8,128)(2,1)S(1)}, u32[]{:S(2)}, u32[]{:S(2)}) collective-permute-start(bf16[4,128,256]{2,1,0:T(8,128)(2,1)S(1)} %pad_maximum_fusion.6.refs_0_), channel_id=1, source_target_pairs={{0,2},{1,3},{2,0},{3,1},{4,6},{5,7},{6,4},{7,5},{8,10},{9,11},{10,... | collective-permute-start | bytes 786440 | tf_op jit(solution)/shard_map/ppermute | solution.py:276
  102.7 20.0 %collective-permute-start.16 = (bf16[4,128,512]{2,1,0:T(8,128)(2,1)S(1)}, bf16[4,128,512]{2,1,0:T(8,128)(2,1)S(1)}, u32[]{:S(2)}, u32[]{:S(2)}) collective-permute-start(bf16[4,128,512]{2,1,0:T(8,128)(2,1)S(1)} %pad_maximum_fusion.1.refs_0_), channel_id=1, source_target_pairs={{0,2},{1,3},{2,0},{3,1},{4,6},{5,7},{6,4},{7,5},{8,10},{9,11},{10,... | collective-permute-start | bytes 1572872 | tf_op jit(solution)/shard_map/ppermute | solution.py:276
  105.5 10.1 %collective-permute-start.37 = (bf16[128,512]{1,0:T(8,128)(2,1)S(1)}, bf16[128,512]{1,0:T(8,128)(2,1)S(1)}, u32[]{:S(2)}, u32[]{:S(2)}) collective-permute-start(bf16[128,512]{1,0:T(8,128)(2,1)S(1)} %project_out.6), channel_id=1, source_target_pairs={{0,16},{1,17},{2,18},{3,19},{4,20},{5,21},{6,22},{7,23},{8,24},{9,... | collective-permute-start | bytes 393224 | tf_op jit(solution)/shard_map/ppermute | solution.py:284
  106.4 9.3 %collective-permute-start.38 = (bf16[128,512]{1,0:T(8,128)(2,1)S(1)}, bf16[128,512]{1,0:T(8,128)(2,1)S(1)}, u32[]{:S(2)}, u32[]{:S(2)}) collective-permute-start(bf16[128,512]{1,0:T(8,128)(2,1)S(1)} %project_out.6), channel_id=1, source_target_pairs={{0,20},{1,21},{2,22},{3,23},{4,16},{5,17},{6,18},{7,19},{8,28},{9,... | collective-permute-start | bytes 393224 | tf_op jit(solution)/shard_map/ppermute | solution.py:284
  109.0 13.6 %collective-permute-start.39 = (bf16[128,512]{1,0:T(8,128)(2,1)S(1)}, bf16[128,512]{1,0:T(8,128)(2,1)S(1)}, u32[]{:S(2)}, u32[]{:S(2)}) collective-permute-start(bf16[128,512]{1,0:T(8,128)(2,1)S(1)} %project_out.6), channel_id=1, source_target_pairs={{0,24},{1,25},{2,26},{3,27},{4,28},{5,29},{6,30},{7,31},{8,16},{9,... | collective-permute-start | bytes 393224 | tf_op jit(solution)/shard_map/ppermute | solution.py:284
  110.2 12.3 %collective-permute-start.40 = (bf16[128,512]{1,0:T(8,128)(2,1)S(1)}, bf16[128,512]{1,0:T(8,128)(2,1)S(1)}, u32[]{:S(2)}, u32[]{:S(2)}) collective-permute-start(bf16[128,512]{1,0:T(8,128)(2,1)S(1)} %project_out.6), channel_id=1, source_target_pairs={{0,28},{1,29},{2,30},{3,31},{4,24},{5,25},{6,26},{7,27},{8,20},{9,... | collective-permute-start | bytes 393224 | tf_op jit(solution)/shard_map/ppermute | solution.py:284
  122.8 14.3 %collective-permute-start.41 = (bf16[4,128,512]{2,1,0:T(8,128)(2,1)S(1)}, bf16[4,128,512]{2,1,0:T(8,128)(2,1)S(1)}, u32[]{:S(2)}, u32[]{:S(2)}) collective-permute-start(bf16[4,128,512]{2,1,0:T(8,128)(2,1)S(1)} %pad_maximum_fusion.3.refs_0_), channel_id=1, source_target_pairs={{0,2},{1,3},{2,0},{3,1},{4,6},{5,7},{6,4},{7,5},{8,10},{9,11},{10,... | collective-permute-start | bytes 1572872 | tf_op jit(solution)/shard_map/ppermute | solution.py:276
  123.4 13.7 %collective-permute-start.18 = (bf16[4,128,512]{2,1,0:T(8,128)(2,1)S(1)}, bf16[4,128,512]{2,1,0:T(8,128)(2,1)S(1)}, u32[]{:S(2)}, u32[]{:S(2)}) collective-permute-start(bf16[4,128,512]{2,1,0:T(8,128)(2,1)S(1)} %collective-permute-done.16.refs_0_), channel_id=1, source_target_pairs={{0,1},{1,0},{2,3},{3,2},{4,5},{5,4},{6,7},{7,6},{8,9},{9,8},{10,11... | collective-permute-start | bytes 1572872 | tf_op jit(solution)/shard_map/ppermute | solution.py:276
  137.1 16.7 %collective-permute-start.43 = (bf16[4,128,512]{2,1,0:T(8,128)(2,1)S(1)}, bf16[4,128,512]{2,1,0:T(8,128)(2,1)S(1)}, u32[]{:S(2)}, u32[]{:S(2)}) collective-permute-start(bf16[4,128,512]{2,1,0:T(8,128)(2,1)S(1)} %collective-permute-done.41.refs_0_), channel_id=1, source_target_pairs={{0,1},{1,0},{2,3},{3,2},{4,5},{5,4},{6,7},{7,6},{8,9},{9,8},{10,11... | collective-permute-start | bytes 1572872 | tf_op jit(solution)/shard_map/ppermute | solution.py:276
  143.5 8.5 %collective-permute-start.20 = (bf16[128,256]{1,0:T(8,128)(2,1)S(1)}, bf16[128,256]{1,0:T(8,128)(2,1)S(1)}, u32[]{:S(2)}, u32[]{:S(2)}) collective-permute-start(bf16[128,256]{1,0:T(8,128)(2,1)S(1)} %project_mix.5), channel_id=1, source_target_pairs={{0,8},{1,9},{2,10},{3,11},{4,12},{5,13},{6,14},{7,15},{8,0},{9,1},... | collective-permute-start | bytes 196616 | tf_op jit(solution)/shard_map/ppermute | solution.py:276
  152.2 8.7 %collective-permute-start.23 = (bf16[4,128,256]{2,1,0:T(8,128)(2,1)S(1)}, bf16[4,128,256]{2,1,0:T(8,128)(2,1)S(1)}, u32[]{:S(2)}, u32[]{:S(2)}) collective-permute-start(bf16[4,128,256]{2,1,0:T(8,128)(2,1)S(1)} %pad_maximum_fusion.5.refs_0_), channel_id=1, source_target_pairs={{0,2},{1,3},{2,0},{3,1},{4,6},{5,7},{6,4},{7,5},{8,10},{9,11},{10,... | collective-permute-start | bytes 786440 | tf_op jit(solution)/shard_map/ppermute | solution.py:276
  (34 other events, 234.4 us)

commit v4 on v3

--- a/solution.py
+++ b/solution.py
@@ -8,6 +8,7 @@
 from jax.sharding import PartitionSpec as P
 
 EPS = 1e-06
+SENT = object()
 VMEM_LIMIT = 12 * 1024 * 1024
 PAD = 8
 
@@ -51,6 +52,13 @@
         mine = functools.reduce(jnp.logical_or, [section_idx == s for s in members])
         result = jnp.where(mine, value, result)
     return result
+
+
+def routes(far, near):
+    if (far, near) == (4, 2):
+        return [4, 2, 1], [(1, [4, 2]), (2, [4]), (3, [4])]
+    line = [d * near for d in range(far)]
+    return line[1:], [(d, line) for d in range(1, near)]
 
 
 def project_cells(cells, sides, rank_ref, w_ref, gain_ref, acc_ref, sq_ref, ready=None):
@@ -93,10 +101,12 @@
 
 def first_kernel(cells, later, core, rank_ref, *refs):
     sides = refs[:core]
-    w_far, gain_ref, taps_ref, decay_ref, acc_ref, sq_ref, w_ref, gain_here, long_ref = refs[core : core + 9]
-    sems = refs[-1]
+    w_far, gain_far, taps_far, decay_far, acc_ref, sq_ref, w_ref, gain_ref, long_ref = refs[core : core + 9]
+    taps_ref, decay_ref, sems, small_sems = refs[core + 9 :]
     wide = core * sides[0].shape[2]
     chip = lax.div(rank_ref[0], core)
+    small = [(gain_far, gain_ref), (taps_far, taps_ref), (decay_far, decay_ref)]
+    small = [pltpu.make_async_copy(src, dst, small_sems.at[n]) for n, (src, dst) in enumerate(small)]
     copies = []
     for n, cell in enumerate(cells + later):
         columns = pl.ds(pl.multiple_of((chip ^ cell) * wide, wide), wide)
@@ -106,11 +116,11 @@
                 for i in range(w_far.shape[0])
             ]
         )
-    for group in copies:
+    for group in [small] + copies:
         for copy in group:
             copy.start()
-
-    gain_here[...] = gain_ref[...]
+    for copy in small:
+        copy.wait()
     lags = lax.broadcasted_iota(jnp.int32, long_ref.shape, 0).astype(jnp.float32)
     long_ref[...] = taps_ref[...].T * jnp.exp(-decay_ref[...] * lags)
 
@@ -218,13 +228,16 @@
     operands = [rank, *sides, w_in, gain]
     if taps is not None:
         operands += [taps, decay]
-        operands[1 + core] = pltpu.with_memory_space_constraint(w_in, pltpu.HBM)
+        operands[1 + core :] = [pltpu.with_memory_space_constraint(x, pltpu.HBM) for x in operands[1 + core :]]
+        scratch.append(pltpu.VMEM(taps.shape, taps.dtype))
+        scratch.append(pltpu.VMEM(decay.shape, decay.dtype))
         outs.append(pltpu.VMEM(w_in.shape, w_in.dtype))
         outs.append(pltpu.VMEM(gain.shape, gain.dtype))
         outs.append(pltpu.VMEM(taps.shape[::-1], taps.dtype))
         scratch.append(pltpu.SemaphoreType.DMA((len(cells) + len(later), branches)))
+        scratch.append(pltpu.SemaphoreType.DMA((3,)))
         kernel = functools.partial(first_kernel, cells, later, core)
-        return call(kernel, operands, outs, scratch, flops, "load_project", (1 + core,), 4 * w_in.size)
+        return call(kernel, operands, outs, scratch, flops, "load_project", range(1 + core, 5 + core), 4 * w_in.size)
     return call(functools.partial(early_kernel, cells, core), operands, outs, scratch, flops, "project_early")
 
 
@@ -275,80 +288,93 @@
     def swap(value, offset):
         return lax.ppermute(value, "dp", [(r, r ^ offset) for r in range(dp_count)])
 
-    def onward(value, offset):
-        pairs = [
-            (s * dp_count + r, (s + 1) % section_count * dp_count + (r ^ offset))
-            for s in range(section_count)
-            for r in range(dp_count)
-        ]
-        return lax.ppermute(value, ("section", "dp"), pairs)
-
-    def after(value, earlier):
-        return value if earlier is None else lax.optimization_barrier((value, earlier))[0]
-
-    def gather(source, cross, order):
-        source = after(source, order.get("near"))
-        blocks = [onward(source, 0) if cross else source]
-        blocks += [(onward if cross else swap)(source, d * group) for d in range(1, far)]
-        blocks = after(blocks, order.get("early"))
-        line = jnp.stack(blocks)
-        cells = [d * near for d in range(far)]
-        leaving = after(line, order.get("rest"))
-        rest = [swap(leaving, d * core) for d in range(1, near)]
-        rest = rest[0] if near == 2 else jnp.concatenate(rest)
-        more = [cell ^ d for d in range(1, near) for cell in cells]
-        early = both_cores(cells, line)
-        order["near"], order["rest"] = early[1][-1], rest
-        return early, (more, rest), blocks[0]
-
-    def both_cores(cells, line):
-        return cells, [line] + [swap(line, c) for c in range(1, core)]
+    first_round, second_round = routes(far, near)
+
+    def after(value, *earlier):
+        return lax.optimization_barrier((value, [x for x in earlier if x is not None]))[0]
+
+    def to_core(blocks):
+        return [blocks] + [swap(blocks, c) for c in range(1, core)]
+
+    def round_one(source):
+        return {0: source} | {d: swap(source, d * core) for d in first_round}
+
+    def round_two(blocks):
+        cells, rest = [], []
+        for d, sent in second_round:
+            rest.append(swap(jnp.stack([blocks[b] for b in sent]), d * core))
+            cells += [d ^ b for b in sent]
+        return cells, rest
 
     short_rows = short_filter[0].transpose(0, 2, 1).reshape(-1, short_filter.shape[2])
-    w_in_here, gain, loaded = w_in[0], norm_gain, (filter_taps[0], decay_rate)
+    weights, loaded = {"in": w_in[0], "gain": norm_gain}, [filter_taps[0], decay_rate]
     waiting = carried[0]
     results = {}
-    for w, slots in enumerate(waves):
-        slot_count = max(len(ticks) for ticks in slots)
-        sources = []
-        for i in range(slot_count):
+
+    def start(slot, before, behind):
+        source = after(slot["own"], before["line"]) if before else slot["own"]
+        slot["blocks"] = after(round_one(source), before.get("acc"), before.get("rest"))
+        slot["line"] = jnp.stack(list(slot["blocks"].values()))
+
+    def spread(slot, before, behind):
+        blocks = after(slot["blocks"], before.get("rest"))
+        slot["cells"], slot["rest"] = round_two(blocks)
+        early = list(blocks), after(to_core(slot["line"]), before.get("y"))
+        slot["acc"], slot["sq"], *loads = project_early(early, slot["cells"], weights["in"], weights["gain"], rank, *loaded)
+        if loads:
+            weights["in"], weights["gain"], weights["long"] = loads
+            loaded.clear()
+
+    def work(slot, before, behind):
+        rest = jnp.concatenate(after(slot["rest"], slot["acc"], before.get("y_blocks")))
+        late = slot["cells"], to_core(rest)
+        slot["y"] = mix(late, weights["in"], weights["gain"], slot["acc"], slot["sq"], short_rows, weights["long"], rank)
+        slot["y_blocks"] = after(round_one(slot["y"]), before.get("y_rest"))
+        slot["y_line"] = jnp.stack(list(slot["y_blocks"].values()))
+
+    def spread_y(slot, before, behind):
+        blocks = after(slot["y_blocks"], before.get("y_rest"), behind.get("rest"))
+        slot["y_cells"], slot["y_rest"] = round_two(blocks)
+        slot["y_early"] = list(blocks), to_core(slot["y_line"])
+
+    def finish(slot, before, behind):
+        late = slot["y_cells"], to_core(jnp.concatenate(after(slot["y_rest"], behind.get("y"))))
+        slot["out"] = project_out([slot["y_early"], late], w_out[0], slot["own"], rank)
+
+    phases = [start, spread, work, spread_y, finish]
+    for w, ticks in enumerate(waves):
+        slots = []
+        for i in range(max(len(mine) for mine in ticks)):
             options = []
             for s in range(section_count):
-                if w == 0:
-                    ticks = slots[s]
-                    if i >= len(ticks):
-                        options.append(None)
-                    elif s == 0:
-                        options.append(fresh_acts[ticks[i]])
-                    else:
-                        options.append(waiting)
+                if i >= len(ticks[s]):
+                    options.append(None)
+                elif s == 0:
+                    options.append(fresh_acts[ticks[s][i]])
+                elif w == 0:
+                    options.append(waiting)
                 else:
-                    ticks = slots[(s + 1) % section_count]
-                    if i >= len(ticks):
-                        options.append(None)
-                    elif s + 1 == section_count:
-                        options.append(fresh_acts[ticks[i]])
-                    else:
-                        options.append(results[s, ticks[i] - 1])
-            sources.append(pick(section_idx, options))
-        made = []
-        order, y_order = {}, {}
-        for source in sources:
-            early, (cells, rest), own = gather(source, w > 0, order)
-            acc, sq, *loads = project_early(early, cells, w_in_here, gain, rank, *loaded)
-            if loads:
-                w_in_here, gain, long_rows = [pltpu.with_memory_space_constraint(x, pltpu.VMEM) for x in loads]
-                loaded = ()
-            order["early"] = acc
-            late = both_cores(cells, after(rest, acc))
-            acc = after(acc, y_order.get("near"))
-            y = mix(late, w_in_here, gain, acc, sq, short_rows, long_rows, rank)
-            y_order["near"] = y_order.get("rest")
-            early, late, _ = gather(y, False, y_order)
-            made.append(project_out([early, both_cores(*late)], w_out[0], own, rank))
+                    options.append(SENT)
+            if any(option is SENT for option in options):
+                leaving = pick(
+                    section_idx,
+                    [
+                        results[s, ticks[s + 1][i] - 1] if s + 1 < section_count and i < len(ticks[s + 1]) else None
+                        for s in range(section_count)
+                    ],
+                )
+                sent = lax.ppermute(leaving, "section", [(s, s + 1) for s in range(section_count - 1)])
+                options = [sent if option is SENT else option for option in options]
+            slots.append({"own": pick(section_idx, options)})
+        for t in range(len(phases) + len(slots) - 1):
+            for i, slot in enumerate(slots):
+                if 0 <= t - i < len(phases):
+                    before = slots[i - 1] if i > 0 else {}
+                    behind = slots[i + 1] if i + 1 < len(slots) else {}
+                    phases[t - i](slot, before, behind)
         for s in range(section_count):
-            for i, k in enumerate(slots[s]):
-                results[s, k] = made[i]
+            for i, k in enumerate(ticks[s]):
+                results[s, k] = slots[i]["out"]
     outputs = []
     for k in range(tick_count):
         outputs.append(pick(section_idx, [results[s, k] for s in range(section_count)]))

time: 180 us -> 159 us (0.88)
  waiting for transfers between devices: 81.5 us -> 42.2 us
  starting transfers between devices: 51.5 us -> 67.4 us
  Pallas kernels: 31.7 us -> 34.6 us
    ppermute x42 -> x64, starting transfers between devices: 37.7 us -> 62.3 us  [swap(): return lax.ppermute(value, 'dp', [(r, r ^ offset) for r in range(dp_count)])]
    ppermute x42 -> x64, waiting for transfers between devices: 65.8 us -> 41.7 us  [swap(): return lax.ppermute(value, 'dp', [(r, r ^ offset) for r in range(dp_count)])]
    ppermute x8 -> x2, waiting for transfers between devices: 15.7 us -> 0.56 us  [body(): lax.ppermute(leaving, 'section', [(s, s + 1) for s in range(section_count...]
    ppermute x8 -> x2, starting transfers between devices: 13.9 us -> 5.1 us  [body(): lax.ppermute(leaving, 'section', [(s, s + 1) for s in range(section_count...]
    pallas_call x12, Pallas kernels: 31.7 us -> 34.6 us  [call(): pl.pallas_call(kernel, in_specs=specs, out_specs=in_vmem(len(outs)), out_...]
    unnamed x17 -> x27, local copies, waits for them, and re-layouts: 11.5 us -> 10.3 us
  transfers between devices with their start and end apart: 50 -> 66, of which waited for: 26 -> 26; matrix products, arithmetic and copies ran while one was open for 1% -> 1% of each run, Pallas kernels for 15% -> 21%
where the time goes in v4:
time: 159 us
  starting transfers between devices  67.4 us (42%)
  waiting for transfers between devices  42.2 us (27%)
  Pallas kernels  34.6 us (22%)
  local copies, waits for them, and re-layouts  10.4 us (7%)
  other arithmetic  3.33 us (2%)
    ppermute x64, starting transfers between devices, swap(): return lax.ppermute(value, 'dp', [(r, r ^ offset) for r in range(dp_count)])  62.3 us
    ppermute x64, waiting for transfers between devices, swap(): return lax.ppermute(value, 'dp', [(r, r ^ offset) for r in range(dp_count)])  41.7 us
    pallas_call x12, Pallas kernels, call(): pl.pallas_call(kernel, in_specs=specs, out_specs=in_vmem(len(outs)), out_...  34.6 us
    unnamed x27, local copies, waits for them, and re-layouts  10.3 us
    ppermute x2, starting transfers between devices, body(): lax.ppermute(leaving, 'section', [(s, s + 1) for s in range(section_count...  5.1 us
  transfers between devices with their start and end apart: 66, of which 26 were waited for; matrix products, arithmetic and copies ran while one was open for 1% of the time, Pallas kernels for 21%

profile of v4, /device:TPU:0, one launch (start us, length us, event | category | flops | bytes accessed | tf_op | source)
XLA Modules:
  0.0 158.6 jit_solution(11209234687036513806)
XLA Ops:
  1.0 4.1 %collective-permute-start.2 = (bf16[128,512]{1,0:T(8,128)(2,1)S(1)}, bf16[128,512]{1,0:T(8,128)(2,1)S(1)}, u32[]{:S(2)}, u32[]{:S(2)}) collective-permute-start(bf16[128,512]{1,0:T(8,128)(2,1)S(1)} %get-tuple-element.106.refs_5_), channel_id=1, source_target_pairs={{0,8},{1,9},{2,10},{3,11},{4,12},{5,13},{6,14},{7,15},{8,0},{9,1},... | collective-permute-start | bytes 393224 | tf_op jit(solution)/shard_map/ppermute | solution.py:289
  8.2 3.3 %collective-permute-done.2 = bf16[128,512]{1,0:T(8,128)(2,1)S(1)} collective-permute-done((bf16[128,512]{1,0:T(8,128)(2,1)S(1)}, bf16[128,512]{1,0:T(8,128)(2,1)S(1)}, u32[]{:S(2)}, u32[]{:S(2)}) %collective-permute-start.2) | collective-permute-done | bytes 131104 | tf_op jit(solution)/shard_map/ppermute | solution.py:289
  19.3 8.1 %load_project.1 = (f32[3,128,256]{2,1,0:T(8,128)S(1)}, f32[128,128]{1,0:T(8,128)S(1)}, bf16[3,256,8192]{2,1,0:T(8,128)(2,1)S(1)}, f32[1,8192]{1,0:T(1,128)S(1)}, f32[128,256]{1,0:T(8,128)S(1)}) custom-call(s32[1]{0:T(128)} %bitcast.rank_ref, bf16[4,128,512]{2,1,0:T(8,128)(2,1)S(1)} %pad_maximum_fusion.refs_0_, ...), custom_call_target="tpu_custom_call" | custom-call | flops 805306368 | bytes 25952256 | tf_op jit(solution)/shard_map/load_project/pallas_call | solution.py:205
  27.4 4.6 %copy-done = bf16[3,256,8192]{2,1,0:T(8,128)(2,1)} copy-done((bf16[3,256,8192]{2,1,0:T(8,128)(2,1)}, bf16[3,256,8192]{2,1,0:T(8,128)(2,1)S(1)}, u32[]{:S(2)}) %copy-start) | copy-done | bytes 12582936
  33.7 3.3 %collective-permute-done.12 = bf16[128,512]{1,0:T(8,128)(2,1)S(1)} collective-permute-done((bf16[128,512]{1,0:T(8,128)(2,1)S(1)}, bf16[128,512]{1,0:T(8,128)(2,1)S(1)}, u32[]{:S(2)}, u32[]{:S(2)}) %collective-permute-start.12) | collective-permute-done | bytes 131104 | tf_op jit(solution)/shard_map/ppermute | solution.py:289
  38.8 4.6 %copy-done.1 = bf16[3,256,8192]{2,1,0:T(8,128)(2,1)S(1)} copy-done((bf16[3,256,8192]{2,1,0:T(8,128)(2,1)S(1)}, bf16[3,256,8192]{2,1,0:T(8,128)(2,1)}, u32[]{:S(2)}) %copy-start.1) | copy-done | bytes 12582936
  43.3 4.2 %project_mix.4 = bf16[128,256]{1,0:T(8,128)(2,1)S(1)} custom-call(s32[1]{0:T(128)} %bitcast.rank_ref, bf16[4,128,512]{2,1,0:T(8,128)(2,1)S(1)} %constant_dynamic-update-slice_fusion.refs_0_, bf16[4,128,512]{2,1,0:T(8,128)(2,1)S(1)} %collective-permute-done.7.refs_1_, bf16[3,256,8192]{2,1,0:T(8,128)(2,1)S(1)} %copy-done.1, ...), custom_call_target="tpu_custom_call" | custom-call | flops 805306368 | bytes 786432 | tf_op jit(solution)/shard_map/project_mix/pallas_call | solution.py:205
  50.7 2.8 %collective-permute-done.10 = bf16[128,256]{1,0:T(8,128)(2,1)S(1)} collective-permute-done((bf16[128,256]{1,0:T(8,128)(2,1)S(1)}, bf16[128,256]{1,0:T(8,128)(2,1)S(1)}, u32[]{:S(2)}, u32[]{:S(2)}) %collective-permute-start.10) | collective-permute-done | bytes 65568 | tf_op jit(solution)/shard_map/ppermute | solution.py:289
  56.4 2.6 %collective-permute-done.9 = bf16[128,256]{1,0:T(8,128)(2,1)S(1)} collective-permute-done((bf16[128,256]{1,0:T(8,128)(2,1)S(1)}, bf16[128,256]{1,0:T(8,128)(2,1)S(1)}, u32[]{:S(2)}, u32[]{:S(2)}) %collective-permute-start.9) | collective-permute-done | bytes 65568 | tf_op jit(solution)/shard_map/ppermute | solution.py:289
  60.7 2.5 %collective-permute-start.19 = (bf16[1,128,256]{2,1,0:T(8,128)(2,1)S(1)}, bf16[1,128,256]{2,1,0:T(8,128)(2,1)S(1)}, u32[]{:S(2)}, u32[]{:S(2)}) collective-permute-start(bf16[1,128,256]{2,1,0:T(8,128)(2,1)S(1)} %bitcast.113), channel_id=1, source_target_pairs={{0,4},{1,5},{2,6},{3,7},{4,0},{5,1},{6,2},{7,3},{8,12},{9,13},{10,... | collective-permute-start | bytes 196616 | tf_op jit(solution)/shard_map/ppermute | solution.py:289
  64.0 4.4 %project_mix.5 = bf16[128,256]{1,0:T(8,128)(2,1)S(1)} custom-call(s32[1]{0:T(128)} %bitcast.rank_ref, bf16[4,128,512]{2,1,0:T(8,128)(2,1)S(1)} %constant_dynamic-update-slice_fusion.3.refs_0_, bf16[4,128,512]{2,1,0:T(8,128)(2,1)S(1)} %collective-permute-done.22.refs_1_, bf16[3,256,8192]{2,1,0:T(8,128)(2,1)S(1)} %copy-done.2, ...), custom_call_target="tpu_custom_call" | custom-call | flops 805306368 | bytes 786432 | tf_op jit(solution)/shard_map/project_mix/pallas_call | solution.py:205
  71.9 3.4 %collective-permute-done.39 = bf16[128,256]{1,0:T(8,128)(2,1)S(1)} collective-permute-done((bf16[128,256]{1,0:T(8,128)(2,1)S(1)}, bf16[128,256]{1,0:T(8,128)(2,1)S(1)}, u32[]{:S(2)}, u32[]{:S(2)}) %collective-permute-start.39) | collective-permute-done | bytes 65568 | tf_op jit(solution)/shard_map/ppermute | solution.py:289
  77.7 3.5 %collective-permute-start.24 = (bf16[128,512]{1,0:T(8,128)(2,1)S(1)}, bf16[128,512]{1,0:T(8,128)(2,1)S(1)}, u32[]{:S(2)}, u32[]{:S(2)}) collective-permute-start(bf16[128,512]{1,0:T(8,128)(2,1)S(1)} %project_out.4), channel_id=1, source_target_pairs={{0,16},{1,17},{2,18},{3,19},{4,20},{5,21},{6,22},{7,23},{8,24},{9,... | collective-permute-start | bytes 393224 | tf_op jit(solution)/shard_map/ppermute | solution.py:366
  83.5 3.0 %collective-permute-done.43 = bf16[1,128,256]{2,1,0:T(8,128)(2,1)S(1)} collective-permute-done((bf16[1,128,256]{2,1,0:T(8,128)(2,1)S(1)}, bf16[1,128,256]{2,1,0:T(8,128)(2,1)S(1)}, u32[]{:S(2)}, u32[]{:S(2)}) %collective-permute-start.43) | collective-permute-done | bytes 65568 | tf_op jit(solution)/shard_map/ppermute | solution.py:289
  91.5 3.4 %collective-permute-done.27 = bf16[128,512]{1,0:T(8,128)(2,1)S(1)} collective-permute-done((bf16[128,512]{1,0:T(8,128)(2,1)S(1)}, bf16[128,512]{1,0:T(8,128)(2,1)S(1)}, u32[]{:S(2)}, u32[]{:S(2)}) %collective-permute-start.27) | collective-permute-done | bytes 131104 | tf_op jit(solution)/shard_map/ppermute | solution.py:289
  105.3 2.2 %project_early.4 = (f32[3,128,256]{2,1,0:T(8,128)S(1)}, f32[128,128]{1,0:T(8,128)S(1)}) custom-call(s32[1]{0:T(128)} %bitcast.rank_ref, bf16[4,128,512]{2,1,0:T(8,128)(2,1)S(1)} %pad_maximum_fusion.2.refs_0_, bf16[4,128,512]{2,1,0:T(8,128)(2,1)S(1)} %collective-permute-done.31.refs_1_, bf16[3,256,8192]{2,1,0:T(8,128)(2,1)S(1)} %copy-done.2, ...), custom_call_target="tpu_custom_call" | custom-call | flops 805306368 | bytes 786432 | tf_op jit(solution)/shard_map/project_early/pallas_call | solution.py:205
  107.5 2.5 %collective-permute-done.30 = bf16[1,128,512]{2,1,0:T(8,128)(2,1)S(1)} collective-permute-done((bf16[1,128,512]{2,1,0:T(8,128)(2,1)S(1)}, bf16[1,128,512]{2,1,0:T(8,128)(2,1)S(1)}, u32[]{:S(2)}, u32[]{:S(2)}) %collective-permute-start.30) | collective-permute-done | bytes 131104 | tf_op jit(solution)/shard_map/ppermute | solution.py:289
  116.2 4.2 %project_mix.6 = bf16[128,256]{1,0:T(8,128)(2,1)S(1)} custom-call(s32[1]{0:T(128)} %bitcast.rank_ref, bf16[4,128,512]{2,1,0:T(8,128)(2,1)S(1)} %constant_dynamic-update-slice_fusion.9.refs_0_, bf16[4,128,512]{2,1,0:T(8,128)(2,1)S(1)} %collective-permute-done.32.refs_1_, bf16[3,256,8192]{2,1,0:T(8,128)(2,1)S(1)} %copy-done.2, ...), custom_call_target="tpu_custom_call" | custom-call | flops 805306368 | bytes 786432 | tf_op jit(solution)/shard_map/project_mix/pallas_call | solution.py:205
  121.0 2.3 %collective-permute-start.51 = (bf16[1,128,512]{2,1,0:T(8,128)(2,1)S(1)}, bf16[1,128,512]{2,1,0:T(8,128)(2,1)S(1)}, u32[]{:S(2)}, u32[]{:S(2)}) collective-permute-start(bf16[1,128,512]{2,1,0:T(8,128)(2,1)S(1)} %bitcast.90), channel_id=1, source_target_pairs={{0,6},{1,7},{2,4},{3,5},{4,2},{5,3},{6,0},{7,1},{8,14},{9,15},{10,... | collective-permute-start | bytes 393224 | tf_op jit(solution)/shard_map/ppermute | solution.py:289
  128.1 2.2 %project_early.5 = (f32[3,128,256]{2,1,0:T(8,128)S(1)}, f32[128,128]{1,0:T(8,128)S(1)}) custom-call(s32[1]{0:T(128)} %bitcast.rank_ref, bf16[4,128,512]{2,1,0:T(8,128)(2,1)S(1)} %pad_maximum_fusion.3.refs_0_, bf16[4,128,512]{2,1,0:T(8,128)(2,1)S(1)} %collective-permute-done.55.refs_1_, bf16[3,256,8192]{2,1,0:T(8,128)(2,1)S(1)} %copy-done.2, ...), custom_call_target="tpu_custom_call" | custom-call | flops 805306368 | bytes 786432 | tf_op jit(solution)/shard_map/project_early/pallas_call | solution.py:205
  130.3 2.5 %collective-permute-done.34 = bf16[128,256]{1,0:T(8,128)(2,1)S(1)} collective-permute-done((bf16[128,256]{1,0:T(8,128)(2,1)S(1)}, bf16[128,256]{1,0:T(8,128)(2,1)S(1)}, u32[]{:S(2)}, u32[]{:S(2)}) %collective-permute-start.34) | collective-permute-done | bytes 65568 | tf_op jit(solution)/shard_map/ppermute | solution.py:289
  136.7 4.2 %project_mix.7 = bf16[128,256]{1,0:T(8,128)(2,1)S(1)} custom-call(s32[1]{0:T(128)} %bitcast.rank_ref, bf16[4,128,512]{2,1,0:T(8,128)(2,1)S(1)} %constant_dynamic-update-slice_fusion.15.refs_0_, bf16[4,128,512]{2,1,0:T(8,128)(2,1)S(1)} %collective-permute-done.56.refs_1_, bf16[3,256,8192]{2,1,0:T(8,128)(2,1)S(1)} %copy-done.2, ...), custom_call_target="tpu_custom_call" | custom-call | flops 805306368 | bytes 786432 | tf_op jit(solution)/shard_map/project_mix/pallas_call | solution.py:205
  144.3 3.1 %collective-permute-done.60 = bf16[128,256]{1,0:T(8,128)(2,1)S(1)} collective-permute-done((bf16[128,256]{1,0:T(8,128)(2,1)S(1)}, bf16[128,256]{1,0:T(8,128)(2,1)S(1)}, u32[]{:S(2)}, u32[]{:S(2)}) %collective-permute-start.60) | collective-permute-done | bytes 65568 | tf_op jit(solution)/shard_map/ppermute | solution.py:289
  151.6 2.8 %collective-permute-done.64 = bf16[1,128,256]{2,1,0:T(8,128)(2,1)S(1)} collective-permute-done((bf16[1,128,256]{2,1,0:T(8,128)(2,1)S(1)}, bf16[1,128,256]{2,1,0:T(8,128)(2,1)S(1)}, u32[]{:S(2)}, u32[]{:S(2)}) %collective-permute-start.64) | collective-permute-done | bytes 65568 | tf_op jit(solution)/shard_map/ppermute | solution.py:289
  (176 shorter events, 74.2 us)
Async XLA Ops:
  1.0 10.5 %collective-permute-start.2 = (bf16[128,512]{1,0:T(8,128)(2,1)S(1)}, bf16[128,512]{1,0:T(8,128)(2,1)S(1)}, u32[]{:S(2)}, u32[]{:S(2)}) collective-permute-start(bf16[128,512]{1,0:T(8,128)(2,1)S(1)} %get-tuple-element.106.refs_5_), channel_id=1, source_target_pairs={{0,8},{1,9},{2,10},{3,11},{4,12},{5,13},{6,14},{7,15},{8,0},{9,1},... | collective-permute-start | bytes 393224 | tf_op jit(solution)/shard_map/ppermute | solution.py:289
  11.9 21.6 %collective-permute-start.3 = (bf16[2,128,512]{2,1,0:T(8,128)(2,1)S(1)}, bf16[2,128,512]{2,1,0:T(8,128)(2,1)S(1)}, u32[]{:S(2)}, u32[]{:S(2)}) collective-permute-start(bf16[2,128,512]{2,1,0:T(8,128)(2,1)S(1)} %pad_maximum_fusion.4), channel_id=1, source_target_pairs={{0,2},{1,3},{2,0},{3,1},{4,6},{5,7},{6,4},{7,5},{8,10},{9,11},{10,... | collective-permute-start | bytes 786440 | tf_op jit(solution)/shard_map/ppermute | solution.py:289
  13.5 18.5 %collective-permute-start.5 = (bf16[1,128,512]{2,1,0:T(8,128)(2,1)S(1)}, bf16[1,128,512]{2,1,0:T(8,128)(2,1)S(1)}, u32[]{:S(2)}, u32[]{:S(2)}) collective-permute-start(bf16[1,128,512]{2,1,0:T(8,128)(2,1)S(1)} %bitcast.98), channel_id=1, source_target_pairs={{0,6},{1,7},{2,4},{3,5},{4,2},{5,3},{6,0},{7,1},{8,14},{9,15},{10,... | collective-permute-start | bytes 393224 | tf_op jit(solution)/shard_map/ppermute | solution.py:289
  14.9 18.6 %collective-permute-start.4 = (bf16[1,128,512]{2,1,0:T(8,128)(2,1)S(1)}, bf16[1,128,512]{2,1,0:T(8,128)(2,1)S(1)}, u32[]{:S(2)}, u32[]{:S(2)}) collective-permute-start(bf16[1,128,512]{2,1,0:T(8,128)(2,1)S(1)} %bitcast.99), channel_id=1, source_target_pairs={{0,4},{1,5},{2,6},{3,7},{4,0},{5,1},{6,2},{7,3},{8,12},{9,13},{10,... | collective-permute-start | bytes 393224 | tf_op jit(solution)/shard_map/ppermute | solution.py:289
  15.5 18.2 %collective-permute-start.14 = (bf16[128,512]{1,0:T(8,128)(2,1)S(1)}, bf16[128,512]{1,0:T(8,128)(2,1)S(1)}, u32[]{:S(2)}, u32[]{:S(2)}) collective-permute-start(bf16[128,512]{1,0:T(8,128)(2,1)S(1)} %get-tuple-element.123.refs_5_), channel_id=1, source_target_pairs={{0,8},{1,9},{2,10},{3,11},{4,12},{5,13},{6,14},{7,15},{8,0},{9,1},... | collective-permute-start | bytes 393224 | tf_op jit(solution)/shard_map/ppermute | solution.py:289
  17.3 16.4 %collective-permute-start.13 = (bf16[128,512]{1,0:T(8,128)(2,1)S(1)}, bf16[128,512]{1,0:T(8,128)(2,1)S(1)}, u32[]{:S(2)}, u32[]{:S(2)}) collective-permute-start(bf16[128,512]{1,0:T(8,128)(2,1)S(1)} %get-tuple-element.123.refs_5_), channel_id=1, source_target_pairs={{0,4},{1,5},{2,6},{3,7},{4,0},{5,1},{6,2},{7,3},{8,12},{9,13},{10,... | collective-permute-start | bytes 393224 | tf_op jit(solution)/shard_map/ppermute | solution.py:289
  37.0 13.1 %collective-permute-start.21 = (bf16[4,128,512]{2,1,0:T(8,128)(2,1)S(1)}, bf16[4,128,512]{2,1,0:T(8,128)(2,1)S(1)}, u32[]{:S(2)}, u32[]{:S(2)}) collective-permute-start(bf16[4,128,512]{2,1,0:T(8,128)(2,1)S(1)} %pad_maximum_fusion.1.refs_0_), channel_id=1, source_target_pairs={{0,1},{1,0},{2,3},{3,2},{4,5},{5,4},{6,7},{7,6},{8,9},{9,8},{10,11... | collective-permute-start | bytes 1572872 | tf_op jit(solution)/shard_map/ppermute | solution.py:289
  37.2 21.9 %collective-permute-start.15 = (bf16[2,128,512]{2,1,0:T(8,128)(2,1)S(1)}, bf16[2,128,512]{2,1,0:T(8,128)(2,1)}, u32[]{:S(2)}, u32[]{:S(2)}) collective-permute-start(bf16[2,128,512]{2,1,0:T(8,128)(2,1)S(1)} %pad_maximum_fusion.6), channel_id=1, source_target_pairs={{0,2},{1,3},{2,0},{3,1},{4,6},{5,7},{6,4},{7,5},{8,10},{9,11},{10,... | collective-permute-start | bytes 786440 | tf_op jit(solution)/shard_map/ppermute | solution.py:289
  48.2 10.9 %collective-permute-start.17 = (bf16[1,128,512]{2,1,0:T(8,128)(2,1)S(1)}, bf16[1,128,512]{2,1,0:T(8,128)(2,1)S(1)}, u32[]{:S(2)}, u32[]{:S(2)}) collective-permute-start(bf16[1,128,512]{2,1,0:T(8,128)(2,1)S(1)} %bitcast.86), channel_id=1, source_target_pairs={{0,6},{1,7},{2,4},{3,5},{4,2},{5,3},{6,0},{7,1},{8,14},{9,15},{10,... | collective-permute-start | bytes 393224 | tf_op jit(solution)/shard_map/ppermute | solution.py:289
  48.7 10.4 %collective-permute-start.16 = (bf16[1,128,512]{2,1,0:T(8,128)(2,1)S(1)}, bf16[1,128,512]{2,1,0:T(8,128)(2,1)S(1)}, u32[]{:S(2)}, u32[]{:S(2)}) collective-permute-start(bf16[1,128,512]{2,1,0:T(8,128)(2,1)S(1)} %bitcast.87), channel_id=1, source_target_pairs={{0,4},{1,5},{2,6},{3,7},{4,0},{5,1},{6,2},{7,3},{8,12},{9,13},{10,... | collective-permute-start | bytes 393224 | tf_op jit(solution)/shard_map/ppermute | solution.py:289
  63.9 13.1 %collective-permute-start.11 = (bf16[4,128,256]{2,1,0:T(8,128)(2,1)S(1)}, bf16[4,128,256]{2,1,0:T(8,128)(2,1)S(1)}, u32[]{:S(2)}, u32[]{:S(2)}) collective-permute-start(bf16[4,128,256]{2,1,0:T(8,128)(2,1)S(1)} %pad_maximum_fusion.5.refs_0_), channel_id=1, source_target_pairs={{0,1},{1,0},{2,3},{3,2},{4,5},{5,4},{6,7},{7,6},{8,9},{9,8},{10,11... | collective-permute-start | bytes 786440 | tf_op jit(solution)/shard_map/ppermute | solution.py:289
  75.5 10.9 %collective-permute-start.41 = (bf16[2,128,256]{2,1,0:T(8,128)(2,1)S(1)}, bf16[2,128,256]{2,1,0:T(8,128)(2,1)S(1)}, u32[]{:S(2)}, u32[]{:S(2)}) collective-permute-start(bf16[2,128,256]{2,1,0:T(8,128)(2,1)S(1)} %pad_maximum_fusion.13), channel_id=1, source_target_pairs={{0,2},{1,3},{2,0},{3,1},{4,6},{5,7},{6,4},{7,5},{8,10},{9,11},{10,... | collective-permute-start | bytes 393224 | tf_op jit(solution)/shard_map/ppermute | solution.py:289
  83.4 13.8 %collective-permute-start.40 = (bf16[4,128,256]{2,1,0:T(8,128)(2,1)S(1)}, bf16[4,128,256]{2,1,0:T(8,128)(2,1)S(1)}, u32[]{:S(2)}, u32[]{:S(2)}) collective-permute-start(bf16[4,128,256]{2,1,0:T(8,128)(2,1)S(1)} %pad_maximum_fusion.9.refs_0_), channel_id=1, source_target_pairs={{0,1},{1,0},{2,3},{3,2},{4,5},{5,4},{6,7},{7,6},{8,9},{9,8},{10,11... | collective-permute-start | bytes 786440 | tf_op jit(solution)/shard_map/ppermute | solution.py:289
  95.8 16.5 %collective-permute-start.28 = (bf16[2,128,512]{2,1,0:T(8,128)(2,1)S(1)}, bf16[2,128,512]{2,1,0:T(8,128)(2,1)S(1)}, u32[]{:S(2)}, u32[]{:S(2)}) collective-permute-start(bf16[2,128,512]{2,1,0:T(8,128)(2,1)S(1)} %pad_maximum_fusion.7), channel_id=1, source_target_pairs={{0,2},{1,3},{2,0},{3,1},{4,6},{5,7},{6,4},{7,5},{8,10},{9,11},{10,... | collective-permute-start | bytes 786440 | tf_op jit(solution)/shard_map/ppermute | solution.py:289
  99.9 10.0 %collective-permute-start.30 = (bf16[1,128,512]{2,1,0:T(8,128)(2,1)S(1)}, bf16[1,128,512]{2,1,0:T(8,128)(2,1)S(1)}, u32[]{:S(2)}, u32[]{:S(2)}) collective-permute-start(bf16[1,128,512]{2,1,0:T(8,128)(2,1)S(1)} %bitcast.94), channel_id=1, source_target_pairs={{0,6},{1,7},{2,4},{3,5},{4,2},{5,3},{6,0},{7,1},{8,14},{9,15},{10,... | collective-permute-start | bytes 393224 | tf_op jit(solution)/shard_map/ppermute | solution.py:289
  101.7 10.7 %collective-permute-start.29 = (bf16[1,128,512]{2,1,0:T(8,128)(2,1)S(1)}, bf16[1,128,512]{2,1,0:T(8,128)(2,1)S(1)}, u32[]{:S(2)}, u32[]{:S(2)}) collective-permute-start(bf16[1,128,512]{2,1,0:T(8,128)(2,1)S(1)} %bitcast.95), channel_id=1, source_target_pairs={{0,4},{1,5},{2,6},{3,7},{4,0},{5,1},{6,2},{7,3},{8,12},{9,13},{10,... | collective-permute-start | bytes 393224 | tf_op jit(solution)/shard_map/ppermute | solution.py:289
  102.9 9.6 %collective-permute-start.48 = (bf16[128,512]{1,0:T(8,128)(2,1)S(1)}, bf16[128,512]{1,0:T(8,128)(2,1)S(1)}, u32[]{:S(2)}, u32[]{:S(2)}) collective-permute-start(bf16[128,512]{1,0:T(8,128)(2,1)S(1)} %collective-permute-done.45.refs_5_), channel_id=1, source_target_pairs={{0,8},{1,9},{2,10},{3,11},{4,12},{5,13},{6,14},{7,15},{8,0},{9,1},... | collective-permute-start | bytes 393224 | tf_op jit(solution)/shard_map/ppermute | solution.py:289
  104.3 10.1 %collective-permute-start.47 = (bf16[128,512]{1,0:T(8,128)(2,1)S(1)}, bf16[128,512]{1,0:T(8,128)(2,1)S(1)}, u32[]{:S(2)}, u32[]{:S(2)}) collective-permute-start(bf16[128,512]{1,0:T(8,128)(2,1)S(1)} %collective-permute-done.45.refs_5_), channel_id=1, source_target_pairs={{0,4},{1,5},{2,6},{3,7},{4,0},{5,1},{6,2},{7,3},{8,12},{9,13},{10,... | collective-permute-start | bytes 393224 | tf_op jit(solution)/shard_map/ppermute | solution.py:289
  115.1 17.7 %collective-permute-start.49 = (bf16[2,128,512]{2,1,0:T(8,128)(2,1)S(1)}, bf16[2,128,512]{2,1,0:T(8,128)(2,1)S(1)}, u32[]{:S(2)}, u32[]{:S(2)}) collective-permute-start(bf16[2,128,512]{2,1,0:T(8,128)(2,1)S(1)} %pad_maximum_fusion.10), channel_id=1, source_target_pairs={{0,2},{1,3},{2,0},{3,1},{4,6},{5,7},{6,4},{7,5},{8,10},{9,11},{10,... | collective-permute-start | bytes 786440 | tf_op jit(solution)/shard_map/ppermute | solution.py:289
  121.0 11.8 %collective-permute-start.51 = (bf16[1,128,512]{2,1,0:T(8,128)(2,1)S(1)}, bf16[1,128,512]{2,1,0:T(8,128)(2,1)S(1)}, u32[]{:S(2)}, u32[]{:S(2)}) collective-permute-start(bf16[1,128,512]{2,1,0:T(8,128)(2,1)S(1)} %bitcast.90), channel_id=1, source_target_pairs={{0,6},{1,7},{2,4},{3,5},{4,2},{5,3},{6,0},{7,1},{8,14},{9,15},{10,... | collective-permute-start | bytes 393224 | tf_op jit(solution)/shard_map/ppermute | solution.py:289
  123.3 9.5 %collective-permute-start.50 = (bf16[1,128,512]{2,1,0:T(8,128)(2,1)S(1)}, bf16[1,128,512]{2,1,0:T(8,128)(2,1)S(1)}, u32[]{:S(2)}, u32[]{:S(2)}) collective-permute-start(bf16[1,128,512]{2,1,0:T(8,128)(2,1)S(1)} %bitcast.91), channel_id=1, source_target_pairs={{0,4},{1,5},{2,6},{3,7},{4,0},{5,1},{6,2},{7,3},{8,12},{9,13},{10,... | collective-permute-start | bytes 393224 | tf_op jit(solution)/shard_map/ppermute | solution.py:289
  133.5 10.2 %collective-permute-start.53 = (bf16[1,128,256]{2,1,0:T(8,128)(2,1)S(1)}, bf16[1,128,256]{2,1,0:T(8,128)(2,1)S(1)}, u32[]{:S(2)}, u32[]{:S(2)}) collective-permute-start(bf16[1,128,256]{2,1,0:T(8,128)(2,1)S(1)} %bitcast.109), channel_id=1, source_target_pairs={{0,4},{1,5},{2,6},{3,7},{4,0},{5,1},{6,2},{7,3},{8,12},{9,13},{10,... | collective-permute-start | bytes 196616 | tf_op jit(solution)/shard_map/ppermute | solution.py:289
  135.2 9.1 %collective-permute-start.52 = (bf16[2,128,256]{2,1,0:T(8,128)(2,1)S(1)}, bf16[2,128,256]{2,1,0:T(8,128)(2,1)S(1)}, u32[]{:S(2)}, u32[]{:S(2)}) collective-permute-start(bf16[2,128,256]{2,1,0:T(8,128)(2,1)S(1)} %pad_maximum_fusion.14), channel_id=1, source_target_pairs={{0,2},{1,3},{2,0},{3,1},{4,6},{5,7},{6,4},{7,5},{8,10},{9,11},{10,... | collective-permute-start | bytes 393224 | tf_op jit(solution)/shard_map/ppermute | solution.py:289
  136.7 18.9 %collective-permute-start.36 = (bf16[4,128,256]{2,1,0:T(8,128)(2,1)S(1)}, bf16[4,128,256]{2,1,0:T(8,128)(2,1)S(1)}, u32[]{:S(2)}, u32[]{:S(2)}) collective-permute-start(bf16[4,128,256]{2,1,0:T(8,128)(2,1)S(1)} %pad_maximum_fusion.8.refs_0_), channel_id=1, source_target_pairs={{0,1},{1,0},{2,3},{3,2},{4,5},{5,4},{6,7},{7,6},{8,9},{9,8},{10,11... | collective-permute-start | bytes 786440 | tf_op jit(solution)/shard_map/ppermute | solution.py:289
  (47 other events, 335.8 us)

commit v5 on v4

v5 whole, which is shorter than its diff:
```python
import functools

import jax
import jax.numpy as jnp
from jax import lax
from jax.experimental import pallas as pl
from jax.experimental.pallas import tpu as pltpu
from jax.sharding import PartitionSpec as P

EPS = 1e-06
VMEM_LIMIT = 12 * 1024 * 1024
PAD = 8


def split_dp(dp_count):
    core = 2 if dp_count % 2 == 0 else 1
    chips = dp_count // core
    near = 1
    while near * near * 4 <= chips:
        near *= 2
    return chips // near, near, core


def routes(far, near):
    if (far, near) == (4, 2):
        return [4, 2, 1], [(1, [4, 2]), (2, [4]), (3, [4])]
    line = [d * near for d in range(far)]
    return line[1:], [(d, line) for d in range(1, near)]


def fetch(cells, core, feat, rank_ref, w_far, w_ref, sems):
    wide = core * feat
    chip = lax.div(rank_ref[0], core)
    copies = []
    for n, cell in enumerate(cells):
        columns = pl.ds(pl.multiple_of((chip ^ cell) * wide, wide), wide)
        copies.append(
            [
                pltpu.make_async_copy(w_far.at[i, :, columns], w_ref.at[n, i], sems.at[n, i])
                for i in range(w_far.shape[0])
            ]
        )
    for group in copies:
        for copy in group:
            copy.start()

    def ready(n):
        for copy in copies[n]:
            copy.wait()

    return ready


def project_cells(cells, sides, rank_ref, w_ref, gain_ref, acc_ref, sq_ref, ready):
    feat = sides[0].shape[2]
    core = len(sides)
    lanes = sq_ref.shape[1]
    chip, side = lax.div(rank_ref[0], core), lax.rem(rank_ref[0], core)
    for n, cell in enumerate(cells):
        normed, columns = [], []
        for c in range(core):
            values = sides[c][n].astype(jnp.float32)
            columns.append(pl.ds(pl.multiple_of((side ^ c) * feat, feat), feat))
            gains = gain_ref[:, pl.ds(pl.multiple_of(((chip ^ cell) * core + (side ^ c)) * feat, feat), feat)]
            normed.append((values * gains).astype(jnp.bfloat16))
            squares = values * values
            part = squares[:, :lanes]
            for m in range(1, feat // lanes):
                part = part + squares[:, m * lanes : (m + 1) * lanes]
            sq_ref[...] = part if n == 0 and c == 0 else sq_ref[...] + part
        ready(n)
        for i in range(w_ref.shape[1]):
            terms = [
                lax.dot_general(
                    normed[c],
                    w_ref[n, i, :, columns[c]],
                    (((1,), (1,)), ((), ())),
                    preferred_element_type=jnp.float32,
                )
                for c in range(core)
            ]
            term = functools.reduce(jnp.add, terms)
            acc_ref[i] = term if n == 0 else acc_ref[i] + term


def early_kernel(cells, core, rank_ref, *refs):
    sides = refs[:core]
    w_far, gain_ref, acc_ref, sq_ref, w_ref, sems = refs[core:]
    ready = fetch(cells, core, sides[0].shape[2], rank_ref, w_far, w_ref, sems)
    project_cells(cells, sides, rank_ref, w_ref, gain_ref, acc_ref, sq_ref, ready)


def first_kernel(cells, core, rank_ref, *refs):
    sides = refs[:core]
    w_far, gain_far, taps_far, decay_far, acc_ref, sq_ref, gain_ref, long_ref = refs[core : core + 8]
    w_ref, sems, taps_ref, decay_ref, small_sems = refs[core + 8 :]
    ready = fetch(cells, core, sides[0].shape[2], rank_ref, w_far, w_ref, sems)
    small = [(gain_far, gain_ref), (taps_far, taps_ref), (decay_far, decay_ref)]
    small = [pltpu.make_async_copy(src, dst, small_sems.at[n]) for n, (src, dst) in enumerate(small)]
    for copy in small:
        copy.start()
    for copy in small:
        copy.wait()
    lags = lax.broadcasted_iota(jnp.int32, long_ref.shape, 0).astype(jnp.float32)
    long_ref[...] = taps_ref[...].T * jnp.exp(-decay_ref[...] * lags)
    project_cells(cells, sides, rank_ref, w_ref, gain_ref, acc_ref, sq_ref, ready)


def mix_kernel(cells, core, rank_ref, *refs):
    sides = refs[:core]
    w_far, gain_ref, acc_in, sq_in, short_ref, long_ref, y_ref = refs[core : core + 7]
    acc_ref, sq_ref, pad_ref, query_ref, w_ref, sems = refs[core + 7 :]
    branches, chan, model_width = w_far.shape
    tok_len = y_ref.shape[0]
    ready = fetch(cells, core, sides[0].shape[2], rank_ref, w_far, w_ref, sems)
    project_cells(cells, sides, rank_ref, w_ref, gain_ref, acc_ref, sq_ref, ready)

    total = jnp.sum(sq_in[...] + sq_ref[...], axis=1, keepdims=True)
    factor = lax.rsqrt(total / model_width + EPS)
    taps = short_ref.shape[0] // branches
    pad_ref[0:PAD, :] = jnp.zeros((PAD, chan), jnp.float32)

    def branch(i):
        u = (acc_in[i] + acc_ref[i]) * factor
        pad_ref[PAD : PAD + tok_len, :] = u
        z = short_ref[i * taps : i * taps + 1, :] * u
        for j in range(1, taps):
            z = z + short_ref[i * taps + j : i * taps + j + 1, :] * pad_ref[PAD - j : PAD - j + tok_len, :]
        return z

    query_ref[...] = branch(1)
    product = query_ref[...] * branch(2)
    query_ref[...] = branch(0)
    pad_ref[PAD : PAD + tok_len, :] = product
    width = min(chan, 128)
    tiles = tok_len // 8
    for c in range(0, chan, width):
        cols = slice(c, c + width)
        conv = [None] * tiles
        for b in range(8):
            moved = [pad_ref[PAD - b + 8 * i : PAD - b + 8 * i + 8, cols] for i in range(tiles)]
            for a in range(long_ref.shape[0] // 8):
                tap = long_ref[8 * a + b : 8 * a + b + 1, cols]
                for i in range(a, tiles):
                    term = tap * moved[i - a]
                    conv[i] = term if conv[i] is None else conv[i] + term
        for i in range(0, tiles, 2):
            at = slice(8 * i, 8 * i + 16)
            both = jnp.concatenate(conv[i : i + 2], axis=0)
            y_ref[at, cols] = (query_ref[at, cols] * both).astype(jnp.bfloat16)


def out_kernel(parts, core, rank_ref, *refs):
    w_ref, own_ref, result_ref, acc_ref = refs[-4:]
    chan = refs[0].shape[2]
    chip, side = lax.div(rank_ref[0], core), lax.rem(rank_ref[0], core)
    acc_ref[...] = own_ref[...].astype(jnp.float32)
    for p, cells in enumerate(parts):
        sides = refs[p * core : (p + 1) * core]
        for n, cell in enumerate(cells):
            terms = []
            for c in range(core):
                at = pl.multiple_of(((chip ^ cell) * core + (side ^ c)) * chan, chan)
                terms.append(
                    jnp.dot(sides[c][n], w_ref[pl.ds(at, chan), :], preferred_element_type=jnp.float32)
                )
            acc_ref[...] += functools.reduce(jnp.add, terms)
    result_ref[...] = acc_ref[...].astype(jnp.bfloat16)


def in_vmem(count):
    return [pl.BlockSpec(memory_space=pltpu.VMEM)] * count


def call(kernel, operands, outs, scratch, flops, name, far_operands=()):
    specs = [pl.BlockSpec(memory_space=pltpu.SMEM)] + in_vmem(len(operands) - 1)
    operands = list(operands)
    for n in far_operands:
        specs[n] = pl.BlockSpec(memory_space=pltpu.HBM)
        operands[n] = pltpu.with_memory_space_constraint(operands[n], pltpu.HBM)
    return pl.pallas_call(
        kernel,
        in_specs=specs,
        out_specs=in_vmem(len(outs)),
        out_shape=outs,
        scratch_shapes=scratch,
        compiler_params=pltpu.CompilerParams(vmem_limit_bytes=VMEM_LIMIT),
        cost_estimate=pl.CostEstimate(flops=flops, bytes_accessed=flops // 1024, transcendentals=0),
        name=name,
    )(*operands)


def streamed(cells, w_in, wide):
    branches, chan, _ = w_in.shape
    return [
        pltpu.VMEM((len(cells), branches, chan, wide), w_in.dtype),
        pltpu.SemaphoreType.DMA((len(cells), branches)),
    ]


def project_early(part, w_in, gain, rank, taps=None, decay=None):
    cells, sides = part
    core = len(sides)
    rows, feat = sides[0].shape[1:]
    branches, chan, model_width = w_in.shape
    outs = [
        jax.ShapeDtypeStruct((branches, rows, chan), jnp.float32),
        jax.ShapeDtypeStruct((rows, min(feat, 128)), jnp.float32),
    ]
    scratch = streamed(cells, w_in, core * feat)
    flops = 2 * rows * branches * chan * feat * core * len(cells)
    operands, far = [rank, *sides, w_in, gain], [1 + core]
    kernel = functools.partial(early_kernel, cells, core)
    if taps is not None:
        operands += [taps, decay]
        far = range(1 + core, 5 + core)
        outs.append(jax.ShapeDtypeStruct(gain.shape, gain.dtype))
        outs.append(jax.ShapeDtypeStruct(taps.shape[::-1], taps.dtype))
        scratch.append(pltpu.VMEM(taps.shape, taps.dtype))
        scratch.append(pltpu.VMEM(decay.shape, decay.dtype))
        scratch.append(pltpu.SemaphoreType.DMA((3,)))
        kernel = functools.partial(first_kernel, cells, core)
    return call(kernel, operands, outs, scratch, flops, "project_early", far)


def mix(part, w_in, gain, acc, sq, short_rows, long_rows, rank):
    cells, sides = part
    core = len(sides)
    rows, feat = sides[0].shape[1:]
    branches, chan, _ = w_in.shape
    scratch = [
        pltpu.VMEM(acc.shape, jnp.float32),
        pltpu.VMEM(sq.shape, jnp.float32),
        pltpu.VMEM((PAD + rows, chan), jnp.float32),
        pltpu.VMEM((rows, chan), jnp.float32),
    ]
    return call(
        functools.partial(mix_kernel, cells, core),
        [rank, *sides, w_in, gain, acc, sq, short_rows, long_rows],
        [jax.ShapeDtypeStruct((rows, chan), jnp.bfloat16)],
        scratch + streamed(cells, w_in, core * feat),
        2 * rows * branches * chan * feat * core * len(cells),
        "project_mix",
        [1 + core],
    )[0]


def project_out(parts, w_out, own, rank):
    core = len(parts[0][1])
    rows, feat = own.shape
    arrays = [side for _, sides in parts for side in sides]
    return call(
        functools.partial(out_kernel, [cells for cells, _ in parts], core),
        [rank, *arrays, w_out, own],
        [jax.ShapeDtypeStruct((rows, feat), jnp.bfloat16)],
        [pltpu.VMEM((rows, feat), jnp.float32)],
        2 * rows * w_out.shape[0] * feat,
        "project_out",
    )[0]


def body(section_count, dp_count, fresh_acts, carried, norm_gain, w_in, short_filter, filter_taps, decay_rate, w_out):
    tick_count, tok_len, _ = fresh_acts.shape
    far, near, core = split_dp(dp_count)
    group = near * core
    section_idx = lax.axis_index("section")
    rank = lax.axis_index("dp").astype(jnp.int32).reshape(1)

    def swap(value, offset):
        return lax.ppermute(value, "dp", [(r, r ^ offset) for r in range(dp_count)])

    first_round, second_round = routes(far, near)

    def after(value, *earlier):
        return lax.optimization_barrier((value, earlier))[0]

    def to_core(blocks):
        return [blocks] + [swap(blocks, c) for c in range(1, core)]

    def round_one(source):
        return lax.optimization_barrier({0: source} | {d: swap(source, d * core) for d in first_round})

    def round_two(blocks):
        cells, rest = [], []
        for d, sent in second_round:
            rest.append(swap(jnp.stack([blocks[b] for b in sent]), d * core))
            cells += [d ^ b for b in sent]
        return cells, rest

    def early_part(blocks):
        return list(blocks), to_core(jnp.stack(list(blocks.values())))

    short_rows = short_filter[0].transpose(0, 2, 1).reshape(-1, short_filter.shape[2])
    gain, small = norm_gain, (filter_taps[0], decay_rate)
    is_first = section_idx == 0
    onward = [(s, s + 1) for s in range(section_count - 1)]
    made = []
    for k in range(tick_count):
        before = carried[0] if k == 0 else lax.ppermute(made[-1], "section", onward)
        own = jnp.where(is_first, fresh_acts[k], before)
        blocks = round_one(own)
        cells, rest = round_two(blocks)
        acc, sq, *loads = project_early(early_part(blocks), w_in[0], gain, rank, *small)
        if loads:
            (gain, long_rows), small = loads, ()
        late = cells, to_core(jnp.concatenate(after(rest, acc)))
        y = mix(late, w_in[0], gain, acc, sq, short_rows, long_rows, rank)
        blocks = round_one(y)
        cells, rest = round_two(blocks)
        parts = [early_part(blocks), (cells, to_core(jnp.concatenate(rest)))]
        made.append(project_out(parts, w_out[0], own, rank))
    return jnp.stack(made)[None]


def solution(mesh):
    run = functools.partial(body, mesh.shape["section"], mesh.shape["dp"])
    return jax.shard_map(
        run,
        mesh=mesh,
        in_specs=(
            P(None, None, "dp"),
            P("section", None, "dp"),
            P("section", None),
            P("section", None, "dp", None),
            P("section", None, "dp", None),
            P("section", "dp", None),
            P("section", "dp"),
            P("section", None, "dp"),
        ),
        out_specs=P("section", None, None, "dp"),
        check_vma=False,
    )
```

time: 159 us -> 161 us (1.013)
  waiting for transfers between devices: 42.2 us -> 65.1 us
  starting transfers between devices: 67.4 us -> 54.1 us
  local copies, waits for them, and re-layouts: 10.4 us -> 0.22 us
  Pallas kernels: 34.6 us -> 38.4 us
    ppermute x64 -> x48, waiting for transfers between devices: 41.7 us -> 59.5 us  [swap(): return lax.ppermute(value, 'dp', [(r, r ^ offset) for r in range(dp_count)])]
    ppermute x64 -> x48, starting transfers between devices: 62.3 us -> 45.8 us  [swap(): return lax.ppermute(value, 'dp', [(r, r ^ offset) for r in range(dp_count)])]
    unnamed x27 -> x19, local copies, waits for them, and re-layouts: 10.3 us -> 0.16 us
    ppermute x2, waiting for transfers between devices: 0.56 us -> 5.66 us  [body(): before = carried[0] if k == 0 else lax.ppermute(made[-1], 'section', onward)]
    pallas_call x12 -> x9, Pallas kernels: 34.6 us -> 38.4 us  [call(): pl.pallas_call(kernel, in_specs=specs, out_specs=in_vmem(len(outs)), out_...]
    ppermute x2, starting transfers between devices: 5.1 us -> 8.29 us  [body(): before = carried[0] if k == 0 else lax.ppermute(made[-1], 'section', onward)]
  transfers between devices with their start and end apart: 66 -> 50, of which waited for: 26 -> 36; matrix products, arithmetic and copies ran while one was open for 1% -> 0% of each run, Pallas kernels for 21% -> 10%
where the time goes in v5:
time: 161 us; the launch traced here: 160 us
  waiting for transfers between devices  65.1 us (40%)
  starting transfers between devices  54.1 us (34%)
  Pallas kernels  38.4 us (24%)
  other arithmetic  2.2 us (1%)
    ppermute x48, waiting for transfers between devices, swap(): return lax.ppermute(value, 'dp', [(r, r ^ offset) for r in range(dp_count)])  59.5 us
    ppermute x48, starting transfers between devices, swap(): return lax.ppermute(value, 'dp', [(r, r ^ offset) for r in range(dp_count)])  45.8 us
    pallas_call x9, Pallas kernels, call(): pl.pallas_call(kernel, in_specs=specs, out_specs=in_vmem(len(outs)), out_...  38.4 us
    ppermute x2, starting transfers between devices, body(): before = carried[0] if k == 0 else lax.ppermute(made[-1], 'section', onward)  8.29 us
    ppermute x2, waiting for transfers between devices, body(): before = carried[0] if k == 0 else lax.ppermute(made[-1], 'section', onward)  5.66 us
  transfers between devices with their start and end apart: 50, of which 36 were waited for; matrix products, arithmetic and copies ran while one was open for 0% of the time, Pallas kernels for 10%

profile of v5, /device:TPU:0, one launch (start us, length us, event | category | flops | bytes accessed | tf_op | source)
XLA Modules:
  0.0 160.5 jit_solution(13641101562459933629)
XLA Ops:
  0.9 3.0 %collective-permute-start = (bf16[128,512]{1,0:T(8,128)(2,1)S(1)}, bf16[128,512]{1,0:T(8,128)(2,1)S(1)}, u32[]{:S(2)}, u32[]{:S(2)}) collective-permute-start(bf16[128,512]{1,0:T(8,128)(2,1)S(1)} %select_bitcast_fusion.refs_5_), channel_id=1, source_target_pairs={{0,2},{1,3},{2,0},{3,1},{4,6},{5,7},{6,4},{7,5},{8,10},{9,11},{10,... | collective-permute-start | bytes 393224 | tf_op jit(solution)/shard_map/ppermute | solution.py:270
  5.5 2.6 %collective-permute-start.2 = (bf16[128,512]{1,0:T(8,128)(2,1)S(1)}, bf16[128,512]{1,0:T(8,128)(2,1)S(1)}, u32[]{:S(2)}, u32[]{:S(2)}) collective-permute-start(bf16[128,512]{1,0:T(8,128)(2,1)S(1)} %select_bitcast_fusion.refs_5_), channel_id=1, source_target_pairs={{0,8},{1,9},{2,10},{3,11},{4,12},{5,13},{6,14},{7,15},{8,0},{9,1},... | collective-permute-start | bytes 393224 | tf_op jit(solution)/shard_map/ppermute | solution.py:270
  8.1 2.5 %collective-permute-done.1 = bf16[128,512]{1,0:T(8,128)(2,1)S(1)} collective-permute-done((bf16[128,512]{1,0:T(8,128)(2,1)S(1)}, bf16[128,512]{1,0:T(8,128)(2,1)S(1)}, u32[]{:S(2)}, u32[]{:S(2)}) %collective-permute-start.1) | collective-permute-done | bytes 131104 | tf_op jit(solution)/shard_map/ppermute | solution.py:270
  10.6 3.3 %collective-permute-done.2 = bf16[128,512]{1,0:T(8,128)(2,1)S(1)} collective-permute-done((bf16[128,512]{1,0:T(8,128)(2,1)S(1)}, bf16[128,512]{1,0:T(8,128)(2,1)S(1)}, u32[]{:S(2)}, u32[]{:S(2)}) %collective-permute-start.2) | collective-permute-done | bytes 131104 | tf_op jit(solution)/shard_map/ppermute | solution.py:270
  15.1 2.6 %collective-permute-start.5 = (bf16[1,128,512]{2,1,0:T(8,128)(2,1)S(1)}, bf16[1,128,512]{2,1,0:T(8,128)(2,1)S(1)}, u32[]{:S(2)}, u32[]{:S(2)}) collective-permute-start(bf16[1,128,512]{2,1,0:T(8,128)(2,1)S(1)} %bitcast.65), channel_id=1, source_target_pairs={{0,6},{1,7},{2,4},{3,5},{4,2},{5,3},{6,0},{7,1},{8,14},{9,15},{10,... | collective-permute-start | bytes 393224 | tf_op jit(solution)/shard_map/ppermute | solution.py:270
  17.7 6.3 %project_early.3 = (f32[3,128,256]{2,1,0:T(8,128)S(1)}, f32[128,128]{1,0:T(8,128)S(1)}, f32[1,8192]{1,0:T(1,128)S(1)}, f32[128,256]{1,0:T(8,128)S(1)}) custom-call(s32[1]{0:T(128)} %bitcast.rank_ref, bf16[4,128,512]{2,1,0:T(8,128)(2,1)S(1)} %pad_maximum_fusion.refs_0_, bf16[4,128,512]{2,1,0:T(8,128)(2,1)S(1)} %collective-permute-done.6.refs_1_, ...), custom_call_target="tpu_custom_call" | custom-call | flops 805306368 | bytes 786432 | tf_op jit(solution)/shard_map/project_early/pallas_call | solution.py:181
  27.8 6.8 %project_mix.3 = bf16[128,256]{1,0:T(8,128)(2,1)S(1)} custom-call(s32[1]{0:T(128)} %bitcast.rank_ref, bf16[4,128,512]{2,1,0:T(8,128)(2,1)S(1)} %constant_dynamic-update-slice_fusion.refs_0_, bf16[4,128,512]{2,1,0:T(8,128)(2,1)S(1)} %collective-permute-done.7.refs_1_, bf16[3,256,8192]{2,1,0:T(8,128)(2,1)} %bitcast.57, ...), custom_call_target="tpu_custom_call" | custom-call | flops 805306368 | bytes 786432 | tf_op jit(solution)/shard_map/project_mix/pallas_call | solution.py:181
  35.4 2.8 %collective-permute-start.9 = (bf16[128,256]{1,0:T(8,128)(2,1)S(1)}, bf16[128,256]{1,0:T(8,128)(2,1)S(1)}, u32[]{:S(2)}, u32[]{:S(2)}) collective-permute-start(bf16[128,256]{1,0:T(8,128)(2,1)S(1)} %project_mix.3), channel_id=1, source_target_pairs={{0,4},{1,5},{2,6},{3,7},{4,0},{5,1},{6,2},{7,3},{8,12},{9,13},{10,... | collective-permute-start | bytes 196616 | tf_op jit(solution)/shard_map/ppermute | solution.py:270
  38.2 2.8 %collective-permute-done.10 = bf16[128,256]{1,0:T(8,128)(2,1)S(1)} collective-permute-done((bf16[128,256]{1,0:T(8,128)(2,1)S(1)}, bf16[128,256]{1,0:T(8,128)(2,1)S(1)}, u32[]{:S(2)}, u32[]{:S(2)}) %collective-permute-start.10) | collective-permute-done | bytes 65568 | tf_op jit(solution)/shard_map/ppermute | solution.py:270
  51.4 3.7 %collective-permute-start.16 = (bf16[128,512]{1,0:T(8,128)(2,1)S(1)}, bf16[128,512]{1,0:T(8,128)(2,1)S(1)}, u32[]{:S(2)}, u32[]{:S(2)}) collective-permute-start(bf16[128,512]{1,0:T(8,128)(2,1)S(1)} %project_out.3), channel_id=1, source_target_pairs={{0,16},{1,17},{2,18},{3,19},{4,20},{5,21},{6,22},{7,23},{8,24},{9,... | collective-permute-start | bytes 393224 | tf_op jit(solution)/shard_map/ppermute | solution.py:299
  55.1 2.9 %collective-permute-done.16 = bf16[128,512]{1,0:T(8,128)(2,1)S(1)} collective-permute-done((bf16[128,512]{1,0:T(8,128)(2,1)S(1)}, bf16[128,512]{1,0:T(8,128)(2,1)S(1)}, u32[]{:S(2)}, u32[]{:S(2)}) %collective-permute-start.16) | collective-permute-done | bytes 131104 | tf_op jit(solution)/shard_map/ppermute | solution.py:299
  60.6 2.4 %collective-permute-done.17 = bf16[128,512]{1,0:T(8,128)(2,1)S(1)} collective-permute-done((bf16[128,512]{1,0:T(8,128)(2,1)S(1)}, bf16[128,512]{1,0:T(8,128)(2,1)S(1)}, u32[]{:S(2)}, u32[]{:S(2)}) %collective-permute-start.17) | collective-permute-done | bytes 131104 | tf_op jit(solution)/shard_map/ppermute | solution.py:270
  64.7 2.9 %collective-permute-done.19 = bf16[128,512]{1,0:T(8,128)(2,1)S(1)} collective-permute-done((bf16[128,512]{1,0:T(8,128)(2,1)S(1)}, bf16[128,512]{1,0:T(8,128)(2,1)S(1)}, u32[]{:S(2)}, u32[]{:S(2)}) %collective-permute-start.19) | collective-permute-done | bytes 131104 | tf_op jit(solution)/shard_map/ppermute | solution.py:270
  69.1 2.3 %collective-permute-start.22 = (bf16[1,128,512]{2,1,0:T(8,128)(2,1)S(1)}, bf16[1,128,512]{2,1,0:T(8,128)(2,1)S(1)}, u32[]{:S(2)}, u32[]{:S(2)}) collective-permute-start(bf16[1,128,512]{2,1,0:T(8,128)(2,1)S(1)} %bitcast.69), channel_id=1, source_target_pairs={{0,6},{1,7},{2,4},{3,5},{4,2},{5,3},{6,0},{7,1},{8,14},{9,15},{10,... | collective-permute-start | bytes 393224 | tf_op jit(solution)/shard_map/ppermute | solution.py:270
  71.3 4.8 %project_early.4 = (f32[3,128,256]{2,1,0:T(8,128)S(1)}, f32[128,128]{1,0:T(8,128)S(1)}) custom-call(s32[1]{0:T(128)} %bitcast.rank_ref, bf16[4,128,512]{2,1,0:T(8,128)(2,1)S(1)} %pad_maximum_fusion.1.refs_0_, bf16[4,128,512]{2,1,0:T(8,128)(2,1)S(1)} %collective-permute-done.23.refs_1_, bf16[3,256,8192]{2,1,0:T(8,128)(2,1)} %bitcast.58, ...), custom_call_target="tpu_custom_call" | custom-call | flops 805306368 | bytes 786432 | tf_op jit(solution)/shard_map/project_early/pallas_call | solution.py:181
  81.4 6.8 %project_mix.4 = bf16[128,256]{1,0:T(8,128)(2,1)S(1)} custom-call(s32[1]{0:T(128)} %bitcast.rank_ref, bf16[4,128,512]{2,1,0:T(8,128)(2,1)S(1)} %constant_dynamic-update-slice_fusion.6.refs_0_, bf16[4,128,512]{2,1,0:T(8,128)(2,1)S(1)} %collective-permute-done.24.refs_1_, bf16[3,256,8192]{2,1,0:T(8,128)(2,1)} %bitcast.59, ...), custom_call_target="tpu_custom_call" | custom-call | flops 805306368 | bytes 786432 | tf_op jit(solution)/shard_map/project_mix/pallas_call | solution.py:181
  105.0 4.6 %collective-permute-start.33 = (bf16[128,512]{1,0:T(8,128)(2,1)S(1)}, bf16[128,512]{1,0:T(8,128)(2,1)S(1)}, u32[]{:S(2)}, u32[]{:S(2)}) collective-permute-start(bf16[128,512]{1,0:T(8,128)(2,1)S(1)} %project_out.4), channel_id=1, source_target_pairs={{0,16},{1,17},{2,18},{3,19},{4,20},{5,21},{6,22},{7,23},{8,24},{9,... | collective-permute-start | bytes 393224 | tf_op jit(solution)/shard_map/ppermute | solution.py:299
  109.6 2.8 %collective-permute-done.33 = bf16[128,512]{1,0:T(8,128)(2,1)S(1)} collective-permute-done((bf16[128,512]{1,0:T(8,128)(2,1)S(1)}, bf16[128,512]{1,0:T(8,128)(2,1)S(1)}, u32[]{:S(2)}, u32[]{:S(2)}) %collective-permute-start.33) | collective-permute-done | bytes 131104 | tf_op jit(solution)/shard_map/ppermute | solution.py:299
  117.5 2.5 %collective-permute-done.35 = bf16[128,512]{1,0:T(8,128)(2,1)S(1)} collective-permute-done((bf16[128,512]{1,0:T(8,128)(2,1)S(1)}, bf16[128,512]{1,0:T(8,128)(2,1)S(1)}, u32[]{:S(2)}, u32[]{:S(2)}) %collective-permute-start.35) | collective-permute-done | bytes 131104 | tf_op jit(solution)/shard_map/ppermute | solution.py:270
  120.0 2.3 %collective-permute-done.36 = bf16[128,512]{1,0:T(8,128)(2,1)S(1)} collective-permute-done((bf16[128,512]{1,0:T(8,128)(2,1)S(1)}, bf16[128,512]{1,0:T(8,128)(2,1)S(1)}, u32[]{:S(2)}, u32[]{:S(2)}) %collective-permute-start.36) | collective-permute-done | bytes 131104 | tf_op jit(solution)/shard_map/ppermute | solution.py:270
  123.6 2.4 %collective-permute-start.39 = (bf16[1,128,512]{2,1,0:T(8,128)(2,1)S(1)}, bf16[1,128,512]{2,1,0:T(8,128)(2,1)S(1)}, u32[]{:S(2)}, u32[]{:S(2)}) collective-permute-start(bf16[1,128,512]{2,1,0:T(8,128)(2,1)S(1)} %bitcast.73), channel_id=1, source_target_pairs={{0,6},{1,7},{2,4},{3,5},{4,2},{5,3},{6,0},{7,1},{8,14},{9,15},{10,... | collective-permute-start | bytes 393224 | tf_op jit(solution)/shard_map/ppermute | solution.py:270
  126.1 4.8 %project_early.5 = (f32[3,128,256]{2,1,0:T(8,128)S(1)}, f32[128,128]{1,0:T(8,128)S(1)}) custom-call(s32[1]{0:T(128)} %bitcast.rank_ref, bf16[4,128,512]{2,1,0:T(8,128)(2,1)S(1)} %pad_maximum_fusion.2.refs_0_, bf16[4,128,512]{2,1,0:T(8,128)(2,1)S(1)} %collective-permute-done.40.refs_1_, bf16[3,256,8192]{2,1,0:T(8,128)(2,1)} %bitcast.60, ...), custom_call_target="tpu_custom_call" | custom-call | flops 805306368 | bytes 786432 | tf_op jit(solution)/shard_map/project_early/pallas_call | solution.py:181
  136.1 6.8 %project_mix.5 = bf16[128,256]{1,0:T(8,128)(2,1)S(1)} custom-call(s32[1]{0:T(128)} %bitcast.rank_ref, bf16[4,128,512]{2,1,0:T(8,128)(2,1)S(1)} %constant_dynamic-update-slice_fusion.12.refs_0_, bf16[4,128,512]{2,1,0:T(8,128)(2,1)S(1)} %collective-permute-done.41.refs_1_, bf16[3,256,8192]{2,1,0:T(8,128)(2,1)} %bitcast.61, ...), custom_call_target="tpu_custom_call" | custom-call | flops 805306368 | bytes 786432 | tf_op jit(solution)/shard_map/project_mix/pallas_call | solution.py:181
  144.0 2.5 %collective-permute-start.44 = (bf16[128,256]{1,0:T(8,128)(2,1)S(1)}, bf16[128,256]{1,0:T(8,128)(2,1)S(1)}, u32[]{:S(2)}, u32[]{:S(2)}) collective-permute-start(bf16[128,256]{1,0:T(8,128)(2,1)S(1)} %project_mix.5), channel_id=1, source_target_pairs={{0,8},{1,9},{2,10},{3,11},{4,12},{5,13},{6,14},{7,15},{8,0},{9,1},... | collective-permute-start | bytes 196616 | tf_op jit(solution)/shard_map/ppermute | solution.py:270
  (127 shorter events, 72.8 us)
Async XLA Ops:
  0.9 7.2 %collective-permute-start = (bf16[128,512]{1,0:T(8,128)(2,1)S(1)}, bf16[128,512]{1,0:T(8,128)(2,1)S(1)}, u32[]{:S(2)}, u32[]{:S(2)}) collective-permute-start(bf16[128,512]{1,0:T(8,128)(2,1)S(1)} %select_bitcast_fusion.refs_5_), channel_id=1, source_target_pairs={{0,2},{1,3},{2,0},{3,1},{4,6},{5,7},{6,4},{7,5},{8,10},{9,11},{10,... | collective-permute-start | bytes 393224 | tf_op jit(solution)/shard_map/ppermute | solution.py:270
  3.9 6.7 %collective-permute-start.1 = (bf16[128,512]{1,0:T(8,128)(2,1)S(1)}, bf16[128,512]{1,0:T(8,128)(2,1)S(1)}, u32[]{:S(2)}, u32[]{:S(2)}) collective-permute-start(bf16[128,512]{1,0:T(8,128)(2,1)S(1)} %select_bitcast_fusion.refs_5_), channel_id=1, source_target_pairs={{0,4},{1,5},{2,6},{3,7},{4,0},{5,1},{6,2},{7,3},{8,12},{9,13},{10,... | collective-permute-start | bytes 393224 | tf_op jit(solution)/shard_map/ppermute | solution.py:270
  5.5 8.4 %collective-permute-start.2 = (bf16[128,512]{1,0:T(8,128)(2,1)S(1)}, bf16[128,512]{1,0:T(8,128)(2,1)S(1)}, u32[]{:S(2)}, u32[]{:S(2)}) collective-permute-start(bf16[128,512]{1,0:T(8,128)(2,1)S(1)} %select_bitcast_fusion.refs_5_), channel_id=1, source_target_pairs={{0,8},{1,9},{2,10},{3,11},{4,12},{5,13},{6,14},{7,15},{8,0},{9,1},... | collective-permute-start | bytes 393224 | tf_op jit(solution)/shard_map/ppermute | solution.py:270
  14.1 11.6 %collective-permute-start.3 = (bf16[2,128,512]{2,1,0:T(8,128)(2,1)S(1)}, bf16[2,128,512]{2,1,0:T(8,128)(2,1)S(1)}, u32[]{:S(2)}, u32[]{:S(2)}) collective-permute-start(bf16[2,128,512]{2,1,0:T(8,128)(2,1)S(1)} %pad_maximum_fusion.3), channel_id=1, source_target_pairs={{0,2},{1,3},{2,0},{3,1},{4,6},{5,7},{6,4},{7,5},{8,10},{9,11},{10,... | collective-permute-start | bytes 786440 | tf_op jit(solution)/shard_map/ppermute | solution.py:270
  14.7 9.3 %collective-permute-start.4 = (bf16[1,128,512]{2,1,0:T(8,128)(2,1)S(1)}, bf16[1,128,512]{2,1,0:T(8,128)(2,1)S(1)}, u32[]{:S(2)}, u32[]{:S(2)}) collective-permute-start(bf16[1,128,512]{2,1,0:T(8,128)(2,1)S(1)} %bitcast.64), channel_id=1, source_target_pairs={{0,4},{1,5},{2,6},{3,7},{4,0},{5,1},{6,2},{7,3},{8,12},{9,13},{10,... | collective-permute-start | bytes 393224 | tf_op jit(solution)/shard_map/ppermute | solution.py:270
  15.1 9.1 %collective-permute-start.5 = (bf16[1,128,512]{2,1,0:T(8,128)(2,1)S(1)}, bf16[1,128,512]{2,1,0:T(8,128)(2,1)S(1)}, u32[]{:S(2)}, u32[]{:S(2)}) collective-permute-start(bf16[1,128,512]{2,1,0:T(8,128)(2,1)S(1)} %bitcast.65), channel_id=1, source_target_pairs={{0,6},{1,7},{2,4},{3,5},{4,2},{5,3},{6,0},{7,1},{8,14},{9,15},{10,... | collective-permute-start | bytes 393224 | tf_op jit(solution)/shard_map/ppermute | solution.py:270
  34.5 6.4 %collective-permute-start.10 = (bf16[128,256]{1,0:T(8,128)(2,1)S(1)}, bf16[128,256]{1,0:T(8,128)(2,1)S(1)}, u32[]{:S(2)}, u32[]{:S(2)}) collective-permute-start(bf16[128,256]{1,0:T(8,128)(2,1)S(1)} %project_mix.3), channel_id=1, source_target_pairs={{0,8},{1,9},{2,10},{3,11},{4,12},{5,13},{6,14},{7,15},{8,0},{9,1},... | collective-permute-start | bytes 196616 | tf_op jit(solution)/shard_map/ppermute | solution.py:270
  34.8 6.1 %collective-permute-start.8 = (bf16[128,256]{1,0:T(8,128)(2,1)S(1)}, bf16[128,256]{1,0:T(8,128)(2,1)S(1)}, u32[]{:S(2)}, u32[]{:S(2)}) collective-permute-start(bf16[128,256]{1,0:T(8,128)(2,1)S(1)} %project_mix.3), channel_id=1, source_target_pairs={{0,2},{1,3},{2,0},{3,1},{4,6},{5,7},{6,4},{7,5},{8,10},{9,11},{10,... | collective-permute-start | bytes 196616 | tf_op jit(solution)/shard_map/ppermute | solution.py:270
  35.4 6.2 %collective-permute-start.9 = (bf16[128,256]{1,0:T(8,128)(2,1)S(1)}, bf16[128,256]{1,0:T(8,128)(2,1)S(1)}, u32[]{:S(2)}, u32[]{:S(2)}) collective-permute-start(bf16[128,256]{1,0:T(8,128)(2,1)S(1)} %project_mix.3), channel_id=1, source_target_pairs={{0,4},{1,5},{2,6},{3,7},{4,0},{5,1},{6,2},{7,3},{8,12},{9,13},{10,... | collective-permute-start | bytes 196616 | tf_op jit(solution)/shard_map/ppermute | solution.py:270
  41.6 5.7 %collective-permute-start.12 = (bf16[2,128,256]{2,1,0:T(8,128)(2,1)S(1)}, bf16[2,128,256]{2,1,0:T(8,128)(2,1)S(1)}, u32[]{:S(2)}, u32[]{:S(2)}) collective-permute-start(bf16[2,128,256]{2,1,0:T(8,128)(2,1)S(1)} %pad_maximum_fusion.9), channel_id=1, source_target_pairs={{0,2},{1,3},{2,0},{3,1},{4,6},{5,7},{6,4},{7,5},{8,10},{9,11},{10,... | collective-permute-start | bytes 393224 | tf_op jit(solution)/shard_map/ppermute | solution.py:270
  51.4 6.5 %collective-permute-start.16 = (bf16[128,512]{1,0:T(8,128)(2,1)S(1)}, bf16[128,512]{1,0:T(8,128)(2,1)S(1)}, u32[]{:S(2)}, u32[]{:S(2)}) collective-permute-start(bf16[128,512]{1,0:T(8,128)(2,1)S(1)} %project_out.3), channel_id=1, source_target_pairs={{0,16},{1,17},{2,18},{3,19},{4,20},{5,21},{6,22},{7,23},{8,24},{9,... | collective-permute-start | bytes 393224 | tf_op jit(solution)/shard_map/ppermute | solution.py:299
  58.6 6.2 %collective-permute-start.18 = (bf16[128,512]{1,0:T(8,128)(2,1)S(1)}, bf16[128,512]{1,0:T(8,128)(2,1)S(1)}, u32[]{:S(2)}, u32[]{:S(2)}) collective-permute-start(bf16[128,512]{1,0:T(8,128)(2,1)S(1)} %bitcast_select_fusion.1.refs_5_), channel_id=1, source_target_pairs={{0,4},{1,5},{2,6},{3,7},{4,0},{5,1},{6,2},{7,3},{8,12},{9,13},{10,... | collective-permute-start | bytes 393224 | tf_op jit(solution)/shard_map/ppermute | solution.py:270
  59.7 7.9 %collective-permute-start.19 = (bf16[128,512]{1,0:T(8,128)(2,1)S(1)}, bf16[128,512]{1,0:T(8,128)(2,1)S(1)}, u32[]{:S(2)}, u32[]{:S(2)}) collective-permute-start(bf16[128,512]{1,0:T(8,128)(2,1)S(1)} %bitcast_select_fusion.1.refs_5_), channel_id=1, source_target_pairs={{0,8},{1,9},{2,10},{3,11},{4,12},{5,13},{6,14},{7,15},{8,0},{9,1},... | collective-permute-start | bytes 393224 | tf_op jit(solution)/shard_map/ppermute | solution.py:270
  67.8 11.6 %collective-permute-start.20 = (bf16[2,128,512]{2,1,0:T(8,128)(2,1)S(1)}, bf16[2,128,512]{2,1,0:T(8,128)(2,1)S(1)}, u32[]{:S(2)}, u32[]{:S(2)}) collective-permute-start(bf16[2,128,512]{2,1,0:T(8,128)(2,1)S(1)} %pad_maximum_fusion.5), channel_id=1, source_target_pairs={{0,2},{1,3},{2,0},{3,1},{4,6},{5,7},{6,4},{7,5},{8,10},{9,11},{10,... | collective-permute-start | bytes 786440 | tf_op jit(solution)/shard_map/ppermute | solution.py:270
  69.1 7.1 %collective-permute-start.21 = (bf16[1,128,512]{2,1,0:T(8,128)(2,1)S(1)}, bf16[1,128,512]{2,1,0:T(8,128)(2,1)S(1)}, u32[]{:S(2)}, u32[]{:S(2)}) collective-permute-start(bf16[1,128,512]{2,1,0:T(8,128)(2,1)S(1)} %bitcast.68), channel_id=1, source_target_pairs={{0,4},{1,5},{2,6},{3,7},{4,0},{5,1},{6,2},{7,3},{8,12},{9,13},{10,... | collective-permute-start | bytes 393224 | tf_op jit(solution)/shard_map/ppermute | solution.py:270
  69.1 8.8 %collective-permute-start.22 = (bf16[1,128,512]{2,1,0:T(8,128)(2,1)S(1)}, bf16[1,128,512]{2,1,0:T(8,128)(2,1)S(1)}, u32[]{:S(2)}, u32[]{:S(2)}) collective-permute-start(bf16[1,128,512]{2,1,0:T(8,128)(2,1)S(1)} %bitcast.69), channel_id=1, source_target_pairs={{0,6},{1,7},{2,4},{3,5},{4,2},{5,3},{6,0},{7,1},{8,14},{9,15},{10,... | collective-permute-start | bytes 393224 | tf_op jit(solution)/shard_map/ppermute | solution.py:270
  89.5 5.9 %collective-permute-start.27 = (bf16[128,256]{1,0:T(8,128)(2,1)S(1)}, bf16[128,256]{1,0:T(8,128)(2,1)S(1)}, u32[]{:S(2)}, u32[]{:S(2)}) collective-permute-start(bf16[128,256]{1,0:T(8,128)(2,1)S(1)} %project_mix.4), channel_id=1, source_target_pairs={{0,8},{1,9},{2,10},{3,11},{4,12},{5,13},{6,14},{7,15},{8,0},{9,1},... | collective-permute-start | bytes 196616 | tf_op jit(solution)/shard_map/ppermute | solution.py:270
  95.4 5.7 %collective-permute-start.29 = (bf16[2,128,256]{2,1,0:T(8,128)(2,1)S(1)}, bf16[2,128,256]{2,1,0:T(8,128)(2,1)S(1)}, u32[]{:S(2)}, u32[]{:S(2)}) collective-permute-start(bf16[2,128,256]{2,1,0:T(8,128)(2,1)S(1)} %pad_maximum_fusion.10), channel_id=1, source_target_pairs={{0,2},{1,3},{2,0},{3,1},{4,6},{5,7},{6,4},{7,5},{8,10},{9,11},{10,... | collective-permute-start | bytes 393224 | tf_op jit(solution)/shard_map/ppermute | solution.py:270
  105.0 7.4 %collective-permute-start.33 = (bf16[128,512]{1,0:T(8,128)(2,1)S(1)}, bf16[128,512]{1,0:T(8,128)(2,1)S(1)}, u32[]{:S(2)}, u32[]{:S(2)}) collective-permute-start(bf16[128,512]{1,0:T(8,128)(2,1)S(1)} %project_out.4), channel_id=1, source_target_pairs={{0,16},{1,17},{2,18},{3,19},{4,20},{5,21},{6,22},{7,23},{8,24},{9,... | collective-permute-start | bytes 393224 | tf_op jit(solution)/shard_map/ppermute | solution.py:299
  113.7 6.3 %collective-permute-start.35 = (bf16[128,512]{1,0:T(8,128)(2,1)S(1)}, bf16[128,512]{1,0:T(8,128)(2,1)S(1)}, u32[]{:S(2)}, u32[]{:S(2)}) collective-permute-start(bf16[128,512]{1,0:T(8,128)(2,1)S(1)} %bitcast_select_fusion.refs_5_), channel_id=1, source_target_pairs={{0,4},{1,5},{2,6},{3,7},{4,0},{5,1},{6,2},{7,3},{8,12},{9,13},{10,... | collective-permute-start | bytes 393224 | tf_op jit(solution)/shard_map/ppermute | solution.py:270
  114.4 7.9 %collective-permute-start.36 = (bf16[128,512]{1,0:T(8,128)(2,1)S(1)}, bf16[128,512]{1,0:T(8,128)(2,1)S(1)}, u32[]{:S(2)}, u32[]{:S(2)}) collective-permute-start(bf16[128,512]{1,0:T(8,128)(2,1)S(1)} %bitcast_select_fusion.refs_5_), channel_id=1, source_target_pairs={{0,8},{1,9},{2,10},{3,11},{4,12},{5,13},{6,14},{7,15},{8,0},{9,1},... | collective-permute-start | bytes 393224 | tf_op jit(solution)/shard_map/ppermute | solution.py:270
  122.5 11.6 %collective-permute-start.37 = (bf16[2,128,512]{2,1,0:T(8,128)(2,1)S(1)}, bf16[2,128,512]{2,1,0:T(8,128)(2,1)S(1)}, u32[]{:S(2)}, u32[]{:S(2)}) collective-permute-start(bf16[2,128,512]{2,1,0:T(8,128)(2,1)S(1)} %pad_maximum_fusion.7), channel_id=1, source_target_pairs={{0,2},{1,3},{2,0},{3,1},{4,6},{5,7},{6,4},{7,5},{8,10},{9,11},{10,... | collective-permute-start | bytes 786440 | tf_op jit(solution)/shard_map/ppermute | solution.py:270
  123.4 7.5 %collective-permute-start.38 = (bf16[1,128,512]{2,1,0:T(8,128)(2,1)S(1)}, bf16[1,128,512]{2,1,0:T(8,128)(2,1)S(1)}, u32[]{:S(2)}, u32[]{:S(2)}) collective-permute-start(bf16[1,128,512]{2,1,0:T(8,128)(2,1)S(1)} %bitcast.72), channel_id=1, source_target_pairs={{0,4},{1,5},{2,6},{3,7},{4,0},{5,1},{6,2},{7,3},{8,12},{9,13},{10,... | collective-permute-start | bytes 393224 | tf_op jit(solution)/shard_map/ppermute | solution.py:270
  123.6 8.9 %collective-permute-start.39 = (bf16[1,128,512]{2,1,0:T(8,128)(2,1)S(1)}, bf16[1,128,512]{2,1,0:T(8,128)(2,1)S(1)}, u32[]{:S(2)}, u32[]{:S(2)}) collective-permute-start(bf16[1,128,512]{2,1,0:T(8,128)(2,1)S(1)} %bitcast.73), channel_id=1, source_target_pairs={{0,6},{1,7},{2,4},{3,5},{4,2},{5,3},{6,0},{7,1},{8,14},{9,15},{10,... | collective-permute-start | bytes 393224 | tf_op jit(solution)/shard_map/ppermute | solution.py:270
  (29 other events, 187.2 us)

commit v6 on v5

v6 whole, which is shorter than its diff:
```python
import functools

import jax
import jax.numpy as jnp
from jax import lax
from jax.experimental import pallas as pl
from jax.experimental.pallas import tpu as pltpu
from jax.sharding import PartitionSpec as P

EPS = 1e-06
VMEM_LIMIT = 12 * 1024 * 1024
PAD = 8
SPLIT = 2


def split_dp(dp_count):
    core = 2 if dp_count % 2 == 0 else 1
    chips = dp_count // core
    near = 1
    while near * near * 4 <= chips:
        near *= 2
    return chips // near, near, core


def routes(far, near):
    if (far, near) == (4, 2):
        return [4, 2, 1], [(1, [4, 2]), (2, [4]), (3, [4])]
    line = [d * near for d in range(far)]
    return line[1:], [(d, line) for d in range(1, near)]


def columns_of(rank_ref, core, cell, c, size):
    chip, side = lax.div(rank_ref[0], core), lax.rem(rank_ref[0], core)
    return pl.ds(pl.multiple_of(((chip ^ cell) * core + (side ^ c)) * size, size), size)


def fetch(blocks, core, feat, rank_ref, w_far, w_ref, sems):
    branches, chan, _ = w_far.shape
    part = chan // sems.shape[2]
    copies = []
    for n, (cell, c) in enumerate(blocks):
        columns = columns_of(rank_ref, core, cell, c, feat)
        copies.append(
            [
                pltpu.make_async_copy(
                    w_far.at[i, pl.ds(m * part, part), columns], w_ref.at[n, i, pl.ds(m * part, part)], sems.at[n, i, m]
                )
                for i in range(branches)
                for m in range(sems.shape[2])
            ]
        )
    for group in copies:
        for copy in group:
            copy.start()

    def ready(n):
        for copy in copies[n]:
            copy.wait()

    return ready


def project(blocks, core, values_of, rank_ref, w_ref, gain_ref, acc_ref, sq_ref, ready):
    lanes = sq_ref.shape[1]
    for n, (cell, c) in enumerate(blocks):
        values = values_of(n).astype(jnp.float32)
        feat = values.shape[1]
        gains = gain_ref[:, columns_of(rank_ref, core, cell, c, feat)]
        normed = (values * gains).astype(jnp.bfloat16)
        squares = values * values
        part = squares[:, :lanes]
        for m in range(1, feat // lanes):
            part = part + squares[:, m * lanes : (m + 1) * lanes]
        sq_ref[...] += part
        ready(n)
        for i in range(w_ref.shape[1]):
            acc_ref[i] += lax.dot_general(
                normed, w_ref[n, i], (((1,), (1,)), ((), ())), preferred_element_type=jnp.float32
            )


def first_kernel(blocks, core, prepare, rank_ref, x_ref, w_far, gain_far, *refs):
    if prepare:
        taps_far, decay_far, acc_ref, sq_ref, gain_ref, long_ref, w_ref, sems, taps_ref, decay_ref, small_sems = refs
    else:
        acc_ref, sq_ref, w_ref, sems = refs
        gain_ref = gain_far
    ready = fetch(blocks, core, x_ref.shape[2], rank_ref, w_far, w_ref, sems)
    if prepare:
        small = [(gain_far, gain_ref), (taps_far, taps_ref), (decay_far, decay_ref)]
        small = [pltpu.make_async_copy(src, dst, small_sems.at[n]) for n, (src, dst) in enumerate(small)]
        for copy in small:
            copy.start()
        for copy in small:
            copy.wait()
        lags = lax.broadcasted_iota(jnp.int32, long_ref.shape, 0).astype(jnp.float32)
        long_ref[...] = taps_ref[...].T * jnp.exp(-decay_ref[...] * lags)
    acc_ref[...] = jnp.zeros_like(acc_ref)
    sq_ref[...] = jnp.zeros_like(sq_ref)
    project(blocks, core, lambda n: x_ref[n], rank_ref, w_ref, gain_ref, acc_ref, sq_ref, ready)


def more_kernel(blocks, core, rank_ref, x_ref, w_far, gain_ref, acc_in, sq_in, acc_ref, sq_ref, w_ref, sems):
    ready = fetch(blocks, core, x_ref.shape[2], rank_ref, w_far, w_ref, sems)
    acc_ref[...] = acc_in[...]
    sq_ref[...] = sq_in[...]
    project(blocks, core, lambda n: x_ref[n], rank_ref, w_ref, gain_ref, acc_ref, sq_ref, ready)


def mix_kernel(blocks, core, rank_ref, *refs):
    sides = refs[: core - 1]
    w_far, gain_ref, acc_in, sq_in, short_ref, long_ref, y_ref = refs[core - 1 : core + 6]
    acc_ref, sq_ref, pad_ref, query_ref, w_ref, sems = refs[core + 6 :]
    branches, chan, model_width = w_far.shape
    tok_len = y_ref.shape[0]
    acc_ref[...] = acc_in[...]
    sq_ref[...] = sq_in[...]
    if core > 1:
        count, _, feat = sides[0].shape
        ready = fetch(blocks, core, feat, rank_ref, w_far, w_ref, sems)
        project(
            blocks,
            core,
            lambda n: sides[n // count][n % count],
            rank_ref,
            w_ref,
            gain_ref,
            acc_ref,
            sq_ref,
            ready,
        )

    total = jnp.sum(sq_ref[...], axis=1, keepdims=True)
    factor = lax.rsqrt(total / model_width + EPS)
    taps = short_ref.shape[0] // branches
    pad_ref[0:PAD, :] = jnp.zeros((PAD, chan), jnp.float32)

    def branch(i):
        u = acc_ref[i] * factor
        pad_ref[PAD : PAD + tok_len, :] = u
        z = short_ref[i * taps : i * taps + 1, :] * u
        for j in range(1, taps):
            z = z + short_ref[i * taps + j : i * taps + j + 1, :] * pad_ref[PAD - j : PAD - j + tok_len, :]
        return z

    query_ref[...] = branch(1)
    product = query_ref[...] * branch(2)
    query_ref[...] = branch(0)
    pad_ref[PAD : PAD + tok_len, :] = product
    width = min(chan, 128)
    tiles = tok_len // 8
    for c in range(0, chan, width):
        cols = slice(c, c + width)
        conv = [None] * tiles
        for b in range(8):
            moved = [pad_ref[PAD - b + 8 * i : PAD - b + 8 * i + 8, cols] for i in range(tiles)]
            for a in range(long_ref.shape[0] // 8):
                tap = long_ref[8 * a + b : 8 * a + b + 1, cols]
                for i in range(a, tiles):
                    term = tap * moved[i - a]
                    conv[i] = term if conv[i] is None else conv[i] + term
        for i in range(0, tiles, 2):
            at = slice(8 * i, 8 * i + 16)
            both = jnp.concatenate(conv[i : i + 2], axis=0)
            y_ref[at, cols] = (query_ref[at, cols] * both).astype(jnp.bfloat16)


def out_kernel(blocks, core, rank_ref, *refs):
    sides = refs[:core]
    w_ref, own_ref, result_ref, acc_ref = refs[core:]
    count, _, chan = sides[0].shape
    acc_ref[...] = own_ref[...].astype(jnp.float32)
    for n, (cell, c) in enumerate(blocks):
        rows = columns_of(rank_ref, core, cell, c, chan)
        acc_ref[...] += jnp.dot(sides[n // count][n % count], w_ref[rows, :], preferred_element_type=jnp.float32)
    result_ref[...] = acc_ref[...].astype(jnp.bfloat16)


def in_vmem(count):
    return [pl.BlockSpec(memory_space=pltpu.VMEM)] * count


def call(kernel, operands, outs, scratch, flops, name, far_operands=()):
    specs = [pl.BlockSpec(memory_space=pltpu.SMEM)] + in_vmem(len(operands) - 1)
    operands = list(operands)
    for n in far_operands:
        specs[n] = pl.BlockSpec(memory_space=pltpu.HBM)
        operands[n] = pltpu.with_memory_space_constraint(operands[n], pltpu.HBM)
    return pl.pallas_call(
        kernel,
        in_specs=specs,
        out_specs=in_vmem(len(outs)),
        out_shape=outs,
        scratch_shapes=scratch,
        compiler_params=pltpu.CompilerParams(vmem_limit_bytes=VMEM_LIMIT),
        cost_estimate=pl.CostEstimate(flops=flops, bytes_accessed=flops // 1024, transcendentals=0),
        name=name,
    )(*operands)


def streamed(count, w_in, feat):
    branches, chan, _ = w_in.shape
    return [
        pltpu.VMEM((count, branches, chan, feat), w_in.dtype),
        pltpu.SemaphoreType.DMA((count, branches, max(1, min(SPLIT, chan // 16)))),
    ]


def sums_of(rows, feat, w_in):
    return [
        jax.ShapeDtypeStruct((w_in.shape[0], rows, w_in.shape[1]), jnp.float32),
        jax.ShapeDtypeStruct((rows, min(feat, 128)), jnp.float32),
    ]


def work_of(x, w_in):
    return 2 * x.size * w_in.shape[0] * w_in.shape[1]


def project_first(blocks, core, x, w_in, gain, rank, taps=None, decay=None):
    count, rows, feat = x.shape
    operands, far, outs = [rank, x, w_in, gain], [2], sums_of(rows, feat, w_in)
    scratch = streamed(count, w_in, feat)
    if taps is not None:
        operands += [taps, decay]
        far = [2, 3, 4, 5]
        outs.append(jax.ShapeDtypeStruct(gain.shape, gain.dtype))
        outs.append(jax.ShapeDtypeStruct(taps.shape[::-1], taps.dtype))
        scratch += [pltpu.VMEM(taps.shape, taps.dtype), pltpu.VMEM(decay.shape, decay.dtype), pltpu.SemaphoreType.DMA((3,))]
    kernel = functools.partial(first_kernel, blocks, core, taps is not None)
    return call(kernel, operands, outs, scratch, work_of(x, w_in), "project_first", far)


def project_more(blocks, core, x, w_in, gain, sums, rank):
    count, rows, feat = x.shape
    kernel = functools.partial(more_kernel, blocks, core)
    operands, scratch = [rank, x, w_in, gain, *sums], streamed(count, w_in, feat)
    return call(kernel, operands, sums_of(rows, feat, w_in), scratch, work_of(x, w_in), "project_more", [2])


def mix(blocks, core, sides, w_in, gain, sums, short_rows, long_rows, rank):
    rows, chan = sums[0].shape[1:]
    feat = w_in.shape[2] // (len(blocks) // max(core - 1, 1) * core) if blocks else 128
    scratch = [pltpu.VMEM(total.shape, total.dtype) for total in sums]
    scratch += [pltpu.VMEM((PAD + rows, chan), jnp.float32), pltpu.VMEM((rows, chan), jnp.float32)]
    return call(
        functools.partial(mix_kernel, blocks, core),
        [rank, *sides, w_in, gain, *sums, short_rows, long_rows],
        [jax.ShapeDtypeStruct((rows, chan), jnp.bfloat16)],
        scratch + streamed(max(len(blocks), 1), w_in, feat),
        sum(work_of(x, w_in) for x in sides),
        "project_mix",
        [core],
    )[0]


def project_out(blocks, core, sides, w_out, own, rank):
    rows, feat = own.shape
    return call(
        functools.partial(out_kernel, blocks, core),
        [rank, *sides, w_out, own],
        [jax.ShapeDtypeStruct((rows, feat), jnp.bfloat16)],
        [pltpu.VMEM((rows, feat), jnp.float32)],
        2 * rows * w_out.shape[0] * feat,
        "project_out",
    )[0]


def body(section_count, dp_count, fresh_acts, carried, norm_gain, w_in, short_filter, filter_taps, decay_rate, w_out):
    tick_count, tok_len, _ = fresh_acts.shape
    far, near, core = split_dp(dp_count)
    group = near * core
    section_idx = lax.axis_index("section")
    rank = lax.axis_index("dp").astype(jnp.int32).reshape(1)

    def swap(value, offset):
        return lax.ppermute(value, "dp", [(r, r ^ offset) for r in range(dp_count)])

    first_round, second_round = routes(far, near)

    def after(value, *earlier):
        return lax.optimization_barrier((value, earlier))[0]

    def round_one(source):
        return lax.optimization_barrier({0: source} | {d: swap(source, d * core) for d in first_round})

    def round_two(blocks):
        leaving = lax.optimization_barrier([jnp.stack([blocks[b] for b in sent]) for _, sent in second_round])
        rest = [swap(payload, d * core) for payload, (d, _) in zip(leaving, second_round)]
        return [d ^ b for d, sent in second_round for b in sent], rest

    def of_core(cells, c):
        return [(cell, c) for cell in cells]

    short_rows = short_filter[0].transpose(0, 2, 1).reshape(-1, short_filter.shape[2])
    gain, small = norm_gain, (filter_taps[0], decay_rate)
    is_first = section_idx == 0
    onward = [(s, s + 1) for s in range(section_count - 1)]
    made = []
    for k in range(tick_count):
        before = carried[0] if k == 0 else lax.ppermute(made[-1], "section", onward)
        own = jnp.where(is_first, fresh_acts[k], before)
        blocks = round_one(own)
        cells, rest = round_two(blocks)
        direct = jnp.stack(list(blocks.values()))
        *sums, = project_first(of_core(blocks, 0), core, direct, w_in[0], gain, rank, *small)
        if small:
            *sums, gain, long_rows = sums
            small = ()
        relayed = jnp.concatenate(after(rest, sums))
        everything = jnp.concatenate([direct, relayed])
        sides = [swap(everything, c) for c in range(1, core)]
        sums = project_more(of_core(cells, 0), core, relayed, w_in[0], gain, sums, rank)
        sides = after(sides, sums)
        order = [*blocks, *cells]
        far_blocks = [block for c in range(1, core) for block in of_core(order, c)]
        y = mix(far_blocks, core, sides, w_in[0], gain, sums, short_rows, long_rows, rank)
        blocks = round_one(y)
        cells, rest = round_two(blocks)
        everything = jnp.concatenate([jnp.stack(list(blocks.values())), *rest])
        sides = [everything] + [swap(everything, c) for c in range(1, core)]
        order = [*blocks, *cells]
        all_blocks = [block for c in range(core) for block in of_core(order, c)]
        made.append(project_out(all_blocks, core, sides, w_out[0], own, rank))
    return jnp.stack(made)[None]


def solution(mesh):
    run = functools.partial(body, mesh.shape["section"], mesh.shape["dp"])
    return jax.shard_map(
        run,
        mesh=mesh,
        in_specs=(
            P(None, None, "dp"),
            P("section", None, "dp"),
            P("section", None),
            P("section", None, "dp", None),
            P("section", None, "dp", None),
            P("section", "dp", None),
            P("section", "dp"),
            P("section", None, "dp"),
        ),
        out_specs=P("section", None, None, "dp"),
        check_vma=False,
    )
```

time: 161 us -> 159 us (0.988)
  waiting for transfers between devices: 65.1 us -> 55.2 us
  Pallas kernels: 38.4 us -> 42.6 us
  starting transfers between devices: 54.1 us -> 57.6 us
    ppermute x48 -> x42, waiting for transfers between devices: 59.5 us -> 49.5 us  [swap(): return lax.ppermute(value, 'dp', [(r, r ^ offset) for r in range(dp_count)])]
    pallas_call x9 -> x12, Pallas kernels: 38.4 us -> 42.6 us  [call(): pl.pallas_call(kernel, in_specs=specs, out_specs=in_vmem(len(outs)), out_...]
    ppermute x48 -> x42, starting transfers between devices: 45.8 us -> 49.3 us  [swap(): return lax.ppermute(value, 'dp', [(r, r ^ offset) for r in range(dp_count)])]
  transfers between devices with their start and end apart: 50 -> 44, of which waited for: 36 -> 32; matrix products, arithmetic and copies ran while one was open for 0% -> 0% of each run, Pallas kernels for 10% -> 13%
where the time goes in v6:
time: 159 us
  starting transfers between devices  57.6 us (36%)
  waiting for transfers between devices  55.2 us (35%)
  Pallas kernels  42.6 us (27%)
  other arithmetic  2.3 us (1%)
    ppermute x42, waiting for transfers between devices, swap(): return lax.ppermute(value, 'dp', [(r, r ^ offset) for r in range(dp_count)])  49.5 us
    ppermute x42, starting transfers between devices, swap(): return lax.ppermute(value, 'dp', [(r, r ^ offset) for r in range(dp_count)])  49.3 us
    pallas_call x12, Pallas kernels, call(): pl.pallas_call(kernel, in_specs=specs, out_specs=in_vmem(len(outs)), out_...  42.6 us
    ppermute x2, starting transfers between devices, body(): before = carried[0] if k == 0 else lax.ppermute(made[-1], 'section', onward)  8.29 us
    ppermute x2, waiting for transfers between devices, body(): before = carried[0] if k == 0 else lax.ppermute(made[-1], 'section', onward)  5.66 us
  transfers between devices with their start and end apart: 44, of which 32 were waited for; matrix products, arithmetic and copies ran while one was open for 0% of the time, Pallas kernels for 13%

profile of v6, /device:TPU:0, one launch (start us, length us, event | category | flops | bytes accessed | tf_op | source)
XLA Modules:
  0.0 158.6 jit_solution(8680525425034971536)
XLA Ops:
  0.9 3.0 %collective-permute-start = (bf16[128,512]{1,0:T(8,128)(2,1)S(1)}, bf16[128,512]{1,0:T(8,128)(2,1)S(1)}, u32[]{:S(2)}, u32[]{:S(2)}) collective-permute-start(bf16[128,512]{1,0:T(8,128)(2,1)S(1)} %select_bitcast_fusion.refs_3_), channel_id=1, source_target_pairs={{0,2},{1,3},{2,0},{3,1},{4,6},{5,7},{6,4},{7,5},{8,10},{9,11},{10,... | collective-permute-start | bytes 393224 | tf_op jit(solution)/shard_map/ppermute | solution.py:277
  5.5 2.6 %collective-permute-start.2 = (bf16[128,512]{1,0:T(8,128)(2,1)S(1)}, bf16[128,512]{1,0:T(8,128)(2,1)S(1)}, u32[]{:S(2)}, u32[]{:S(2)}) collective-permute-start(bf16[128,512]{1,0:T(8,128)(2,1)S(1)} %select_bitcast_fusion.refs_3_), channel_id=1, source_target_pairs={{0,8},{1,9},{2,10},{3,11},{4,12},{5,13},{6,14},{7,15},{8,0},{9,1},... | collective-permute-start | bytes 393224 | tf_op jit(solution)/shard_map/ppermute | solution.py:277
  8.1 2.5 %collective-permute-done.1 = bf16[128,512]{1,0:T(8,128)(2,1)S(1)} collective-permute-done((bf16[128,512]{1,0:T(8,128)(2,1)S(1)}, bf16[128,512]{1,0:T(8,128)(2,1)S(1)}, u32[]{:S(2)}, u32[]{:S(2)}) %collective-permute-start.1) | collective-permute-done | bytes 131104 | tf_op jit(solution)/shard_map/ppermute | solution.py:277
  10.6 3.3 %collective-permute-done.2 = bf16[128,512]{1,0:T(8,128)(2,1)S(1)} collective-permute-done((bf16[128,512]{1,0:T(8,128)(2,1)S(1)}, bf16[128,512]{1,0:T(8,128)(2,1)S(1)}, u32[]{:S(2)}, u32[]{:S(2)}) %collective-permute-start.2) | collective-permute-done | bytes 131104 | tf_op jit(solution)/shard_map/ppermute | solution.py:277
  15.1 2.6 %collective-permute-start.5 = (bf16[1,128,512]{2,1,0:T(8,128)(2,1)S(1)}, bf16[1,128,512]{2,1,0:T(8,128)(2,1)S(1)}, u32[]{:S(2)}, u32[]{:S(2)}) collective-permute-start(bf16[1,128,512]{2,1,0:T(8,128)(2,1)S(1)} %bitcast.88), channel_id=1, source_target_pairs={{0,6},{1,7},{2,4},{3,5},{4,2},{5,3},{6,0},{7,1},{8,14},{9,15},{10,... | collective-permute-start | bytes 393224 | tf_op jit(solution)/shard_map/ppermute | solution.py:277
  17.7 4.1 %project_first.3 = (f32[3,128,256]{2,1,0:T(8,128)S(1)}, f32[128,128]{1,0:T(8,128)S(1)}, f32[1,8192]{1,0:T(1,128)S(1)}, f32[128,256]{1,0:T(8,128)S(1)}) custom-call(s32[1]{0:T(128)} %bitcast.rank_ref, bf16[4,128,512]{2,1,0:T(8,128)(2,1)S(1)} %pad_maximum_fusion.x_ref, bf16[3,256,8192]{2,1,0:T(8,128)(2,1)} %bitcast.77, f32[1,8192]{1,0:T(1,128)} %gain_far.1, ...), custom_call_target="tpu_custom_call" | custom-call | flops 402653184 | bytes 393216 | tf_op jit(solution)/shard_map/project_first/pallas_call | solution.py:189
  22.3 3.3 %project_more.3 = (f32[3,128,256]{2,1,0:T(8,128)S(1)}, f32[128,128]{1,0:T(8,128)S(1)}) custom-call(s32[1]{0:T(128)} %bitcast.rank_ref, bf16[4,128,512]{2,1,0:T(8,128)(2,1)S(1)} %pad_maximum_fusion.1.x_ref, bf16[3,256,8192]{2,1,0:T(8,128)(2,1)} %bitcast.78, f32[1,8192]{1,0:T(1,128)S(1)} %get-tuple-element.85.gain_ref.refs_2_.gain_far, ...), custom_call_target="tpu_custom_call" | custom-call | flops 402653184 | bytes 393216 | tf_op jit(solution)/shard_map/project_more/pallas_call | solution.py:189
  25.6 6.8 %project_mix.3 = bf16[128,256]{1,0:T(8,128)(2,1)S(1)} custom-call(s32[1]{0:T(128)} %bitcast.rank_ref, bf16[8,128,512]{2,1,0:T(8,128)(2,1)S(1)} %collective-permute-done.6.refs_0_, bf16[3,256,8192]{2,1,0:T(8,128)(2,1)} %bitcast.79, f32[1,8192]{1,0:T(1,128)S(1)} %get-tuple-element.85.gain_ref.refs_2_.gain_far, f32[3,128,256]{2,1,0:T(8,128)S(1)} %get-tuple-element.86.refs_3_, ...), custom_call_target="tpu_custom_call" | custom-call | flops 805306368 | bytes 786432 | tf_op jit(solution)/shard_map/project_mix/pallas_call | solution.py:189
  38.2 3.0 %collective-permute-done.9 = bf16[128,256]{1,0:T(8,128)(2,1)S(1)} collective-permute-done((bf16[128,256]{1,0:T(8,128)(2,1)S(1)}, bf16[128,256]{1,0:T(8,128)(2,1)S(1)}, u32[]{:S(2)}, u32[]{:S(2)}) %collective-permute-start.9) | collective-permute-done | bytes 65568 | tf_op jit(solution)/shard_map/ppermute | solution.py:277
  50.4 3.7 %collective-permute-start.14 = (bf16[128,512]{1,0:T(8,128)(2,1)S(1)}, bf16[128,512]{1,0:T(8,128)(2,1)S(1)}, u32[]{:S(2)}, u32[]{:S(2)}) collective-permute-start(bf16[128,512]{1,0:T(8,128)(2,1)S(1)} %project_out.3), channel_id=1, source_target_pairs={{0,16},{1,17},{2,18},{3,19},{4,20},{5,21},{6,22},{7,23},{8,24},{9,... | collective-permute-start | bytes 393224 | tf_op jit(solution)/shard_map/ppermute | solution.py:301
  54.1 2.9 %collective-permute-done.14 = bf16[128,512]{1,0:T(8,128)(2,1)S(1)} collective-permute-done((bf16[128,512]{1,0:T(8,128)(2,1)S(1)}, bf16[128,512]{1,0:T(8,128)(2,1)S(1)}, u32[]{:S(2)}, u32[]{:S(2)}) %collective-permute-start.14) | collective-permute-done | bytes 131104 | tf_op jit(solution)/shard_map/ppermute | solution.py:301
  62.0 2.9 %collective-permute-done.16 = bf16[128,512]{1,0:T(8,128)(2,1)S(1)} collective-permute-done((bf16[128,512]{1,0:T(8,128)(2,1)S(1)}, bf16[128,512]{1,0:T(8,128)(2,1)S(1)}, u32[]{:S(2)}, u32[]{:S(2)}) %collective-permute-start.16) | collective-permute-done | bytes 131104 | tf_op jit(solution)/shard_map/ppermute | solution.py:277
  64.8 2.8 %collective-permute-done.17 = bf16[128,512]{1,0:T(8,128)(2,1)S(1)} collective-permute-done((bf16[128,512]{1,0:T(8,128)(2,1)S(1)}, bf16[128,512]{1,0:T(8,128)(2,1)S(1)}, u32[]{:S(2)}, u32[]{:S(2)}) %collective-permute-start.17) | collective-permute-done | bytes 131104 | tf_op jit(solution)/shard_map/ppermute | solution.py:277
  71.4 3.2 %project_first.4 = (f32[3,128,256]{2,1,0:T(8,128)S(1)}, f32[128,128]{1,0:T(8,128)S(1)}) custom-call(s32[1]{0:T(128)} %bitcast.rank_ref, bf16[4,128,512]{2,1,0:T(8,128)(2,1)S(1)} %pad_maximum_fusion.2.x_ref, bf16[3,256,8192]{2,1,0:T(8,128)(2,1)} %bitcast.80, f32[1,8192]{1,0:T(1,128)S(1)} %get-tuple-element.85.gain_ref.refs_2_.gain_far), custom_call_target="tpu_custom_call" | custom-call | flops 402653184 | bytes 393216 | tf_op jit(solution)/shard_map/project_first/pallas_call | solution.py:189
  76.1 3.2 %project_more.4 = (f32[3,128,256]{2,1,0:T(8,128)S(1)}, f32[128,128]{1,0:T(8,128)S(1)}) custom-call(s32[1]{0:T(128)} %bitcast.rank_ref, bf16[4,128,512]{2,1,0:T(8,128)(2,1)S(1)} %pad_maximum_fusion.3.x_ref, bf16[3,256,8192]{2,1,0:T(8,128)(2,1)} %bitcast.81, f32[1,8192]{1,0:T(1,128)S(1)} %get-tuple-element.85.gain_ref.refs_2_.gain_far, ...), custom_call_target="tpu_custom_call" | custom-call | flops 402653184 | bytes 393216 | tf_op jit(solution)/shard_map/project_more/pallas_call | solution.py:189
  79.3 6.8 %project_mix.4 = bf16[128,256]{1,0:T(8,128)(2,1)S(1)} custom-call(s32[1]{0:T(128)} %bitcast.rank_ref, bf16[8,128,512]{2,1,0:T(8,128)(2,1)S(1)} %collective-permute-done.21.refs_0_, bf16[3,256,8192]{2,1,0:T(8,128)(2,1)} %bitcast.82, f32[1,8192]{1,0:T(1,128)S(1)} %get-tuple-element.85.gain_ref.refs_2_.gain_far, f32[3,128,256]{2,1,0:T(8,128)S(1)} %get-tuple-element.109.refs_3_, ...), custom_call_target="tpu_custom_call" | custom-call | flops 805306368 | bytes 786432 | tf_op jit(solution)/shard_map/project_mix/pallas_call | solution.py:189
  103.8 4.6 %collective-permute-start.29 = (bf16[128,512]{1,0:T(8,128)(2,1)S(1)}, bf16[128,512]{1,0:T(8,128)(2,1)S(1)}, u32[]{:S(2)}, u32[]{:S(2)}) collective-permute-start(bf16[128,512]{1,0:T(8,128)(2,1)S(1)} %project_out.4), channel_id=1, source_target_pairs={{0,16},{1,17},{2,18},{3,19},{4,20},{5,21},{6,22},{7,23},{8,24},{9,... | collective-permute-start | bytes 393224 | tf_op jit(solution)/shard_map/ppermute | solution.py:301
  108.4 2.8 %collective-permute-done.29 = bf16[128,512]{1,0:T(8,128)(2,1)S(1)} collective-permute-done((bf16[128,512]{1,0:T(8,128)(2,1)S(1)}, bf16[128,512]{1,0:T(8,128)(2,1)S(1)}, u32[]{:S(2)}, u32[]{:S(2)}) %collective-permute-start.29) | collective-permute-done | bytes 131104 | tf_op jit(solution)/shard_map/ppermute | solution.py:301
  116.3 2.6 %collective-permute-done.31 = bf16[128,512]{1,0:T(8,128)(2,1)S(1)} collective-permute-done((bf16[128,512]{1,0:T(8,128)(2,1)S(1)}, bf16[128,512]{1,0:T(8,128)(2,1)S(1)}, u32[]{:S(2)}, u32[]{:S(2)}) %collective-permute-start.31) | collective-permute-done | bytes 131104 | tf_op jit(solution)/shard_map/ppermute | solution.py:277
  118.9 3.0 %collective-permute-done.32 = bf16[128,512]{1,0:T(8,128)(2,1)S(1)} collective-permute-done((bf16[128,512]{1,0:T(8,128)(2,1)S(1)}, bf16[128,512]{1,0:T(8,128)(2,1)S(1)}, u32[]{:S(2)}, u32[]{:S(2)}) %collective-permute-start.32) | collective-permute-done | bytes 131104 | tf_op jit(solution)/shard_map/ppermute | solution.py:277
  125.7 3.2 %project_first.5 = (f32[3,128,256]{2,1,0:T(8,128)S(1)}, f32[128,128]{1,0:T(8,128)S(1)}) custom-call(s32[1]{0:T(128)} %bitcast.rank_ref, bf16[4,128,512]{2,1,0:T(8,128)(2,1)S(1)} %pad_maximum_fusion.4.x_ref, bf16[3,256,8192]{2,1,0:T(8,128)(2,1)} %bitcast.83, f32[1,8192]{1,0:T(1,128)S(1)} %get-tuple-element.85.gain_ref.refs_2_.gain_far), custom_call_target="tpu_custom_call" | custom-call | flops 402653184 | bytes 393216 | tf_op jit(solution)/shard_map/project_first/pallas_call | solution.py:189
  130.4 3.2 %project_more.5 = (f32[3,128,256]{2,1,0:T(8,128)S(1)}, f32[128,128]{1,0:T(8,128)S(1)}) custom-call(s32[1]{0:T(128)} %bitcast.rank_ref, bf16[4,128,512]{2,1,0:T(8,128)(2,1)S(1)} %pad_maximum_fusion.5.x_ref, bf16[3,256,8192]{2,1,0:T(8,128)(2,1)} %bitcast.84, f32[1,8192]{1,0:T(1,128)S(1)} %get-tuple-element.85.gain_ref.refs_2_.gain_far, ...), custom_call_target="tpu_custom_call" | custom-call | flops 402653184 | bytes 393216 | tf_op jit(solution)/shard_map/project_more/pallas_call | solution.py:189
  133.5 6.8 %project_mix.5 = bf16[128,256]{1,0:T(8,128)(2,1)S(1)} custom-call(s32[1]{0:T(128)} %bitcast.rank_ref, bf16[8,128,512]{2,1,0:T(8,128)(2,1)S(1)} %collective-permute-done.36.refs_0_, bf16[3,256,8192]{2,1,0:T(8,128)(2,1)} %bitcast.85, f32[1,8192]{1,0:T(1,128)S(1)} %get-tuple-element.85.gain_ref.refs_2_.gain_far, f32[3,128,256]{2,1,0:T(8,128)S(1)} %get-tuple-element.131.refs_3_, ...), custom_call_target="tpu_custom_call" | custom-call | flops 805306368 | bytes 786432 | tf_op jit(solution)/shard_map/project_mix/pallas_call | solution.py:189
  145.7 3.0 %collective-permute-done.39 = bf16[128,256]{1,0:T(8,128)(2,1)S(1)} collective-permute-done((bf16[128,256]{1,0:T(8,128)(2,1)S(1)}, bf16[128,256]{1,0:T(8,128)(2,1)S(1)}, u32[]{:S(2)}, u32[]{:S(2)}) %collective-permute-start.39) | collective-permute-done | bytes 65568 | tf_op jit(solution)/shard_map/ppermute | solution.py:277
  (142 shorter events, 72.4 us)
Async XLA Ops:
  0.9 7.2 %collective-permute-start = (bf16[128,512]{1,0:T(8,128)(2,1)S(1)}, bf16[128,512]{1,0:T(8,128)(2,1)S(1)}, u32[]{:S(2)}, u32[]{:S(2)}) collective-permute-start(bf16[128,512]{1,0:T(8,128)(2,1)S(1)} %select_bitcast_fusion.refs_3_), channel_id=1, source_target_pairs={{0,2},{1,3},{2,0},{3,1},{4,6},{5,7},{6,4},{7,5},{8,10},{9,11},{10,... | collective-permute-start | bytes 393224 | tf_op jit(solution)/shard_map/ppermute | solution.py:277
  3.9 6.7 %collective-permute-start.1 = (bf16[128,512]{1,0:T(8,128)(2,1)S(1)}, bf16[128,512]{1,0:T(8,128)(2,1)S(1)}, u32[]{:S(2)}, u32[]{:S(2)}) collective-permute-start(bf16[128,512]{1,0:T(8,128)(2,1)S(1)} %select_bitcast_fusion.refs_3_), channel_id=1, source_target_pairs={{0,4},{1,5},{2,6},{3,7},{4,0},{5,1},{6,2},{7,3},{8,12},{9,13},{10,... | collective-permute-start | bytes 393224 | tf_op jit(solution)/shard_map/ppermute | solution.py:277
  5.5 8.4 %collective-permute-start.2 = (bf16[128,512]{1,0:T(8,128)(2,1)S(1)}, bf16[128,512]{1,0:T(8,128)(2,1)S(1)}, u32[]{:S(2)}, u32[]{:S(2)}) collective-permute-start(bf16[128,512]{1,0:T(8,128)(2,1)S(1)} %select_bitcast_fusion.refs_3_), channel_id=1, source_target_pairs={{0,8},{1,9},{2,10},{3,11},{4,12},{5,13},{6,14},{7,15},{8,0},{9,1},... | collective-permute-start | bytes 393224 | tf_op jit(solution)/shard_map/ppermute | solution.py:277
  14.0 8.0 %collective-permute-start.3 = (bf16[2,128,512]{2,1,0:T(8,128)(2,1)S(1)}, bf16[2,128,512]{2,1,0:T(8,128)(2,1)S(1)}, u32[]{:S(2)}, u32[]{:S(2)}) collective-permute-start(bf16[2,128,512]{2,1,0:T(8,128)(2,1)S(1)} %pad_maximum_fusion.6), channel_id=1, source_target_pairs={{0,2},{1,3},{2,0},{3,1},{4,6},{5,7},{6,4},{7,5},{8,10},{9,11},{10,... | collective-permute-start | bytes 786440 | tf_op jit(solution)/shard_map/ppermute | solution.py:277
  14.6 7.2 %collective-permute-start.4 = (bf16[1,128,512]{2,1,0:T(8,128)(2,1)S(1)}, bf16[1,128,512]{2,1,0:T(8,128)(2,1)S(1)}, u32[]{:S(2)}, u32[]{:S(2)}) collective-permute-start(bf16[1,128,512]{2,1,0:T(8,128)(2,1)S(1)} %bitcast.87), channel_id=1, source_target_pairs={{0,4},{1,5},{2,6},{3,7},{4,0},{5,1},{6,2},{7,3},{8,12},{9,13},{10,... | collective-permute-start | bytes 393224 | tf_op jit(solution)/shard_map/ppermute | solution.py:277
  15.1 7.0 %collective-permute-start.5 = (bf16[1,128,512]{2,1,0:T(8,128)(2,1)S(1)}, bf16[1,128,512]{2,1,0:T(8,128)(2,1)S(1)}, u32[]{:S(2)}, u32[]{:S(2)}) collective-permute-start(bf16[1,128,512]{2,1,0:T(8,128)(2,1)S(1)} %bitcast.88), channel_id=1, source_target_pairs={{0,6},{1,7},{2,4},{3,5},{4,2},{5,3},{6,0},{7,1},{8,14},{9,15},{10,... | collective-permute-start | bytes 393224 | tf_op jit(solution)/shard_map/ppermute | solution.py:277
  34.8 6.3 %collective-permute-start.9 = (bf16[128,256]{1,0:T(8,128)(2,1)S(1)}, bf16[128,256]{1,0:T(8,128)(2,1)S(1)}, u32[]{:S(2)}, u32[]{:S(2)}) collective-permute-start(bf16[128,256]{1,0:T(8,128)(2,1)S(1)} %project_mix.3), channel_id=1, source_target_pairs={{0,8},{1,9},{2,10},{3,11},{4,12},{5,13},{6,14},{7,15},{8,0},{9,1},... | collective-permute-start | bytes 196616 | tf_op jit(solution)/shard_map/ppermute | solution.py:277
  41.2 5.7 %collective-permute-start.10 = (bf16[2,128,256]{2,1,0:T(8,128)(2,1)S(1)}, bf16[2,128,256]{2,1,0:T(8,128)(2,1)S(1)}, u32[]{:S(2)}, u32[]{:S(2)}) collective-permute-start(bf16[2,128,256]{2,1,0:T(8,128)(2,1)S(1)} %pad_maximum_fusion.9), channel_id=1, source_target_pairs={{0,2},{1,3},{2,0},{3,1},{4,6},{5,7},{6,4},{7,5},{8,10},{9,11},{10,... | collective-permute-start | bytes 393224 | tf_op jit(solution)/shard_map/ppermute | solution.py:277
  50.4 6.5 %collective-permute-start.14 = (bf16[128,512]{1,0:T(8,128)(2,1)S(1)}, bf16[128,512]{1,0:T(8,128)(2,1)S(1)}, u32[]{:S(2)}, u32[]{:S(2)}) collective-permute-start(bf16[128,512]{1,0:T(8,128)(2,1)S(1)} %project_out.3), channel_id=1, source_target_pairs={{0,16},{1,17},{2,18},{3,19},{4,20},{5,21},{6,22},{7,23},{8,24},{9,... | collective-permute-start | bytes 393224 | tf_op jit(solution)/shard_map/ppermute | solution.py:301
  58.3 6.6 %collective-permute-start.16 = (bf16[128,512]{1,0:T(8,128)(2,1)S(1)}, bf16[128,512]{1,0:T(8,128)(2,1)S(1)}, u32[]{:S(2)}, u32[]{:S(2)}) collective-permute-start(bf16[128,512]{1,0:T(8,128)(2,1)S(1)} %bitcast_select_fusion.1.refs_3_), channel_id=1, source_target_pairs={{0,4},{1,5},{2,6},{3,7},{4,0},{5,1},{6,2},{7,3},{8,12},{9,13},{10,... | collective-permute-start | bytes 393224 | tf_op jit(solution)/shard_map/ppermute | solution.py:277
  59.8 7.9 %collective-permute-start.17 = (bf16[128,512]{1,0:T(8,128)(2,1)S(1)}, bf16[128,512]{1,0:T(8,128)(2,1)S(1)}, u32[]{:S(2)}, u32[]{:S(2)}) collective-permute-start(bf16[128,512]{1,0:T(8,128)(2,1)S(1)} %bitcast_select_fusion.1.refs_3_), channel_id=1, source_target_pairs={{0,8},{1,9},{2,10},{3,11},{4,12},{5,13},{6,14},{7,15},{8,0},{9,1},... | collective-permute-start | bytes 393224 | tf_op jit(solution)/shard_map/ppermute | solution.py:277
  67.7 8.2 %collective-permute-start.18 = (bf16[2,128,512]{2,1,0:T(8,128)(2,1)S(1)}, bf16[2,128,512]{2,1,0:T(8,128)(2,1)S(1)}, u32[]{:S(2)}, u32[]{:S(2)}) collective-permute-start(bf16[2,128,512]{2,1,0:T(8,128)(2,1)S(1)} %pad_maximum_fusion.7), channel_id=1, source_target_pairs={{0,2},{1,3},{2,0},{3,1},{4,6},{5,7},{6,4},{7,5},{8,10},{9,11},{10,... | collective-permute-start | bytes 786440 | tf_op jit(solution)/shard_map/ppermute | solution.py:277
  69.1 5.5 %collective-permute-start.19 = (bf16[1,128,512]{2,1,0:T(8,128)(2,1)S(1)}, bf16[1,128,512]{2,1,0:T(8,128)(2,1)S(1)}, u32[]{:S(2)}, u32[]{:S(2)}) collective-permute-start(bf16[1,128,512]{2,1,0:T(8,128)(2,1)S(1)} %bitcast.93), channel_id=1, source_target_pairs={{0,4},{1,5},{2,6},{3,7},{4,0},{5,1},{6,2},{7,3},{8,12},{9,13},{10,... | collective-permute-start | bytes 393224 | tf_op jit(solution)/shard_map/ppermute | solution.py:277
  69.2 6.6 %collective-permute-start.20 = (bf16[1,128,512]{2,1,0:T(8,128)(2,1)S(1)}, bf16[1,128,512]{2,1,0:T(8,128)(2,1)S(1)}, u32[]{:S(2)}, u32[]{:S(2)}) collective-permute-start(bf16[1,128,512]{2,1,0:T(8,128)(2,1)S(1)} %bitcast.94), channel_id=1, source_target_pairs={{0,6},{1,7},{2,4},{3,5},{4,2},{5,3},{6,0},{7,1},{8,14},{9,15},{10,... | collective-permute-start | bytes 393224 | tf_op jit(solution)/shard_map/ppermute | solution.py:277
  88.0 6.6 %collective-permute-start.24 = (bf16[128,256]{1,0:T(8,128)(2,1)S(1)}, bf16[128,256]{1,0:T(8,128)(2,1)S(1)}, u32[]{:S(2)}, u32[]{:S(2)}) collective-permute-start(bf16[128,256]{1,0:T(8,128)(2,1)S(1)} %project_mix.4), channel_id=1, source_target_pairs={{0,8},{1,9},{2,10},{3,11},{4,12},{5,13},{6,14},{7,15},{8,0},{9,1},... | collective-permute-start | bytes 196616 | tf_op jit(solution)/shard_map/ppermute | solution.py:277
  94.7 5.5 %collective-permute-start.25 = (bf16[2,128,256]{2,1,0:T(8,128)(2,1)S(1)}, bf16[2,128,256]{2,1,0:T(8,128)(2,1)S(1)}, u32[]{:S(2)}, u32[]{:S(2)}) collective-permute-start(bf16[2,128,256]{2,1,0:T(8,128)(2,1)S(1)} %pad_maximum_fusion.10), channel_id=1, source_target_pairs={{0,2},{1,3},{2,0},{3,1},{4,6},{5,7},{6,4},{7,5},{8,10},{9,11},{10,... | collective-permute-start | bytes 393224 | tf_op jit(solution)/shard_map/ppermute | solution.py:277
  103.8 7.4 %collective-permute-start.29 = (bf16[128,512]{1,0:T(8,128)(2,1)S(1)}, bf16[128,512]{1,0:T(8,128)(2,1)S(1)}, u32[]{:S(2)}, u32[]{:S(2)}) collective-permute-start(bf16[128,512]{1,0:T(8,128)(2,1)S(1)} %project_out.4), channel_id=1, source_target_pairs={{0,16},{1,17},{2,18},{3,19},{4,20},{5,21},{6,22},{7,23},{8,24},{9,... | collective-permute-start | bytes 393224 | tf_op jit(solution)/shard_map/ppermute | solution.py:301
  112.5 6.4 %collective-permute-start.31 = (bf16[128,512]{1,0:T(8,128)(2,1)S(1)}, bf16[128,512]{1,0:T(8,128)(2,1)S(1)}, u32[]{:S(2)}, u32[]{:S(2)}) collective-permute-start(bf16[128,512]{1,0:T(8,128)(2,1)S(1)} %bitcast_select_fusion.refs_3_), channel_id=1, source_target_pairs={{0,4},{1,5},{2,6},{3,7},{4,0},{5,1},{6,2},{7,3},{8,12},{9,13},{10,... | collective-permute-start | bytes 393224 | tf_op jit(solution)/shard_map/ppermute | solution.py:277
  114.1 7.9 %collective-permute-start.32 = (bf16[128,512]{1,0:T(8,128)(2,1)S(1)}, bf16[128,512]{1,0:T(8,128)(2,1)S(1)}, u32[]{:S(2)}, u32[]{:S(2)}) collective-permute-start(bf16[128,512]{1,0:T(8,128)(2,1)S(1)} %bitcast_select_fusion.refs_3_), channel_id=1, source_target_pairs={{0,8},{1,9},{2,10},{3,11},{4,12},{5,13},{6,14},{7,15},{8,0},{9,1},... | collective-permute-start | bytes 393224 | tf_op jit(solution)/shard_map/ppermute | solution.py:277
  122.0 8.1 %collective-permute-start.33 = (bf16[2,128,512]{2,1,0:T(8,128)(2,1)S(1)}, bf16[2,128,512]{2,1,0:T(8,128)(2,1)S(1)}, u32[]{:S(2)}, u32[]{:S(2)}) collective-permute-start(bf16[2,128,512]{2,1,0:T(8,128)(2,1)S(1)} %pad_maximum_fusion.8), channel_id=1, source_target_pairs={{0,2},{1,3},{2,0},{3,1},{4,6},{5,7},{6,4},{7,5},{8,10},{9,11},{10,... | collective-permute-start | bytes 786440 | tf_op jit(solution)/shard_map/ppermute | solution.py:277
  123.1 5.8 %collective-permute-start.34 = (bf16[1,128,512]{2,1,0:T(8,128)(2,1)S(1)}, bf16[1,128,512]{2,1,0:T(8,128)(2,1)S(1)}, u32[]{:S(2)}, u32[]{:S(2)}) collective-permute-start(bf16[1,128,512]{2,1,0:T(8,128)(2,1)S(1)} %bitcast.97), channel_id=1, source_target_pairs={{0,4},{1,5},{2,6},{3,7},{4,0},{5,1},{6,2},{7,3},{8,12},{9,13},{10,... | collective-permute-start | bytes 393224 | tf_op jit(solution)/shard_map/ppermute | solution.py:277
  123.4 6.7 %collective-permute-start.35 = (bf16[1,128,512]{2,1,0:T(8,128)(2,1)S(1)}, bf16[1,128,512]{2,1,0:T(8,128)(2,1)S(1)}, u32[]{:S(2)}, u32[]{:S(2)}) collective-permute-start(bf16[1,128,512]{2,1,0:T(8,128)(2,1)S(1)} %bitcast.98), channel_id=1, source_target_pairs={{0,6},{1,7},{2,4},{3,5},{4,2},{5,3},{6,0},{7,1},{8,14},{9,15},{10,... | collective-permute-start | bytes 393224 | tf_op jit(solution)/shard_map/ppermute | solution.py:277
  142.4 6.3 %collective-permute-start.39 = (bf16[128,256]{1,0:T(8,128)(2,1)S(1)}, bf16[128,256]{1,0:T(8,128)(2,1)S(1)}, u32[]{:S(2)}, u32[]{:S(2)}) collective-permute-start(bf16[128,256]{1,0:T(8,128)(2,1)S(1)} %project_mix.5), channel_id=1, source_target_pairs={{0,8},{1,9},{2,10},{3,11},{4,12},{5,13},{6,14},{7,15},{8,0},{9,1},... | collective-permute-start | bytes 196616 | tf_op jit(solution)/shard_map/ppermute | solution.py:277
  148.7 5.7 %collective-permute-start.40 = (bf16[2,128,256]{2,1,0:T(8,128)(2,1)S(1)}, bf16[2,128,256]{2,1,0:T(8,128)(2,1)S(1)}, u32[]{:S(2)}, u32[]{:S(2)}) collective-permute-start(bf16[2,128,256]{2,1,0:T(8,128)(2,1)S(1)} %pad_maximum_fusion.11), channel_id=1, source_target_pairs={{0,2},{1,3},{2,0},{3,1},{4,6},{5,7},{6,4},{7,5},{8,10},{9,11},{10,... | collective-permute-start | bytes 393224 | tf_op jit(solution)/shard_map/ppermute | solution.py:277
  (23 other events, 163.6 us)

commit v7 on v4

v7 whole, which is shorter than its diff:
```python
import functools

import jax
import jax.numpy as jnp
from jax import lax
from jax.experimental import pallas as pl
from jax.experimental.pallas import tpu as pltpu
from jax.sharding import PartitionSpec as P

EPS = 1e-06
VMEM_LIMIT = 20 * 1024 * 1024
PAD = 8


def plan(section_count, tick_count):
    wave_count = min(section_count, tick_count)
    waves = [[[] for _ in range(section_count)] for _ in range(wave_count)]
    where = {}
    for k in range(tick_count):
        for s in range(section_count):
            first = where[s - 1, k - 1][0] + 1 if s > 0 and k > 0 else 0
            last = wave_count - 1 - min(section_count - 1 - s, tick_count - 1 - k)
            best = min(range(first, last + 1), key=lambda w: (len(waves[w][s]), w))
            where[s, k] = (best, len(waves[best][s]))
            waves[best][s].append(k)
    return waves


def split_dp(dp_count):
    core = 2 if dp_count % 2 == 0 else 1
    chips = dp_count // core
    near = 1
    while near * near * 4 <= chips:
        near *= 2
    return chips // near, near, core


def pick(section_idx, options):
    distinct = []
    for s, value in enumerate(options):
        if value is None:
            continue
        for held, members in distinct:
            if held is value:
                members.append(s)
                break
        else:
            distinct.append((value, [s]))
    result = distinct[0][0]
    for value, members in distinct[1:]:
        mine = functools.reduce(jnp.logical_or, [section_idx == s for s in members])
        result = jnp.where(mine, value, result)
    return result


def routes(far, near, cross):
    if (far, near) == (4, 2):
        if cross:
            return [0, 4, 2], [(1, [4, 2, 0]), (2, [4]), (3, [4])]
        return [0, 4, 2, 1], [(1, [4, 2]), (2, [4]), (3, [4])]
    line = [d * near for d in range(far)]
    return line, [(d, line) for d in range(1, near)]


def columns_of(rank_ref, core, cell, c, size):
    chip, side = lax.div(rank_ref[0], core), lax.rem(rank_ref[0], core)
    return pl.ds(pl.multiple_of(((chip ^ cell) * core + (side ^ c)) * size, size), size)


def project(blocks, core, values_of, weights_of, rank_ref, gain_ref, acc_ref, sq_ref, ready=None):
    lanes = sq_ref.shape[1]
    side = lax.rem(rank_ref[0], core)
    for n, (cell, c) in enumerate(blocks):
        values = values_of(n).astype(jnp.float32)
        feat = values.shape[1]
        gains = gain_ref[:, columns_of(rank_ref, core, cell, c, feat)]
        normed = (values * gains).astype(jnp.bfloat16)
        squares = values * values
        part = squares[:, :lanes]
        for m in range(1, feat // lanes):
            part = part + squares[:, m * lanes : (m + 1) * lanes]
        sq_ref[...] += part
        if ready is not None:
            ready(n)
        inner = pl.ds(pl.multiple_of((side ^ c) * feat, feat), feat)
        for i in range(acc_ref.shape[0]):
            acc_ref[i] += lax.dot_general(
                normed, weights_of(n)[i, :, inner], (((1,), (1,)), ((), ())), preferred_element_type=jnp.float32
            )


def load_kernel(blocks, order, core, rank_ref, x_ref, w_far, gain_far, taps_far, decay_far, *refs):
    w_refs, (acc_ref, sq_ref, gain_ref, long_ref) = refs[: len(order)], refs[len(order) : len(order) + 4]
    sems, taps_ref, decay_ref, small_sems = refs[len(order) + 4 :]
    small = [(gain_far, gain_ref), (taps_far, taps_ref), (decay_far, decay_ref)]
    small = [pltpu.make_async_copy(src, dst, small_sems.at[n]) for n, (src, dst) in enumerate(small)]
    wide = w_refs[0].shape[2]
    chip = lax.div(rank_ref[0], core)
    copies = []
    for n, cell in enumerate(order):
        columns = pl.ds(pl.multiple_of((chip ^ cell) * wide, wide), wide)
        copies.append(
            [
                pltpu.make_async_copy(w_far.at[i, :, columns], w_refs[n].at[i], sems.at[n, i])
                for i in range(w_far.shape[0])
            ]
        )
    for group in [small] + copies:
        for copy in group:
            copy.start()
    for copy in small:
        copy.wait()
    lags = lax.broadcasted_iota(jnp.int32, long_ref.shape, 0).astype(jnp.float32)
    long_ref[...] = taps_ref[...].T * jnp.exp(-decay_ref[...] * lags)
    acc_ref[...] = jnp.zeros_like(acc_ref)
    sq_ref[...] = jnp.zeros_like(sq_ref)

    def ready(n):
        for copy in copies[n]:
            copy.wait()

    project(blocks, core, lambda n: x_ref[n], lambda n: w_refs[n], rank_ref, gain_ref, acc_ref, sq_ref, ready)
    for n in range(len(blocks), len(order)):
        ready(n)


def first_kernel(blocks, core, rank_ref, x_ref, gain_ref, *refs):
    w_refs, (acc_ref, sq_ref) = refs[:-2], refs[-2:]
    acc_ref[...] = jnp.zeros_like(acc_ref)
    sq_ref[...] = jnp.zeros_like(sq_ref)
    project(blocks, core, lambda n: x_ref[n], lambda n: w_refs[n], rank_ref, gain_ref, acc_ref, sq_ref)


def more_kernel(blocks, core, rank_ref, x_ref, gain_ref, acc_in, sq_in, *refs):
    w_refs, (acc_ref, sq_ref) = refs[:-2], refs[-2:]
    acc_ref[...] = acc_in[...]
    sq_ref[...] = sq_in[...]
    project(blocks, core, lambda n: x_ref[n], lambda n: w_refs[n], rank_ref, gain_ref, acc_ref, sq_ref)


def mix_kernel(blocks, core, model_width, rank_ref, *refs):
    sides, refs = refs[: core - 1], refs[core - 1 :]
    count = len(blocks) // max(core - 1, 1)
    gain_ref, acc_in, sq_in, short_ref, long_ref = refs[:5]
    w_refs = refs[5 : 5 + count]
    y_ref, acc_ref, sq_ref, pad_ref, query_ref = refs[5 + count :]
    branches, tok_len, chan = acc_in.shape
    acc_ref[...] = acc_in[...]
    sq_ref[...] = sq_in[...]
    project(
        blocks,
        core,
        lambda n: sides[n // count][n % count],
        lambda n: w_refs[n % count],
        rank_ref,
        gain_ref,
        acc_ref,
        sq_ref,
    )

    total = jnp.sum(sq_ref[...], axis=1, keepdims=True)
    factor = lax.rsqrt(total / model_width + EPS)
    taps = short_ref.shape[0] // branches
    pad_ref[0:PAD, :] = jnp.zeros((PAD, chan), jnp.float32)

    def branch(i):
        u = acc_ref[i] * factor
        pad_ref[PAD : PAD + tok_len, :] = u
        z = short_ref[i * taps : i * taps + 1, :] * u
        for j in range(1, taps):
            z = z + short_ref[i * taps + j : i * taps + j + 1, :] * pad_ref[PAD - j : PAD - j + tok_len, :]
        return z

    query_ref[...] = branch(1)
    product = query_ref[...] * branch(2)
    query_ref[...] = branch(0)
    pad_ref[PAD : PAD + tok_len, :] = product
    width = min(chan, 128)
    tiles = tok_len // 8
    for c in range(0, chan, width):
        cols = slice(c, c + width)
        conv = [None] * tiles
        for b in range(8):
            moved = [pad_ref[PAD - b + 8 * i : PAD - b + 8 * i + 8, cols] for i in range(tiles)]
            for a in range(long_ref.shape[0] // 8):
                tap = long_ref[8 * a + b : 8 * a + b + 1, cols]
                for i in range(a, tiles):
                    term = tap * moved[i - a]
                    conv[i] = term if conv[i] is None else conv[i] + term
        for i in range(0, tiles, 2):
            at = slice(8 * i, 8 * i + 16)
            both = jnp.concatenate(conv[i : i + 2], axis=0)
            y_ref[at, cols] = (query_ref[at, cols] * both).astype(jnp.bfloat16)


def out_kernel(blocks, core, rank_ref, *refs):
    sides = refs[:core]
    w_ref, own_ref, result_ref, acc_ref = refs[core:]
    count, _, chan = sides[0].shape
    acc_ref[...] = own_ref[...].astype(jnp.float32)
    for n, (cell, c) in enumerate(blocks):
        rows = columns_of(rank_ref, core, cell, c, chan)
        acc_ref[...] += jnp.dot(sides[n // count][n % count], w_ref[rows, :], preferred_element_type=jnp.float32)
    result_ref[...] = acc_ref[...].astype(jnp.bfloat16)


def in_vmem(count):
    return [pl.BlockSpec(memory_space=pltpu.VMEM)] * count


def call(kernel, operands, outs, scratch, flops, name, far_operands=()):
    specs = [pl.BlockSpec(memory_space=pltpu.SMEM)] + in_vmem(len(operands) - 1)
    operands = list(operands)
    for n in far_operands:
        specs[n] = pl.BlockSpec(memory_space=pltpu.HBM)
        operands[n] = pltpu.with_memory_space_constraint(operands[n], pltpu.HBM)
    return pl.pallas_call(
        kernel,
        in_specs=specs,
        out_specs=in_vmem(len(outs)),
        out_shape=outs,
        scratch_shapes=scratch,
        compiler_params=pltpu.CompilerParams(vmem_limit_bytes=VMEM_LIMIT),
        cost_estimate=pl.CostEstimate(flops=flops, bytes_accessed=flops // 1024, transcendentals=0),
        name=name,
    )(*operands)


def sums_of(x, branches, chan):
    _, rows, feat = x.shape
    return [
        jax.ShapeDtypeStruct((branches, rows, chan), jnp.float32),
        jax.ShapeDtypeStruct((rows, min(feat, 128)), jnp.float32),
    ]


def project_load(blocks, order, core, x, w_in, gain, taps, decay, rank):
    branches, chan, model_width = w_in.shape
    piece = jax.ShapeDtypeStruct((branches, chan, model_width // len(order)), w_in.dtype)
    outs = [piece] * len(order) + sums_of(x, branches, chan)
    outs += [jax.ShapeDtypeStruct(gain.shape, gain.dtype), jax.ShapeDtypeStruct(taps.shape[::-1], taps.dtype)]
    scratch = [
        pltpu.SemaphoreType.DMA((len(order), branches)),
        pltpu.VMEM(taps.shape, taps.dtype),
        pltpu.VMEM(decay.shape, decay.dtype),
        pltpu.SemaphoreType.DMA((3,)),
    ]
    kernel = functools.partial(load_kernel, blocks, order, core)
    flops = 2 * x.size * branches * chan
    *pieces, acc, sq, gain, long_rows = call(
        kernel, [rank, x, w_in, gain, taps, decay], outs, scratch, flops, "project_load", [2, 3, 4, 5]
    )
    return [acc, sq], {"in": dict(zip(order, pieces)), "gain": gain, "long": long_rows}


def project_part(blocks, core, x, params, sums, rank):
    w_refs = [params["in"][cell] for cell, _ in blocks]
    branches, chan, _ = w_refs[0].shape
    kernel, name = (more_kernel, "project_more") if sums else (first_kernel, "project_first")
    operands = [rank, x, params["gain"], *sums, *w_refs]
    flops = 2 * x.size * branches * chan
    return call(functools.partial(kernel, blocks, core), operands, sums_of(x, branches, chan), [], flops, name)


def mix(blocks, core, model_width, sides, params, sums, short_rows, rank):
    rows, chan = sums[0].shape[1:]
    scratch = [pltpu.VMEM(total.shape, total.dtype) for total in sums]
    scratch += [pltpu.VMEM((PAD + rows, chan), jnp.float32), pltpu.VMEM((rows, chan), jnp.float32)]
    w_refs = [params["in"][cell] for cell, _ in blocks[: len(blocks) // max(core - 1, 1)]]
    return call(
        functools.partial(mix_kernel, blocks, core, model_width),
        [rank, *sides, params["gain"], *sums, short_rows, params["long"], *w_refs],
        [jax.ShapeDtypeStruct((rows, chan), jnp.bfloat16)],
        scratch,
        2 * rows * model_width * 3 * chan,
        "project_mix",
    )[0]


def project_out(blocks, core, sides, w_out, own, rank):
    rows, feat = own.shape
    return call(
        functools.partial(out_kernel, blocks, core),
        [rank, *sides, w_out, own],
        [jax.ShapeDtypeStruct((rows, feat), jnp.bfloat16)],
        [pltpu.VMEM((rows, feat), jnp.float32)],
        2 * rows * w_out.shape[0] * feat,
        "project_out",
    )[0]


def body(section_count, dp_count, fresh_acts, carried, norm_gain, w_in, short_filter, filter_taps, decay_rate, w_out):
    tick_count, tok_len, _ = fresh_acts.shape
    far, near, core = split_dp(dp_count)
    group = near * core
    section_idx = lax.axis_index("section")
    rank = lax.axis_index("dp").astype(jnp.int32).reshape(1)

    def swap(value, offset):
        return lax.ppermute(value, "dp", [(r, r ^ offset) for r in range(dp_count)])


    def onward(value, offset):
        pairs = [
            (s * dp_count + r, (s + 1) % section_count * dp_count + (r ^ offset))
            for s in range(section_count)
            for r in range(dp_count)
        ]
        return lax.ppermute(value, ("section", "dp"), pairs)

    def after(value, *earlier):
        return lax.optimization_barrier((value, [x for x in earlier if x is not None]))[0]

    def round_one(source, cross=False):
        first, _ = routes(far, near, cross)
        if cross:
            return {d: onward(source, d * core) for d in first}
        return {d: swap(source, d * core) if d else source for d in first}

    def round_two(blocks, cross=False):
        _, second = routes(far, near, cross)
        leaving = lax.optimization_barrier([jnp.stack([blocks[b] for b in sent]) for _, sent in second])
        rest = [swap(payload, d * core) for payload, (d, _) in zip(leaving, second)]
        return [d ^ b for d, sent in second for b in sent], rest

    def of_cores(cells, cores):
        return [(cell, c) for c in cores for cell in cells]

    short_rows = short_filter[0].transpose(0, 2, 1).reshape(-1, short_filter.shape[2])
    waiting = carried[0]
    params, results, last = {}, {}, None

    def start(slot, before, behind):
        source = after(slot["source"], before["blocks"]) if before else slot["source"]
        slot["blocks"] = after(round_one(source, slot["cross"]), before.get("sums"), slot["last"])

    def spread(slot, before, behind):
        slot["cells"], slot["rest"] = round_two(after(slot["blocks"], before.get("rest")), slot["cross"])
        blocks = of_cores(slot["blocks"], [0])
        direct = after(jnp.stack(list(slot["blocks"].values())), before.get("y"))
        slot["direct"] = direct
        if params:
            slot["sums"] = project_part(blocks, core, direct, params, [], rank)
        else:
            order = [*slot["blocks"], *slot["cells"]]
            slot["sums"], loaded = project_load(
                blocks, order, core, direct, w_in[0], norm_gain, filter_taps[0], decay_rate, rank
            )
            params.update(loaded)

    def work(slot, before, behind):
        relayed = jnp.concatenate(after(slot["rest"], slot["sums"], behind.get("blocks"), before.get("y_blocks")))
        everything = jnp.concatenate([slot["direct"], relayed])
        sides = [swap(everything, c) for c in range(1, core)]
        sums = project_part(of_cores(slot["cells"], [0]), core, relayed, params, slot["sums"], rank)
        order = [*slot["blocks"], *slot["cells"]]
        sides = after(sides, sums)
        blocks = of_cores(order, range(1, core))
        slot["y"] = mix(blocks, core, norm_gain.shape[1], sides, params, sums, short_rows, rank)
        slot["y_blocks"] = after(round_one(slot["y"]), before.get("y_rest"))

    def spread_y(slot, before, behind):
        blocks = after(slot["y_blocks"], before.get("y_rest"), before.get("out"), behind.get("rest"))
        slot["y_cells"], slot["y_rest"] = round_two(blocks)

    def finish(slot, before, behind):
        direct = jnp.stack(list(slot["y_blocks"].values()))
        everything = jnp.concatenate([direct, *after(slot["y_rest"], behind.get("y"))])
        sides = [everything] + [swap(everything, c) for c in range(1, core)]
        blocks = of_cores([*slot["y_blocks"], *slot["y_cells"]], range(core))
        slot["out"] = project_out(blocks, core, sides, w_out[0], slot["blocks"][0], rank)

    phases = [start, spread, work, spread_y, finish]
    for w, ticks in enumerate(plan(section_count, tick_count)):
        slots = []
        for i in range(max(len(mine) for mine in ticks)):
            options = []
            for s in range(section_count):
                if w == 0:
                    mine = ticks[s]
                    options.append(None if i >= len(mine) else waiting if s > 0 else fresh_acts[mine[i]])
                else:
                    mine = ticks[(s + 1) % section_count]
                    if i >= len(mine):
                        options.append(None)
                    elif s + 1 == section_count:
                        options.append(fresh_acts[mine[i]])
                    else:
                        options.append(results[s, mine[i] - 1])
            slots.append({"source": pick(section_idx, options), "cross": w > 0, "last": None if i > 0 else last})
        for t in range(len(phases) + len(slots) - 1):
            for i, slot in enumerate(slots):
                if 0 <= t - i < len(phases):
                    before = slots[i - 1] if i > 0 else {}
                    behind = slots[i + 1] if i + 1 < len(slots) else {}
                    phases[t - i](slot, before, behind)
        last = slots[-1]["out"]
        for s in range(section_count):
            for i, k in enumerate(ticks[s]):
                results[s, k] = slots[i]["out"]
    outputs = [pick(section_idx, [results[s, k] for s in range(section_count)]) for k in range(tick_count)]
    return jnp.stack(outputs)[None]


def solution(mesh):
    run = functools.partial(body, mesh.shape["section"], mesh.shape["dp"])
    return jax.shard_map(
        run,
        mesh=mesh,
        in_specs=(
            P(None, None, "dp"),
            P("section", None, "dp"),
            P("section", None),
            P("section", None, "dp", None),
            P("section", None, "dp", None),
            P("section", "dp", None),
            P("section", "dp"),
            P("section", None, "dp"),
        ),
        out_specs=P("section", None, None, "dp"),
        check_vma=False,
    )
```

time: 159 us -> 175 us (1.10)
  waiting for transfers between devices: 42.2 us -> 50.9 us
  other arithmetic: 3.33 us -> 11 us
  starting transfers between devices: 67.4 us -> 62.9 us
  local copies, waits for them, and re-layouts: 10.4 us -> 12.7 us
    ppermute x2 -> x6, waiting for transfers between devices: 0.56 us -> 13.5 us  [onward(): return lax.ppermute(value, ('section', 'dp'), pairs)]
    ppermute x64 -> x50, starting transfers between devices: 62.3 us -> 53.6 us  [swap(): return lax.ppermute(value, 'dp', [(r, r ^ offset) for r in range(dp_count)])]
    ppermute x64 -> x50, waiting for transfers between devices: 41.7 us -> 37.4 us  [swap(): return lax.ppermute(value, 'dp', [(r, r ^ offset) for r in range(dp_count)])]
    concatenate x0 -> x8, other arithmetic: none -> 4.16 us  [the longest x4 2.79 us: work(): everything = jnp.concatenate([slot['direct'], relayed])]
    ppermute x2 -> x6, starting transfers between devices: 5.1 us -> 9.25 us  [onward(): return lax.ppermute(value, ('section', 'dp'), pairs)]
    another operation x16 -> x12, other arithmetic: 0.58 us -> 4.06 us  [the longest x8 2.9 us: round_two(): jnp.stack([blocks[b] for b in sent])]
    unnamed x27 -> x81, local copies, waits for them, and re-layouts: 10.3 us -> 12.6 us
    pallas_call x12 -> x16, Pallas kernels: 34.6 us -> 36.3 us  [call(): pl.pallas_call(kernel, in_specs=specs, out_specs=in_vmem(len(outs)), out_...]
  transfers between devices with their start and end apart: 66 -> 56, of which waited for: 26 -> 28; matrix products, arithmetic and copies ran while one was open for 1% -> 4% of each run, Pallas kernels for 21% -> 20%
where the time goes in v7:
time: 175 us; the launch traced here: 174 us
  starting transfers between devices  62.9 us (36%)
  waiting for transfers between devices  50.9 us (29%)
  Pallas kernels  36.3 us (21%)
  local copies, waits for them, and re-layouts  12.7 us (7%)
  other arithmetic  11 us (6%)
    ppermute x50, starting transfers between devices, swap(): return lax.ppermute(value, 'dp', [(r, r ^ offset) for r in range(dp_count)])  53.6 us
    ppermute x50, waiting for transfers between devices, swap(): return lax.ppermute(value, 'dp', [(r, r ^ offset) for r in range(dp_count)])  37.4 us
    pallas_call x16, Pallas kernels, call(): pl.pallas_call(kernel, in_specs=specs, out_specs=in_vmem(len(outs)), out_...  36.3 us
    ppermute x6, waiting for transfers between devices, onward(): return lax.ppermute(value, ('section', 'dp'), pairs)  13.5 us
    unnamed x81, local copies, waits for them, and re-layouts  12.6 us
    ppermute x6, starting transfers between devices, onward(): return lax.ppermute(value, ('section', 'dp'), pairs)  9.25 us
  transfers between devices with their start and end apart: 56, of which 28 were waited for; matrix products, arithmetic and copies ran while one was open for 4% of the time, Pallas kernels for 20%

profile of v7, /device:TPU:0, one launch (start us, length us, event | category | flops | bytes accessed | tf_op | source)
XLA Modules:
  0.0 174.4 jit_solution(4313821139502829640)
XLA Ops:
  1.0 4.1 %collective-permute-start.2 = (bf16[128,512]{1,0:T(8,128)(2,1)S(1)}, bf16[128,512]{1,0:T(8,128)(2,1)}, u32[]{:S(2)}, u32[]{:S(2)}) collective-permute-start(bf16[128,512]{1,0:T(8,128)(2,1)S(1)} %get-tuple-element.137.refs_3_), channel_id=1, source_target_pairs={{0,8},{1,9},{2,10},{3,11},{4,12},{5,13},{6,14},{7,15},{8,0},{9,1},... | collective-permute-start | bytes 393224 | tf_op jit(solution)/shard_map/ppermute | solution.py:300
  8.2 3.4 %collective-permute-done.2 = bf16[128,512]{1,0:T(8,128)(2,1)} collective-permute-done((bf16[128,512]{1,0:T(8,128)(2,1)S(1)}, bf16[128,512]{1,0:T(8,128)(2,1)}, u32[]{:S(2)}, u32[]{:S(2)}) %collective-permute-start.2) | collective-permute-done | bytes 131104 | tf_op jit(solution)/shard_map/ppermute | solution.py:300
  16.2 2.5 %collective-permute-start.7 = (bf16[128,512]{1,0:T(8,128)(2,1)S(1)}, bf16[128,512]{1,0:T(8,128)(2,1)S(1)}, u32[]{:S(2)}, u32[]{:S(2)}) collective-permute-start(bf16[128,512]{1,0:T(8,128)(2,1)S(1)} %get-tuple-element.149.refs_3_), channel_id=1, source_target_pairs={{0,4},{1,5},{2,6},{3,7},{4,0},{5,1},{6,2},{7,3},{8,12},{9,13},{10,... | collective-permute-start | bytes 393224 | tf_op jit(solution)/shard_map/ppermute | solution.py:300
  23.3 6.6 %project_load.1 = (bf16[3,256,1024]{2,1,0:T(8,128)(2,1)S(1)}, bf16[3,256,1024]{2,1,0:T(8,128)(2,1)S(1)}, bf16[3,256,1024]{2,1,0:T(8,128)(2,1)S(1)}, bf16[3,256,1...) custom-call(s32[1]{0:T(128)} %bitcast.rank_ref, ...), custom_call_target="tpu_custom_call" | custom-call | flops 402653184 | bytes 393216 | tf_op jit(solution)/shard_map/project_load/pallas_call | solution.py:217
  37.0 2.3 %pad_maximum_fusion = bf16[8,128,512]{2,1,0:T(8,128)(2,1)} fusion(bf16[1,128,512]{2,1,0:T(8,128)(2,1)S(1)} %collective-permute-done.5, bf16[1,128,512]{2,1,0:T(8,128)(2,1)S(1)} %collective-permute-done.4, bf16[2,128,512]{2,1,0:T(8,128)(2,1)} %collective-permute-done.3, bf16[4,128,512]{2,1,0:T(8,128)(2,1)S(1)} %pad_maximum_fusion.6.x_ref), kind=kLoop, calls=%fused_computation | loop fusion | flops 1572864 | bytes 2097152 | tf_op jit(solution)/shard_map/concatenate | solution.py:353
  48.9 5.5 %project_mix.4 = bf16[128,256]{1,0:T(8,128)(2,1)S(1)} custom-call(s32[1]{0:T(128)} %bitcast.rank_ref, bf16[8,128,512]{2,1,0:T(8,128)(2,1)} %collective-permute-done.9.refs_0_, f32[1,8192]{1,0:T(1,128)S(1)} %get-tuple-element.156.gain_ref.refs_1_, f32[3,128,256]{2,1,0:T(8,128)S(1)} %get-tuple-element.161.refs_2_, f32[128,128]{1,0:T(8,128)S(1)} %get-tuple-element.162.refs_3_, ...), custom_call_target="tpu_custom_call" | custom-call | flops 1610612736 | bytes 1572864 | tf_op jit(solution)/shard_map/project_mix/pallas_call | solution.py:217
  56.5 2.9 %collective-permute-start.15 = (bf16[1,128,512]{2,1,0:T(8,128)(2,1)S(1)}, bf16[1,128,512]{2,1,0:T(8,128)(2,1)S(1)}, u32[]{:S(2)}, u32[]{:S(2)}) collective-permute-start(bf16[1,128,512]{2,1,0:T(8,128)(2,1)S(1)} %bitcast.112), channel_id=1, source_target_pairs={{0,6},{1,7},{2,4},{3,5},{4,2},{5,3},{6,0},{7,1},{8,14},{9,15},{10,... | collective-permute-start | bytes 393224 | tf_op jit(solution)/shard_map/ppermute | solution.py:300
  63.8 3.1 %collective-permute-done.11 = bf16[128,256]{1,0:T(8,128)(2,1)S(1)} collective-permute-done((bf16[128,256]{1,0:T(8,128)(2,1)S(1)}, bf16[128,256]{1,0:T(8,128)(2,1)S(1)}, u32[]{:S(2)}, u32[]{:S(2)}) %collective-permute-start.11) | collective-permute-done | bytes 65568 | tf_op jit(solution)/shard_map/ppermute | solution.py:300
  73.6 4.4 %project_mix.5 = bf16[128,256]{1,0:T(8,128)(2,1)S(1)} custom-call(s32[1]{0:T(128)} %bitcast.rank_ref, bf16[8,128,512]{2,1,0:T(8,128)(2,1)S(1)} %collective-permute-done.19.refs_0_, f32[1,8192]{1,0:T(1,128)S(1)} %get-tuple-element.156.gain_ref.refs_1_, f32[3,128,256]{2,1,0:T(8,128)S(1)} %get-tuple-element.189.refs_2_, ...), custom_call_target="tpu_custom_call" | custom-call | flops 1610612736 | bytes 1572864 | tf_op jit(solution)/shard_map/project_mix/pallas_call | solution.py:217
  80.5 4.0 %collective-permute-done.26 = bf16[128,256]{1,0:T(8,128)(2,1)S(1)} collective-permute-done((bf16[128,256]{1,0:T(8,128)(2,1)S(1)}, bf16[128,256]{1,0:T(8,128)(2,1)S(1)}, u32[]{:S(2)}, u32[]{:S(2)}) %collective-permute-start.26) | collective-permute-done | bytes 65568 | tf_op jit(solution)/shard_map/ppermute | solution.py:300
  85.9 2.2 %collective-permute-start.29 = (bf16[1,128,256]{2,1,0:T(8,128)(2,1)S(1)}, bf16[1,128,256]{2,1,0:T(8,128)(2,1)S(1)}, u32[]{:S(2)}, u32[]{:S(2)}) collective-permute-start(bf16[1,128,256]{2,1,0:T(8,128)(2,1)S(1)} %bitcast.126), channel_id=1, source_target_pairs={{0,6},{1,7},{2,4},{3,5},{4,2},{5,3},{6,0},{7,1},{8,14},{9,15},{10,... | collective-permute-start | bytes 196616 | tf_op jit(solution)/shard_map/ppermute | solution.py:300
  91.4 2.1 %collective-permute-done.27 = bf16[2,128,256]{2,1,0:T(8,128)(2,1)S(1)} collective-permute-done((bf16[2,128,256]{2,1,0:T(8,128)(2,1)S(1)}, bf16[2,128,256]{2,1,0:T(8,128)(2,1)S(1)}, u32[]{:S(2)}, u32[]{:S(2)}) %collective-permute-start.27) | collective-permute-done | bytes 131104 | tf_op jit(solution)/shard_map/ppermute | solution.py:300
  94.6 2.3 %collective-permute-start.23 = (bf16[128,512]{1,0:T(8,128)(2,1)S(1)}, bf16[128,512]{1,0:T(8,128)(2,1)S(1)}, u32[]{:S(2)}, u32[]{:S(2)}) collective-permute-start(bf16[128,512]{1,0:T(8,128)(2,1)S(1)} %bitcast_select_fusion), channel_id=1, source_target_pairs={{0,24},{1,25},{2,26},{3,27},{4,28},{5,29},{6,30},{7,31},{8,16},{9,... | collective-permute-start | bytes 393224 | tf_op jit(solution)/shard_map/ppermute | solution.py:309
  100.2 5.1 %collective-permute-done.23 = bf16[128,512]{1,0:T(8,128)(2,1)S(1)} collective-permute-done((bf16[128,512]{1,0:T(8,128)(2,1)S(1)}, bf16[128,512]{1,0:T(8,128)(2,1)S(1)}, u32[]{:S(2)}, u32[]{:S(2)}) %collective-permute-start.23) | collective-permute-done | bytes 131104 | tf_op jit(solution)/shard_map/ppermute | solution.py:309
  105.8 2.5 %collective-permute-done.21.refs_3_ = bf16[128,512]{1,0:T(8,128)(2,1)S(1)} collective-permute-done((bf16[128,512]{1,0:T(8,128)(2,1)S(1)}, bf16[128,512]{1,0:T(8,128)(2,1)S(1)}, u32[]{:S(2)}, u32[]{:S(2)}) %collective-permute-start.21) | collective-permute-done | bytes 131104 | tf_op jit(solution)/shard_map/ppermute | solution.py:309
  109.5 2.2 %collective-permute-start.36 = (bf16[128,512]{1,0:T(8,128)(2,1)S(1)}, bf16[128,512]{1,0:T(8,128)(2,1)S(1)}, u32[]{:S(2)}, u32[]{:S(2)}) collective-permute-start(bf16[128,512]{1,0:T(8,128)(2,1)S(1)} %project_out.5), channel_id=1, source_target_pairs={{0,24},{1,25},{2,26},{3,27},{4,28},{5,29},{6,30},{7,31},{8,16},{9,... | collective-permute-start | bytes 393224 | tf_op jit(solution)/shard_map/ppermute | solution.py:309
  115.2 3.7 %collective-permute-done.36 = bf16[128,512]{1,0:T(8,128)(2,1)S(1)} collective-permute-done((bf16[128,512]{1,0:T(8,128)(2,1)S(1)}, bf16[128,512]{1,0:T(8,128)(2,1)S(1)}, u32[]{:S(2)}, u32[]{:S(2)}) %collective-permute-start.36) | collective-permute-done | bytes 131104 | tf_op jit(solution)/shard_map/ppermute | solution.py:309
  122.2 2.7 %collective-permute-done.33 = bf16[1,128,512]{2,1,0:T(8,128)(2,1)S(1)} collective-permute-done((bf16[1,128,512]{2,1,0:T(8,128)(2,1)S(1)}, bf16[1,128,512]{2,1,0:T(8,128)(2,1)S(1)}, u32[]{:S(2)}, u32[]{:S(2)}) %collective-permute-start.33) | collective-permute-done | bytes 131104 | tf_op jit(solution)/shard_map/ppermute | solution.py:300
  127.9 4.2 %project_mix.6 = bf16[128,256]{1,0:T(8,128)(2,1)S(1)} custom-call(s32[1]{0:T(128)} %bitcast.rank_ref, bf16[8,128,512]{2,1,0:T(8,128)(2,1)S(1)} %collective-permute-done.37.refs_0_, f32[1,8192]{1,0:T(1,128)S(1)} %get-tuple-element.156.gain_ref.refs_1_, f32[3,128,256]{2,1,0:T(8,128)S(1)} %get-tuple-element.225.refs_2_, ...), custom_call_target="tpu_custom_call" | custom-call | flops 1610612736 | bytes 1572864 | tf_op jit(solution)/shard_map/project_mix/pallas_call | solution.py:217
  140.7 3.6 %collective-permute-done.39 = bf16[128,256]{1,0:T(8,128)(2,1)S(1)} collective-permute-done((bf16[128,256]{1,0:T(8,128)(2,1)S(1)}, bf16[128,256]{1,0:T(8,128)(2,1)S(1)}, u32[]{:S(2)}, u32[]{:S(2)}) %collective-permute-start.39) | collective-permute-done | bytes 65568 | tf_op jit(solution)/shard_map/ppermute | solution.py:300
  144.8 2.5 %collective-permute-start.46 = (bf16[1,128,256]{2,1,0:T(8,128)(2,1)S(1)}, bf16[1,128,256]{2,1,0:T(8,128)(2,1)S(1)}, u32[]{:S(2)}, u32[]{:S(2)}) collective-permute-start(bf16[1,128,256]{2,1,0:T(8,128)(2,1)S(1)} %bitcast.120), channel_id=1, source_target_pairs={{0,6},{1,7},{2,4},{3,5},{4,2},{5,3},{6,0},{7,1},{8,14},{9,15},{10,... | collective-permute-start | bytes 196616 | tf_op jit(solution)/shard_map/ppermute | solution.py:300
  151.1 4.4 %project_mix.7 = bf16[128,256]{1,0:T(8,128)(2,1)S(1)} custom-call(s32[1]{0:T(128)} %bitcast.rank_ref, bf16[8,128,512]{2,1,0:T(8,128)(2,1)S(1)} %collective-permute-done.47.refs_0_, f32[1,8192]{1,0:T(1,128)S(1)} %get-tuple-element.156.gain_ref.refs_1_, f32[3,128,256]{2,1,0:T(8,128)S(1)} %get-tuple-element.249.refs_2_, ...), custom_call_target="tpu_custom_call" | custom-call | flops 1610612736 | bytes 1572864 | tf_op jit(solution)/shard_map/project_mix/pallas_call | solution.py:217
  159.4 2.2 %collective-permute-done.51 = bf16[128,256]{1,0:T(8,128)(2,1)S(1)} collective-permute-done((bf16[128,256]{1,0:T(8,128)(2,1)S(1)}, bf16[128,256]{1,0:T(8,128)(2,1)S(1)}, u32[]{:S(2)}, u32[]{:S(2)}) %collective-permute-start.51) | collective-permute-done | bytes 65568 | tf_op jit(solution)/shard_map/ppermute | solution.py:300
  163.3 2.5 %collective-permute-start.54 = (bf16[1,128,256]{2,1,0:T(8,128)(2,1)S(1)}, bf16[1,128,256]{2,1,0:T(8,128)(2,1)S(1)}, u32[]{:S(2)}, u32[]{:S(2)}) collective-permute-start(bf16[1,128,256]{2,1,0:T(8,128)(2,1)S(1)} %bitcast.129), channel_id=1, source_target_pairs={{0,6},{1,7},{2,4},{3,5},{4,2},{5,3},{6,0},{7,1},{8,14},{9,15},{10,... | collective-permute-start | bytes 196616 | tf_op jit(solution)/shard_map/ppermute | solution.py:300
  (214 shorter events, 92.3 us)
Async XLA Ops:
  1.0 10.6 %collective-permute-start.2 = (bf16[128,512]{1,0:T(8,128)(2,1)S(1)}, bf16[128,512]{1,0:T(8,128)(2,1)}, u32[]{:S(2)}, u32[]{:S(2)}) collective-permute-start(bf16[128,512]{1,0:T(8,128)(2,1)S(1)} %get-tuple-element.137.refs_3_), channel_id=1, source_target_pairs={{0,8},{1,9},{2,10},{3,11},{4,12},{5,13},{6,14},{7,15},{8,0},{9,1},... | collective-permute-start | bytes 393224 | tf_op jit(solution)/shard_map/ppermute | solution.py:300
  14.7 22.2 %collective-permute-start.3 = (bf16[2,128,512]{2,1,0:T(8,128)(2,1)}, bf16[2,128,512]{2,1,0:T(8,128)(2,1)}, u32[]{:S(2)}, u32[]{:S(2)}) collective-permute-start(bf16[2,128,512]{2,1,0:T(8,128)(2,1)} %pad_maximum_fusion.14), channel_id=1, source_target_pairs={{0,2},{1,3},{2,0},{3,1},{4,6},{5,7},{6,4},{7,5},{8,10},{9,11},{10,... | collective-permute-start | bytes 786440 | tf_op jit(solution)/shard_map/ppermute | solution.py:300
  16.2 20.7 %collective-permute-start.7 = (bf16[128,512]{1,0:T(8,128)(2,1)S(1)}, bf16[128,512]{1,0:T(8,128)(2,1)S(1)}, u32[]{:S(2)}, u32[]{:S(2)}) collective-permute-start(bf16[128,512]{1,0:T(8,128)(2,1)S(1)} %get-tuple-element.149.refs_3_), channel_id=1, source_target_pairs={{0,4},{1,5},{2,6},{3,7},{4,0},{5,1},{6,2},{7,3},{8,12},{9,13},{10,... | collective-permute-start | bytes 393224 | tf_op jit(solution)/shard_map/ppermute | solution.py:300
  18.8 18.1 %collective-permute-start.6 = (bf16[128,512]{1,0:T(8,128)(2,1)S(1)}, bf16[128,512]{1,0:T(8,128)(2,1)S(1)}, u32[]{:S(2)}, u32[]{:S(2)}) collective-permute-start(bf16[128,512]{1,0:T(8,128)(2,1)S(1)} %get-tuple-element.149.refs_3_), channel_id=1, source_target_pairs={{0,2},{1,3},{2,0},{3,1},{4,6},{5,7},{6,4},{7,5},{8,10},{9,11},{10,... | collective-permute-start | bytes 393224 | tf_op jit(solution)/shard_map/ppermute | solution.py:300
  19.3 17.6 %collective-permute-start.4 = (bf16[1,128,512]{2,1,0:T(8,128)(2,1)}, bf16[1,128,512]{2,1,0:T(8,128)(2,1)S(1)}, u32[]{:S(2)}, u32[]{:S(2)}) collective-permute-start(bf16[1,128,512]{2,1,0:T(8,128)(2,1)} %bitcast.6), channel_id=1, source_target_pairs={{0,4},{1,5},{2,6},{3,7},{4,0},{5,1},{6,2},{7,3},{8,12},{9,13},{10,... | collective-permute-start | bytes 393224 | tf_op jit(solution)/shard_map/ppermute | solution.py:300
  20.3 16.7 %collective-permute-start.5 = (bf16[1,128,512]{2,1,0:T(8,128)(2,1)}, bf16[1,128,512]{2,1,0:T(8,128)(2,1)S(1)}, u32[]{:S(2)}, u32[]{:S(2)}) collective-permute-start(bf16[1,128,512]{2,1,0:T(8,128)(2,1)} %bitcast.6), channel_id=1, source_target_pairs={{0,6},{1,7},{2,4},{3,5},{4,2},{5,3},{6,0},{7,1},{8,14},{9,15},{10,... | collective-permute-start | bytes 393224 | tf_op jit(solution)/shard_map/ppermute | solution.py:300
  40.5 26.7 %collective-permute-start.13 = (bf16[2,128,512]{2,1,0:T(8,128)(2,1)S(1)}, bf16[2,128,512]{2,1,0:T(8,128)(2,1)S(1)}, u32[]{:S(2)}, u32[]{:S(2)}) collective-permute-start(bf16[2,128,512]{2,1,0:T(8,128)(2,1)S(1)} %pad_maximum_fusion.15), channel_id=1, source_target_pairs={{0,2},{1,3},{2,0},{3,1},{4,6},{5,7},{6,4},{7,5},{8,10},{9,11},{10,... | collective-permute-start | bytes 786440 | tf_op jit(solution)/shard_map/ppermute | solution.py:300
  56.5 10.7 %collective-permute-start.14 = (bf16[1,128,512]{2,1,0:T(8,128)(2,1)S(1)}, bf16[1,128,512]{2,1,0:T(8,128)(2,1)S(1)}, u32[]{:S(2)}, u32[]{:S(2)}) collective-permute-start(bf16[1,128,512]{2,1,0:T(8,128)(2,1)S(1)} %bitcast.111), channel_id=1, source_target_pairs={{0,4},{1,5},{2,6},{3,7},{4,0},{5,1},{6,2},{7,3},{8,12},{9,13},{10,... | collective-permute-start | bytes 393224 | tf_op jit(solution)/shard_map/ppermute | solution.py:300
  56.5 10.7 %collective-permute-start.15 = (bf16[1,128,512]{2,1,0:T(8,128)(2,1)S(1)}, bf16[1,128,512]{2,1,0:T(8,128)(2,1)S(1)}, u32[]{:S(2)}, u32[]{:S(2)}) collective-permute-start(bf16[1,128,512]{2,1,0:T(8,128)(2,1)S(1)} %bitcast.112), channel_id=1, source_target_pairs={{0,6},{1,7},{2,4},{3,5},{4,2},{5,3},{6,0},{7,1},{8,14},{9,15},{10,... | collective-permute-start | bytes 393224 | tf_op jit(solution)/shard_map/ppermute | solution.py:300
  67.2 12.4 %collective-permute-start.17 = (bf16[1,128,256]{2,1,0:T(8,128)(2,1)S(1)}, bf16[1,128,256]{2,1,0:T(8,128)(2,1)S(1)}, u32[]{:S(2)}, u32[]{:S(2)}) collective-permute-start(bf16[1,128,256]{2,1,0:T(8,128)(2,1)S(1)} %bitcast.122), channel_id=1, source_target_pairs={{0,4},{1,5},{2,6},{3,7},{4,0},{5,1},{6,2},{7,3},{8,12},{9,13},{10,... | collective-permute-start | bytes 196616 | tf_op jit(solution)/shard_map/ppermute | solution.py:300
  68.1 12.3 %collective-permute-start.18 = (bf16[1,128,256]{2,1,0:T(8,128)(2,1)S(1)}, bf16[1,128,256]{2,1,0:T(8,128)(2,1)S(1)}, u32[]{:S(2)}, u32[]{:S(2)}) collective-permute-start(bf16[1,128,256]{2,1,0:T(8,128)(2,1)S(1)} %bitcast.123), channel_id=1, source_target_pairs={{0,6},{1,7},{2,4},{3,5},{4,2},{5,3},{6,0},{7,1},{8,14},{9,15},{10,... | collective-permute-start | bytes 196616 | tf_op jit(solution)/shard_map/ppermute | solution.py:300
  70.0 10.3 %collective-permute-start.16 = (bf16[2,128,256]{2,1,0:T(8,128)(2,1)S(1)}, bf16[2,128,256]{2,1,0:T(8,128)(2,1)S(1)}, u32[]{:S(2)}, u32[]{:S(2)}) collective-permute-start(bf16[2,128,256]{2,1,0:T(8,128)(2,1)S(1)} %pad_maximum_fusion.16), channel_id=1, source_target_pairs={{0,2},{1,3},{2,0},{3,1},{4,6},{5,7},{6,4},{7,5},{8,10},{9,11},{10,... | collective-permute-start | bytes 393224 | tf_op jit(solution)/shard_map/ppermute | solution.py:300
  94.6 10.7 %collective-permute-start.23 = (bf16[128,512]{1,0:T(8,128)(2,1)S(1)}, bf16[128,512]{1,0:T(8,128)(2,1)S(1)}, u32[]{:S(2)}, u32[]{:S(2)}) collective-permute-start(bf16[128,512]{1,0:T(8,128)(2,1)S(1)} %bitcast_select_fusion), channel_id=1, source_target_pairs={{0,24},{1,25},{2,26},{3,27},{4,28},{5,29},{6,30},{7,31},{8,16},{9,... | collective-permute-start | bytes 393224 | tf_op jit(solution)/shard_map/ppermute | solution.py:309
  97.9 10.4 %collective-permute-start.21 = (bf16[128,512]{1,0:T(8,128)(2,1)S(1)}, bf16[128,512]{1,0:T(8,128)(2,1)S(1)}, u32[]{:S(2)}, u32[]{:S(2)}) collective-permute-start(bf16[128,512]{1,0:T(8,128)(2,1)S(1)} %bitcast_select_fusion), channel_id=1, source_target_pairs={{0,16},{1,17},{2,18},{3,19},{4,20},{5,21},{6,22},{7,23},{8,24},{9,... | collective-permute-start | bytes 393224 | tf_op jit(solution)/shard_map/ppermute | solution.py:309
  108.4 16.6 %collective-permute-start.31 = (bf16[3,128,512]{2,1,0:T(8,128)(2,1)S(1)}, bf16[3,128,512]{2,1,0:T(8,128)(2,1)S(1)}, u32[]{:S(2)}, u32[]{:S(2)}) collective-permute-start(bf16[3,128,512]{2,1,0:T(8,128)(2,1)S(1)} %pad_maximum_fusion.11), channel_id=1, source_target_pairs={{0,2},{1,3},{2,0},{3,1},{4,6},{5,7},{6,4},{7,5},{8,10},{9,11},{10,... | collective-permute-start | bytes 1179656 | tf_op jit(solution)/shard_map/ppermute | solution.py:300
  109.5 9.3 %collective-permute-start.36 = (bf16[128,512]{1,0:T(8,128)(2,1)S(1)}, bf16[128,512]{1,0:T(8,128)(2,1)S(1)}, u32[]{:S(2)}, u32[]{:S(2)}) collective-permute-start(bf16[128,512]{1,0:T(8,128)(2,1)S(1)} %project_out.5), channel_id=1, source_target_pairs={{0,24},{1,25},{2,26},{3,27},{4,28},{5,29},{6,30},{7,31},{8,16},{9,... | collective-permute-start | bytes 393224 | tf_op jit(solution)/shard_map/ppermute | solution.py:309
  111.7 9.3 %collective-permute-start.35 = (bf16[128,512]{1,0:T(8,128)(2,1)S(1)}, bf16[128,512]{1,0:T(8,128)(2,1)S(1)}, u32[]{:S(2)}, u32[]{:S(2)}) collective-permute-start(bf16[128,512]{1,0:T(8,128)(2,1)S(1)} %project_out.5), channel_id=1, source_target_pairs={{0,20},{1,21},{2,22},{3,23},{4,16},{5,17},{6,18},{7,19},{8,28},{9,... | collective-permute-start | bytes 393224 | tf_op jit(solution)/shard_map/ppermute | solution.py:309
  112.6 9.6 %collective-permute-start.34 = (bf16[128,512]{1,0:T(8,128)(2,1)S(1)}, bf16[128,512]{1,0:T(8,128)(2,1)S(1)}, u32[]{:S(2)}, u32[]{:S(2)}) collective-permute-start(bf16[128,512]{1,0:T(8,128)(2,1)S(1)} %project_out.5), channel_id=1, source_target_pairs={{0,16},{1,17},{2,18},{3,19},{4,20},{5,21},{6,22},{7,23},{8,24},{9,... | collective-permute-start | bytes 393224 | tf_op jit(solution)/shard_map/ppermute | solution.py:309
  125.3 19.4 %collective-permute-start.41 = (bf16[3,128,512]{2,1,0:T(8,128)(2,1)S(1)}, bf16[3,128,512]{2,1,0:T(8,128)(2,1)S(1)}, u32[]{:S(2)}, u32[]{:S(2)}) collective-permute-start(bf16[3,128,512]{2,1,0:T(8,128)(2,1)S(1)} %pad_maximum_fusion.12), channel_id=1, source_target_pairs={{0,2},{1,3},{2,0},{3,1},{4,6},{5,7},{6,4},{7,5},{8,10},{9,11},{10,... | collective-permute-start | bytes 1179656 | tf_op jit(solution)/shard_map/ppermute | solution.py:300
  133.3 11.3 %collective-permute-start.42 = (bf16[1,128,512]{2,1,0:T(8,128)(2,1)S(1)}, bf16[1,128,512]{2,1,0:T(8,128)(2,1)S(1)}, u32[]{:S(2)}, u32[]{:S(2)}) collective-permute-start(bf16[1,128,512]{2,1,0:T(8,128)(2,1)S(1)} %bitcast.99), channel_id=1, source_target_pairs={{0,4},{1,5},{2,6},{3,7},{4,0},{5,1},{6,2},{7,3},{8,12},{9,13},{10,... | collective-permute-start | bytes 393224 | tf_op jit(solution)/shard_map/ppermute | solution.py:300
  135.2 9.5 %collective-permute-start.43 = (bf16[1,128,512]{2,1,0:T(8,128)(2,1)S(1)}, bf16[1,128,512]{2,1,0:T(8,128)(2,1)S(1)}, u32[]{:S(2)}, u32[]{:S(2)}) collective-permute-start(bf16[1,128,512]{2,1,0:T(8,128)(2,1)S(1)} %bitcast.100), channel_id=1, source_target_pairs={{0,6},{1,7},{2,4},{3,5},{4,2},{5,3},{6,0},{7,1},{8,14},{9,15},{10,... | collective-permute-start | bytes 393224 | tf_op jit(solution)/shard_map/ppermute | solution.py:300
  144.7 13.4 %collective-permute-start.45 = (bf16[1,128,256]{2,1,0:T(8,128)(2,1)S(1)}, bf16[1,128,256]{2,1,0:T(8,128)(2,1)S(1)}, u32[]{:S(2)}, u32[]{:S(2)}) collective-permute-start(bf16[1,128,256]{2,1,0:T(8,128)(2,1)S(1)} %bitcast.119), channel_id=1, source_target_pairs={{0,4},{1,5},{2,6},{3,7},{4,0},{5,1},{6,2},{7,3},{8,12},{9,13},{10,... | collective-permute-start | bytes 196616 | tf_op jit(solution)/shard_map/ppermute | solution.py:300
  144.8 14.5 %collective-permute-start.46 = (bf16[1,128,256]{2,1,0:T(8,128)(2,1)S(1)}, bf16[1,128,256]{2,1,0:T(8,128)(2,1)S(1)}, u32[]{:S(2)}, u32[]{:S(2)}) collective-permute-start(bf16[1,128,256]{2,1,0:T(8,128)(2,1)S(1)} %bitcast.120), channel_id=1, source_target_pairs={{0,6},{1,7},{2,4},{3,5},{4,2},{5,3},{6,0},{7,1},{8,14},{9,15},{10,... | collective-permute-start | bytes 196616 | tf_op jit(solution)/shard_map/ppermute | solution.py:300
  147.3 12.0 %collective-permute-start.44 = (bf16[2,128,256]{2,1,0:T(8,128)(2,1)S(1)}, bf16[2,128,256]{2,1,0:T(8,128)(2,1)S(1)}, u32[]{:S(2)}, u32[]{:S(2)}) collective-permute-start(bf16[2,128,256]{2,1,0:T(8,128)(2,1)S(1)} %pad_maximum_fusion.18), channel_id=1, source_target_pairs={{0,2},{1,3},{2,0},{3,1},{4,6},{5,7},{6,4},{7,5},{8,10},{9,11},{10,... | collective-permute-start | bytes 393224 | tf_op jit(solution)/shard_map/ppermute | solution.py:300
  (60 other events, 316.2 us)

commit v8 on v7

--- a/solution.py
+++ b/solution.py
@@ -166,9 +166,9 @@
     def branch(i):
         u = acc_ref[i] * factor
         pad_ref[PAD : PAD + tok_len, :] = u
-        z = short_ref[i * taps : i * taps + 1, :] * u
+        z = short_ref[i * taps] * u
         for j in range(1, taps):
-            z = z + short_ref[i * taps + j : i * taps + j + 1, :] * pad_ref[PAD - j : PAD - j + tok_len, :]
+            z = z + short_ref[i * taps + j] * pad_ref[PAD - j : PAD - j + tok_len, :]
         return z
 
     query_ref[...] = branch(1)
@@ -326,7 +326,7 @@
     def of_cores(cells, cores):
         return [(cell, c) for c in cores for cell in cells]
 
-    short_rows = short_filter[0].transpose(0, 2, 1).reshape(-1, short_filter.shape[2])
+    short_rows = short_filter[0].transpose(0, 2, 1).reshape(-1, 1, short_filter.shape[2])
     waiting = carried[0]
     params, results, last = {}, {}, None
 

time: 175 us -> 175 us (level)
  no operation moved by 1% of the time
where the time goes in v8:
time: 175 us; the launch traced here: 174 us
  starting transfers between devices  62.9 us (36%)
  waiting for transfers between devices  50.9 us (29%)
  Pallas kernels  36.2 us (21%)
  local copies, waits for them, and re-layouts  12.7 us (7%)
  other arithmetic  11 us (6%)
    ppermute x50, starting transfers between devices, swap(): return lax.ppermute(value, 'dp', [(r, r ^ offset) for r in range(dp_count)])  53.6 us
    ppermute x50, waiting for transfers between devices, swap(): return lax.ppermute(value, 'dp', [(r, r ^ offset) for r in range(dp_count)])  37.4 us
    pallas_call x16, Pallas kernels, call(): pl.pallas_call(kernel, in_specs=specs, out_specs=in_vmem(len(outs)), out_...  36.2 us
    ppermute x6, waiting for transfers between devices, onward(): return lax.ppermute(value, ('section', 'dp'), pairs)  13.5 us
    unnamed x81, local copies, waits for them, and re-layouts  12.6 us
    ppermute x6, starting transfers between devices, onward(): return lax.ppermute(value, ('section', 'dp'), pairs)  9.25 us
  transfers between devices with their start and end apart: 56, of which 28 were waited for; matrix products, arithmetic and copies ran while one was open for 4% of the time, Pallas kernels for 20%

profile of v8, /device:TPU:0, one launch (start us, length us, event | category | flops | bytes accessed | tf_op | source)
XLA Modules:
  0.0 174.4 jit_solution(7978498464058884085)
XLA Ops:
  1.0 4.1 %collective-permute-start.2 = (bf16[128,512]{1,0:T(8,128)(2,1)S(1)}, bf16[128,512]{1,0:T(8,128)(2,1)}, u32[]{:S(2)}, u32[]{:S(2)}) collective-permute-start(bf16[128,512]{1,0:T(8,128)(2,1)S(1)} %get-tuple-element.137.refs_3_), channel_id=1, source_target_pairs={{0,8},{1,9},{2,10},{3,11},{4,12},{5,13},{6,14},{7,15},{8,0},{9,1},... | collective-permute-start | bytes 393224 | tf_op jit(solution)/shard_map/ppermute | solution.py:300
  8.2 3.4 %collective-permute-done.2 = bf16[128,512]{1,0:T(8,128)(2,1)} collective-permute-done((bf16[128,512]{1,0:T(8,128)(2,1)S(1)}, bf16[128,512]{1,0:T(8,128)(2,1)}, u32[]{:S(2)}, u32[]{:S(2)}) %collective-permute-start.2) | collective-permute-done | bytes 131104 | tf_op jit(solution)/shard_map/ppermute | solution.py:300
  16.2 2.5 %collective-permute-start.7 = (bf16[128,512]{1,0:T(8,128)(2,1)S(1)}, bf16[128,512]{1,0:T(8,128)(2,1)S(1)}, u32[]{:S(2)}, u32[]{:S(2)}) collective-permute-start(bf16[128,512]{1,0:T(8,128)(2,1)S(1)} %get-tuple-element.149.refs_3_), channel_id=1, source_target_pairs={{0,4},{1,5},{2,6},{3,7},{4,0},{5,1},{6,2},{7,3},{8,12},{9,13},{10,... | collective-permute-start | bytes 393224 | tf_op jit(solution)/shard_map/ppermute | solution.py:300
  23.3 6.6 %project_load.1 = (bf16[3,256,1024]{2,1,0:T(8,128)(2,1)S(1)}, bf16[3,256,1024]{2,1,0:T(8,128)(2,1)S(1)}, bf16[3,256,1024]{2,1,0:T(8,128)(2,1)S(1)}, bf16[3,256,1...) custom-call(s32[1]{0:T(128)} %bitcast.rank_ref, ...), custom_call_target="tpu_custom_call" | custom-call | flops 402653184 | bytes 393216 | tf_op jit(solution)/shard_map/project_load/pallas_call | solution.py:217
  37.0 2.3 %pad_maximum_fusion = bf16[8,128,512]{2,1,0:T(8,128)(2,1)} fusion(bf16[1,128,512]{2,1,0:T(8,128)(2,1)S(1)} %collective-permute-done.5, bf16[1,128,512]{2,1,0:T(8,128)(2,1)S(1)} %collective-permute-done.4, bf16[2,128,512]{2,1,0:T(8,128)(2,1)} %collective-permute-done.3, bf16[4,128,512]{2,1,0:T(8,128)(2,1)S(1)} %pad_maximum_fusion.6.x_ref), kind=kLoop, calls=%fused_computation | loop fusion | flops 1572864 | bytes 2097152 | tf_op jit(solution)/shard_map/concatenate | solution.py:353
  48.9 5.5 %project_mix.4 = bf16[128,256]{1,0:T(8,128)(2,1)S(1)} custom-call(s32[1]{0:T(128)} %bitcast.rank_ref, bf16[8,128,512]{2,1,0:T(8,128)(2,1)} %collective-permute-done.9.refs_0_, f32[1,8192]{1,0:T(1,128)S(1)} %get-tuple-element.156.gain_ref.refs_1_, f32[3,128,256]{2,1,0:T(8,128)S(1)} %get-tuple-element.161.refs_2_, f32[128,128]{1,0:T(8,128)S(1)} %get-tuple-element.162.refs_3_, ...), custom_call_target="tpu_custom_call" | custom-call | flops 1610612736 | bytes 1572864 | tf_op jit(solution)/shard_map/project_mix/pallas_call | solution.py:217
  56.5 2.9 %collective-permute-start.15 = (bf16[1,128,512]{2,1,0:T(8,128)(2,1)S(1)}, bf16[1,128,512]{2,1,0:T(8,128)(2,1)S(1)}, u32[]{:S(2)}, u32[]{:S(2)}) collective-permute-start(bf16[1,128,512]{2,1,0:T(8,128)(2,1)S(1)} %bitcast.112), channel_id=1, source_target_pairs={{0,6},{1,7},{2,4},{3,5},{4,2},{5,3},{6,0},{7,1},{8,14},{9,15},{10,... | collective-permute-start | bytes 393224 | tf_op jit(solution)/shard_map/ppermute | solution.py:300
  63.8 3.1 %collective-permute-done.11 = bf16[128,256]{1,0:T(8,128)(2,1)S(1)} collective-permute-done((bf16[128,256]{1,0:T(8,128)(2,1)S(1)}, bf16[128,256]{1,0:T(8,128)(2,1)S(1)}, u32[]{:S(2)}, u32[]{:S(2)}) %collective-permute-start.11) | collective-permute-done | bytes 65568 | tf_op jit(solution)/shard_map/ppermute | solution.py:300
  73.6 4.4 %project_mix.5 = bf16[128,256]{1,0:T(8,128)(2,1)S(1)} custom-call(s32[1]{0:T(128)} %bitcast.rank_ref, bf16[8,128,512]{2,1,0:T(8,128)(2,1)S(1)} %collective-permute-done.19.refs_0_, f32[1,8192]{1,0:T(1,128)S(1)} %get-tuple-element.156.gain_ref.refs_1_, f32[3,128,256]{2,1,0:T(8,128)S(1)} %get-tuple-element.189.refs_2_, ...), custom_call_target="tpu_custom_call" | custom-call | flops 1610612736 | bytes 1572864 | tf_op jit(solution)/shard_map/project_mix/pallas_call | solution.py:217
  80.4 4.0 %collective-permute-done.26 = bf16[128,256]{1,0:T(8,128)(2,1)S(1)} collective-permute-done((bf16[128,256]{1,0:T(8,128)(2,1)S(1)}, bf16[128,256]{1,0:T(8,128)(2,1)S(1)}, u32[]{:S(2)}, u32[]{:S(2)}) %collective-permute-start.26) | collective-permute-done | bytes 65568 | tf_op jit(solution)/shard_map/ppermute | solution.py:300
  85.9 2.2 %collective-permute-start.29 = (bf16[1,128,256]{2,1,0:T(8,128)(2,1)S(1)}, bf16[1,128,256]{2,1,0:T(8,128)(2,1)S(1)}, u32[]{:S(2)}, u32[]{:S(2)}) collective-permute-start(bf16[1,128,256]{2,1,0:T(8,128)(2,1)S(1)} %bitcast.126), channel_id=1, source_target_pairs={{0,6},{1,7},{2,4},{3,5},{4,2},{5,3},{6,0},{7,1},{8,14},{9,15},{10,... | collective-permute-start | bytes 196616 | tf_op jit(solution)/shard_map/ppermute | solution.py:300
  91.4 2.1 %collective-permute-done.27 = bf16[2,128,256]{2,1,0:T(8,128)(2,1)S(1)} collective-permute-done((bf16[2,128,256]{2,1,0:T(8,128)(2,1)S(1)}, bf16[2,128,256]{2,1,0:T(8,128)(2,1)S(1)}, u32[]{:S(2)}, u32[]{:S(2)}) %collective-permute-start.27) | collective-permute-done | bytes 131104 | tf_op jit(solution)/shard_map/ppermute | solution.py:300
  94.5 2.3 %collective-permute-start.23 = (bf16[128,512]{1,0:T(8,128)(2,1)S(1)}, bf16[128,512]{1,0:T(8,128)(2,1)S(1)}, u32[]{:S(2)}, u32[]{:S(2)}) collective-permute-start(bf16[128,512]{1,0:T(8,128)(2,1)S(1)} %bitcast_select_fusion), channel_id=1, source_target_pairs={{0,24},{1,25},{2,26},{3,27},{4,28},{5,29},{6,30},{7,31},{8,16},{9,... | collective-permute-start | bytes 393224 | tf_op jit(solution)/shard_map/ppermute | solution.py:309
  100.2 5.1 %collective-permute-done.23 = bf16[128,512]{1,0:T(8,128)(2,1)S(1)} collective-permute-done((bf16[128,512]{1,0:T(8,128)(2,1)S(1)}, bf16[128,512]{1,0:T(8,128)(2,1)S(1)}, u32[]{:S(2)}, u32[]{:S(2)}) %collective-permute-start.23) | collective-permute-done | bytes 131104 | tf_op jit(solution)/shard_map/ppermute | solution.py:309
  105.8 2.6 %collective-permute-done.21.refs_3_ = bf16[128,512]{1,0:T(8,128)(2,1)S(1)} collective-permute-done((bf16[128,512]{1,0:T(8,128)(2,1)S(1)}, bf16[128,512]{1,0:T(8,128)(2,1)S(1)}, u32[]{:S(2)}, u32[]{:S(2)}) %collective-permute-start.21) | collective-permute-done | bytes 131104 | tf_op jit(solution)/shard_map/ppermute | solution.py:309
  109.5 2.2 %collective-permute-start.36 = (bf16[128,512]{1,0:T(8,128)(2,1)S(1)}, bf16[128,512]{1,0:T(8,128)(2,1)S(1)}, u32[]{:S(2)}, u32[]{:S(2)}) collective-permute-start(bf16[128,512]{1,0:T(8,128)(2,1)S(1)} %project_out.5), channel_id=1, source_target_pairs={{0,24},{1,25},{2,26},{3,27},{4,28},{5,29},{6,30},{7,31},{8,16},{9,... | collective-permute-start | bytes 393224 | tf_op jit(solution)/shard_map/ppermute | solution.py:309
  115.2 3.6 %collective-permute-done.36 = bf16[128,512]{1,0:T(8,128)(2,1)S(1)} collective-permute-done((bf16[128,512]{1,0:T(8,128)(2,1)S(1)}, bf16[128,512]{1,0:T(8,128)(2,1)S(1)}, u32[]{:S(2)}, u32[]{:S(2)}) %collective-permute-start.36) | collective-permute-done | bytes 131104 | tf_op jit(solution)/shard_map/ppermute | solution.py:309
  122.2 2.7 %collective-permute-done.33 = bf16[1,128,512]{2,1,0:T(8,128)(2,1)S(1)} collective-permute-done((bf16[1,128,512]{2,1,0:T(8,128)(2,1)S(1)}, bf16[1,128,512]{2,1,0:T(8,128)(2,1)S(1)}, u32[]{:S(2)}, u32[]{:S(2)}) %collective-permute-start.33) | collective-permute-done | bytes 131104 | tf_op jit(solution)/shard_map/ppermute | solution.py:300
  127.9 4.2 %project_mix.6 = bf16[128,256]{1,0:T(8,128)(2,1)S(1)} custom-call(s32[1]{0:T(128)} %bitcast.rank_ref, bf16[8,128,512]{2,1,0:T(8,128)(2,1)S(1)} %collective-permute-done.37.refs_0_, f32[1,8192]{1,0:T(1,128)S(1)} %get-tuple-element.156.gain_ref.refs_1_, f32[3,128,256]{2,1,0:T(8,128)S(1)} %get-tuple-element.225.refs_2_, ...), custom_call_target="tpu_custom_call" | custom-call | flops 1610612736 | bytes 1572864 | tf_op jit(solution)/shard_map/project_mix/pallas_call | solution.py:217
  140.7 3.7 %collective-permute-done.39 = bf16[128,256]{1,0:T(8,128)(2,1)S(1)} collective-permute-done((bf16[128,256]{1,0:T(8,128)(2,1)S(1)}, bf16[128,256]{1,0:T(8,128)(2,1)S(1)}, u32[]{:S(2)}, u32[]{:S(2)}) %collective-permute-start.39) | collective-permute-done | bytes 65568 | tf_op jit(solution)/shard_map/ppermute | solution.py:300
  144.8 2.5 %collective-permute-start.46 = (bf16[1,128,256]{2,1,0:T(8,128)(2,1)S(1)}, bf16[1,128,256]{2,1,0:T(8,128)(2,1)S(1)}, u32[]{:S(2)}, u32[]{:S(2)}) collective-permute-start(bf16[1,128,256]{2,1,0:T(8,128)(2,1)S(1)} %bitcast.120), channel_id=1, source_target_pairs={{0,6},{1,7},{2,4},{3,5},{4,2},{5,3},{6,0},{7,1},{8,14},{9,15},{10,... | collective-permute-start | bytes 196616 | tf_op jit(solution)/shard_map/ppermute | solution.py:300
  151.1 4.4 %project_mix.7 = bf16[128,256]{1,0:T(8,128)(2,1)S(1)} custom-call(s32[1]{0:T(128)} %bitcast.rank_ref, bf16[8,128,512]{2,1,0:T(8,128)(2,1)S(1)} %collective-permute-done.47.refs_0_, f32[1,8192]{1,0:T(1,128)S(1)} %get-tuple-element.156.gain_ref.refs_1_, f32[3,128,256]{2,1,0:T(8,128)S(1)} %get-tuple-element.249.refs_2_, ...), custom_call_target="tpu_custom_call" | custom-call | flops 1610612736 | bytes 1572864 | tf_op jit(solution)/shard_map/project_mix/pallas_call | solution.py:217
  159.4 2.3 %collective-permute-done.51 = bf16[128,256]{1,0:T(8,128)(2,1)S(1)} collective-permute-done((bf16[128,256]{1,0:T(8,128)(2,1)S(1)}, bf16[128,256]{1,0:T(8,128)(2,1)S(1)}, u32[]{:S(2)}, u32[]{:S(2)}) %collective-permute-start.51) | collective-permute-done | bytes 65568 | tf_op jit(solution)/shard_map/ppermute | solution.py:300
  163.3 2.5 %collective-permute-start.54 = (bf16[1,128,256]{2,1,0:T(8,128)(2,1)S(1)}, bf16[1,128,256]{2,1,0:T(8,128)(2,1)S(1)}, u32[]{:S(2)}, u32[]{:S(2)}) collective-permute-start(bf16[1,128,256]{2,1,0:T(8,128)(2,1)S(1)} %bitcast.129), channel_id=1, source_target_pairs={{0,6},{1,7},{2,4},{3,5},{4,2},{5,3},{6,0},{7,1},{8,14},{9,15},{10,... | collective-permute-start | bytes 196616 | tf_op jit(solution)/shard_map/ppermute | solution.py:300
  (214 shorter events, 92.3 us)
Async XLA Ops:
  1.0 10.6 %collective-permute-start.2 = (bf16[128,512]{1,0:T(8,128)(2,1)S(1)}, bf16[128,512]{1,0:T(8,128)(2,1)}, u32[]{:S(2)}, u32[]{:S(2)}) collective-permute-start(bf16[128,512]{1,0:T(8,128)(2,1)S(1)} %get-tuple-element.137.refs_3_), channel_id=1, source_target_pairs={{0,8},{1,9},{2,10},{3,11},{4,12},{5,13},{6,14},{7,15},{8,0},{9,1},... | collective-permute-start | bytes 393224 | tf_op jit(solution)/shard_map/ppermute | solution.py:300
  14.7 22.2 %collective-permute-start.3 = (bf16[2,128,512]{2,1,0:T(8,128)(2,1)}, bf16[2,128,512]{2,1,0:T(8,128)(2,1)}, u32[]{:S(2)}, u32[]{:S(2)}) collective-permute-start(bf16[2,128,512]{2,1,0:T(8,128)(2,1)} %pad_maximum_fusion.14), channel_id=1, source_target_pairs={{0,2},{1,3},{2,0},{3,1},{4,6},{5,7},{6,4},{7,5},{8,10},{9,11},{10,... | collective-permute-start | bytes 786440 | tf_op jit(solution)/shard_map/ppermute | solution.py:300
  16.2 20.7 %collective-permute-start.7 = (bf16[128,512]{1,0:T(8,128)(2,1)S(1)}, bf16[128,512]{1,0:T(8,128)(2,1)S(1)}, u32[]{:S(2)}, u32[]{:S(2)}) collective-permute-start(bf16[128,512]{1,0:T(8,128)(2,1)S(1)} %get-tuple-element.149.refs_3_), channel_id=1, source_target_pairs={{0,4},{1,5},{2,6},{3,7},{4,0},{5,1},{6,2},{7,3},{8,12},{9,13},{10,... | collective-permute-start | bytes 393224 | tf_op jit(solution)/shard_map/ppermute | solution.py:300
  18.8 18.1 %collective-permute-start.6 = (bf16[128,512]{1,0:T(8,128)(2,1)S(1)}, bf16[128,512]{1,0:T(8,128)(2,1)S(1)}, u32[]{:S(2)}, u32[]{:S(2)}) collective-permute-start(bf16[128,512]{1,0:T(8,128)(2,1)S(1)} %get-tuple-element.149.refs_3_), channel_id=1, source_target_pairs={{0,2},{1,3},{2,0},{3,1},{4,6},{5,7},{6,4},{7,5},{8,10},{9,11},{10,... | collective-permute-start | bytes 393224 | tf_op jit(solution)/shard_map/ppermute | solution.py:300
  19.3 17.6 %collective-permute-start.4 = (bf16[1,128,512]{2,1,0:T(8,128)(2,1)}, bf16[1,128,512]{2,1,0:T(8,128)(2,1)S(1)}, u32[]{:S(2)}, u32[]{:S(2)}) collective-permute-start(bf16[1,128,512]{2,1,0:T(8,128)(2,1)} %bitcast.6), channel_id=1, source_target_pairs={{0,4},{1,5},{2,6},{3,7},{4,0},{5,1},{6,2},{7,3},{8,12},{9,13},{10,... | collective-permute-start | bytes 393224 | tf_op jit(solution)/shard_map/ppermute | solution.py:300
  20.3 16.7 %collective-permute-start.5 = (bf16[1,128,512]{2,1,0:T(8,128)(2,1)}, bf16[1,128,512]{2,1,0:T(8,128)(2,1)S(1)}, u32[]{:S(2)}, u32[]{:S(2)}) collective-permute-start(bf16[1,128,512]{2,1,0:T(8,128)(2,1)} %bitcast.6), channel_id=1, source_target_pairs={{0,6},{1,7},{2,4},{3,5},{4,2},{5,3},{6,0},{7,1},{8,14},{9,15},{10,... | collective-permute-start | bytes 393224 | tf_op jit(solution)/shard_map/ppermute | solution.py:300
  40.5 26.6 %collective-permute-start.13 = (bf16[2,128,512]{2,1,0:T(8,128)(2,1)S(1)}, bf16[2,128,512]{2,1,0:T(8,128)(2,1)S(1)}, u32[]{:S(2)}, u32[]{:S(2)}) collective-permute-start(bf16[2,128,512]{2,1,0:T(8,128)(2,1)S(1)} %pad_maximum_fusion.15), channel_id=1, source_target_pairs={{0,2},{1,3},{2,0},{3,1},{4,6},{5,7},{6,4},{7,5},{8,10},{9,11},{10,... | collective-permute-start | bytes 786440 | tf_op jit(solution)/shard_map/ppermute | solution.py:300
  56.5 10.6 %collective-permute-start.14 = (bf16[1,128,512]{2,1,0:T(8,128)(2,1)S(1)}, bf16[1,128,512]{2,1,0:T(8,128)(2,1)S(1)}, u32[]{:S(2)}, u32[]{:S(2)}) collective-permute-start(bf16[1,128,512]{2,1,0:T(8,128)(2,1)S(1)} %bitcast.111), channel_id=1, source_target_pairs={{0,4},{1,5},{2,6},{3,7},{4,0},{5,1},{6,2},{7,3},{8,12},{9,13},{10,... | collective-permute-start | bytes 393224 | tf_op jit(solution)/shard_map/ppermute | solution.py:300
  56.5 10.6 %collective-permute-start.15 = (bf16[1,128,512]{2,1,0:T(8,128)(2,1)S(1)}, bf16[1,128,512]{2,1,0:T(8,128)(2,1)S(1)}, u32[]{:S(2)}, u32[]{:S(2)}) collective-permute-start(bf16[1,128,512]{2,1,0:T(8,128)(2,1)S(1)} %bitcast.112), channel_id=1, source_target_pairs={{0,6},{1,7},{2,4},{3,5},{4,2},{5,3},{6,0},{7,1},{8,14},{9,15},{10,... | collective-permute-start | bytes 393224 | tf_op jit(solution)/shard_map/ppermute | solution.py:300
  67.2 12.4 %collective-permute-start.17 = (bf16[1,128,256]{2,1,0:T(8,128)(2,1)S(1)}, bf16[1,128,256]{2,1,0:T(8,128)(2,1)S(1)}, u32[]{:S(2)}, u32[]{:S(2)}) collective-permute-start(bf16[1,128,256]{2,1,0:T(8,128)(2,1)S(1)} %bitcast.122), channel_id=1, source_target_pairs={{0,4},{1,5},{2,6},{3,7},{4,0},{5,1},{6,2},{7,3},{8,12},{9,13},{10,... | collective-permute-start | bytes 196616 | tf_op jit(solution)/shard_map/ppermute | solution.py:300
  68.0 12.3 %collective-permute-start.18 = (bf16[1,128,256]{2,1,0:T(8,128)(2,1)S(1)}, bf16[1,128,256]{2,1,0:T(8,128)(2,1)S(1)}, u32[]{:S(2)}, u32[]{:S(2)}) collective-permute-start(bf16[1,128,256]{2,1,0:T(8,128)(2,1)S(1)} %bitcast.123), channel_id=1, source_target_pairs={{0,6},{1,7},{2,4},{3,5},{4,2},{5,3},{6,0},{7,1},{8,14},{9,15},{10,... | collective-permute-start | bytes 196616 | tf_op jit(solution)/shard_map/ppermute | solution.py:300
  70.0 10.4 %collective-permute-start.16 = (bf16[2,128,256]{2,1,0:T(8,128)(2,1)S(1)}, bf16[2,128,256]{2,1,0:T(8,128)(2,1)S(1)}, u32[]{:S(2)}, u32[]{:S(2)}) collective-permute-start(bf16[2,128,256]{2,1,0:T(8,128)(2,1)S(1)} %pad_maximum_fusion.16), channel_id=1, source_target_pairs={{0,2},{1,3},{2,0},{3,1},{4,6},{5,7},{6,4},{7,5},{8,10},{9,11},{10,... | collective-permute-start | bytes 393224 | tf_op jit(solution)/shard_map/ppermute | solution.py:300
  94.5 10.7 %collective-permute-start.23 = (bf16[128,512]{1,0:T(8,128)(2,1)S(1)}, bf16[128,512]{1,0:T(8,128)(2,1)S(1)}, u32[]{:S(2)}, u32[]{:S(2)}) collective-permute-start(bf16[128,512]{1,0:T(8,128)(2,1)S(1)} %bitcast_select_fusion), channel_id=1, source_target_pairs={{0,24},{1,25},{2,26},{3,27},{4,28},{5,29},{6,30},{7,31},{8,16},{9,... | collective-permute-start | bytes 393224 | tf_op jit(solution)/shard_map/ppermute | solution.py:309
  97.9 10.4 %collective-permute-start.21 = (bf16[128,512]{1,0:T(8,128)(2,1)S(1)}, bf16[128,512]{1,0:T(8,128)(2,1)S(1)}, u32[]{:S(2)}, u32[]{:S(2)}) collective-permute-start(bf16[128,512]{1,0:T(8,128)(2,1)S(1)} %bitcast_select_fusion), channel_id=1, source_target_pairs={{0,16},{1,17},{2,18},{3,19},{4,20},{5,21},{6,22},{7,23},{8,24},{9,... | collective-permute-start | bytes 393224 | tf_op jit(solution)/shard_map/ppermute | solution.py:309
  108.4 16.6 %collective-permute-start.31 = (bf16[3,128,512]{2,1,0:T(8,128)(2,1)S(1)}, bf16[3,128,512]{2,1,0:T(8,128)(2,1)S(1)}, u32[]{:S(2)}, u32[]{:S(2)}) collective-permute-start(bf16[3,128,512]{2,1,0:T(8,128)(2,1)S(1)} %pad_maximum_fusion.11), channel_id=1, source_target_pairs={{0,2},{1,3},{2,0},{3,1},{4,6},{5,7},{6,4},{7,5},{8,10},{9,11},{10,... | collective-permute-start | bytes 1179656 | tf_op jit(solution)/shard_map/ppermute | solution.py:300
  109.5 9.3 %collective-permute-start.36 = (bf16[128,512]{1,0:T(8,128)(2,1)S(1)}, bf16[128,512]{1,0:T(8,128)(2,1)S(1)}, u32[]{:S(2)}, u32[]{:S(2)}) collective-permute-start(bf16[128,512]{1,0:T(8,128)(2,1)S(1)} %project_out.5), channel_id=1, source_target_pairs={{0,24},{1,25},{2,26},{3,27},{4,28},{5,29},{6,30},{7,31},{8,16},{9,... | collective-permute-start | bytes 393224 | tf_op jit(solution)/shard_map/ppermute | solution.py:309
  111.7 9.3 %collective-permute-start.35 = (bf16[128,512]{1,0:T(8,128)(2,1)S(1)}, bf16[128,512]{1,0:T(8,128)(2,1)S(1)}, u32[]{:S(2)}, u32[]{:S(2)}) collective-permute-start(bf16[128,512]{1,0:T(8,128)(2,1)S(1)} %project_out.5), channel_id=1, source_target_pairs={{0,20},{1,21},{2,22},{3,23},{4,16},{5,17},{6,18},{7,19},{8,28},{9,... | collective-permute-start | bytes 393224 | tf_op jit(solution)/shard_map/ppermute | solution.py:309
  112.6 9.7 %collective-permute-start.34 = (bf16[128,512]{1,0:T(8,128)(2,1)S(1)}, bf16[128,512]{1,0:T(8,128)(2,1)S(1)}, u32[]{:S(2)}, u32[]{:S(2)}) collective-permute-start(bf16[128,512]{1,0:T(8,128)(2,1)S(1)} %project_out.5), channel_id=1, source_target_pairs={{0,16},{1,17},{2,18},{3,19},{4,20},{5,21},{6,22},{7,23},{8,24},{9,... | collective-permute-start | bytes 393224 | tf_op jit(solution)/shard_map/ppermute | solution.py:309
  125.2 19.4 %collective-permute-start.41 = (bf16[3,128,512]{2,1,0:T(8,128)(2,1)S(1)}, bf16[3,128,512]{2,1,0:T(8,128)(2,1)S(1)}, u32[]{:S(2)}, u32[]{:S(2)}) collective-permute-start(bf16[3,128,512]{2,1,0:T(8,128)(2,1)S(1)} %pad_maximum_fusion.12), channel_id=1, source_target_pairs={{0,2},{1,3},{2,0},{3,1},{4,6},{5,7},{6,4},{7,5},{8,10},{9,11},{10,... | collective-permute-start | bytes 1179656 | tf_op jit(solution)/shard_map/ppermute | solution.py:300
  133.3 11.3 %collective-permute-start.42 = (bf16[1,128,512]{2,1,0:T(8,128)(2,1)S(1)}, bf16[1,128,512]{2,1,0:T(8,128)(2,1)S(1)}, u32[]{:S(2)}, u32[]{:S(2)}) collective-permute-start(bf16[1,128,512]{2,1,0:T(8,128)(2,1)S(1)} %bitcast.99), channel_id=1, source_target_pairs={{0,4},{1,5},{2,6},{3,7},{4,0},{5,1},{6,2},{7,3},{8,12},{9,13},{10,... | collective-permute-start | bytes 393224 | tf_op jit(solution)/shard_map/ppermute | solution.py:300
  135.1 9.5 %collective-permute-start.43 = (bf16[1,128,512]{2,1,0:T(8,128)(2,1)S(1)}, bf16[1,128,512]{2,1,0:T(8,128)(2,1)S(1)}, u32[]{:S(2)}, u32[]{:S(2)}) collective-permute-start(bf16[1,128,512]{2,1,0:T(8,128)(2,1)S(1)} %bitcast.100), channel_id=1, source_target_pairs={{0,6},{1,7},{2,4},{3,5},{4,2},{5,3},{6,0},{7,1},{8,14},{9,15},{10,... | collective-permute-start | bytes 393224 | tf_op jit(solution)/shard_map/ppermute | solution.py:300
  144.7 13.3 %collective-permute-start.45 = (bf16[1,128,256]{2,1,0:T(8,128)(2,1)S(1)}, bf16[1,128,256]{2,1,0:T(8,128)(2,1)S(1)}, u32[]{:S(2)}, u32[]{:S(2)}) collective-permute-start(bf16[1,128,256]{2,1,0:T(8,128)(2,1)S(1)} %bitcast.119), channel_id=1, source_target_pairs={{0,4},{1,5},{2,6},{3,7},{4,0},{5,1},{6,2},{7,3},{8,12},{9,13},{10,... | collective-permute-start | bytes 196616 | tf_op jit(solution)/shard_map/ppermute | solution.py:300
  144.8 14.5 %collective-permute-start.46 = (bf16[1,128,256]{2,1,0:T(8,128)(2,1)S(1)}, bf16[1,128,256]{2,1,0:T(8,128)(2,1)S(1)}, u32[]{:S(2)}, u32[]{:S(2)}) collective-permute-start(bf16[1,128,256]{2,1,0:T(8,128)(2,1)S(1)} %bitcast.120), channel_id=1, source_target_pairs={{0,6},{1,7},{2,4},{3,5},{4,2},{5,3},{6,0},{7,1},{8,14},{9,15},{10,... | collective-permute-start | bytes 196616 | tf_op jit(solution)/shard_map/ppermute | solution.py:300
  147.3 12.0 %collective-permute-start.44 = (bf16[2,128,256]{2,1,0:T(8,128)(2,1)S(1)}, bf16[2,128,256]{2,1,0:T(8,128)(2,1)S(1)}, u32[]{:S(2)}, u32[]{:S(2)}) collective-permute-start(bf16[2,128,256]{2,1,0:T(8,128)(2,1)S(1)} %pad_maximum_fusion.18), channel_id=1, source_target_pairs={{0,2},{1,3},{2,0},{3,1},{4,6},{5,7},{6,4},{7,5},{8,10},{9,11},{10,... | collective-permute-start | bytes 393224 | tf_op jit(solution)/shard_map/ppermute | solution.py:300
  (60 other events, 316.0 us)

commit v9 on v8

--- a/solution.py
+++ b/solution.py
@@ -10,20 +10,6 @@
 EPS = 1e-06
 VMEM_LIMIT = 20 * 1024 * 1024
 PAD = 8
-
-
-def plan(section_count, tick_count):
-    wave_count = min(section_count, tick_count)
-    waves = [[[] for _ in range(section_count)] for _ in range(wave_count)]
-    where = {}
-    for k in range(tick_count):
-        for s in range(section_count):
-            first = where[s - 1, k - 1][0] + 1 if s > 0 and k > 0 else 0
-            last = wave_count - 1 - min(section_count - 1 - s, tick_count - 1 - k)
-            best = min(range(first, last + 1), key=lambda w: (len(waves[w][s]), w))
-            where[s, k] = (best, len(waves[best][s]))
-            waves[best][s].append(k)
-    return waves
 
 
 def split_dp(dp_count):
@@ -33,24 +19,6 @@
     while near * near * 4 <= chips:
         near *= 2
     return chips // near, near, core
-
-
-def pick(section_idx, options):
-    distinct = []
-    for s, value in enumerate(options):
-        if value is None:
-            continue
-        for held, members in distinct:
-            if held is value:
-                members.append(s)
-                break
-        else:
-            distinct.append((value, [s]))
-    result = distinct[0][0]
-    for value, members in distinct[1:]:
-        mine = functools.reduce(jnp.logical_or, [section_idx == s for s in members])
-        result = jnp.where(mine, value, result)
-    return result
 
 
 def routes(far, near, cross):
@@ -160,15 +128,15 @@
 
     total = jnp.sum(sq_ref[...], axis=1, keepdims=True)
     factor = lax.rsqrt(total / model_width + EPS)
-    taps = short_ref.shape[0] // branches
+    taps = short_ref.shape[1]
     pad_ref[0:PAD, :] = jnp.zeros((PAD, chan), jnp.float32)
 
     def branch(i):
         u = acc_ref[i] * factor
         pad_ref[PAD : PAD + tok_len, :] = u
-        z = short_ref[i * taps] * u
+        z = short_ref[i, 0] * u
         for j in range(1, taps):
-            z = z + short_ref[i * taps + j] * pad_ref[PAD - j : PAD - j + tok_len, :]
+            z = z + short_ref[i, j] * pad_ref[PAD - j : PAD - j + tok_len, :]
         return z
 
     query_ref[...] = branch(1)
@@ -194,14 +162,21 @@
 
 
 def out_kernel(blocks, core, rank_ref, *refs):
-    sides = refs[:core]
-    w_ref, own_ref, result_ref, acc_ref = refs[core:]
+    sides, refs = refs[:core], refs[core:]
+    w_ref, own_ref = refs[:2]
     count, _, chan = sides[0].shape
+    acc_ref = refs[-1]
     acc_ref[...] = own_ref[...].astype(jnp.float32)
     for n, (cell, c) in enumerate(blocks):
         rows = columns_of(rank_ref, core, cell, c, chan)
         acc_ref[...] += jnp.dot(sides[n // count][n % count], w_ref[rows, :], preferred_element_type=jnp.float32)
-    result_ref[...] = acc_ref[...].astype(jnp.bfloat16)
+    result = acc_ref[...].astype(jnp.bfloat16)
+    if len(refs) == 4:
+        refs[2][...] = result
+    else:
+        following_ref, result_ref, leaving_ref = refs[2:5]
+        result_ref[...] = result
+        leaving_ref[...] = jnp.where(rank_ref[1] == 1, following_ref[...], result)
 
 
 def in_vmem(count):
@@ -277,16 +252,17 @@
     )[0]
 
 
-def project_out(blocks, core, sides, w_out, own, rank):
+def project_out(blocks, core, sides, w_out, own, following, rank):
     rows, feat = own.shape
+    result = jax.ShapeDtypeStruct((rows, feat), jnp.bfloat16)
     return call(
         functools.partial(out_kernel, blocks, core),
-        [rank, *sides, w_out, own],
-        [jax.ShapeDtypeStruct((rows, feat), jnp.bfloat16)],
+        [rank, *sides, w_out, own] + ([] if following is None else [following]),
+        [result] if following is None else [result, result],
         [pltpu.VMEM((rows, feat), jnp.float32)],
         2 * rows * w_out.shape[0] * feat,
         "project_out",
-    )[0]
+    )
 
 
 def body(section_count, dp_count, fresh_acts, carried, norm_gain, w_in, short_filter, filter_taps, decay_rate, w_out):
@@ -294,7 +270,7 @@
     far, near, core = split_dp(dp_count)
     group = near * core
     section_idx = lax.axis_index("section")
-    rank = lax.axis_index("dp").astype(jnp.int32).reshape(1)
+    rank = jnp.stack([lax.axis_index("dp"), (section_idx == section_count - 1).astype(jnp.int32)])
 
     def swap(value, offset):
         return lax.ppermute(value, "dp", [(r, r ^ offset) for r in range(dp_count)])
@@ -326,80 +302,37 @@
     def of_cores(cells, cores):
         return [(cell, c) for c in cores for cell in cells]
 
-    short_rows = short_filter[0].transpose(0, 2, 1).reshape(-1, 1, short_filter.shape[2])
-    waiting = carried[0]
-    params, results, last = {}, {}, None
-
-    def start(slot, before, behind):
-        source = after(slot["source"], before["blocks"]) if before else slot["source"]
-        slot["blocks"] = after(round_one(source, slot["cross"]), before.get("sums"), slot["last"])
-
-    def spread(slot, before, behind):
-        slot["cells"], slot["rest"] = round_two(after(slot["blocks"], before.get("rest")), slot["cross"])
-        blocks = of_cores(slot["blocks"], [0])
-        direct = after(jnp.stack(list(slot["blocks"].values())), before.get("y"))
-        slot["direct"] = direct
+    short_rows = short_filter.transpose(1, 3, 0, 2)
+    source = jnp.where(section_idx == 0, fresh_acts[0], carried[0])
+    params, made = {}, []
+    for k in range(tick_count):
+        blocks = after(round_one(source, k > 0))
+        cells, rest = round_two(blocks, k > 0)
+        order = [*blocks, *cells]
+        direct = jnp.stack(list(blocks.values()))
+        here = of_cores(blocks, [0])
         if params:
-            slot["sums"] = project_part(blocks, core, direct, params, [], rank)
+            sums = project_part(here, core, direct, params, [], rank)
         else:
-            order = [*slot["blocks"], *slot["cells"]]
-            slot["sums"], loaded = project_load(
-                blocks, order, core, direct, w_in[0], norm_gain, filter_taps[0], decay_rate, rank
+            sums, params = project_load(
+                here, order, core, direct, w_in[0], norm_gain, filter_taps[0], decay_rate, rank
             )
-            params.update(loaded)
-
-    def work(slot, before, behind):
-        relayed = jnp.concatenate(after(slot["rest"], slot["sums"], behind.get("blocks"), before.get("y_blocks")))
-        everything = jnp.concatenate([slot["direct"], relayed])
+        relayed = jnp.concatenate(after(rest, sums))
+        everything = jnp.concatenate([direct, relayed])
         sides = [swap(everything, c) for c in range(1, core)]
-        sums = project_part(of_cores(slot["cells"], [0]), core, relayed, params, slot["sums"], rank)
-        order = [*slot["blocks"], *slot["cells"]]
+        sums = project_part(of_cores(cells, [0]), core, relayed, params, sums, rank)
         sides = after(sides, sums)
-        blocks = of_cores(order, range(1, core))
-        slot["y"] = mix(blocks, core, norm_gain.shape[1], sides, params, sums, short_rows, rank)
-        slot["y_blocks"] = after(round_one(slot["y"]), before.get("y_rest"))
-
-    def spread_y(slot, before, behind):
-        blocks = after(slot["y_blocks"], before.get("y_rest"), before.get("out"), behind.get("rest"))
-        slot["y_cells"], slot["y_rest"] = round_two(blocks)
-
-    def finish(slot, before, behind):
-        direct = jnp.stack(list(slot["y_blocks"].values()))
-        everything = jnp.concatenate([direct, *after(slot["y_rest"], behind.get("y"))])
+        y = mix(of_cores(order, range(1, core)), core, norm_gain.shape[1], sides, params, sums, short_rows, rank)
+        y_blocks = after(round_one(y))
+        cells, rest = round_two(y_blocks)
+        everything = jnp.concatenate([jnp.stack(list(y_blocks.values())), *rest])
         sides = [everything] + [swap(everything, c) for c in range(1, core)]
-        blocks = of_cores([*slot["y_blocks"], *slot["y_cells"]], range(core))
-        slot["out"] = project_out(blocks, core, sides, w_out[0], slot["blocks"][0], rank)
-
-    phases = [start, spread, work, spread_y, finish]
-    for w, ticks in enumerate(plan(section_count, tick_count)):
-        slots = []
-        for i in range(max(len(mine) for mine in ticks)):
-            options = []
-            for s in range(section_count):
-                if w == 0:
-                    mine = ticks[s]
-                    options.append(None if i >= len(mine) else waiting if s > 0 else fresh_acts[mine[i]])
-                else:
-                    mine = ticks[(s + 1) % section_count]
-                    if i >= len(mine):
-                        options.append(None)
-                    elif s + 1 == section_count:
-                        options.append(fresh_acts[mine[i]])
-                    else:
-                        options.append(results[s, mine[i] - 1])
-            slots.append({"source": pick(section_idx, options), "cross": w > 0, "last": None if i > 0 else last})
-        for t in range(len(phases) + len(slots) - 1):
-            for i, slot in enumerate(slots):
-                if 0 <= t - i < len(phases):
-                    before = slots[i - 1] if i > 0 else {}
-                    behind = slots[i + 1] if i + 1 < len(slots) else {}
-                    phases[t - i](slot, before, behind)
-        last = slots[-1]["out"]
-        for s in range(section_count):
-            for i, k in enumerate(ticks[s]):
-                results[s, k] = slots[i]["out"]
-    outputs = [pick(section_idx, [results[s, k] for s in range(section_count)]) for k in range(tick_count)]
-    return jnp.stack(outputs)[None]
+        following = fresh_acts[k + 1] if k + 1 < tick_count else None
+        around = of_cores([*y_blocks, *cells], range(core))
+        result, *leaving = project_out(around, core, sides, w_out[0], blocks[0], following, rank)
+        made.append(result)
+        source = leaving[0] if leaving else None
+    return jnp.stack(made)[None]
 
 
 def solution(mesh):

time: 175 us -> 152 us (0.87)
  waiting for transfers between devices: 50.9 us -> 63.4 us
  local copies, waits for them, and re-layouts: 12.7 us -> 0.38 us
  starting transfers between devices: 62.9 us -> 50.9 us
  other arithmetic: 11 us -> 2.44 us
  Pallas kernels: 36.2 us -> 34.4 us
    ppermute x50 -> x36, starting transfers between devices: 53.6 us -> 39.1 us  [swap(): return lax.ppermute(value, 'dp', [(r, r ^ offset) for r in range(dp_count)])]
    unnamed x81 -> x38, local copies, waits for them, and re-layouts: 12.6 us -> 0.33 us
    ppermute x50 -> x36, waiting for transfers between devices: 37.4 us -> 49 us  [swap(): return lax.ppermute(value, 'dp', [(r, r ^ offset) for r in range(dp_count)])]
    concatenate x8 -> x3, other arithmetic: 4.16 us -> 0.23 us  [body(): relayed = jnp.concatenate(after(rest, sums))]
    another operation x8 -> x4, other arithmetic: 2.9 us -> 0.07 us  [round_two(): jnp.stack([blocks[b] for b in sent])]
    ppermute x6, starting transfers between devices: 9.25 us -> 11.8 us  [onward(): return lax.ppermute(value, ('section', 'dp'), pairs)]
    select_n x2 -> x0, other arithmetic: 1.92 us -> none  [pick(): result = jnp.where(mine, value, result)]
    pallas_call x16 -> x12, Pallas kernels: 36.2 us -> 34.4 us  [call(): pl.pallas_call(kernel, in_specs=specs, out_specs=in_vmem(len(outs)), out_...]
  transfers between devices with their start and end apart: 56 -> 42, of which waited for: 28 -> 36; matrix products, arithmetic and copies ran while one was open for 4% -> 0% of each run, Pallas kernels for 20% -> 10%
where the time goes in v9:
time: 152 us
  waiting for transfers between devices  63.4 us (42%)
  starting transfers between devices  50.9 us (33%)
  Pallas kernels  34.4 us (23%)
  other arithmetic  2.44 us (2%)
    ppermute x36, waiting for transfers between devices, swap(): return lax.ppermute(value, 'dp', [(r, r ^ offset) for r in range(dp_count)])  49 us
    ppermute x36, starting transfers between devices, swap(): return lax.ppermute(value, 'dp', [(r, r ^ offset) for r in range(dp_count)])  39.1 us
    pallas_call x12, Pallas kernels, call(): pl.pallas_call(kernel, in_specs=specs, out_specs=in_vmem(len(outs)), out_...  34.4 us
    ppermute x6, waiting for transfers between devices, onward(): return lax.ppermute(value, ('section', 'dp'), pairs)  14.4 us
    ppermute x6, starting transfers between devices, onward(): return lax.ppermute(value, ('section', 'dp'), pairs)  11.8 us
  transfers between devices with their start and end apart: 42, of which 36 were waited for; matrix products, arithmetic and copies ran while one was open for 0% of the time, Pallas kernels for 10%

profile of v9, /device:TPU:0, one launch (start us, length us, event | category | flops | bytes accessed | tf_op | source)
XLA Modules:
  0.0 151.9 jit_solution(16078064787084786411)
XLA Ops:
  1.1 3.0 %collective-permute-start = (bf16[128,512]{1,0:T(8,128)(2,1)S(1)}, bf16[128,512]{1,0:T(8,128)(2,1)S(1)}, u32[]{:S(2)}, u32[]{:S(2)}) collective-permute-start(bf16[128,512]{1,0:T(8,128)(2,1)S(1)} %get-tuple-element.83.refs_3_), channel_id=1, source_target_pairs={{0,2},{1,3},{2,0},{3,1},{4,6},{5,7},{6,4},{7,5},{8,10},{9,11},{10,... | collective-permute-start | bytes 393224 | tf_op jit(solution)/shard_map/ppermute | solution.py:276
  5.6 2.6 %collective-permute-start.2 = (bf16[128,512]{1,0:T(8,128)(2,1)S(1)}, bf16[128,512]{1,0:T(8,128)(2,1)S(1)}, u32[]{:S(2)}, u32[]{:S(2)}) collective-permute-start(bf16[128,512]{1,0:T(8,128)(2,1)S(1)} %get-tuple-element.83.refs_3_), channel_id=1, source_target_pairs={{0,8},{1,9},{2,10},{3,11},{4,12},{5,13},{6,14},{7,15},{8,0},{9,1},... | collective-permute-start | bytes 393224 | tf_op jit(solution)/shard_map/ppermute | solution.py:276
  8.3 2.4 %collective-permute-done.1 = bf16[128,512]{1,0:T(8,128)(2,1)S(1)} collective-permute-done((bf16[128,512]{1,0:T(8,128)(2,1)S(1)}, bf16[128,512]{1,0:T(8,128)(2,1)S(1)}, u32[]{:S(2)}, u32[]{:S(2)}) %collective-permute-start.1) | collective-permute-done | bytes 131104 | tf_op jit(solution)/shard_map/ppermute | solution.py:276
  10.7 3.3 %collective-permute-done.2 = bf16[128,512]{1,0:T(8,128)(2,1)S(1)} collective-permute-done((bf16[128,512]{1,0:T(8,128)(2,1)S(1)}, bf16[128,512]{1,0:T(8,128)(2,1)S(1)}, u32[]{:S(2)}, u32[]{:S(2)}) %collective-permute-start.2) | collective-permute-done | bytes 131104 | tf_op jit(solution)/shard_map/ppermute | solution.py:276
  15.2 2.6 %collective-permute-start.5 = (bf16[1,128,512]{2,1,0:T(8,128)(2,1)S(1)}, bf16[1,128,512]{2,1,0:T(8,128)(2,1)S(1)}, u32[]{:S(2)}, u32[]{:S(2)}) collective-permute-start(bf16[1,128,512]{2,1,0:T(8,128)(2,1)S(1)} %bitcast.76), channel_id=1, source_target_pairs={{0,6},{1,7},{2,4},{3,5},{4,2},{5,3},{6,0},{7,1},{8,14},{9,15},{10,... | collective-permute-start | bytes 393224 | tf_op jit(solution)/shard_map/ppermute | solution.py:276
  17.9 7.3 %project_load.1 = (bf16[3,256,1024]{2,1,0:T(8,128)(2,1)S(1)}, bf16[3,256,1024]{2,1,0:T(8,128)(2,1)S(1)}, bf16[3,256,1024]{2,1,0:T(8,128)(2,1)S(1)}, bf16[3,256,1...) custom-call(s32[2]{0:T(128)S(1)} %pad_add_fusion.rank_ref, ...), custom_call_target="tpu_custom_call" | custom-call | flops 402653184 | bytes 393216 | tf_op jit(solution)/shard_map/project_load/pallas_call | solution.py:192
  28.0 4.9 %project_mix.3 = bf16[128,256]{1,0:T(8,128)(2,1)S(1)} custom-call(s32[2]{0:T(128)S(1)} %pad_add_fusion.rank_ref, bf16[8,128,512]{2,1,0:T(8,128)(2,1)S(1)} %collective-permute-done.6.refs_0_, f32[1,8192]{1,0:T(1,128)S(1)} %get-tuple-element.95.gain_ref.refs_1_, f32[3,128,256]{2,1,0:T(8,128)S(1)} %get-tuple-element.100.refs_2_, ...), custom_call_target="tpu_custom_call" | custom-call | flops 1610612736 | bytes 1572864 | tf_op jit(solution)/shard_map/project_mix/pallas_call | solution.py:192
  33.8 2.7 %collective-permute-start.9 = (bf16[128,256]{1,0:T(8,128)(2,1)S(1)}, bf16[128,256]{1,0:T(8,128)(2,1)S(1)}, u32[]{:S(2)}, u32[]{:S(2)}) collective-permute-start(bf16[128,256]{1,0:T(8,128)(2,1)S(1)} %project_mix.3), channel_id=1, source_target_pairs={{0,8},{1,9},{2,10},{3,11},{4,12},{5,13},{6,14},{7,15},{8,0},{9,1},... | collective-permute-start | bytes 196616 | tf_op jit(solution)/shard_map/ppermute | solution.py:276
  53.7 2.5 %collective-permute-start.16 = (bf16[128,512]{1,0:T(8,128)(2,1)S(1)}, bf16[128,512]{1,0:T(8,128)(2,1)S(1)}, u32[]{:S(2)}, u32[]{:S(2)}) collective-permute-start(bf16[128,512]{1,0:T(8,128)(2,1)S(1)} %get-tuple-element.116), channel_id=1, source_target_pairs={{0,24},{1,25},{2,26},{3,27},{4,28},{5,29},{6,30},{7,31},{8,16},{9,... | collective-permute-start | bytes 393224 | tf_op jit(solution)/shard_map/ppermute | solution.py:285
  56.2 4.8 %collective-permute-done.14.refs_3_ = bf16[128,512]{1,0:T(8,128)(2,1)S(1)} collective-permute-done((bf16[128,512]{1,0:T(8,128)(2,1)S(1)}, bf16[128,512]{1,0:T(8,128)(2,1)S(1)}, u32[]{:S(2)}, u32[]{:S(2)}) %collective-permute-start.14) | collective-permute-done | bytes 131104 | tf_op jit(solution)/shard_map/ppermute | solution.py:285
  61.0 2.3 %collective-permute-done.16 = bf16[128,512]{1,0:T(8,128)(2,1)S(1)} collective-permute-done((bf16[128,512]{1,0:T(8,128)(2,1)S(1)}, bf16[128,512]{1,0:T(8,128)(2,1)S(1)}, u32[]{:S(2)}, u32[]{:S(2)}) %collective-permute-start.16) | collective-permute-done | bytes 131104 | tf_op jit(solution)/shard_map/ppermute | solution.py:285
  64.1 2.9 %collective-permute-start.19 = (bf16[1,128,512]{2,1,0:T(8,128)(2,1)S(1)}, bf16[1,128,512]{2,1,0:T(8,128)(2,1)S(1)}, u32[]{:S(2)}, u32[]{:S(2)}) collective-permute-start(bf16[1,128,512]{2,1,0:T(8,128)(2,1)S(1)} %bitcast.82), channel_id=1, source_target_pairs={{0,6},{1,7},{2,4},{3,5},{4,2},{5,3},{6,0},{7,1},{8,14},{9,15},{10,... | collective-permute-start | bytes 393224 | tf_op jit(solution)/shard_map/ppermute | solution.py:276
  69.0 2.4 %collective-permute-done.19 = bf16[1,128,512]{2,1,0:T(8,128)(2,1)S(1)} collective-permute-done((bf16[1,128,512]{2,1,0:T(8,128)(2,1)S(1)}, bf16[1,128,512]{2,1,0:T(8,128)(2,1)S(1)}, u32[]{:S(2)}, u32[]{:S(2)}) %collective-permute-start.19) | collective-permute-done | bytes 131104 | tf_op jit(solution)/shard_map/ppermute | solution.py:276
  71.4 2.6 %collective-permute-done.17 = bf16[3,128,512]{2,1,0:T(8,128)(2,1)S(1)} collective-permute-done((bf16[3,128,512]{2,1,0:T(8,128)(2,1)S(1)}, bf16[3,128,512]{2,1,0:T(8,128)(2,1)S(1)}, u32[]{:S(2)}, u32[]{:S(2)}) %collective-permute-start.17) | collective-permute-done | bytes 393248 | tf_op jit(solution)/shard_map/ppermute | solution.py:276
  76.8 5.1 %project_mix.4 = bf16[128,256]{1,0:T(8,128)(2,1)S(1)} custom-call(s32[2]{0:T(128)S(1)} %pad_add_fusion.rank_ref, bf16[8,128,512]{2,1,0:T(8,128)(2,1)S(1)} %collective-permute-done.20.refs_0_, f32[1,8192]{1,0:T(1,128)S(1)} %get-tuple-element.95.gain_ref.refs_1_, f32[3,128,256]{2,1,0:T(8,128)S(1)} %get-tuple-element.128.refs_2_, ...), custom_call_target="tpu_custom_call" | custom-call | flops 1610612736 | bytes 1572864 | tf_op jit(solution)/shard_map/project_mix/pallas_call | solution.py:192
  86.8 3.6 %collective-permute-done.23 = bf16[128,256]{1,0:T(8,128)(2,1)S(1)} collective-permute-done((bf16[128,256]{1,0:T(8,128)(2,1)S(1)}, bf16[128,256]{1,0:T(8,128)(2,1)S(1)}, u32[]{:S(2)}, u32[]{:S(2)}) %collective-permute-start.23) | collective-permute-done | bytes 65568 | tf_op jit(solution)/shard_map/ppermute | solution.py:276
  100.5 3.3 %collective-permute-start.28 = (bf16[128,512]{1,0:T(8,128)(2,1)S(1)}, bf16[128,512]{1,0:T(8,128)(2,1)S(1)}, u32[]{:S(2)}, u32[]{:S(2)}) collective-permute-start(bf16[128,512]{1,0:T(8,128)(2,1)S(1)} %get-tuple-element.139), channel_id=1, source_target_pairs={{0,16},{1,17},{2,18},{3,19},{4,20},{5,21},{6,22},{7,23},{8,24},{9,... | collective-permute-start | bytes 393224 | tf_op jit(solution)/shard_map/ppermute | solution.py:285
  104.1 2.6 %collective-permute-start.30 = (bf16[128,512]{1,0:T(8,128)(2,1)S(1)}, bf16[128,512]{1,0:T(8,128)(2,1)S(1)}, u32[]{:S(2)}, u32[]{:S(2)}) collective-permute-start(bf16[128,512]{1,0:T(8,128)(2,1)S(1)} %get-tuple-element.139), channel_id=1, source_target_pairs={{0,24},{1,25},{2,26},{3,27},{4,28},{5,29},{6,30},{7,31},{8,16},{9,... | collective-permute-start | bytes 393224 | tf_op jit(solution)/shard_map/ppermute | solution.py:285
  106.7 6.5 %collective-permute-done.28.refs_3_ = bf16[128,512]{1,0:T(8,128)(2,1)S(1)} collective-permute-done((bf16[128,512]{1,0:T(8,128)(2,1)S(1)}, bf16[128,512]{1,0:T(8,128)(2,1)S(1)}, u32[]{:S(2)}, u32[]{:S(2)}) %collective-permute-start.28) | collective-permute-done | bytes 131104 | tf_op jit(solution)/shard_map/ppermute | solution.py:285
  115.1 2.5 %collective-permute-start.33 = (bf16[1,128,512]{2,1,0:T(8,128)(2,1)S(1)}, bf16[1,128,512]{2,1,0:T(8,128)(2,1)S(1)}, u32[]{:S(2)}, u32[]{:S(2)}) collective-permute-start(bf16[1,128,512]{2,1,0:T(8,128)(2,1)S(1)} %bitcast.85), channel_id=1, source_target_pairs={{0,6},{1,7},{2,4},{3,5},{4,2},{5,3},{6,0},{7,1},{8,14},{9,15},{10,... | collective-permute-start | bytes 393224 | tf_op jit(solution)/shard_map/ppermute | solution.py:276
  122.1 3.1 %collective-permute-done.31 = bf16[3,128,512]{2,1,0:T(8,128)(2,1)S(1)} collective-permute-done((bf16[3,128,512]{2,1,0:T(8,128)(2,1)S(1)}, bf16[3,128,512]{2,1,0:T(8,128)(2,1)S(1)}, u32[]{:S(2)}, u32[]{:S(2)}) %collective-permute-start.31) | collective-permute-done | bytes 393248 | tf_op jit(solution)/shard_map/ppermute | solution.py:276
  127.9 4.9 %project_mix.5 = bf16[128,256]{1,0:T(8,128)(2,1)S(1)} custom-call(s32[2]{0:T(128)S(1)} %pad_add_fusion.rank_ref, bf16[8,128,512]{2,1,0:T(8,128)(2,1)S(1)} %collective-permute-done.34.refs_0_, f32[1,8192]{1,0:T(1,128)S(1)} %get-tuple-element.95.gain_ref.refs_1_, f32[3,128,256]{2,1,0:T(8,128)S(1)} %get-tuple-element.151.refs_2_, ...), custom_call_target="tpu_custom_call" | custom-call | flops 1610612736 | bytes 1572864 | tf_op jit(solution)/shard_map/project_mix/pallas_call | solution.py:192
  133.4 2.2 %collective-permute-start.36 = (bf16[128,256]{1,0:T(8,128)(2,1)S(1)}, bf16[128,256]{1,0:T(8,128)(2,1)S(1)}, u32[]{:S(2)}, u32[]{:S(2)}) collective-permute-start(bf16[128,256]{1,0:T(8,128)(2,1)S(1)} %project_mix.5), channel_id=1, source_target_pairs={{0,4},{1,5},{2,6},{3,7},{4,0},{5,1},{6,2},{7,3},{8,12},{9,13},{10,... | collective-permute-start | bytes 196616 | tf_op jit(solution)/shard_map/ppermute | solution.py:276
  137.9 3.3 %collective-permute-done.37 = bf16[128,256]{1,0:T(8,128)(2,1)S(1)} collective-permute-done((bf16[128,256]{1,0:T(8,128)(2,1)S(1)}, bf16[128,256]{1,0:T(8,128)(2,1)S(1)}, u32[]{:S(2)}, u32[]{:S(2)}) %collective-permute-start.37) | collective-permute-done | bytes 65568 | tf_op jit(solution)/shard_map/ppermute | solution.py:276
  (129 shorter events, 68.2 us)
Async XLA Ops:
  1.1 7.2 %collective-permute-start = (bf16[128,512]{1,0:T(8,128)(2,1)S(1)}, bf16[128,512]{1,0:T(8,128)(2,1)S(1)}, u32[]{:S(2)}, u32[]{:S(2)}) collective-permute-start(bf16[128,512]{1,0:T(8,128)(2,1)S(1)} %get-tuple-element.83.refs_3_), channel_id=1, source_target_pairs={{0,2},{1,3},{2,0},{3,1},{4,6},{5,7},{6,4},{7,5},{8,10},{9,11},{10,... | collective-permute-start | bytes 393224 | tf_op jit(solution)/shard_map/ppermute | solution.py:276
  4.1 6.7 %collective-permute-start.1 = (bf16[128,512]{1,0:T(8,128)(2,1)S(1)}, bf16[128,512]{1,0:T(8,128)(2,1)S(1)}, u32[]{:S(2)}, u32[]{:S(2)}) collective-permute-start(bf16[128,512]{1,0:T(8,128)(2,1)S(1)} %get-tuple-element.83.refs_3_), channel_id=1, source_target_pairs={{0,4},{1,5},{2,6},{3,7},{4,0},{5,1},{6,2},{7,3},{8,12},{9,13},{10,... | collective-permute-start | bytes 393224 | tf_op jit(solution)/shard_map/ppermute | solution.py:276
  5.6 8.4 %collective-permute-start.2 = (bf16[128,512]{1,0:T(8,128)(2,1)S(1)}, bf16[128,512]{1,0:T(8,128)(2,1)S(1)}, u32[]{:S(2)}, u32[]{:S(2)}) collective-permute-start(bf16[128,512]{1,0:T(8,128)(2,1)S(1)} %get-tuple-element.83.refs_3_), channel_id=1, source_target_pairs={{0,8},{1,9},{2,10},{3,11},{4,12},{5,13},{6,14},{7,15},{8,0},{9,1},... | collective-permute-start | bytes 393224 | tf_op jit(solution)/shard_map/ppermute | solution.py:276
  14.2 11.0 %collective-permute-start.3 = (bf16[2,128,512]{2,1,0:T(8,128)(2,1)S(1)}, bf16[2,128,512]{2,1,0:T(8,128)(2,1)S(1)}, u32[]{:S(2)}, u32[]{:S(2)}) collective-permute-start(bf16[2,128,512]{2,1,0:T(8,128)(2,1)S(1)} %pad_maximum_fusion.8), channel_id=1, source_target_pairs={{0,2},{1,3},{2,0},{3,1},{4,6},{5,7},{6,4},{7,5},{8,10},{9,11},{10,... | collective-permute-start | bytes 786440 | tf_op jit(solution)/shard_map/ppermute | solution.py:276
  14.8 10.4 %collective-permute-start.4 = (bf16[1,128,512]{2,1,0:T(8,128)(2,1)S(1)}, bf16[1,128,512]{2,1,0:T(8,128)(2,1)S(1)}, u32[]{:S(2)}, u32[]{:S(2)}) collective-permute-start(bf16[1,128,512]{2,1,0:T(8,128)(2,1)S(1)} %bitcast.75), channel_id=1, source_target_pairs={{0,4},{1,5},{2,6},{3,7},{4,0},{5,1},{6,2},{7,3},{8,12},{9,13},{10,... | collective-permute-start | bytes 393224 | tf_op jit(solution)/shard_map/ppermute | solution.py:276
  15.2 10.0 %collective-permute-start.5 = (bf16[1,128,512]{2,1,0:T(8,128)(2,1)S(1)}, bf16[1,128,512]{2,1,0:T(8,128)(2,1)S(1)}, u32[]{:S(2)}, u32[]{:S(2)}) collective-permute-start(bf16[1,128,512]{2,1,0:T(8,128)(2,1)S(1)} %bitcast.76), channel_id=1, source_target_pairs={{0,6},{1,7},{2,4},{3,5},{4,2},{5,3},{6,0},{7,1},{8,14},{9,15},{10,... | collective-permute-start | bytes 393224 | tf_op jit(solution)/shard_map/ppermute | solution.py:276
  33.8 6.4 %collective-permute-start.9 = (bf16[128,256]{1,0:T(8,128)(2,1)S(1)}, bf16[128,256]{1,0:T(8,128)(2,1)S(1)}, u32[]{:S(2)}, u32[]{:S(2)}) collective-permute-start(bf16[128,256]{1,0:T(8,128)(2,1)S(1)} %project_mix.3), channel_id=1, source_target_pairs={{0,8},{1,9},{2,10},{3,11},{4,12},{5,13},{6,14},{7,15},{8,0},{9,1},... | collective-permute-start | bytes 196616 | tf_op jit(solution)/shard_map/ppermute | solution.py:276
  40.2 5.7 %collective-permute-start.10 = (bf16[2,128,256]{2,1,0:T(8,128)(2,1)S(1)}, bf16[2,128,256]{2,1,0:T(8,128)(2,1)S(1)}, u32[]{:S(2)}, u32[]{:S(2)}) collective-permute-start(bf16[2,128,256]{2,1,0:T(8,128)(2,1)S(1)} %pad_maximum_fusion.9), channel_id=1, source_target_pairs={{0,2},{1,3},{2,0},{3,1},{4,6},{5,7},{6,4},{7,5},{8,10},{9,11},{10,... | collective-permute-start | bytes 393224 | tf_op jit(solution)/shard_map/ppermute | solution.py:276
  42.3 5.2 %collective-permute-start.12 = (bf16[1,128,256]{2,1,0:T(8,128)(2,1)S(1)}, bf16[1,128,256]{2,1,0:T(8,128)(2,1)S(1)}, u32[]{:S(2)}, u32[]{:S(2)}) collective-permute-start(bf16[1,128,256]{2,1,0:T(8,128)(2,1)S(1)} %bitcast.91), channel_id=1, source_target_pairs={{0,6},{1,7},{2,4},{3,5},{4,2},{5,3},{6,0},{7,1},{8,14},{9,15},{10,... | collective-permute-start | bytes 196616 | tf_op jit(solution)/shard_map/ppermute | solution.py:276
  50.6 10.4 %collective-permute-start.14 = (bf16[128,512]{1,0:T(8,128)(2,1)S(1)}, bf16[128,512]{1,0:T(8,128)(2,1)S(1)}, u32[]{:S(2)}, u32[]{:S(2)}) collective-permute-start(bf16[128,512]{1,0:T(8,128)(2,1)S(1)} %get-tuple-element.116), channel_id=1, source_target_pairs={{0,16},{1,17},{2,18},{3,19},{4,20},{5,21},{6,22},{7,23},{8,24},{9,... | collective-permute-start | bytes 393224 | tf_op jit(solution)/shard_map/ppermute | solution.py:285
  52.3 8.8 %collective-permute-start.15 = (bf16[128,512]{1,0:T(8,128)(2,1)S(1)}, bf16[128,512]{1,0:T(8,128)(2,1)S(1)}, u32[]{:S(2)}, u32[]{:S(2)}) collective-permute-start(bf16[128,512]{1,0:T(8,128)(2,1)S(1)} %get-tuple-element.116), channel_id=1, source_target_pairs={{0,20},{1,21},{2,22},{3,23},{4,16},{5,17},{6,18},{7,19},{8,28},{9,... | collective-permute-start | bytes 393224 | tf_op jit(solution)/shard_map/ppermute | solution.py:285
  53.7 9.6 %collective-permute-start.16 = (bf16[128,512]{1,0:T(8,128)(2,1)S(1)}, bf16[128,512]{1,0:T(8,128)(2,1)S(1)}, u32[]{:S(2)}, u32[]{:S(2)}) collective-permute-start(bf16[128,512]{1,0:T(8,128)(2,1)S(1)} %get-tuple-element.116), channel_id=1, source_target_pairs={{0,24},{1,25},{2,26},{3,27},{4,28},{5,29},{6,30},{7,31},{8,16},{9,... | collective-permute-start | bytes 393224 | tf_op jit(solution)/shard_map/ppermute | solution.py:285
  63.4 10.6 %collective-permute-start.17 = (bf16[3,128,512]{2,1,0:T(8,128)(2,1)S(1)}, bf16[3,128,512]{2,1,0:T(8,128)(2,1)S(1)}, u32[]{:S(2)}, u32[]{:S(2)}) collective-permute-start(bf16[3,128,512]{2,1,0:T(8,128)(2,1)S(1)} %get-tuple-element.120), channel_id=1, source_target_pairs={{0,2},{1,3},{2,0},{3,1},{4,6},{5,7},{6,4},{7,5},{8,10},{9,11},{10,... | collective-permute-start | bytes 1179656 | tf_op jit(solution)/shard_map/ppermute | solution.py:276
  64.1 7.3 %collective-permute-start.19 = (bf16[1,128,512]{2,1,0:T(8,128)(2,1)S(1)}, bf16[1,128,512]{2,1,0:T(8,128)(2,1)S(1)}, u32[]{:S(2)}, u32[]{:S(2)}) collective-permute-start(bf16[1,128,512]{2,1,0:T(8,128)(2,1)S(1)} %bitcast.82), channel_id=1, source_target_pairs={{0,6},{1,7},{2,4},{3,5},{4,2},{5,3},{6,0},{7,1},{8,14},{9,15},{10,... | collective-permute-start | bytes 393224 | tf_op jit(solution)/shard_map/ppermute | solution.py:276
  84.5 5.9 %collective-permute-start.23 = (bf16[128,256]{1,0:T(8,128)(2,1)S(1)}, bf16[128,256]{1,0:T(8,128)(2,1)S(1)}, u32[]{:S(2)}, u32[]{:S(2)}) collective-permute-start(bf16[128,256]{1,0:T(8,128)(2,1)S(1)} %project_mix.4), channel_id=1, source_target_pairs={{0,8},{1,9},{2,10},{3,11},{4,12},{5,13},{6,14},{7,15},{8,0},{9,1},... | collective-permute-start | bytes 196616 | tf_op jit(solution)/shard_map/ppermute | solution.py:276
  90.4 5.3 %collective-permute-start.24 = (bf16[2,128,256]{2,1,0:T(8,128)(2,1)S(1)}, bf16[2,128,256]{2,1,0:T(8,128)(2,1)S(1)}, u32[]{:S(2)}, u32[]{:S(2)}) collective-permute-start(bf16[2,128,256]{2,1,0:T(8,128)(2,1)S(1)} %pad_maximum_fusion.10), channel_id=1, source_target_pairs={{0,2},{1,3},{2,0},{3,1},{4,6},{5,7},{6,4},{7,5},{8,10},{9,11},{10,... | collective-permute-start | bytes 393224 | tf_op jit(solution)/shard_map/ppermute | solution.py:276
  100.5 12.6 %collective-permute-start.28 = (bf16[128,512]{1,0:T(8,128)(2,1)S(1)}, bf16[128,512]{1,0:T(8,128)(2,1)S(1)}, u32[]{:S(2)}, u32[]{:S(2)}) collective-permute-start(bf16[128,512]{1,0:T(8,128)(2,1)S(1)} %get-tuple-element.139), channel_id=1, source_target_pairs={{0,16},{1,17},{2,18},{3,19},{4,20},{5,21},{6,22},{7,23},{8,24},{9,... | collective-permute-start | bytes 393224 | tf_op jit(solution)/shard_map/ppermute | solution.py:285
  103.8 9.3 %collective-permute-start.29 = (bf16[128,512]{1,0:T(8,128)(2,1)S(1)}, bf16[128,512]{1,0:T(8,128)(2,1)S(1)}, u32[]{:S(2)}, u32[]{:S(2)}) collective-permute-start(bf16[128,512]{1,0:T(8,128)(2,1)S(1)} %get-tuple-element.139), channel_id=1, source_target_pairs={{0,20},{1,21},{2,22},{3,23},{4,16},{5,17},{6,18},{7,19},{8,28},{9,... | collective-permute-start | bytes 393224 | tf_op jit(solution)/shard_map/ppermute | solution.py:285
  104.1 9.9 %collective-permute-start.30 = (bf16[128,512]{1,0:T(8,128)(2,1)S(1)}, bf16[128,512]{1,0:T(8,128)(2,1)S(1)}, u32[]{:S(2)}, u32[]{:S(2)}) collective-permute-start(bf16[128,512]{1,0:T(8,128)(2,1)S(1)} %get-tuple-element.139), channel_id=1, source_target_pairs={{0,24},{1,25},{2,26},{3,27},{4,28},{5,29},{6,30},{7,31},{8,16},{9,... | collective-permute-start | bytes 393224 | tf_op jit(solution)/shard_map/ppermute | solution.py:285
  114.1 11.1 %collective-permute-start.31 = (bf16[3,128,512]{2,1,0:T(8,128)(2,1)S(1)}, bf16[3,128,512]{2,1,0:T(8,128)(2,1)S(1)}, u32[]{:S(2)}, u32[]{:S(2)}) collective-permute-start(bf16[3,128,512]{2,1,0:T(8,128)(2,1)S(1)} %get-tuple-element.143), channel_id=1, source_target_pairs={{0,2},{1,3},{2,0},{3,1},{4,6},{5,7},{6,4},{7,5},{8,10},{9,11},{10,... | collective-permute-start | bytes 1179656 | tf_op jit(solution)/shard_map/ppermute | solution.py:276
  114.7 5.2 %collective-permute-start.32 = (bf16[1,128,512]{2,1,0:T(8,128)(2,1)S(1)}, bf16[1,128,512]{2,1,0:T(8,128)(2,1)S(1)}, u32[]{:S(2)}, u32[]{:S(2)}) collective-permute-start(bf16[1,128,512]{2,1,0:T(8,128)(2,1)S(1)} %bitcast.84), channel_id=1, source_target_pairs={{0,4},{1,5},{2,6},{3,7},{4,0},{5,1},{6,2},{7,3},{8,12},{9,13},{10,... | collective-permute-start | bytes 393224 | tf_op jit(solution)/shard_map/ppermute | solution.py:276
  115.1 6.9 %collective-permute-start.33 = (bf16[1,128,512]{2,1,0:T(8,128)(2,1)S(1)}, bf16[1,128,512]{2,1,0:T(8,128)(2,1)S(1)}, u32[]{:S(2)}, u32[]{:S(2)}) collective-permute-start(bf16[1,128,512]{2,1,0:T(8,128)(2,1)S(1)} %bitcast.85), channel_id=1, source_target_pairs={{0,6},{1,7},{2,4},{3,5},{4,2},{5,3},{6,0},{7,1},{8,14},{9,15},{10,... | collective-permute-start | bytes 393224 | tf_op jit(solution)/shard_map/ppermute | solution.py:276
  135.6 5.6 %collective-permute-start.37 = (bf16[128,256]{1,0:T(8,128)(2,1)S(1)}, bf16[128,256]{1,0:T(8,128)(2,1)S(1)}, u32[]{:S(2)}, u32[]{:S(2)}) collective-permute-start(bf16[128,256]{1,0:T(8,128)(2,1)S(1)} %project_mix.5), channel_id=1, source_target_pairs={{0,8},{1,9},{2,10},{3,11},{4,12},{5,13},{6,14},{7,15},{8,0},{9,1},... | collective-permute-start | bytes 196616 | tf_op jit(solution)/shard_map/ppermute | solution.py:276
  141.3 5.3 %collective-permute-start.38 = (bf16[2,128,256]{2,1,0:T(8,128)(2,1)S(1)}, bf16[2,128,256]{2,1,0:T(8,128)(2,1)S(1)}, u32[]{:S(2)}, u32[]{:S(2)}) collective-permute-start(bf16[2,128,256]{2,1,0:T(8,128)(2,1)S(1)} %pad_maximum_fusion.11), channel_id=1, source_target_pairs={{0,2},{1,3},{2,0},{3,1},{4,6},{5,7},{6,4},{7,5},{8,10},{9,11},{10,... | collective-permute-start | bytes 393224 | tf_op jit(solution)/shard_map/ppermute | solution.py:276
  (20 other events, 92.6 us)

commit v10 on v9

--- a/solution.py
+++ b/solution.py
@@ -10,6 +10,7 @@
 EPS = 1e-06
 VMEM_LIMIT = 20 * 1024 * 1024
 PAD = 8
+GROUP = 4
 
 
 def split_dp(dp_count):
@@ -24,8 +25,8 @@
 def routes(far, near, cross):
     if (far, near) == (4, 2):
         if cross:
-            return [0, 4, 2], [(1, [4, 2, 0]), (2, [4]), (3, [4])]
-        return [0, 4, 2, 1], [(1, [4, 2]), (2, [4]), (3, [4])]
+            return [4, 2, 0], [(1, [4, 2, 0]), (2, [4]), (3, [4])]
+        return [4, 2, 1, 0], [(1, [4, 2]), (2, [4]), (3, [4])]
     line = [d * near for d in range(far)]
     return line, [(d, line) for d in range(1, near)]
 
@@ -35,26 +36,43 @@
     return pl.ds(pl.multiple_of(((chip ^ cell) * core + (side ^ c)) * size, size), size)
 
 
-def project(blocks, core, values_of, weights_of, rank_ref, gain_ref, acc_ref, sq_ref, ready=None):
+def project(blocks, core, values_of, weights_of, rank_ref, gain_ref, acc_ref, sq_ref, before=None, ready=None):
     lanes = sq_ref.shape[1]
     side = lax.rem(rank_ref[0], core)
-    for n, (cell, c) in enumerate(blocks):
-        values = values_of(n).astype(jnp.float32)
-        feat = values.shape[1]
-        gains = gain_ref[:, columns_of(rank_ref, core, cell, c, feat)]
-        normed = (values * gains).astype(jnp.bfloat16)
-        squares = values * values
-        part = squares[:, :lanes]
-        for m in range(1, feat // lanes):
-            part = part + squares[:, m * lanes : (m + 1) * lanes]
-        sq_ref[...] += part
+    for first in range(0, len(blocks), GROUP):
+        group = range(first, min(first + GROUP, len(blocks)))
+        normed, columns, parts = [], [], []
+        for n in group:
+            cell, c = blocks[n]
+            values = values_of(n).astype(jnp.float32)
+            feat = values.shape[1]
+            gains = gain_ref[:, columns_of(rank_ref, core, cell, c, feat)]
+            normed.append((values * gains).astype(jnp.bfloat16))
+            columns.append(pl.ds(pl.multiple_of((side ^ c) * feat, feat), feat))
+            squares = values * values
+            parts += [squares[:, m : m + lanes] for m in range(0, feat, lanes)]
         if ready is not None:
-            ready(n)
-        inner = pl.ds(pl.multiple_of((side ^ c) * feat, feat), feat)
+            for n in group:
+                ready(n)
+        if first == 0 and before is not None:
+            parts.append(before[1][...])
+        part = functools.reduce(jnp.add, parts)
+        sq_ref[...] = part if first == 0 else sq_ref[...] + part
         for i in range(acc_ref.shape[0]):
-            acc_ref[i] += lax.dot_general(
-                normed, weights_of(n)[i, :, inner], (((1,), (1,)), ((), ())), preferred_element_type=jnp.float32
-            )
+            terms = [
+                lax.dot_general(
+                    normed[n - first],
+                    weights_of(n)[i, :, columns[n - first]],
+                    (((1,), (1,)), ((), ())),
+                    preferred_element_type=jnp.float32,
+                )
+                for n in group
+            ]
+            if first > 0:
+                terms.append(acc_ref[i])
+            elif before is not None:
+                terms.append(before[0][i])
+            acc_ref[i] = functools.reduce(jnp.add, terms)
 
 
 def load_kernel(blocks, order, core, rank_ref, x_ref, w_far, gain_far, taps_far, decay_far, *refs):
@@ -80,30 +98,25 @@
         copy.wait()
     lags = lax.broadcasted_iota(jnp.int32, long_ref.shape, 0).astype(jnp.float32)
     long_ref[...] = taps_ref[...].T * jnp.exp(-decay_ref[...] * lags)
-    acc_ref[...] = jnp.zeros_like(acc_ref)
-    sq_ref[...] = jnp.zeros_like(sq_ref)
 
     def ready(n):
         for copy in copies[n]:
             copy.wait()
 
-    project(blocks, core, lambda n: x_ref[n], lambda n: w_refs[n], rank_ref, gain_ref, acc_ref, sq_ref, ready)
+    project(blocks, core, lambda n: x_ref[n], lambda n: w_refs[n], rank_ref, gain_ref, acc_ref, sq_ref, None, ready)
     for n in range(len(blocks), len(order)):
         ready(n)
 
 
 def first_kernel(blocks, core, rank_ref, x_ref, gain_ref, *refs):
     w_refs, (acc_ref, sq_ref) = refs[:-2], refs[-2:]
-    acc_ref[...] = jnp.zeros_like(acc_ref)
-    sq_ref[...] = jnp.zeros_like(sq_ref)
     project(blocks, core, lambda n: x_ref[n], lambda n: w_refs[n], rank_ref, gain_ref, acc_ref, sq_ref)
 
 
 def more_kernel(blocks, core, rank_ref, x_ref, gain_ref, acc_in, sq_in, *refs):
     w_refs, (acc_ref, sq_ref) = refs[:-2], refs[-2:]
-    acc_ref[...] = acc_in[...]
-    sq_ref[...] = sq_in[...]
-    project(blocks, core, lambda n: x_ref[n], lambda n: w_refs[n], rank_ref, gain_ref, acc_ref, sq_ref)
+    before = (acc_in, sq_in)
+    project(blocks, core, lambda n: x_ref[n], lambda n: w_refs[n], rank_ref, gain_ref, acc_ref, sq_ref, before)
 
 
 def mix_kernel(blocks, core, model_width, rank_ref, *refs):
@@ -113,8 +126,6 @@
     w_refs = refs[5 : 5 + count]
     y_ref, acc_ref, sq_ref, pad_ref, query_ref = refs[5 + count :]
     branches, tok_len, chan = acc_in.shape
-    acc_ref[...] = acc_in[...]
-    sq_ref[...] = sq_in[...]
     project(
         blocks,
         core,
@@ -124,6 +135,7 @@
         gain_ref,
         acc_ref,
         sq_ref,
+        (acc_in, sq_in),
     )
 
     total = jnp.sum(sq_ref[...], axis=1, keepdims=True)
@@ -161,22 +173,31 @@
             y_ref[at, cols] = (query_ref[at, cols] * both).astype(jnp.bfloat16)
 
 
-def out_kernel(blocks, core, rank_ref, *refs):
-    sides, refs = refs[:core], refs[core:]
-    w_ref, own_ref = refs[:2]
-    count, _, chan = sides[0].shape
-    acc_ref = refs[-1]
-    acc_ref[...] = own_ref[...].astype(jnp.float32)
-    for n, (cell, c) in enumerate(blocks):
-        rows = columns_of(rank_ref, core, cell, c, chan)
-        acc_ref[...] += jnp.dot(sides[n // count][n % count], w_ref[rows, :], preferred_element_type=jnp.float32)
-    result = acc_ref[...].astype(jnp.bfloat16)
-    if len(refs) == 4:
-        refs[2][...] = result
-    else:
-        following_ref, result_ref, leaving_ref = refs[2:5]
-        result_ref[...] = result
-        leaving_ref[...] = jnp.where(rank_ref[1] == 1, following_ref[...], result)
+def share_of_out(blocks, core, side_ref, rank_ref, w_ref, total):
+    chan = side_ref.shape[2]
+    for first in range(0, len(blocks), GROUP):
+        terms = []
+        for n in range(first, min(first + GROUP, len(blocks))):
+            rows = columns_of(rank_ref, core, *blocks[n], chan)
+            terms.append(jnp.dot(side_ref[n], w_ref[rows, :], preferred_element_type=jnp.float32))
+        total = functools.reduce(jnp.add, terms, total)
+    return total
+
+
+def out_early_kernel(blocks, core, rank_ref, side_ref, w_ref, own_ref, sum_ref):
+    sum_ref[...] = share_of_out(blocks, core, side_ref, rank_ref, w_ref, own_ref[...].astype(jnp.float32))
+
+
+def out_kernel(blocks, core, tick, rank_ref, *refs):
+    sides, (w_ref, sum_ref, fresh_ref, *result_refs) = refs[: core - 1], refs[core - 1 :]
+    total = sum_ref[...]
+    for c, side_ref in enumerate(sides):
+        count = side_ref.shape[0]
+        total = share_of_out(blocks[c * count : (c + 1) * count], core, side_ref, rank_ref, w_ref, total)
+    result = total.astype(jnp.bfloat16)
+    result_refs[0][...] = result
+    if len(result_refs) > 1:
+        result_refs[1][...] = jnp.where(rank_ref[1] == 1, fresh_ref[tick + 1], result)
 
 
 def in_vmem(count):
@@ -252,15 +273,25 @@
     )[0]
 
 
-def project_out(blocks, core, sides, w_out, own, following, rank):
-    rows, feat = own.shape
-    result = jax.ShapeDtypeStruct((rows, feat), jnp.bfloat16)
+def project_out_early(blocks, core, side, w_out, own, rank):
     return call(
-        functools.partial(out_kernel, blocks, core),
-        [rank, *sides, w_out, own] + ([] if following is None else [following]),
-        [result] if following is None else [result, result],
-        [pltpu.VMEM((rows, feat), jnp.float32)],
-        2 * rows * w_out.shape[0] * feat,
+        functools.partial(out_early_kernel, blocks, core),
+        [rank, side, w_out, own],
+        [jax.ShapeDtypeStruct(own.shape, jnp.float32)],
+        [],
+        2 * side.size * w_out.shape[1],
+        "project_out_early",
+    )[0]
+
+
+def project_out(blocks, core, tick, sides, w_out, total, fresh, rank):
+    result = jax.ShapeDtypeStruct(total.shape, jnp.bfloat16)
+    return call(
+        functools.partial(out_kernel, blocks, core, tick),
+        [rank, *sides, w_out, total, fresh],
+        [result, result] if tick + 1 < fresh.shape[0] else [result],
+        [],
+        total.size * w_out.shape[0],
         "project_out",
     )
 
@@ -290,8 +321,10 @@
     def round_one(source, cross=False):
         first, _ = routes(far, near, cross)
         if cross:
-            return {d: onward(source, d * core) for d in first}
-        return {d: swap(source, d * core) if d else source for d in first}
+            blocks = [onward(source, d * core) for d in first]
+        else:
+            blocks = [swap(source, d * core) if d else source for d in first]
+        return dict(zip(first, lax.optimization_barrier(blocks)))
 
     def round_two(blocks, cross=False):
         _, second = routes(far, near, cross)
@@ -306,7 +339,7 @@
     source = jnp.where(section_idx == 0, fresh_acts[0], carried[0])
     params, made = {}, []
     for k in range(tick_count):
-        blocks = after(round_one(source, k > 0))
+        blocks = round_one(source, k > 0)
         cells, rest = round_two(blocks, k > 0)
         order = [*blocks, *cells]
         direct = jnp.stack(list(blocks.values()))
@@ -323,13 +356,15 @@
         sums = project_part(of_cores(cells, [0]), core, relayed, params, sums, rank)
         sides = after(sides, sums)
         y = mix(of_cores(order, range(1, core)), core, norm_gain.shape[1], sides, params, sums, short_rows, rank)
-        y_blocks = after(round_one(y))
+        y_blocks = round_one(y)
         cells, rest = round_two(y_blocks)
         everything = jnp.concatenate([jnp.stack(list(y_blocks.values())), *rest])
-        sides = [everything] + [swap(everything, c) for c in range(1, core)]
-        following = fresh_acts[k + 1] if k + 1 < tick_count else None
-        around = of_cores([*y_blocks, *cells], range(core))
-        result, *leaving = project_out(around, core, sides, w_out[0], blocks[0], following, rank)
+        sides = [swap(everything, c) for c in range(1, core)]
+        order = [*y_blocks, *cells]
+        total = project_out_early(of_cores(order, [0]), core, everything, w_out[0], blocks[0], rank)
+        sides = after(sides, total)
+        blocks = of_cores(order, range(1, core))
+        result, *leaving = project_out(blocks, core, k, sides, w_out[0], total, fresh_acts, rank)
         made.append(result)
         source = leaving[0] if leaving else None
     return jnp.stack(made)[None]

time: 152 us -> 156 us (1.026)
  Pallas kernels: 34.4 us -> 36.3 us
  starting transfers between devices: 50.9 us -> 52.8 us
    ppermute x36, starting transfers between devices: 39.1 us -> 42.1 us  [swap(): return lax.ppermute(value, 'dp', [(r, r ^ offset) for r in range(dp_count)])]
    ppermute x6, waiting for transfers between devices: 14.4 us -> 16.3 us  [onward(): return lax.ppermute(value, ('section', 'dp'), pairs)]
    pallas_call x12 -> x15, Pallas kernels: 34.4 us -> 36.3 us  [call(): pl.pallas_call(kernel, in_specs=specs, out_specs=in_vmem(len(outs)), out_...]
  transfers between devices with their start and end apart: 42 -> 42, of which waited for: 36 -> 34; matrix products, arithmetic and copies ran while one was open for 0% -> 0% of each run, Pallas kernels for 10% -> 10%
where the time goes in v10:
time: 156 us
  waiting for transfers between devices  63.8 us (41%)
  starting transfers between devices  52.8 us (34%)
  Pallas kernels  36.3 us (23%)
  other arithmetic  2.25 us (1%)
    ppermute x36, waiting for transfers between devices, swap(): return lax.ppermute(value, 'dp', [(r, r ^ offset) for r in range(dp_count)])  47.6 us
    ppermute x36, starting transfers between devices, swap(): return lax.ppermute(value, 'dp', [(r, r ^ offset) for r in range(dp_count)])  42.1 us
    pallas_call x15, Pallas kernels, call(): pl.pallas_call(kernel, in_specs=specs, out_specs=in_vmem(len(outs)), out_...  36.3 us
    ppermute x6, waiting for transfers between devices, onward(): return lax.ppermute(value, ('section', 'dp'), pairs)  16.3 us
    ppermute x6, starting transfers between devices, onward(): return lax.ppermute(value, ('section', 'dp'), pairs)  10.7 us
  transfers between devices with their start and end apart: 42, of which 34 were waited for; matrix products, arithmetic and copies ran while one was open for 0% of the time, Pallas kernels for 10%

profile of v10, /device:TPU:0, one launch (start us, length us, event | category | flops | bytes accessed | tf_op | source)
XLA Modules:
  0.0 156.0 jit_solution(9607413394862828359)
XLA Ops:
  0.9 4.1 %collective-permute-start = (bf16[128,512]{1,0:T(8,128)(2,1)S(1)}, bf16[128,512]{1,0:T(8,128)(2,1)S(1)}, u32[]{:S(2)}, u32[]{:S(2)}) collective-permute-start(bf16[128,512]{1,0:T(8,128)(2,1)S(1)} %select_bitcast_fusion.own_ref), channel_id=1, source_target_pairs={{0,8},{1,9},{2,10},{3,11},{4,12},{5,13},{6,14},{7,15},{8,0},{9,1},... | collective-permute-start | bytes 393224 | tf_op jit(solution)/shard_map/ppermute | solution.py:307
  8.2 3.3 %collective-permute-done = bf16[128,512]{1,0:T(8,128)(2,1)S(1)} collective-permute-done((bf16[128,512]{1,0:T(8,128)(2,1)S(1)}, bf16[128,512]{1,0:T(8,128)(2,1)S(1)}, u32[]{:S(2)}, u32[]{:S(2)}) %collective-permute-start) | collective-permute-done | bytes 131104 | tf_op jit(solution)/shard_map/ppermute | solution.py:307
  15.4 6.7 %project_load.1 = (bf16[3,256,1024]{2,1,0:T(8,128)(2,1)S(1)}, bf16[3,256,1024]{2,1,0:T(8,128)(2,1)S(1)}, bf16[3,256,1024]{2,1,0:T(8,128)(2,1)S(1)}, bf16[3,256,1...) custom-call(s32[2]{0:T(128)S(1)} %pad_add_fusion.rank_ref, ...), custom_call_target="tpu_custom_call" | custom-call | flops 402653184 | bytes 393216 | tf_op jit(solution)/shard_map/project_load/pallas_call | solution.py:213
  24.9 4.9 %project_mix.3 = bf16[128,256]{1,0:T(8,128)(2,1)S(1)} custom-call(s32[2]{0:T(128)S(1)} %pad_add_fusion.rank_ref, bf16[8,128,512]{2,1,0:T(8,128)(2,1)S(1)} %collective-permute-done.6.refs_0_, f32[1,8192]{1,0:T(1,128)S(1)} %get-tuple-element.98.gain_ref.refs_1_, f32[3,128,256]{2,1,0:T(8,128)S(1)} %get-tuple-element.103.refs_2_, ...), custom_call_target="tpu_custom_call" | custom-call | flops 1610612736 | bytes 1572864 | tf_op jit(solution)/shard_map/project_mix/pallas_call | solution.py:213
  31.7 2.7 %collective-permute-start.8 = (bf16[128,256]{1,0:T(8,128)(2,1)S(1)}, bf16[128,256]{1,0:T(8,128)(2,1)S(1)}, u32[]{:S(2)}, u32[]{:S(2)}) collective-permute-start(bf16[128,256]{1,0:T(8,128)(2,1)S(1)} %project_mix.3), channel_id=1, source_target_pairs={{0,4},{1,5},{2,6},{3,7},{4,0},{5,1},{6,2},{7,3},{8,12},{9,13},{10,... | collective-permute-start | bytes 196616 | tf_op jit(solution)/shard_map/ppermute | solution.py:307
  48.3 2.6 %collective-permute-start.14 = (bf16[128,512]{1,0:T(8,128)(2,1)S(1)}, bf16[128,512]{1,0:T(8,128)(2,1)S(1)}, u32[]{:S(2)}, u32[]{:S(2)}) collective-permute-start(bf16[128,512]{1,0:T(8,128)(2,1)S(1)} %get-tuple-element.120), channel_id=1, source_target_pairs={{0,24},{1,25},{2,26},{3,27},{4,28},{5,29},{6,30},{7,31},{8,16},{9,... | collective-permute-start | bytes 393224 | tf_op jit(solution)/shard_map/ppermute | solution.py:316
  53.0 5.6 %collective-permute-done.14 = bf16[128,512]{1,0:T(8,128)(2,1)S(1)} collective-permute-done((bf16[128,512]{1,0:T(8,128)(2,1)S(1)}, bf16[128,512]{1,0:T(8,128)(2,1)S(1)}, u32[]{:S(2)}, u32[]{:S(2)}) %collective-permute-start.14) | collective-permute-done | bytes 131104 | tf_op jit(solution)/shard_map/ppermute | solution.py:316
  58.7 2.7 %collective-permute-done.16.own_ref = bf16[128,512]{1,0:T(8,128)(2,1)S(1)} collective-permute-done((bf16[128,512]{1,0:T(8,128)(2,1)S(1)}, bf16[128,512]{1,0:T(8,128)(2,1)S(1)}, u32[]{:S(2)}, u32[]{:S(2)}) %collective-permute-start.16) | collective-permute-done | bytes 131104 | tf_op jit(solution)/shard_map/ppermute | solution.py:316
  66.5 3.8 %collective-permute-done.18 = bf16[1,128,512]{2,1,0:T(8,128)(2,1)S(1)} collective-permute-done((bf16[1,128,512]{2,1,0:T(8,128)(2,1)S(1)}, bf16[1,128,512]{2,1,0:T(8,128)(2,1)S(1)}, u32[]{:S(2)}, u32[]{:S(2)}) %collective-permute-start.18) | collective-permute-done | bytes 131104 | tf_op jit(solution)/shard_map/ppermute | solution.py:307
  70.4 2.4 %collective-permute-done.19 = bf16[1,128,512]{2,1,0:T(8,128)(2,1)S(1)} collective-permute-done((bf16[1,128,512]{2,1,0:T(8,128)(2,1)S(1)}, bf16[1,128,512]{2,1,0:T(8,128)(2,1)S(1)}, u32[]{:S(2)}, u32[]{:S(2)}) %collective-permute-start.19) | collective-permute-done | bytes 131104 | tf_op jit(solution)/shard_map/ppermute | solution.py:307
  72.7 4.1 %collective-permute-done.17 = bf16[3,128,512]{2,1,0:T(8,128)(2,1)S(1)} collective-permute-done((bf16[3,128,512]{2,1,0:T(8,128)(2,1)S(1)}, bf16[3,128,512]{2,1,0:T(8,128)(2,1)S(1)}, u32[]{:S(2)}, u32[]{:S(2)}) %collective-permute-start.17) | collective-permute-done | bytes 393248 | tf_op jit(solution)/shard_map/ppermute | solution.py:307
  77.1 2.0 %project_more.4 = (f32[3,128,256]{2,1,0:T(8,128)S(1)}, f32[128,128]{1,0:T(8,128)S(1)}) custom-call(s32[2]{0:T(128)S(1)} %pad_add_fusion.rank_ref, bf16[5,128,512]{2,1,0:T(8,128)(2,1)S(1)} %pad_maximum_fusion.x_ref, f32[1,8192]{1,0:T(1,128)S(1)} %get-tuple-element.98.gain_ref.refs_1_, f32[3,128,256]{2,1,0:T(8,128)S(1)} %get-tuple-element.127.acc_in, ...), custom_call_target="tpu_custom_call" | custom-call | flops 503316480 | bytes 491520 | tf_op jit(solution)/shard_map/project_more/pallas_call | solution.py:213
  79.6 5.1 %project_mix.4 = bf16[128,256]{1,0:T(8,128)(2,1)S(1)} custom-call(s32[2]{0:T(128)S(1)} %pad_add_fusion.rank_ref, bf16[8,128,512]{2,1,0:T(8,128)(2,1)S(1)} %collective-permute-done.20.refs_0_, f32[1,8192]{1,0:T(1,128)S(1)} %get-tuple-element.98.gain_ref.refs_1_, f32[3,128,256]{2,1,0:T(8,128)S(1)} %get-tuple-element.132.refs_2_, ...), custom_call_target="tpu_custom_call" | custom-call | flops 1610612736 | bytes 1572864 | tf_op jit(solution)/shard_map/project_mix/pallas_call | solution.py:213
  88.3 2.5 %collective-permute-done.21 = bf16[128,256]{1,0:T(8,128)(2,1)S(1)} collective-permute-done((bf16[128,256]{1,0:T(8,128)(2,1)S(1)}, bf16[128,256]{1,0:T(8,128)(2,1)S(1)}, u32[]{:S(2)}, u32[]{:S(2)}) %collective-permute-start.21) | collective-permute-done | bytes 65568 | tf_op jit(solution)/shard_map/ppermute | solution.py:307
  95.0 2.3 %collective-permute-done.24 = bf16[2,128,256]{2,1,0:T(8,128)(2,1)S(1)} collective-permute-done((bf16[2,128,256]{2,1,0:T(8,128)(2,1)S(1)}, bf16[2,128,256]{2,1,0:T(8,128)(2,1)S(1)}, u32[]{:S(2)}, u32[]{:S(2)}) %collective-permute-start.24) | collective-permute-done | bytes 131104 | tf_op jit(solution)/shard_map/ppermute | solution.py:307
  101.2 3.3 %collective-permute-start.28 = (bf16[128,512]{1,0:T(8,128)(2,1)S(1)}, bf16[128,512]{1,0:T(8,128)(2,1)S(1)}, u32[]{:S(2)}, u32[]{:S(2)}) collective-permute-start(bf16[128,512]{1,0:T(8,128)(2,1)S(1)} %get-tuple-element.144), channel_id=1, source_target_pairs={{0,24},{1,25},{2,26},{3,27},{4,28},{5,29},{6,30},{7,31},{8,16},{9,... | collective-permute-start | bytes 393224 | tf_op jit(solution)/shard_map/ppermute | solution.py:316
  107.2 4.3 %collective-permute-done.28 = bf16[128,512]{1,0:T(8,128)(2,1)S(1)} collective-permute-done((bf16[128,512]{1,0:T(8,128)(2,1)S(1)}, bf16[128,512]{1,0:T(8,128)(2,1)S(1)}, u32[]{:S(2)}, u32[]{:S(2)}) %collective-permute-start.28) | collective-permute-done | bytes 131104 | tf_op jit(solution)/shard_map/ppermute | solution.py:316
  112.5 2.6 %collective-permute-done.30.own_ref = bf16[128,512]{1,0:T(8,128)(2,1)S(1)} collective-permute-done((bf16[128,512]{1,0:T(8,128)(2,1)S(1)}, bf16[128,512]{1,0:T(8,128)(2,1)S(1)}, u32[]{:S(2)}, u32[]{:S(2)}) %collective-permute-start.30) | collective-permute-done | bytes 131104 | tf_op jit(solution)/shard_map/ppermute | solution.py:316
  120.3 4.6 %collective-permute-done.32 = bf16[1,128,512]{2,1,0:T(8,128)(2,1)S(1)} collective-permute-done((bf16[1,128,512]{2,1,0:T(8,128)(2,1)S(1)}, bf16[1,128,512]{2,1,0:T(8,128)(2,1)S(1)}, u32[]{:S(2)}, u32[]{:S(2)}) %collective-permute-start.32) | collective-permute-done | bytes 131104 | tf_op jit(solution)/shard_map/ppermute | solution.py:307
  126.3 4.3 %collective-permute-done.31 = bf16[3,128,512]{2,1,0:T(8,128)(2,1)S(1)} collective-permute-done((bf16[3,128,512]{2,1,0:T(8,128)(2,1)S(1)}, bf16[3,128,512]{2,1,0:T(8,128)(2,1)S(1)}, u32[]{:S(2)}, u32[]{:S(2)}) %collective-permute-start.31) | collective-permute-done | bytes 393248 | tf_op jit(solution)/shard_map/ppermute | solution.py:307
  130.8 2.0 %project_more.5 = (f32[3,128,256]{2,1,0:T(8,128)S(1)}, f32[128,128]{1,0:T(8,128)S(1)}) custom-call(s32[2]{0:T(128)S(1)} %pad_add_fusion.rank_ref, bf16[5,128,512]{2,1,0:T(8,128)(2,1)S(1)} %pad_maximum_fusion.1.x_ref, f32[1,8192]{1,0:T(1,128)S(1)} %get-tuple-element.98.gain_ref.refs_1_, f32[3,128,256]{2,1,0:T(8,128)S(1)} %get-tuple-element.151.acc_in, ...), custom_call_target="tpu_custom_call" | custom-call | flops 503316480 | bytes 491520 | tf_op jit(solution)/shard_map/project_more/pallas_call | solution.py:213
  133.4 4.9 %project_mix.5 = bf16[128,256]{1,0:T(8,128)(2,1)S(1)} custom-call(s32[2]{0:T(128)S(1)} %pad_add_fusion.rank_ref, bf16[8,128,512]{2,1,0:T(8,128)(2,1)S(1)} %collective-permute-done.34.refs_0_, f32[1,8192]{1,0:T(1,128)S(1)} %get-tuple-element.98.gain_ref.refs_1_, f32[3,128,256]{2,1,0:T(8,128)S(1)} %get-tuple-element.156.refs_2_, ...), custom_call_target="tpu_custom_call" | custom-call | flops 1610612736 | bytes 1572864 | tf_op jit(solution)/shard_map/project_mix/pallas_call | solution.py:213
  142.1 2.7 %collective-permute-done.35 = bf16[128,256]{1,0:T(8,128)(2,1)S(1)} collective-permute-done((bf16[128,256]{1,0:T(8,128)(2,1)S(1)}, bf16[128,256]{1,0:T(8,128)(2,1)S(1)}, u32[]{:S(2)}, u32[]{:S(2)}) %collective-permute-start.35) | collective-permute-done | bytes 65568 | tf_op jit(solution)/shard_map/ppermute | solution.py:307
  148.7 2.2 %collective-permute-done.38 = bf16[2,128,256]{2,1,0:T(8,128)(2,1)S(1)} collective-permute-done((bf16[2,128,256]{2,1,0:T(8,128)(2,1)S(1)}, bf16[2,128,256]{2,1,0:T(8,128)(2,1)S(1)}, u32[]{:S(2)}, u32[]{:S(2)}) %collective-permute-start.38) | collective-permute-done | bytes 131104 | tf_op jit(solution)/shard_map/ppermute | solution.py:307
  (134 shorter events, 69.8 us)
Async XLA Ops:
  0.9 10.5 %collective-permute-start = (bf16[128,512]{1,0:T(8,128)(2,1)S(1)}, bf16[128,512]{1,0:T(8,128)(2,1)S(1)}, u32[]{:S(2)}, u32[]{:S(2)}) collective-permute-start(bf16[128,512]{1,0:T(8,128)(2,1)S(1)} %select_bitcast_fusion.own_ref), channel_id=1, source_target_pairs={{0,8},{1,9},{2,10},{3,11},{4,12},{5,13},{6,14},{7,15},{8,0},{9,1},... | collective-permute-start | bytes 393224 | tf_op jit(solution)/shard_map/ppermute | solution.py:307
  5.0 6.6 %collective-permute-start.1 = (bf16[128,512]{1,0:T(8,128)(2,1)S(1)}, bf16[128,512]{1,0:T(8,128)(2,1)S(1)}, u32[]{:S(2)}, u32[]{:S(2)}) collective-permute-start(bf16[128,512]{1,0:T(8,128)(2,1)S(1)} %select_bitcast_fusion.own_ref), channel_id=1, source_target_pairs={{0,4},{1,5},{2,6},{3,7},{4,0},{5,1},{6,2},{7,3},{8,12},{9,13},{10,... | collective-permute-start | bytes 393224 | tf_op jit(solution)/shard_map/ppermute | solution.py:307
  11.7 10.4 %collective-permute-start.3 = (bf16[2,128,512]{2,1,0:T(8,128)(2,1)S(1)}, bf16[2,128,512]{2,1,0:T(8,128)(2,1)S(1)}, u32[]{:S(2)}, u32[]{:S(2)}) collective-permute-start(bf16[2,128,512]{2,1,0:T(8,128)(2,1)S(1)} %pad_maximum_fusion.6), channel_id=1, source_target_pairs={{0,2},{1,3},{2,0},{3,1},{4,6},{5,7},{6,4},{7,5},{8,10},{9,11},{10,... | collective-permute-start | bytes 786440 | tf_op jit(solution)/shard_map/ppermute | solution.py:307
  13.3 8.8 %collective-permute-start.4 = (bf16[1,128,512]{2,1,0:T(8,128)(2,1)S(1)}, bf16[1,128,512]{2,1,0:T(8,128)(2,1)S(1)}, u32[]{:S(2)}, u32[]{:S(2)}) collective-permute-start(bf16[1,128,512]{2,1,0:T(8,128)(2,1)S(1)} %bitcast.74), channel_id=1, source_target_pairs={{0,4},{1,5},{2,6},{3,7},{4,0},{5,1},{6,2},{7,3},{8,12},{9,13},{10,... | collective-permute-start | bytes 393224 | tf_op jit(solution)/shard_map/ppermute | solution.py:307
  14.7 7.4 %collective-permute-start.5 = (bf16[1,128,512]{2,1,0:T(8,128)(2,1)S(1)}, bf16[1,128,512]{2,1,0:T(8,128)(2,1)S(1)}, u32[]{:S(2)}, u32[]{:S(2)}) collective-permute-start(bf16[1,128,512]{2,1,0:T(8,128)(2,1)S(1)} %bitcast.75), channel_id=1, source_target_pairs={{0,6},{1,7},{2,4},{3,5},{4,2},{5,3},{6,0},{7,1},{8,14},{9,15},{10,... | collective-permute-start | bytes 393224 | tf_op jit(solution)/shard_map/ppermute | solution.py:307
  29.8 6.4 %collective-permute-start.7 = (bf16[128,256]{1,0:T(8,128)(2,1)S(1)}, bf16[128,256]{1,0:T(8,128)(2,1)S(1)}, u32[]{:S(2)}, u32[]{:S(2)}) collective-permute-start(bf16[128,256]{1,0:T(8,128)(2,1)S(1)} %project_mix.3), channel_id=1, source_target_pairs={{0,8},{1,9},{2,10},{3,11},{4,12},{5,13},{6,14},{7,15},{8,0},{9,1},... | collective-permute-start | bytes 196616 | tf_op jit(solution)/shard_map/ppermute | solution.py:307
  38.7 5.3 %collective-permute-start.10 = (bf16[2,128,256]{2,1,0:T(8,128)(2,1)S(1)}, bf16[2,128,256]{2,1,0:T(8,128)(2,1)S(1)}, u32[]{:S(2)}, u32[]{:S(2)}) collective-permute-start(bf16[2,128,256]{2,1,0:T(8,128)(2,1)S(1)} %pad_maximum_fusion.7), channel_id=1, source_target_pairs={{0,2},{1,3},{2,0},{3,1},{4,6},{5,7},{6,4},{7,5},{8,10},{9,11},{10,... | collective-permute-start | bytes 393224 | tf_op jit(solution)/shard_map/ppermute | solution.py:307
  48.3 10.3 %collective-permute-start.14 = (bf16[128,512]{1,0:T(8,128)(2,1)S(1)}, bf16[128,512]{1,0:T(8,128)(2,1)S(1)}, u32[]{:S(2)}, u32[]{:S(2)}) collective-permute-start(bf16[128,512]{1,0:T(8,128)(2,1)S(1)} %get-tuple-element.120), channel_id=1, source_target_pairs={{0,24},{1,25},{2,26},{3,27},{4,28},{5,29},{6,30},{7,31},{8,16},{9,... | collective-permute-start | bytes 393224 | tf_op jit(solution)/shard_map/ppermute | solution.py:316
  50.9 7.7 %collective-permute-start.15 = (bf16[128,512]{1,0:T(8,128)(2,1)S(1)}, bf16[128,512]{1,0:T(8,128)(2,1)S(1)}, u32[]{:S(2)}, u32[]{:S(2)}) collective-permute-start(bf16[128,512]{1,0:T(8,128)(2,1)S(1)} %get-tuple-element.120), channel_id=1, source_target_pairs={{0,20},{1,21},{2,22},{3,23},{4,16},{5,17},{6,18},{7,19},{8,28},{9,... | collective-permute-start | bytes 393224 | tf_op jit(solution)/shard_map/ppermute | solution.py:316
  51.5 9.8 %collective-permute-start.16 = (bf16[128,512]{1,0:T(8,128)(2,1)S(1)}, bf16[128,512]{1,0:T(8,128)(2,1)S(1)}, u32[]{:S(2)}, u32[]{:S(2)}) collective-permute-start(bf16[128,512]{1,0:T(8,128)(2,1)S(1)} %get-tuple-element.120), channel_id=1, source_target_pairs={{0,16},{1,17},{2,18},{3,19},{4,20},{5,21},{6,22},{7,23},{8,24},{9,... | collective-permute-start | bytes 393224 | tf_op jit(solution)/shard_map/ppermute | solution.py:316
  62.9 13.9 %collective-permute-start.17 = (bf16[3,128,512]{2,1,0:T(8,128)(2,1)S(1)}, bf16[3,128,512]{2,1,0:T(8,128)(2,1)S(1)}, u32[]{:S(2)}, u32[]{:S(2)}) collective-permute-start(bf16[3,128,512]{2,1,0:T(8,128)(2,1)S(1)} %pad_maximum_fusion.4.x_ref), channel_id=1, source_target_pairs={{0,2},{1,3},{2,0},{3,1},{4,6},{5,7},{6,4},{7,5},{8,10},{9,11},{10,... | collective-permute-start | bytes 1179656 | tf_op jit(solution)/shard_map/ppermute | solution.py:307
  64.2 6.1 %collective-permute-start.18 = (bf16[1,128,512]{2,1,0:T(8,128)(2,1)S(1)}, bf16[1,128,512]{2,1,0:T(8,128)(2,1)S(1)}, u32[]{:S(2)}, u32[]{:S(2)}) collective-permute-start(bf16[1,128,512]{2,1,0:T(8,128)(2,1)S(1)} %bitcast.80), channel_id=1, source_target_pairs={{0,4},{1,5},{2,6},{3,7},{4,0},{5,1},{6,2},{7,3},{8,12},{9,13},{10,... | collective-permute-start | bytes 393224 | tf_op jit(solution)/shard_map/ppermute | solution.py:307
  65.6 7.2 %collective-permute-start.19 = (bf16[1,128,512]{2,1,0:T(8,128)(2,1)S(1)}, bf16[1,128,512]{2,1,0:T(8,128)(2,1)S(1)}, u32[]{:S(2)}, u32[]{:S(2)}) collective-permute-start(bf16[1,128,512]{2,1,0:T(8,128)(2,1)S(1)} %bitcast.81), channel_id=1, source_target_pairs={{0,6},{1,7},{2,4},{3,5},{4,2},{5,3},{6,0},{7,1},{8,14},{9,15},{10,... | collective-permute-start | bytes 393224 | tf_op jit(solution)/shard_map/ppermute | solution.py:307
  84.7 6.0 %collective-permute-start.21 = (bf16[128,256]{1,0:T(8,128)(2,1)S(1)}, bf16[128,256]{1,0:T(8,128)(2,1)S(1)}, u32[]{:S(2)}, u32[]{:S(2)}) collective-permute-start(bf16[128,256]{1,0:T(8,128)(2,1)S(1)} %project_mix.4), channel_id=1, source_target_pairs={{0,8},{1,9},{2,10},{3,11},{4,12},{5,13},{6,14},{7,15},{8,0},{9,1},... | collective-permute-start | bytes 196616 | tf_op jit(solution)/shard_map/ppermute | solution.py:307
  91.4 5.9 %collective-permute-start.24 = (bf16[2,128,256]{2,1,0:T(8,128)(2,1)S(1)}, bf16[2,128,256]{2,1,0:T(8,128)(2,1)S(1)}, u32[]{:S(2)}, u32[]{:S(2)}) collective-permute-start(bf16[2,128,256]{2,1,0:T(8,128)(2,1)S(1)} %pad_maximum_fusion.8), channel_id=1, source_target_pairs={{0,2},{1,3},{2,0},{3,1},{4,6},{5,7},{6,4},{7,5},{8,10},{9,11},{10,... | collective-permute-start | bytes 393224 | tf_op jit(solution)/shard_map/ppermute | solution.py:307
  101.2 10.4 %collective-permute-start.28 = (bf16[128,512]{1,0:T(8,128)(2,1)S(1)}, bf16[128,512]{1,0:T(8,128)(2,1)S(1)}, u32[]{:S(2)}, u32[]{:S(2)}) collective-permute-start(bf16[128,512]{1,0:T(8,128)(2,1)S(1)} %get-tuple-element.144), channel_id=1, source_target_pairs={{0,24},{1,25},{2,26},{3,27},{4,28},{5,29},{6,30},{7,31},{8,16},{9,... | collective-permute-start | bytes 393224 | tf_op jit(solution)/shard_map/ppermute | solution.py:316
  104.5 8.0 %collective-permute-start.29 = (bf16[128,512]{1,0:T(8,128)(2,1)S(1)}, bf16[128,512]{1,0:T(8,128)(2,1)S(1)}, u32[]{:S(2)}, u32[]{:S(2)}) collective-permute-start(bf16[128,512]{1,0:T(8,128)(2,1)S(1)} %get-tuple-element.144), channel_id=1, source_target_pairs={{0,20},{1,21},{2,22},{3,23},{4,16},{5,17},{6,18},{7,19},{8,28},{9,... | collective-permute-start | bytes 393224 | tf_op jit(solution)/shard_map/ppermute | solution.py:316
  105.6 9.5 %collective-permute-start.30 = (bf16[128,512]{1,0:T(8,128)(2,1)S(1)}, bf16[128,512]{1,0:T(8,128)(2,1)S(1)}, u32[]{:S(2)}, u32[]{:S(2)}) collective-permute-start(bf16[128,512]{1,0:T(8,128)(2,1)S(1)} %get-tuple-element.144), channel_id=1, source_target_pairs={{0,16},{1,17},{2,18},{3,19},{4,20},{5,21},{6,22},{7,23},{8,24},{9,... | collective-permute-start | bytes 393224 | tf_op jit(solution)/shard_map/ppermute | solution.py:316
  116.7 13.9 %collective-permute-start.31 = (bf16[3,128,512]{2,1,0:T(8,128)(2,1)S(1)}, bf16[3,128,512]{2,1,0:T(8,128)(2,1)S(1)}, u32[]{:S(2)}, u32[]{:S(2)}) collective-permute-start(bf16[3,128,512]{2,1,0:T(8,128)(2,1)S(1)} %pad_maximum_fusion.5.x_ref), channel_id=1, source_target_pairs={{0,2},{1,3},{2,0},{3,1},{4,6},{5,7},{6,4},{7,5},{8,10},{9,11},{10,... | collective-permute-start | bytes 1179656 | tf_op jit(solution)/shard_map/ppermute | solution.py:307
  118.5 6.4 %collective-permute-start.32 = (bf16[1,128,512]{2,1,0:T(8,128)(2,1)S(1)}, bf16[1,128,512]{2,1,0:T(8,128)(2,1)S(1)}, u32[]{:S(2)}, u32[]{:S(2)}) collective-permute-start(bf16[1,128,512]{2,1,0:T(8,128)(2,1)S(1)} %bitcast.83), channel_id=1, source_target_pairs={{0,4},{1,5},{2,6},{3,7},{4,0},{5,1},{6,2},{7,3},{8,12},{9,13},{10,... | collective-permute-start | bytes 393224 | tf_op jit(solution)/shard_map/ppermute | solution.py:307
  118.5 7.9 %collective-permute-start.33 = (bf16[1,128,512]{2,1,0:T(8,128)(2,1)S(1)}, bf16[1,128,512]{2,1,0:T(8,128)(2,1)S(1)}, u32[]{:S(2)}, u32[]{:S(2)}) collective-permute-start(bf16[1,128,512]{2,1,0:T(8,128)(2,1)S(1)} %bitcast.84), channel_id=1, source_target_pairs={{0,6},{1,7},{2,4},{3,5},{4,2},{5,3},{6,0},{7,1},{8,14},{9,15},{10,... | collective-permute-start | bytes 393224 | tf_op jit(solution)/shard_map/ppermute | solution.py:307
  138.3 6.5 %collective-permute-start.35 = (bf16[128,256]{1,0:T(8,128)(2,1)S(1)}, bf16[128,256]{1,0:T(8,128)(2,1)S(1)}, u32[]{:S(2)}, u32[]{:S(2)}) collective-permute-start(bf16[128,256]{1,0:T(8,128)(2,1)S(1)} %project_mix.5), channel_id=1, source_target_pairs={{0,8},{1,9},{2,10},{3,11},{4,12},{5,13},{6,14},{7,15},{8,0},{9,1},... | collective-permute-start | bytes 196616 | tf_op jit(solution)/shard_map/ppermute | solution.py:307
  139.9 5.2 %collective-permute-start.36 = (bf16[128,256]{1,0:T(8,128)(2,1)S(1)}, bf16[128,256]{1,0:T(8,128)(2,1)S(1)}, u32[]{:S(2)}, u32[]{:S(2)}) collective-permute-start(bf16[128,256]{1,0:T(8,128)(2,1)S(1)} %project_mix.5), channel_id=1, source_target_pairs={{0,4},{1,5},{2,6},{3,7},{4,0},{5,1},{6,2},{7,3},{8,12},{9,13},{10,... | collective-permute-start | bytes 196616 | tf_op jit(solution)/shard_map/ppermute | solution.py:307
  145.1 5.7 %collective-permute-start.38 = (bf16[2,128,256]{2,1,0:T(8,128)(2,1)S(1)}, bf16[2,128,256]{2,1,0:T(8,128)(2,1)S(1)}, u32[]{:S(2)}, u32[]{:S(2)}) collective-permute-start(bf16[2,128,256]{2,1,0:T(8,128)(2,1)S(1)} %pad_maximum_fusion.9), channel_id=1, source_target_pairs={{0,2},{1,3},{2,0},{3,1},{4,6},{5,7},{6,4},{7,5},{8,10},{9,11},{10,... | collective-permute-start | bytes 393224 | tf_op jit(solution)/shard_map/ppermute | solution.py:307
  (21 other events, 95.9 us)

commit v11 on v10

--- a/solution.py
+++ b/solution.py
@@ -25,10 +25,10 @@
 def routes(far, near, cross):
     if (far, near) == (4, 2):
         if cross:
-            return [4, 2, 0], [(1, [4, 2, 0]), (2, [4]), (3, [4])]
-        return [4, 2, 1, 0], [(1, [4, 2]), (2, [4]), (3, [4])]
+            return [0, 2, 4], [(1, [2, 4]), (2, [4]), (3, [4])], [1]
+        return [0, 1, 2, 4], [(1, [2, 4]), (2, [4]), (3, [4])], []
     line = [d * near for d in range(far)]
-    return line, [(d, line) for d in range(1, near)]
+    return line, [(d, line) for d in range(1, near)], []
 
 
 def columns_of(rank_ref, core, cell, c, size):
@@ -319,18 +319,20 @@
         return lax.optimization_barrier((value, [x for x in earlier if x is not None]))[0]
 
     def round_one(source, cross=False):
-        first, _ = routes(far, near, cross)
+        first, _, later = routes(far, near, cross)
         if cross:
             blocks = [onward(source, d * core) for d in first]
         else:
             blocks = [swap(source, d * core) if d else source for d in first]
-        return dict(zip(first, lax.optimization_barrier(blocks)))
-
-    def round_two(blocks, cross=False):
-        _, second = routes(far, near, cross)
+        blocks, aside = lax.optimization_barrier((blocks, [swap(source, d * core) for d in later]))
+        return dict(zip(first, blocks)), aside
+
+    def round_two(blocks, aside, cross=False):
+        _, second, later = routes(far, near, cross)
         leaving = lax.optimization_barrier([jnp.stack([blocks[b] for b in sent]) for _, sent in second])
         rest = [swap(payload, d * core) for payload, (d, _) in zip(leaving, second)]
-        return [d ^ b for d, sent in second for b in sent], rest
+        rest += [onward(block, 0)[None] for block in aside]
+        return [d ^ b for d, sent in second for b in sent] + later, rest
 
     def of_cores(cells, cores):
         return [(cell, c) for c in cores for cell in cells]
@@ -339,13 +341,13 @@
     source = jnp.where(section_idx == 0, fresh_acts[0], carried[0])
     params, made = {}, []
     for k in range(tick_count):
-        blocks = round_one(source, k > 0)
-        cells, rest = round_two(blocks, k > 0)
+        blocks, aside = round_one(source, k > 0)
+        cells, rest = round_two(blocks, aside, k > 0)
         order = [*blocks, *cells]
         direct = jnp.stack(list(blocks.values()))
         here = of_cores(blocks, [0])
         if params:
-            sums = project_part(here, core, direct, params, [], rank)
+            sums = project_part(here, core, after(direct, rest[1 % len(rest)]), params, [], rank)
         else:
             sums, params = project_load(
                 here, order, core, direct, w_in[0], norm_gain, filter_taps[0], decay_rate, rank
@@ -356,8 +358,8 @@
         sums = project_part(of_cores(cells, [0]), core, relayed, params, sums, rank)
         sides = after(sides, sums)
         y = mix(of_cores(order, range(1, core)), core, norm_gain.shape[1], sides, params, sums, short_rows, rank)
-        y_blocks = round_one(y)
-        cells, rest = round_two(y_blocks)
+        y_blocks, _ = round_one(y)
+        cells, rest = round_two(y_blocks, [])
         everything = jnp.concatenate([jnp.stack(list(y_blocks.values())), *rest])
         sides = [swap(everything, c) for c in range(1, core)]
         order = [*y_blocks, *cells]

time: 156 us -> 145 us (0.929)
  waiting for transfers between devices: 63.8 us -> 49.6 us
  starting transfers between devices: 52.8 us -> 56.1 us
    ppermute x36 -> x38, waiting for transfers between devices: 47.6 us -> 35.4 us  [swap(): return lax.ppermute(value, 'dp', [(r, r ^ offset) for r in range(dp_count)])]
    ppermute x6 -> x8, starting transfers between devices: 10.7 us -> 15 us  [onward(): return lax.ppermute(value, ('section', 'dp'), pairs)]
    ppermute x6 -> x8, waiting for transfers between devices: 16.3 us -> 14.2 us  [onward(): return lax.ppermute(value, ('section', 'dp'), pairs)]
    ppermute x36 -> x38, starting transfers between devices: 42.1 us -> 41.1 us  [swap(): return lax.ppermute(value, 'dp', [(r, r ^ offset) for r in range(dp_count)])]
  transfers between devices with their start and end apart: 42 -> 46, of which waited for: 34 -> 37; matrix products, arithmetic and copies ran while one was open for 0% -> 0% of each run, Pallas kernels for 10% -> 13%
where the time goes in v11:
time: 145 us
  starting transfers between devices  56.1 us (39%)
  waiting for transfers between devices  49.6 us (34%)
  Pallas kernels  36.3 us (25%)
  other arithmetic  2.32 us (2%)
    ppermute x38, starting transfers between devices, swap(): return lax.ppermute(value, 'dp', [(r, r ^ offset) for r in range(dp_count)])  41.1 us
    pallas_call x15, Pallas kernels, call(): pl.pallas_call(kernel, in_specs=specs, out_specs=in_vmem(len(outs)), out_...  36.3 us
    ppermute x38, waiting for transfers between devices, swap(): return lax.ppermute(value, 'dp', [(r, r ^ offset) for r in range(dp_count)])  35.4 us
    ppermute x8, starting transfers between devices, onward(): return lax.ppermute(value, ('section', 'dp'), pairs)  15 us
    ppermute x8, waiting for transfers between devices, onward(): return lax.ppermute(value, ('section', 'dp'), pairs)  14.2 us
  transfers between devices with their start and end apart: 46, of which 37 were waited for; matrix products, arithmetic and copies ran while one was open for 0% of the time, Pallas kernels for 13%

profile of v11, /device:TPU:0, one launch (start us, length us, event | category | flops | bytes accessed | tf_op | source)
XLA Modules:
  0.0 145.1 jit_solution(18095698572826804180)
XLA Ops:
  0.9 3.0 %collective-permute-start = (bf16[128,512]{1,0:T(8,128)(2,1)S(1)}, bf16[128,512]{1,0:T(8,128)(2,1)S(1)}, u32[]{:S(2)}, u32[]{:S(2)}) collective-permute-start(bf16[128,512]{1,0:T(8,128)(2,1)S(1)} %select_bitcast_fusion.own_ref), channel_id=1, source_target_pairs={{0,2},{1,3},{2,0},{3,1},{4,6},{5,7},{6,4},{7,5},{8,10},{9,11},{10,... | collective-permute-start | bytes 393224 | tf_op jit(solution)/shard_map/ppermute | solution.py:307
  5.5 2.6 %collective-permute-start.2 = (bf16[128,512]{1,0:T(8,128)(2,1)S(1)}, bf16[128,512]{1,0:T(8,128)(2,1)S(1)}, u32[]{:S(2)}, u32[]{:S(2)}) collective-permute-start(bf16[128,512]{1,0:T(8,128)(2,1)S(1)} %select_bitcast_fusion.own_ref), channel_id=1, source_target_pairs={{0,8},{1,9},{2,10},{3,11},{4,12},{5,13},{6,14},{7,15},{8,0},{9,1},... | collective-permute-start | bytes 393224 | tf_op jit(solution)/shard_map/ppermute | solution.py:307
  8.2 2.4 %collective-permute-done.1 = bf16[128,512]{1,0:T(8,128)(2,1)S(1)} collective-permute-done((bf16[128,512]{1,0:T(8,128)(2,1)S(1)}, bf16[128,512]{1,0:T(8,128)(2,1)S(1)}, u32[]{:S(2)}, u32[]{:S(2)}) %collective-permute-start.1) | collective-permute-done | bytes 131104 | tf_op jit(solution)/shard_map/ppermute | solution.py:307
  10.6 3.3 %collective-permute-done.2 = bf16[128,512]{1,0:T(8,128)(2,1)S(1)} collective-permute-done((bf16[128,512]{1,0:T(8,128)(2,1)S(1)}, bf16[128,512]{1,0:T(8,128)(2,1)S(1)}, u32[]{:S(2)}, u32[]{:S(2)}) %collective-permute-start.2) | collective-permute-done | bytes 131104 | tf_op jit(solution)/shard_map/ppermute | solution.py:307
  15.1 2.6 %collective-permute-start.5 = (bf16[1,128,512]{2,1,0:T(8,128)(2,1)S(1)}, bf16[1,128,512]{2,1,0:T(8,128)(2,1)S(1)}, u32[]{:S(2)}, u32[]{:S(2)}) collective-permute-start(bf16[1,128,512]{2,1,0:T(8,128)(2,1)S(1)} %bitcast.89), channel_id=1, source_target_pairs={{0,6},{1,7},{2,4},{3,5},{4,2},{5,3},{6,0},{7,1},{8,14},{9,15},{10,... | collective-permute-start | bytes 393224 | tf_op jit(solution)/shard_map/ppermute | solution.py:307
  17.7 6.8 %project_load.1 = (bf16[3,256,1024]{2,1,0:T(8,128)(2,1)S(1)}, bf16[3,256,1024]{2,1,0:T(8,128)(2,1)S(1)}, bf16[3,256,1024]{2,1,0:T(8,128)(2,1)S(1)}, bf16[3,256,1...) custom-call(s32[2]{0:T(128)S(1)} %pad_add_fusion.rank_ref, ...), custom_call_target="tpu_custom_call" | custom-call | flops 402653184 | bytes 393216 | tf_op jit(solution)/shard_map/project_load/pallas_call | solution.py:213
  27.3 4.9 %project_mix.3 = bf16[128,256]{1,0:T(8,128)(2,1)S(1)} custom-call(s32[2]{0:T(128)S(1)} %pad_add_fusion.rank_ref, bf16[8,128,512]{2,1,0:T(8,128)(2,1)S(1)} %collective-permute-done.6.refs_0_, f32[1,8192]{1,0:T(1,128)S(1)} %get-tuple-element.104.gain_ref.refs_1_, f32[3,128,256]{2,1,0:T(8,128)S(1)} %get-tuple-element.109.refs_2_, ...), custom_call_target="tpu_custom_call" | custom-call | flops 1610612736 | bytes 1572864 | tf_op jit(solution)/shard_map/project_mix/pallas_call | solution.py:213
  33.2 2.7 %collective-permute-start.9 = (bf16[128,256]{1,0:T(8,128)(2,1)S(1)}, bf16[128,256]{1,0:T(8,128)(2,1)S(1)}, u32[]{:S(2)}, u32[]{:S(2)}) collective-permute-start(bf16[128,256]{1,0:T(8,128)(2,1)S(1)} %project_mix.3), channel_id=1, source_target_pairs={{0,8},{1,9},{2,10},{3,11},{4,12},{5,13},{6,14},{7,15},{8,0},{9,1},... | collective-permute-start | bytes 196616 | tf_op jit(solution)/shard_map/ppermute | solution.py:307
  43.2 2.2 %collective-permute-done.10 = bf16[2,128,256]{2,1,0:T(8,128)(2,1)S(1)} collective-permute-done((bf16[2,128,256]{2,1,0:T(8,128)(2,1)S(1)}, bf16[2,128,256]{2,1,0:T(8,128)(2,1)S(1)}, u32[]{:S(2)}, u32[]{:S(2)}) %collective-permute-start.10) | collective-permute-done | bytes 131104 | tf_op jit(solution)/shard_map/ppermute | solution.py:307
  52.8 2.6 %collective-permute-start.16 = (bf16[128,512]{1,0:T(8,128)(2,1)S(1)}, bf16[128,512]{1,0:T(8,128)(2,1)S(1)}, u32[]{:S(2)}, u32[]{:S(2)}) collective-permute-start(bf16[128,512]{1,0:T(8,128)(2,1)S(1)} %get-tuple-element.126), channel_id=1, source_target_pairs={{0,24},{1,25},{2,26},{3,27},{4,28},{5,29},{6,30},{7,31},{8,16},{9,... | collective-permute-start | bytes 393224 | tf_op jit(solution)/shard_map/ppermute | solution.py:316
  55.8 4.3 %collective-permute-done.14.own_ref = bf16[128,512]{1,0:T(8,128)(2,1)S(1)} collective-permute-done((bf16[128,512]{1,0:T(8,128)(2,1)S(1)}, bf16[128,512]{1,0:T(8,128)(2,1)S(1)}, u32[]{:S(2)}, u32[]{:S(2)}) %collective-permute-start.14) | collective-permute-done | bytes 131104 | tf_op jit(solution)/shard_map/ppermute | solution.py:316
  60.2 2.2 %collective-permute-done.16 = bf16[128,512]{1,0:T(8,128)(2,1)S(1)} collective-permute-done((bf16[128,512]{1,0:T(8,128)(2,1)S(1)}, bf16[128,512]{1,0:T(8,128)(2,1)S(1)}, u32[]{:S(2)}, u32[]{:S(2)}) %collective-permute-start.16) | collective-permute-done | bytes 131104 | tf_op jit(solution)/shard_map/ppermute | solution.py:316
  63.2 2.9 %collective-permute-start.20 = (bf16[1,128,512]{2,1,0:T(8,128)(2,1)S(1)}, bf16[1,128,512]{2,1,0:T(8,128)(2,1)S(1)}, u32[]{:S(2)}, u32[]{:S(2)}) collective-permute-start(bf16[1,128,512]{2,1,0:T(8,128)(2,1)S(1)} %bitcast.77), channel_id=1, source_target_pairs={{0,6},{1,7},{2,4},{3,5},{4,2},{5,3},{6,0},{7,1},{8,14},{9,15},{10,... | collective-permute-start | bytes 393224 | tf_op jit(solution)/shard_map/ppermute | solution.py:307
  71.3 2.0 %project_more.4 = (f32[3,128,256]{2,1,0:T(8,128)S(1)}, f32[128,128]{1,0:T(8,128)S(1)}) custom-call(s32[2]{0:T(128)S(1)} %pad_add_fusion.rank_ref, bf16[5,128,512]{2,1,0:T(8,128)(2,1)S(1)} %pad_maximum_fusion.x_ref, f32[1,8192]{1,0:T(1,128)S(1)} %get-tuple-element.104.gain_ref.refs_1_, f32[3,128,256]{2,1,0:T(8,128)S(1)} %get-tuple-element.135.acc_in, ...), custom_call_target="tpu_custom_call" | custom-call | flops 503316480 | bytes 491520 | tf_op jit(solution)/shard_map/project_more/pallas_call | solution.py:213
  73.9 5.1 %project_mix.4 = bf16[128,256]{1,0:T(8,128)(2,1)S(1)} custom-call(s32[2]{0:T(128)S(1)} %pad_add_fusion.rank_ref, bf16[8,128,512]{2,1,0:T(8,128)(2,1)S(1)} %collective-permute-done.22.refs_0_, f32[1,8192]{1,0:T(1,128)S(1)} %get-tuple-element.104.gain_ref.refs_1_, f32[3,128,256]{2,1,0:T(8,128)S(1)} %get-tuple-element.141.refs_2_, ...), custom_call_target="tpu_custom_call" | custom-call | flops 1610612736 | bytes 1572864 | tf_op jit(solution)/shard_map/project_mix/pallas_call | solution.py:213
  84.9 2.0 %collective-permute-done.25 = bf16[128,256]{1,0:T(8,128)(2,1)S(1)} collective-permute-done((bf16[128,256]{1,0:T(8,128)(2,1)S(1)}, bf16[128,256]{1,0:T(8,128)(2,1)S(1)}, u32[]{:S(2)}, u32[]{:S(2)}) %collective-permute-start.25) | collective-permute-done | bytes 65568 | tf_op jit(solution)/shard_map/ppermute | solution.py:307
  88.4 2.2 %collective-permute-start.28 = (bf16[1,128,256]{2,1,0:T(8,128)(2,1)S(1)}, bf16[1,128,256]{2,1,0:T(8,128)(2,1)S(1)}, u32[]{:S(2)}, u32[]{:S(2)}) collective-permute-start(bf16[1,128,256]{2,1,0:T(8,128)(2,1)S(1)} %bitcast.103), channel_id=1, source_target_pairs={{0,6},{1,7},{2,4},{3,5},{4,2},{5,3},{6,0},{7,1},{8,14},{9,15},{10,... | collective-permute-start | bytes 196616 | tf_op jit(solution)/shard_map/ppermute | solution.py:307
  96.5 3.4 %collective-permute-start.30 = (bf16[128,512]{1,0:T(8,128)(2,1)S(1)}, bf16[128,512]{1,0:T(8,128)(2,1)S(1)}, u32[]{:S(2)}, u32[]{:S(2)}) collective-permute-start(bf16[128,512]{1,0:T(8,128)(2,1)S(1)} %get-tuple-element.153), channel_id=1, source_target_pairs={{0,16},{1,17},{2,18},{3,19},{4,20},{5,21},{6,22},{7,23},{8,24},{9,... | collective-permute-start | bytes 393224 | tf_op jit(solution)/shard_map/ppermute | solution.py:316
  100.1 2.6 %collective-permute-start.32 = (bf16[128,512]{1,0:T(8,128)(2,1)S(1)}, bf16[128,512]{1,0:T(8,128)(2,1)S(1)}, u32[]{:S(2)}, u32[]{:S(2)}) collective-permute-start(bf16[128,512]{1,0:T(8,128)(2,1)S(1)} %get-tuple-element.153), channel_id=1, source_target_pairs={{0,24},{1,25},{2,26},{3,27},{4,28},{5,29},{6,30},{7,31},{8,16},{9,... | collective-permute-start | bytes 393224 | tf_op jit(solution)/shard_map/ppermute | solution.py:316
  103.6 5.6 %collective-permute-done.30.own_ref = bf16[128,512]{1,0:T(8,128)(2,1)S(1)} collective-permute-done((bf16[128,512]{1,0:T(8,128)(2,1)S(1)}, bf16[128,512]{1,0:T(8,128)(2,1)S(1)}, u32[]{:S(2)}, u32[]{:S(2)}) %collective-permute-start.30) | collective-permute-done | bytes 131104 | tf_op jit(solution)/shard_map/ppermute | solution.py:316
  111.2 2.5 %collective-permute-start.36 = (bf16[1,128,512]{2,1,0:T(8,128)(2,1)S(1)}, bf16[1,128,512]{2,1,0:T(8,128)(2,1)S(1)}, u32[]{:S(2)}, u32[]{:S(2)}) collective-permute-start(bf16[1,128,512]{2,1,0:T(8,128)(2,1)S(1)} %bitcast.81), channel_id=1, source_target_pairs={{0,6},{1,7},{2,4},{3,5},{4,2},{5,3},{6,0},{7,1},{8,14},{9,15},{10,... | collective-permute-start | bytes 393224 | tf_op jit(solution)/shard_map/ppermute | solution.py:307
  121.6 4.9 %project_mix.5 = bf16[128,256]{1,0:T(8,128)(2,1)S(1)} custom-call(s32[2]{0:T(128)S(1)} %pad_add_fusion.rank_ref, bf16[8,128,512]{2,1,0:T(8,128)(2,1)S(1)} %collective-permute-done.38.refs_0_, f32[1,8192]{1,0:T(1,128)S(1)} %get-tuple-element.104.gain_ref.refs_1_, f32[3,128,256]{2,1,0:T(8,128)S(1)} %get-tuple-element.168.refs_2_, ...), custom_call_target="tpu_custom_call" | custom-call | flops 1610612736 | bytes 1572864 | tf_op jit(solution)/shard_map/project_mix/pallas_call | solution.py:213
  131.9 2.9 %collective-permute-done.41 = bf16[128,256]{1,0:T(8,128)(2,1)S(1)} collective-permute-done((bf16[128,256]{1,0:T(8,128)(2,1)S(1)}, bf16[128,256]{1,0:T(8,128)(2,1)S(1)}, u32[]{:S(2)}, u32[]{:S(2)}) %collective-permute-start.41) | collective-permute-done | bytes 65568 | tf_op jit(solution)/shard_map/ppermute | solution.py:307
  136.1 2.4 %collective-permute-start.44 = (bf16[1,128,256]{2,1,0:T(8,128)(2,1)S(1)}, bf16[1,128,256]{2,1,0:T(8,128)(2,1)S(1)}, u32[]{:S(2)}, u32[]{:S(2)}) collective-permute-start(bf16[1,128,256]{2,1,0:T(8,128)(2,1)S(1)} %bitcast.106), channel_id=1, source_target_pairs={{0,6},{1,7},{2,4},{3,5},{4,2},{5,3},{6,0},{7,1},{8,14},{9,15},{10,... | collective-permute-start | bytes 196616 | tf_op jit(solution)/shard_map/ppermute | solution.py:307
  (146 shorter events, 66.4 us)
Async XLA Ops:
  0.9 7.2 %collective-permute-start = (bf16[128,512]{1,0:T(8,128)(2,1)S(1)}, bf16[128,512]{1,0:T(8,128)(2,1)S(1)}, u32[]{:S(2)}, u32[]{:S(2)}) collective-permute-start(bf16[128,512]{1,0:T(8,128)(2,1)S(1)} %select_bitcast_fusion.own_ref), channel_id=1, source_target_pairs={{0,2},{1,3},{2,0},{3,1},{4,6},{5,7},{6,4},{7,5},{8,10},{9,11},{10,... | collective-permute-start | bytes 393224 | tf_op jit(solution)/shard_map/ppermute | solution.py:307
  3.9 6.7 %collective-permute-start.1 = (bf16[128,512]{1,0:T(8,128)(2,1)S(1)}, bf16[128,512]{1,0:T(8,128)(2,1)S(1)}, u32[]{:S(2)}, u32[]{:S(2)}) collective-permute-start(bf16[128,512]{1,0:T(8,128)(2,1)S(1)} %select_bitcast_fusion.own_ref), channel_id=1, source_target_pairs={{0,4},{1,5},{2,6},{3,7},{4,0},{5,1},{6,2},{7,3},{8,12},{9,13},{10,... | collective-permute-start | bytes 393224 | tf_op jit(solution)/shard_map/ppermute | solution.py:307
  5.5 8.4 %collective-permute-start.2 = (bf16[128,512]{1,0:T(8,128)(2,1)S(1)}, bf16[128,512]{1,0:T(8,128)(2,1)S(1)}, u32[]{:S(2)}, u32[]{:S(2)}) collective-permute-start(bf16[128,512]{1,0:T(8,128)(2,1)S(1)} %select_bitcast_fusion.own_ref), channel_id=1, source_target_pairs={{0,8},{1,9},{2,10},{3,11},{4,12},{5,13},{6,14},{7,15},{8,0},{9,1},... | collective-permute-start | bytes 393224 | tf_op jit(solution)/shard_map/ppermute | solution.py:307
  14.0 10.5 %collective-permute-start.3 = (bf16[2,128,512]{2,1,0:T(8,128)(2,1)S(1)}, bf16[2,128,512]{2,1,0:T(8,128)(2,1)S(1)}, u32[]{:S(2)}, u32[]{:S(2)}) collective-permute-start(bf16[2,128,512]{2,1,0:T(8,128)(2,1)S(1)} %pad_maximum_fusion.6), channel_id=1, source_target_pairs={{0,2},{1,3},{2,0},{3,1},{4,6},{5,7},{6,4},{7,5},{8,10},{9,11},{10,... | collective-permute-start | bytes 786440 | tf_op jit(solution)/shard_map/ppermute | solution.py:307
  14.6 9.9 %collective-permute-start.4 = (bf16[1,128,512]{2,1,0:T(8,128)(2,1)S(1)}, bf16[1,128,512]{2,1,0:T(8,128)(2,1)S(1)}, u32[]{:S(2)}, u32[]{:S(2)}) collective-permute-start(bf16[1,128,512]{2,1,0:T(8,128)(2,1)S(1)} %bitcast.88), channel_id=1, source_target_pairs={{0,4},{1,5},{2,6},{3,7},{4,0},{5,1},{6,2},{7,3},{8,12},{9,13},{10,... | collective-permute-start | bytes 393224 | tf_op jit(solution)/shard_map/ppermute | solution.py:307
  15.1 9.5 %collective-permute-start.5 = (bf16[1,128,512]{2,1,0:T(8,128)(2,1)S(1)}, bf16[1,128,512]{2,1,0:T(8,128)(2,1)S(1)}, u32[]{:S(2)}, u32[]{:S(2)}) collective-permute-start(bf16[1,128,512]{2,1,0:T(8,128)(2,1)S(1)} %bitcast.89), channel_id=1, source_target_pairs={{0,6},{1,7},{2,4},{3,5},{4,2},{5,3},{6,0},{7,1},{8,14},{9,15},{10,... | collective-permute-start | bytes 393224 | tf_op jit(solution)/shard_map/ppermute | solution.py:307
  33.2 6.4 %collective-permute-start.9 = (bf16[128,256]{1,0:T(8,128)(2,1)S(1)}, bf16[128,256]{1,0:T(8,128)(2,1)S(1)}, u32[]{:S(2)}, u32[]{:S(2)}) collective-permute-start(bf16[128,256]{1,0:T(8,128)(2,1)S(1)} %project_mix.3), channel_id=1, source_target_pairs={{0,8},{1,9},{2,10},{3,11},{4,12},{5,13},{6,14},{7,15},{8,0},{9,1},... | collective-permute-start | bytes 196616 | tf_op jit(solution)/shard_map/ppermute | solution.py:307
  39.6 5.7 %collective-permute-start.10 = (bf16[2,128,256]{2,1,0:T(8,128)(2,1)S(1)}, bf16[2,128,256]{2,1,0:T(8,128)(2,1)S(1)}, u32[]{:S(2)}, u32[]{:S(2)}) collective-permute-start(bf16[2,128,256]{2,1,0:T(8,128)(2,1)S(1)} %pad_maximum_fusion.9), channel_id=1, source_target_pairs={{0,2},{1,3},{2,0},{3,1},{4,6},{5,7},{6,4},{7,5},{8,10},{9,11},{10,... | collective-permute-start | bytes 393224 | tf_op jit(solution)/shard_map/ppermute | solution.py:307
  49.7 10.4 %collective-permute-start.14 = (bf16[128,512]{1,0:T(8,128)(2,1)S(1)}, bf16[128,512]{1,0:T(8,128)(2,1)S(1)}, u32[]{:S(2)}, u32[]{:S(2)}) collective-permute-start(bf16[128,512]{1,0:T(8,128)(2,1)S(1)} %get-tuple-element.126), channel_id=1, source_target_pairs={{0,16},{1,17},{2,18},{3,19},{4,20},{5,21},{6,22},{7,23},{8,24},{9,... | collective-permute-start | bytes 393224 | tf_op jit(solution)/shard_map/ppermute | solution.py:316
  51.4 8.8 %collective-permute-start.15 = (bf16[128,512]{1,0:T(8,128)(2,1)S(1)}, bf16[128,512]{1,0:T(8,128)(2,1)S(1)}, u32[]{:S(2)}, u32[]{:S(2)}) collective-permute-start(bf16[128,512]{1,0:T(8,128)(2,1)S(1)} %get-tuple-element.126), channel_id=1, source_target_pairs={{0,20},{1,21},{2,22},{3,23},{4,16},{5,17},{6,18},{7,19},{8,28},{9,... | collective-permute-start | bytes 393224 | tf_op jit(solution)/shard_map/ppermute | solution.py:316
  52.8 9.6 %collective-permute-start.16 = (bf16[128,512]{1,0:T(8,128)(2,1)S(1)}, bf16[128,512]{1,0:T(8,128)(2,1)S(1)}, u32[]{:S(2)}, u32[]{:S(2)}) collective-permute-start(bf16[128,512]{1,0:T(8,128)(2,1)S(1)} %get-tuple-element.126), channel_id=1, source_target_pairs={{0,24},{1,25},{2,26},{3,27},{4,28},{5,29},{6,30},{7,31},{8,16},{9,... | collective-permute-start | bytes 393224 | tf_op jit(solution)/shard_map/ppermute | solution.py:316
  55.4 7.1 %collective-permute-start.17 = (bf16[128,512]{1,0:T(8,128)(2,1)S(1)}, bf16[128,512]{1,0:T(8,128)(2,1)S(1)}, u32[]{:S(2)}, u32[]{:S(2)}) collective-permute-start(bf16[128,512]{1,0:T(8,128)(2,1)S(1)} %get-tuple-element.126), channel_id=1, source_target_pairs={{0,2},{1,3},{2,0},{3,1},{4,6},{5,7},{6,4},{7,5},{8,10},{9,11},{10,... | collective-permute-start | bytes 393224 | tf_op jit(solution)/shard_map/ppermute | solution.py:307
  62.5 8.6 %collective-permute-start.18 = (bf16[2,128,512]{2,1,0:T(8,128)(2,1)S(1)}, bf16[2,128,512]{2,1,0:T(8,128)(2,1)S(1)}, u32[]{:S(2)}, u32[]{:S(2)}) collective-permute-start(bf16[2,128,512]{2,1,0:T(8,128)(2,1)S(1)} %pad_maximum_fusion.7), channel_id=1, source_target_pairs={{0,2},{1,3},{2,0},{3,1},{4,6},{5,7},{6,4},{7,5},{8,10},{9,11},{10,... | collective-permute-start | bytes 786440 | tf_op jit(solution)/shard_map/ppermute | solution.py:307
  63.2 7.3 %collective-permute-start.20 = (bf16[1,128,512]{2,1,0:T(8,128)(2,1)S(1)}, bf16[1,128,512]{2,1,0:T(8,128)(2,1)S(1)}, u32[]{:S(2)}, u32[]{:S(2)}) collective-permute-start(bf16[1,128,512]{2,1,0:T(8,128)(2,1)S(1)} %bitcast.77), channel_id=1, source_target_pairs={{0,6},{1,7},{2,4},{3,5},{4,2},{5,3},{6,0},{7,1},{8,14},{9,15},{10,... | collective-permute-start | bytes 393224 | tf_op jit(solution)/shard_map/ppermute | solution.py:307
  80.9 6.1 %collective-permute-start.25 = (bf16[128,256]{1,0:T(8,128)(2,1)S(1)}, bf16[128,256]{1,0:T(8,128)(2,1)S(1)}, u32[]{:S(2)}, u32[]{:S(2)}) collective-permute-start(bf16[128,256]{1,0:T(8,128)(2,1)S(1)} %project_mix.4), channel_id=1, source_target_pairs={{0,8},{1,9},{2,10},{3,11},{4,12},{5,13},{6,14},{7,15},{8,0},{9,1},... | collective-permute-start | bytes 196616 | tf_op jit(solution)/shard_map/ppermute | solution.py:307
  96.5 12.7 %collective-permute-start.30 = (bf16[128,512]{1,0:T(8,128)(2,1)S(1)}, bf16[128,512]{1,0:T(8,128)(2,1)S(1)}, u32[]{:S(2)}, u32[]{:S(2)}) collective-permute-start(bf16[128,512]{1,0:T(8,128)(2,1)S(1)} %get-tuple-element.153), channel_id=1, source_target_pairs={{0,16},{1,17},{2,18},{3,19},{4,20},{5,21},{6,22},{7,23},{8,24},{9,... | collective-permute-start | bytes 393224 | tf_op jit(solution)/shard_map/ppermute | solution.py:316
  99.9 9.3 %collective-permute-start.31 = (bf16[128,512]{1,0:T(8,128)(2,1)S(1)}, bf16[128,512]{1,0:T(8,128)(2,1)S(1)}, u32[]{:S(2)}, u32[]{:S(2)}) collective-permute-start(bf16[128,512]{1,0:T(8,128)(2,1)S(1)} %get-tuple-element.153), channel_id=1, source_target_pairs={{0,20},{1,21},{2,22},{3,23},{4,16},{5,17},{6,18},{7,19},{8,28},{9,... | collective-permute-start | bytes 393224 | tf_op jit(solution)/shard_map/ppermute | solution.py:316
  100.1 9.9 %collective-permute-start.32 = (bf16[128,512]{1,0:T(8,128)(2,1)S(1)}, bf16[128,512]{1,0:T(8,128)(2,1)S(1)}, u32[]{:S(2)}, u32[]{:S(2)}) collective-permute-start(bf16[128,512]{1,0:T(8,128)(2,1)S(1)} %get-tuple-element.153), channel_id=1, source_target_pairs={{0,24},{1,25},{2,26},{3,27},{4,28},{5,29},{6,30},{7,31},{8,16},{9,... | collective-permute-start | bytes 393224 | tf_op jit(solution)/shard_map/ppermute | solution.py:316
  102.7 7.3 %collective-permute-start.33 = (bf16[128,512]{1,0:T(8,128)(2,1)S(1)}, bf16[128,512]{1,0:T(8,128)(2,1)S(1)}, u32[]{:S(2)}, u32[]{:S(2)}) collective-permute-start(bf16[128,512]{1,0:T(8,128)(2,1)S(1)} %get-tuple-element.153), channel_id=1, source_target_pairs={{0,2},{1,3},{2,0},{3,1},{4,6},{5,7},{6,4},{7,5},{8,10},{9,11},{10,... | collective-permute-start | bytes 393224 | tf_op jit(solution)/shard_map/ppermute | solution.py:307
  110.1 8.7 %collective-permute-start.34 = (bf16[2,128,512]{2,1,0:T(8,128)(2,1)S(1)}, bf16[2,128,512]{2,1,0:T(8,128)(2,1)S(1)}, u32[]{:S(2)}, u32[]{:S(2)}) collective-permute-start(bf16[2,128,512]{2,1,0:T(8,128)(2,1)S(1)} %pad_maximum_fusion.8), channel_id=1, source_target_pairs={{0,2},{1,3},{2,0},{3,1},{4,6},{5,7},{6,4},{7,5},{8,10},{9,11},{10,... | collective-permute-start | bytes 786440 | tf_op jit(solution)/shard_map/ppermute | solution.py:307
  110.7 5.3 %collective-permute-start.35 = (bf16[1,128,512]{2,1,0:T(8,128)(2,1)S(1)}, bf16[1,128,512]{2,1,0:T(8,128)(2,1)S(1)}, u32[]{:S(2)}, u32[]{:S(2)}) collective-permute-start(bf16[1,128,512]{2,1,0:T(8,128)(2,1)S(1)} %bitcast.80), channel_id=1, source_target_pairs={{0,4},{1,5},{2,6},{3,7},{4,0},{5,1},{6,2},{7,3},{8,12},{9,13},{10,... | collective-permute-start | bytes 393224 | tf_op jit(solution)/shard_map/ppermute | solution.py:307
  111.2 6.9 %collective-permute-start.36 = (bf16[1,128,512]{2,1,0:T(8,128)(2,1)S(1)}, bf16[1,128,512]{2,1,0:T(8,128)(2,1)S(1)}, u32[]{:S(2)}, u32[]{:S(2)}) collective-permute-start(bf16[1,128,512]{2,1,0:T(8,128)(2,1)S(1)} %bitcast.81), channel_id=1, source_target_pairs={{0,6},{1,7},{2,4},{3,5},{4,2},{5,3},{6,0},{7,1},{8,14},{9,15},{10,... | collective-permute-start | bytes 393224 | tf_op jit(solution)/shard_map/ppermute | solution.py:307
  129.0 5.9 %collective-permute-start.41 = (bf16[128,256]{1,0:T(8,128)(2,1)S(1)}, bf16[128,256]{1,0:T(8,128)(2,1)S(1)}, u32[]{:S(2)}, u32[]{:S(2)}) collective-permute-start(bf16[128,256]{1,0:T(8,128)(2,1)S(1)} %project_mix.5), channel_id=1, source_target_pairs={{0,8},{1,9},{2,10},{3,11},{4,12},{5,13},{6,14},{7,15},{8,0},{9,1},... | collective-permute-start | bytes 196616 | tf_op jit(solution)/shard_map/ppermute | solution.py:307
  136.1 5.3 %collective-permute-start.44 = (bf16[1,128,256]{2,1,0:T(8,128)(2,1)S(1)}, bf16[1,128,256]{2,1,0:T(8,128)(2,1)S(1)}, u32[]{:S(2)}, u32[]{:S(2)}) collective-permute-start(bf16[1,128,256]{2,1,0:T(8,128)(2,1)S(1)} %bitcast.106), channel_id=1, source_target_pairs={{0,6},{1,7},{2,4},{3,5},{4,2},{5,3},{6,0},{7,1},{8,14},{9,15},{10,... | collective-permute-start | bytes 196616 | tf_op jit(solution)/shard_map/ppermute | solution.py:307
  (25 other events, 113.2 us)

commit v12 on v11

--- a/solution.py
+++ b/solution.py
@@ -25,8 +25,8 @@
 def routes(far, near, cross):
     if (far, near) == (4, 2):
         if cross:
-            return [0, 2, 4], [(1, [2, 4]), (2, [4]), (3, [4])], [1]
-        return [0, 1, 2, 4], [(1, [2, 4]), (2, [4]), (3, [4])], []
+            return [0, 2, 4], [(1, [2, 4]), (3, [4]), (2, [4])], [1]
+        return [0, 1, 2, 4], [(1, [2, 4]), (3, [4]), (2, [4])], []
     line = [d * near for d in range(far)]
     return line, [(d, line) for d in range(1, near)], []
 
@@ -347,7 +347,7 @@
         direct = jnp.stack(list(blocks.values()))
         here = of_cores(blocks, [0])
         if params:
-            sums = project_part(here, core, after(direct, rest[1 % len(rest)]), params, [], rank)
+            sums = project_part(here, core, after(direct, rest[min(2, len(rest) - 1)]), params, [], rank)
         else:
             sums, params = project_load(
                 here, order, core, direct, w_in[0], norm_gain, filter_taps[0], decay_rate, rank

time: 145 us -> 144 us (level)
  transfers between devices with their start and end apart: 46 -> 46, of which waited for: 37 -> 35; matrix products, arithmetic and copies ran while one was open for 0% -> 0% of each run, Pallas kernels for 13% -> 13%
where the time goes in v12:
time: 144 us
  starting transfers between devices  56.1 us (39%)
  waiting for transfers between devices  48.5 us (34%)
  Pallas kernels  36.3 us (25%)
  other arithmetic  2.32 us (2%)
    ppermute x38, starting transfers between devices, swap(): return lax.ppermute(value, 'dp', [(r, r ^ offset) for r in range(dp_count)])  42.2 us
    pallas_call x15, Pallas kernels, call(): pl.pallas_call(kernel, in_specs=specs, out_specs=in_vmem(len(outs)), out_...  36.3 us
    ppermute x38, waiting for transfers between devices, swap(): return lax.ppermute(value, 'dp', [(r, r ^ offset) for r in range(dp_count)])  35.3 us
    ppermute x8, starting transfers between devices, onward(): return lax.ppermute(value, ('section', 'dp'), pairs)  13.9 us
    ppermute x8, waiting for transfers between devices, onward(): return lax.ppermute(value, ('section', 'dp'), pairs)  13.2 us
  transfers between devices with their start and end apart: 46, of which 35 were waited for; matrix products, arithmetic and copies ran while one was open for 0% of the time, Pallas kernels for 13%

profile of v12, /device:TPU:0, one launch (start us, length us, event | category | flops | bytes accessed | tf_op | source)
XLA Modules:
  0.0 144.1 jit_solution(17800242470888251878)
XLA Ops:
  0.9 3.0 %collective-permute-start = (bf16[128,512]{1,0:T(8,128)(2,1)S(1)}, bf16[128,512]{1,0:T(8,128)(2,1)S(1)}, u32[]{:S(2)}, u32[]{:S(2)}) collective-permute-start(bf16[128,512]{1,0:T(8,128)(2,1)S(1)} %select_bitcast_fusion.own_ref), channel_id=1, source_target_pairs={{0,2},{1,3},{2,0},{3,1},{4,6},{5,7},{6,4},{7,5},{8,10},{9,11},{10,... | collective-permute-start | bytes 393224 | tf_op jit(solution)/shard_map/ppermute | solution.py:307
  5.5 2.6 %collective-permute-start.2 = (bf16[128,512]{1,0:T(8,128)(2,1)S(1)}, bf16[128,512]{1,0:T(8,128)(2,1)S(1)}, u32[]{:S(2)}, u32[]{:S(2)}) collective-permute-start(bf16[128,512]{1,0:T(8,128)(2,1)S(1)} %select_bitcast_fusion.own_ref), channel_id=1, source_target_pairs={{0,8},{1,9},{2,10},{3,11},{4,12},{5,13},{6,14},{7,15},{8,0},{9,1},... | collective-permute-start | bytes 393224 | tf_op jit(solution)/shard_map/ppermute | solution.py:307
  8.2 2.4 %collective-permute-done.1 = bf16[128,512]{1,0:T(8,128)(2,1)S(1)} collective-permute-done((bf16[128,512]{1,0:T(8,128)(2,1)S(1)}, bf16[128,512]{1,0:T(8,128)(2,1)S(1)}, u32[]{:S(2)}, u32[]{:S(2)}) %collective-permute-start.1) | collective-permute-done | bytes 131104 | tf_op jit(solution)/shard_map/ppermute | solution.py:307
  10.6 3.3 %collective-permute-done.2 = bf16[128,512]{1,0:T(8,128)(2,1)S(1)} collective-permute-done((bf16[128,512]{1,0:T(8,128)(2,1)S(1)}, bf16[128,512]{1,0:T(8,128)(2,1)S(1)}, u32[]{:S(2)}, u32[]{:S(2)}) %collective-permute-start.2) | collective-permute-done | bytes 131104 | tf_op jit(solution)/shard_map/ppermute | solution.py:307
  17.7 6.8 %project_load.1 = (bf16[3,256,1024]{2,1,0:T(8,128)(2,1)S(1)}, bf16[3,256,1024]{2,1,0:T(8,128)(2,1)S(1)}, bf16[3,256,1024]{2,1,0:T(8,128)(2,1)S(1)}, bf16[3,256,1...) custom-call(s32[2]{0:T(128)S(1)} %pad_add_fusion.rank_ref, ...), custom_call_target="tpu_custom_call" | custom-call | flops 402653184 | bytes 393216 | tf_op jit(solution)/shard_map/project_load/pallas_call | solution.py:213
  24.7 1.7 %project_more.3 = (f32[3,128,256]{2,1,0:T(8,128)S(1)}, f32[128,128]{1,0:T(8,128)S(1)}) custom-call(s32[2]{0:T(128)S(1)} %pad_add_fusion.rank_ref, bf16[4,128,512]{2,1,0:T(8,128)(2,1)S(1)} %pad_maximum_fusion.3.x_ref, f32[1,8192]{1,0:T(1,128)S(1)} %get-tuple-element.104.gain_ref.refs_1_, f32[3,128,256]{2,1,0:T(8,128)S(1)} %get-tuple-element.99.acc_in, ...), custom_call_target="tpu_custom_call" | custom-call | flops 402653184 | bytes 393216 | tf_op jit(solution)/shard_map/project_more/pallas_call | solution.py:213
  27.3 4.9 %project_mix.3 = bf16[128,256]{1,0:T(8,128)(2,1)S(1)} custom-call(s32[2]{0:T(128)S(1)} %pad_add_fusion.rank_ref, bf16[8,128,512]{2,1,0:T(8,128)(2,1)S(1)} %collective-permute-done.6.refs_0_, f32[1,8192]{1,0:T(1,128)S(1)} %get-tuple-element.104.gain_ref.refs_1_, f32[3,128,256]{2,1,0:T(8,128)S(1)} %get-tuple-element.109.refs_2_, ...), custom_call_target="tpu_custom_call" | custom-call | flops 1610612736 | bytes 1572864 | tf_op jit(solution)/shard_map/project_mix/pallas_call | solution.py:213
  33.2 2.7 %collective-permute-start.9 = (bf16[128,256]{1,0:T(8,128)(2,1)S(1)}, bf16[128,256]{1,0:T(8,128)(2,1)S(1)}, u32[]{:S(2)}, u32[]{:S(2)}) collective-permute-start(bf16[128,256]{1,0:T(8,128)(2,1)S(1)} %project_mix.3), channel_id=1, source_target_pairs={{0,8},{1,9},{2,10},{3,11},{4,12},{5,13},{6,14},{7,15},{8,0},{9,1},... | collective-permute-start | bytes 196616 | tf_op jit(solution)/shard_map/ppermute | solution.py:307
  37.7 1.8 %collective-permute-done.9 = bf16[128,256]{1,0:T(8,128)(2,1)S(1)} collective-permute-done((bf16[128,256]{1,0:T(8,128)(2,1)S(1)}, bf16[128,256]{1,0:T(8,128)(2,1)S(1)}, u32[]{:S(2)}, u32[]{:S(2)}) %collective-permute-start.9) | collective-permute-done | bytes 65568 | tf_op jit(solution)/shard_map/ppermute | solution.py:307
  51.9 2.5 %collective-permute-start.16 = (bf16[128,512]{1,0:T(8,128)(2,1)S(1)}, bf16[128,512]{1,0:T(8,128)(2,1)S(1)}, u32[]{:S(2)}, u32[]{:S(2)}) collective-permute-start(bf16[128,512]{1,0:T(8,128)(2,1)S(1)} %get-tuple-element.126), channel_id=1, source_target_pairs={{0,24},{1,25},{2,26},{3,27},{4,28},{5,29},{6,30},{7,31},{8,16},{9,... | collective-permute-start | bytes 393224 | tf_op jit(solution)/shard_map/ppermute | solution.py:316
  55.9 4.2 %collective-permute-done.14.own_ref = bf16[128,512]{1,0:T(8,128)(2,1)S(1)} collective-permute-done((bf16[128,512]{1,0:T(8,128)(2,1)S(1)}, bf16[128,512]{1,0:T(8,128)(2,1)S(1)}, u32[]{:S(2)}, u32[]{:S(2)}) %collective-permute-start.14) | collective-permute-done | bytes 131104 | tf_op jit(solution)/shard_map/ppermute | solution.py:316
  63.2 2.0 %collective-permute-start.19 = (bf16[1,128,512]{2,1,0:T(8,128)(2,1)S(1)}, bf16[1,128,512]{2,1,0:T(8,128)(2,1)S(1)}, u32[]{:S(2)}, u32[]{:S(2)}) collective-permute-start(bf16[1,128,512]{2,1,0:T(8,128)(2,1)S(1)} %bitcast.77), channel_id=1, source_target_pairs={{0,6},{1,7},{2,4},{3,5},{4,2},{5,3},{6,0},{7,1},{8,14},{9,15},{10,... | collective-permute-start | bytes 393224 | tf_op jit(solution)/shard_map/ppermute | solution.py:307
  70.7 2.0 %project_more.4 = (f32[3,128,256]{2,1,0:T(8,128)S(1)}, f32[128,128]{1,0:T(8,128)S(1)}) custom-call(s32[2]{0:T(128)S(1)} %pad_add_fusion.rank_ref, bf16[5,128,512]{2,1,0:T(8,128)(2,1)S(1)} %pad_maximum_fusion.x_ref, f32[1,8192]{1,0:T(1,128)S(1)} %get-tuple-element.104.gain_ref.refs_1_, f32[3,128,256]{2,1,0:T(8,128)S(1)} %get-tuple-element.135.acc_in, ...), custom_call_target="tpu_custom_call" | custom-call | flops 503316480 | bytes 491520 | tf_op jit(solution)/shard_map/project_more/pallas_call | solution.py:213
  73.3 5.1 %project_mix.4 = bf16[128,256]{1,0:T(8,128)(2,1)S(1)} custom-call(s32[2]{0:T(128)S(1)} %pad_add_fusion.rank_ref, bf16[8,128,512]{2,1,0:T(8,128)(2,1)S(1)} %collective-permute-done.22.refs_0_, f32[1,8192]{1,0:T(1,128)S(1)} %get-tuple-element.104.gain_ref.refs_1_, f32[3,128,256]{2,1,0:T(8,128)S(1)} %get-tuple-element.141.refs_2_, ...), custom_call_target="tpu_custom_call" | custom-call | flops 1610612736 | bytes 1572864 | tf_op jit(solution)/shard_map/project_mix/pallas_call | solution.py:213
  83.9 2.8 %collective-permute-done.25 = bf16[128,256]{1,0:T(8,128)(2,1)S(1)} collective-permute-done((bf16[128,256]{1,0:T(8,128)(2,1)S(1)}, bf16[128,256]{1,0:T(8,128)(2,1)S(1)}, u32[]{:S(2)}, u32[]{:S(2)}) %collective-permute-start.25) | collective-permute-done | bytes 65568 | tf_op jit(solution)/shard_map/ppermute | solution.py:307
  88.4 1.9 %collective-permute-start.28 = (bf16[1,128,256]{2,1,0:T(8,128)(2,1)S(1)}, bf16[1,128,256]{2,1,0:T(8,128)(2,1)S(1)}, u32[]{:S(2)}, u32[]{:S(2)}) collective-permute-start(bf16[1,128,256]{2,1,0:T(8,128)(2,1)S(1)} %bitcast.103), channel_id=1, source_target_pairs={{0,4},{1,5},{2,6},{3,7},{4,0},{5,1},{6,2},{7,3},{8,12},{9,13},{10,... | collective-permute-start | bytes 196616 | tf_op jit(solution)/shard_map/ppermute | solution.py:307
  96.2 2.8 %collective-permute-start.30 = (bf16[128,512]{1,0:T(8,128)(2,1)S(1)}, bf16[128,512]{1,0:T(8,128)(2,1)S(1)}, u32[]{:S(2)}, u32[]{:S(2)}) collective-permute-start(bf16[128,512]{1,0:T(8,128)(2,1)S(1)} %get-tuple-element.153), channel_id=1, source_target_pairs={{0,16},{1,17},{2,18},{3,19},{4,20},{5,21},{6,22},{7,23},{8,24},{9,... | collective-permute-start | bytes 393224 | tf_op jit(solution)/shard_map/ppermute | solution.py:316
  99.2 2.7 %collective-permute-start.32 = (bf16[128,512]{1,0:T(8,128)(2,1)S(1)}, bf16[128,512]{1,0:T(8,128)(2,1)S(1)}, u32[]{:S(2)}, u32[]{:S(2)}) collective-permute-start(bf16[128,512]{1,0:T(8,128)(2,1)S(1)} %get-tuple-element.153), channel_id=1, source_target_pairs={{0,24},{1,25},{2,26},{3,27},{4,28},{5,29},{6,30},{7,31},{8,16},{9,... | collective-permute-start | bytes 393224 | tf_op jit(solution)/shard_map/ppermute | solution.py:316
  102.8 5.3 %collective-permute-done.30.own_ref = bf16[128,512]{1,0:T(8,128)(2,1)S(1)} collective-permute-done((bf16[128,512]{1,0:T(8,128)(2,1)S(1)}, bf16[128,512]{1,0:T(8,128)(2,1)S(1)}, u32[]{:S(2)}, u32[]{:S(2)}) %collective-permute-start.30) | collective-permute-done | bytes 131104 | tf_op jit(solution)/shard_map/ppermute | solution.py:316
  110.1 2.8 %collective-permute-start.35 = (bf16[1,128,512]{2,1,0:T(8,128)(2,1)S(1)}, bf16[1,128,512]{2,1,0:T(8,128)(2,1)S(1)}, u32[]{:S(2)}, u32[]{:S(2)}) collective-permute-start(bf16[1,128,512]{2,1,0:T(8,128)(2,1)S(1)} %bitcast.81), channel_id=1, source_target_pairs={{0,6},{1,7},{2,4},{3,5},{4,2},{5,3},{6,0},{7,1},{8,14},{9,15},{10,... | collective-permute-start | bytes 393224 | tf_op jit(solution)/shard_map/ppermute | solution.py:307
  118.1 2.0 %project_more.5 = (f32[3,128,256]{2,1,0:T(8,128)S(1)}, f32[128,128]{1,0:T(8,128)S(1)}) custom-call(s32[2]{0:T(128)S(1)} %pad_add_fusion.rank_ref, bf16[5,128,512]{2,1,0:T(8,128)(2,1)S(1)} %pad_maximum_fusion.1.x_ref, f32[1,8192]{1,0:T(1,128)S(1)} %get-tuple-element.104.gain_ref.refs_1_, f32[3,128,256]{2,1,0:T(8,128)S(1)} %get-tuple-element.162.acc_in, ...), custom_call_target="tpu_custom_call" | custom-call | flops 503316480 | bytes 491520 | tf_op jit(solution)/shard_map/project_more/pallas_call | solution.py:213
  120.6 4.9 %project_mix.5 = bf16[128,256]{1,0:T(8,128)(2,1)S(1)} custom-call(s32[2]{0:T(128)S(1)} %pad_add_fusion.rank_ref, bf16[8,128,512]{2,1,0:T(8,128)(2,1)S(1)} %collective-permute-done.38.refs_0_, f32[1,8192]{1,0:T(1,128)S(1)} %get-tuple-element.104.gain_ref.refs_1_, f32[3,128,256]{2,1,0:T(8,128)S(1)} %get-tuple-element.168.refs_2_, ...), custom_call_target="tpu_custom_call" | custom-call | flops 1610612736 | bytes 1572864 | tf_op jit(solution)/shard_map/project_mix/pallas_call | solution.py:213
  129.9 2.0 %collective-permute-done.40 = bf16[128,256]{1,0:T(8,128)(2,1)S(1)} collective-permute-done((bf16[128,256]{1,0:T(8,128)(2,1)S(1)}, bf16[128,256]{1,0:T(8,128)(2,1)S(1)}, u32[]{:S(2)}, u32[]{:S(2)}) %collective-permute-start.40) | collective-permute-done | bytes 65568 | tf_op jit(solution)/shard_map/ppermute | solution.py:307
  131.9 1.9 %collective-permute-done.41 = bf16[128,256]{1,0:T(8,128)(2,1)S(1)} collective-permute-done((bf16[128,256]{1,0:T(8,128)(2,1)S(1)}, bf16[128,256]{1,0:T(8,128)(2,1)S(1)}, u32[]{:S(2)}, u32[]{:S(2)}) %collective-permute-start.41) | collective-permute-done | bytes 65568 | tf_op jit(solution)/shard_map/ppermute | solution.py:307
  (146 shorter events, 69.3 us)
Async XLA Ops:
  0.9 7.2 %collective-permute-start = (bf16[128,512]{1,0:T(8,128)(2,1)S(1)}, bf16[128,512]{1,0:T(8,128)(2,1)S(1)}, u32[]{:S(2)}, u32[]{:S(2)}) collective-permute-start(bf16[128,512]{1,0:T(8,128)(2,1)S(1)} %select_bitcast_fusion.own_ref), channel_id=1, source_target_pairs={{0,2},{1,3},{2,0},{3,1},{4,6},{5,7},{6,4},{7,5},{8,10},{9,11},{10,... | collective-permute-start | bytes 393224 | tf_op jit(solution)/shard_map/ppermute | solution.py:307
  3.9 6.7 %collective-permute-start.1 = (bf16[128,512]{1,0:T(8,128)(2,1)S(1)}, bf16[128,512]{1,0:T(8,128)(2,1)S(1)}, u32[]{:S(2)}, u32[]{:S(2)}) collective-permute-start(bf16[128,512]{1,0:T(8,128)(2,1)S(1)} %select_bitcast_fusion.own_ref), channel_id=1, source_target_pairs={{0,4},{1,5},{2,6},{3,7},{4,0},{5,1},{6,2},{7,3},{8,12},{9,13},{10,... | collective-permute-start | bytes 393224 | tf_op jit(solution)/shard_map/ppermute | solution.py:307
  5.5 8.4 %collective-permute-start.2 = (bf16[128,512]{1,0:T(8,128)(2,1)S(1)}, bf16[128,512]{1,0:T(8,128)(2,1)S(1)}, u32[]{:S(2)}, u32[]{:S(2)}) collective-permute-start(bf16[128,512]{1,0:T(8,128)(2,1)S(1)} %select_bitcast_fusion.own_ref), channel_id=1, source_target_pairs={{0,8},{1,9},{2,10},{3,11},{4,12},{5,13},{6,14},{7,15},{8,0},{9,1},... | collective-permute-start | bytes 393224 | tf_op jit(solution)/shard_map/ppermute | solution.py:307
  14.0 10.5 %collective-permute-start.3 = (bf16[2,128,512]{2,1,0:T(8,128)(2,1)S(1)}, bf16[2,128,512]{2,1,0:T(8,128)(2,1)S(1)}, u32[]{:S(2)}, u32[]{:S(2)}) collective-permute-start(bf16[2,128,512]{2,1,0:T(8,128)(2,1)S(1)} %pad_maximum_fusion.6), channel_id=1, source_target_pairs={{0,2},{1,3},{2,0},{3,1},{4,6},{5,7},{6,4},{7,5},{8,10},{9,11},{10,... | collective-permute-start | bytes 786440 | tf_op jit(solution)/shard_map/ppermute | solution.py:307
  14.6 9.9 %collective-permute-start.4 = (bf16[1,128,512]{2,1,0:T(8,128)(2,1)S(1)}, bf16[1,128,512]{2,1,0:T(8,128)(2,1)S(1)}, u32[]{:S(2)}, u32[]{:S(2)}) collective-permute-start(bf16[1,128,512]{2,1,0:T(8,128)(2,1)S(1)} %bitcast.88), channel_id=1, source_target_pairs={{0,6},{1,7},{2,4},{3,5},{4,2},{5,3},{6,0},{7,1},{8,14},{9,15},{10,... | collective-permute-start | bytes 393224 | tf_op jit(solution)/shard_map/ppermute | solution.py:307
  16.0 8.5 %collective-permute-start.5 = (bf16[1,128,512]{2,1,0:T(8,128)(2,1)S(1)}, bf16[1,128,512]{2,1,0:T(8,128)(2,1)S(1)}, u32[]{:S(2)}, u32[]{:S(2)}) collective-permute-start(bf16[1,128,512]{2,1,0:T(8,128)(2,1)S(1)} %bitcast.89), channel_id=1, source_target_pairs={{0,4},{1,5},{2,6},{3,7},{4,0},{5,1},{6,2},{7,3},{8,12},{9,13},{10,... | collective-permute-start | bytes 393224 | tf_op jit(solution)/shard_map/ppermute | solution.py:307
  33.2 6.4 %collective-permute-start.9 = (bf16[128,256]{1,0:T(8,128)(2,1)S(1)}, bf16[128,256]{1,0:T(8,128)(2,1)S(1)}, u32[]{:S(2)}, u32[]{:S(2)}) collective-permute-start(bf16[128,256]{1,0:T(8,128)(2,1)S(1)} %project_mix.3), channel_id=1, source_target_pairs={{0,8},{1,9},{2,10},{3,11},{4,12},{5,13},{6,14},{7,15},{8,0},{9,1},... | collective-permute-start | bytes 196616 | tf_op jit(solution)/shard_map/ppermute | solution.py:307
  41.2 5.2 %collective-permute-start.11 = (bf16[1,128,256]{2,1,0:T(8,128)(2,1)S(1)}, bf16[1,128,256]{2,1,0:T(8,128)(2,1)S(1)}, u32[]{:S(2)}, u32[]{:S(2)}) collective-permute-start(bf16[1,128,256]{2,1,0:T(8,128)(2,1)S(1)} %bitcast.99), channel_id=1, source_target_pairs={{0,6},{1,7},{2,4},{3,5},{4,2},{5,3},{6,0},{7,1},{8,14},{9,15},{10,... | collective-permute-start | bytes 196616 | tf_op jit(solution)/shard_map/ppermute | solution.py:307
  49.4 10.7 %collective-permute-start.14 = (bf16[128,512]{1,0:T(8,128)(2,1)S(1)}, bf16[128,512]{1,0:T(8,128)(2,1)S(1)}, u32[]{:S(2)}, u32[]{:S(2)}) collective-permute-start(bf16[128,512]{1,0:T(8,128)(2,1)S(1)} %get-tuple-element.126), channel_id=1, source_target_pairs={{0,16},{1,17},{2,18},{3,19},{4,20},{5,21},{6,22},{7,23},{8,24},{9,... | collective-permute-start | bytes 393224 | tf_op jit(solution)/shard_map/ppermute | solution.py:316
  51.0 9.1 %collective-permute-start.15 = (bf16[128,512]{1,0:T(8,128)(2,1)S(1)}, bf16[128,512]{1,0:T(8,128)(2,1)S(1)}, u32[]{:S(2)}, u32[]{:S(2)}) collective-permute-start(bf16[128,512]{1,0:T(8,128)(2,1)S(1)} %get-tuple-element.126), channel_id=1, source_target_pairs={{0,20},{1,21},{2,22},{3,23},{4,16},{5,17},{6,18},{7,19},{8,28},{9,... | collective-permute-start | bytes 393224 | tf_op jit(solution)/shard_map/ppermute | solution.py:316
  51.9 9.6 %collective-permute-start.16 = (bf16[128,512]{1,0:T(8,128)(2,1)S(1)}, bf16[128,512]{1,0:T(8,128)(2,1)S(1)}, u32[]{:S(2)}, u32[]{:S(2)}) collective-permute-start(bf16[128,512]{1,0:T(8,128)(2,1)S(1)} %get-tuple-element.126), channel_id=1, source_target_pairs={{0,24},{1,25},{2,26},{3,27},{4,28},{5,29},{6,30},{7,31},{8,16},{9,... | collective-permute-start | bytes 393224 | tf_op jit(solution)/shard_map/ppermute | solution.py:316
  54.4 7.1 %collective-permute-start.17 = (bf16[128,512]{1,0:T(8,128)(2,1)S(1)}, bf16[128,512]{1,0:T(8,128)(2,1)S(1)}, u32[]{:S(2)}, u32[]{:S(2)}) collective-permute-start(bf16[128,512]{1,0:T(8,128)(2,1)S(1)} %get-tuple-element.126), channel_id=1, source_target_pairs={{0,2},{1,3},{2,0},{3,1},{4,6},{5,7},{6,4},{7,5},{8,10},{9,11},{10,... | collective-permute-start | bytes 393224 | tf_op jit(solution)/shard_map/ppermute | solution.py:307
  61.6 8.9 %collective-permute-start.18 = (bf16[2,128,512]{2,1,0:T(8,128)(2,1)S(1)}, bf16[2,128,512]{2,1,0:T(8,128)(2,1)S(1)}, u32[]{:S(2)}, u32[]{:S(2)}) collective-permute-start(bf16[2,128,512]{2,1,0:T(8,128)(2,1)S(1)} %pad_maximum_fusion.7), channel_id=1, source_target_pairs={{0,2},{1,3},{2,0},{3,1},{4,6},{5,7},{6,4},{7,5},{8,10},{9,11},{10,... | collective-permute-start | bytes 786440 | tf_op jit(solution)/shard_map/ppermute | solution.py:307
  63.2 6.3 %collective-permute-start.19 = (bf16[1,128,512]{2,1,0:T(8,128)(2,1)S(1)}, bf16[1,128,512]{2,1,0:T(8,128)(2,1)S(1)}, u32[]{:S(2)}, u32[]{:S(2)}) collective-permute-start(bf16[1,128,512]{2,1,0:T(8,128)(2,1)S(1)} %bitcast.77), channel_id=1, source_target_pairs={{0,6},{1,7},{2,4},{3,5},{4,2},{5,3},{6,0},{7,1},{8,14},{9,15},{10,... | collective-permute-start | bytes 393224 | tf_op jit(solution)/shard_map/ppermute | solution.py:307
  80.8 5.9 %collective-permute-start.25 = (bf16[128,256]{1,0:T(8,128)(2,1)S(1)}, bf16[128,256]{1,0:T(8,128)(2,1)S(1)}, u32[]{:S(2)}, u32[]{:S(2)}) collective-permute-start(bf16[128,256]{1,0:T(8,128)(2,1)S(1)} %project_mix.4), channel_id=1, source_target_pairs={{0,8},{1,9},{2,10},{3,11},{4,12},{5,13},{6,14},{7,15},{8,0},{9,1},... | collective-permute-start | bytes 196616 | tf_op jit(solution)/shard_map/ppermute | solution.py:307
  87.7 5.2 %collective-permute-start.27 = (bf16[1,128,256]{2,1,0:T(8,128)(2,1)S(1)}, bf16[1,128,256]{2,1,0:T(8,128)(2,1)S(1)}, u32[]{:S(2)}, u32[]{:S(2)}) collective-permute-start(bf16[1,128,256]{2,1,0:T(8,128)(2,1)S(1)} %bitcast.102), channel_id=1, source_target_pairs={{0,6},{1,7},{2,4},{3,5},{4,2},{5,3},{6,0},{7,1},{8,14},{9,15},{10,... | collective-permute-start | bytes 196616 | tf_op jit(solution)/shard_map/ppermute | solution.py:307
  96.2 11.9 %collective-permute-start.30 = (bf16[128,512]{1,0:T(8,128)(2,1)S(1)}, bf16[128,512]{1,0:T(8,128)(2,1)S(1)}, u32[]{:S(2)}, u32[]{:S(2)}) collective-permute-start(bf16[128,512]{1,0:T(8,128)(2,1)S(1)} %get-tuple-element.153), channel_id=1, source_target_pairs={{0,16},{1,17},{2,18},{3,19},{4,20},{5,21},{6,22},{7,23},{8,24},{9,... | collective-permute-start | bytes 393224 | tf_op jit(solution)/shard_map/ppermute | solution.py:316
  99.0 9.2 %collective-permute-start.31 = (bf16[128,512]{1,0:T(8,128)(2,1)S(1)}, bf16[128,512]{1,0:T(8,128)(2,1)S(1)}, u32[]{:S(2)}, u32[]{:S(2)}) collective-permute-start(bf16[128,512]{1,0:T(8,128)(2,1)S(1)} %get-tuple-element.153), channel_id=1, source_target_pairs={{0,20},{1,21},{2,22},{3,23},{4,16},{5,17},{6,18},{7,19},{8,28},{9,... | collective-permute-start | bytes 393224 | tf_op jit(solution)/shard_map/ppermute | solution.py:316
  99.2 9.9 %collective-permute-start.32 = (bf16[128,512]{1,0:T(8,128)(2,1)S(1)}, bf16[128,512]{1,0:T(8,128)(2,1)S(1)}, u32[]{:S(2)}, u32[]{:S(2)}) collective-permute-start(bf16[128,512]{1,0:T(8,128)(2,1)S(1)} %get-tuple-element.153), channel_id=1, source_target_pairs={{0,24},{1,25},{2,26},{3,27},{4,28},{5,29},{6,30},{7,31},{8,16},{9,... | collective-permute-start | bytes 393224 | tf_op jit(solution)/shard_map/ppermute | solution.py:316
  101.9 7.2 %collective-permute-start.33 = (bf16[128,512]{1,0:T(8,128)(2,1)S(1)}, bf16[128,512]{1,0:T(8,128)(2,1)S(1)}, u32[]{:S(2)}, u32[]{:S(2)}) collective-permute-start(bf16[128,512]{1,0:T(8,128)(2,1)S(1)} %get-tuple-element.153), channel_id=1, source_target_pairs={{0,2},{1,3},{2,0},{3,1},{4,6},{5,7},{6,4},{7,5},{8,10},{9,11},{10,... | collective-permute-start | bytes 393224 | tf_op jit(solution)/shard_map/ppermute | solution.py:307
  109.2 8.6 %collective-permute-start.34 = (bf16[2,128,512]{2,1,0:T(8,128)(2,1)S(1)}, bf16[2,128,512]{2,1,0:T(8,128)(2,1)S(1)}, u32[]{:S(2)}, u32[]{:S(2)}) collective-permute-start(bf16[2,128,512]{2,1,0:T(8,128)(2,1)S(1)} %pad_maximum_fusion.8), channel_id=1, source_target_pairs={{0,2},{1,3},{2,0},{3,1},{4,6},{5,7},{6,4},{7,5},{8,10},{9,11},{10,... | collective-permute-start | bytes 786440 | tf_op jit(solution)/shard_map/ppermute | solution.py:307
  110.1 7.1 %collective-permute-start.35 = (bf16[1,128,512]{2,1,0:T(8,128)(2,1)S(1)}, bf16[1,128,512]{2,1,0:T(8,128)(2,1)S(1)}, u32[]{:S(2)}, u32[]{:S(2)}) collective-permute-start(bf16[1,128,512]{2,1,0:T(8,128)(2,1)S(1)} %bitcast.81), channel_id=1, source_target_pairs={{0,6},{1,7},{2,4},{3,5},{4,2},{5,3},{6,0},{7,1},{8,14},{9,15},{10,... | collective-permute-start | bytes 393224 | tf_op jit(solution)/shard_map/ppermute | solution.py:307
  127.6 6.3 %collective-permute-start.41 = (bf16[128,256]{1,0:T(8,128)(2,1)S(1)}, bf16[128,256]{1,0:T(8,128)(2,1)S(1)}, u32[]{:S(2)}, u32[]{:S(2)}) collective-permute-start(bf16[128,256]{1,0:T(8,128)(2,1)S(1)} %project_mix.5), channel_id=1, source_target_pairs={{0,8},{1,9},{2,10},{3,11},{4,12},{5,13},{6,14},{7,15},{8,0},{9,1},... | collective-permute-start | bytes 196616 | tf_op jit(solution)/shard_map/ppermute | solution.py:307
  135.1 5.2 %collective-permute-start.43 = (bf16[1,128,256]{2,1,0:T(8,128)(2,1)S(1)}, bf16[1,128,256]{2,1,0:T(8,128)(2,1)S(1)}, u32[]{:S(2)}, u32[]{:S(2)}) collective-permute-start(bf16[1,128,256]{2,1,0:T(8,128)(2,1)S(1)} %bitcast.105), channel_id=1, source_target_pairs={{0,6},{1,7},{2,4},{3,5},{4,2},{5,3},{6,0},{7,1},{8,14},{9,15},{10,... | collective-permute-start | bytes 196616 | tf_op jit(solution)/shard_map/ppermute | solution.py:307
  (25 other events, 113.9 us)

commit v13 on v12

--- a/solution.py
+++ b/solution.py
@@ -113,18 +113,12 @@
     project(blocks, core, lambda n: x_ref[n], lambda n: w_refs[n], rank_ref, gain_ref, acc_ref, sq_ref)
 
 
-def more_kernel(blocks, core, rank_ref, x_ref, gain_ref, acc_in, sq_in, *refs):
-    w_refs, (acc_ref, sq_ref) = refs[:-2], refs[-2:]
-    before = (acc_in, sq_in)
-    project(blocks, core, lambda n: x_ref[n], lambda n: w_refs[n], rank_ref, gain_ref, acc_ref, sq_ref, before)
-
-
 def mix_kernel(blocks, core, model_width, rank_ref, *refs):
     sides, refs = refs[: core - 1], refs[core - 1 :]
     count = len(blocks) // max(core - 1, 1)
-    gain_ref, acc_in, sq_in, short_ref, long_ref = refs[:5]
-    w_refs = refs[5 : 5 + count]
-    y_ref, acc_ref, sq_ref, pad_ref, query_ref = refs[5 + count :]
+    gain_ref, acc_in, sq_in, acc_more, sq_more, short_ref, long_ref = refs[:7]
+    w_refs = refs[7 : 7 + count]
+    y_ref, acc_ref, sq_ref, pad_ref, query_ref = refs[7 + count :]
     branches, tok_len, chan = acc_in.shape
     project(
         blocks,
@@ -138,13 +132,13 @@
         (acc_in, sq_in),
     )
 
-    total = jnp.sum(sq_ref[...], axis=1, keepdims=True)
+    total = jnp.sum(sq_ref[...] + sq_more[...], axis=1, keepdims=True)
     factor = lax.rsqrt(total / model_width + EPS)
     taps = short_ref.shape[1]
     pad_ref[0:PAD, :] = jnp.zeros((PAD, chan), jnp.float32)
 
     def branch(i):
-        u = acc_ref[i] * factor
+        u = (acc_ref[i] + acc_more[i]) * factor
         pad_ref[PAD : PAD + tok_len, :] = u
         z = short_ref[i, 0] * u
         for j in range(1, taps):
@@ -249,23 +243,22 @@
     return [acc, sq], {"in": dict(zip(order, pieces)), "gain": gain, "long": long_rows}
 
 
-def project_part(blocks, core, x, params, sums, rank):
+def project_part(blocks, core, x, params, rank, name):
     w_refs = [params["in"][cell] for cell, _ in blocks]
     branches, chan, _ = w_refs[0].shape
-    kernel, name = (more_kernel, "project_more") if sums else (first_kernel, "project_first")
-    operands = [rank, x, params["gain"], *sums, *w_refs]
+    operands = [rank, x, params["gain"], *w_refs]
     flops = 2 * x.size * branches * chan
-    return call(functools.partial(kernel, blocks, core), operands, sums_of(x, branches, chan), [], flops, name)
-
-
-def mix(blocks, core, model_width, sides, params, sums, short_rows, rank):
+    return call(functools.partial(first_kernel, blocks, core), operands, sums_of(x, branches, chan), [], flops, name)
+
+
+def mix(blocks, core, model_width, sides, params, sums, more, short_rows, rank):
     rows, chan = sums[0].shape[1:]
     scratch = [pltpu.VMEM(total.shape, total.dtype) for total in sums]
     scratch += [pltpu.VMEM((PAD + rows, chan), jnp.float32), pltpu.VMEM((rows, chan), jnp.float32)]
     w_refs = [params["in"][cell] for cell, _ in blocks[: len(blocks) // max(core - 1, 1)]]
     return call(
         functools.partial(mix_kernel, blocks, core, model_width),
-        [rank, *sides, params["gain"], *sums, short_rows, params["long"], *w_refs],
+        [rank, *sides, params["gain"], *sums, *more, short_rows, params["long"], *w_refs],
         [jax.ShapeDtypeStruct((rows, chan), jnp.bfloat16)],
         scratch,
         2 * rows * model_width * 3 * chan,
@@ -347,7 +340,7 @@
         direct = jnp.stack(list(blocks.values()))
         here = of_cores(blocks, [0])
         if params:
-            sums = project_part(here, core, after(direct, rest[min(2, len(rest) - 1)]), params, [], rank)
+            sums = project_part(here, core, after(direct, rest[min(2, len(rest) - 1)]), params, rank, "project_first")
         else:
             sums, params = project_load(
                 here, order, core, direct, w_in[0], norm_gain, filter_taps[0], decay_rate, rank
@@ -355,9 +348,9 @@
         relayed = jnp.concatenate(after(rest, sums))
         everything = jnp.concatenate([direct, relayed])
         sides = [swap(everything, c) for c in range(1, core)]
-        sums = project_part(of_cores(cells, [0]), core, relayed, params, sums, rank)
-        sides = after(sides, sums)
-        y = mix(of_cores(order, range(1, core)), core, norm_gain.shape[1], sides, params, sums, short_rows, rank)
+        more = project_part(of_cores(cells, [0]), core, relayed, params, rank, "project_more")
+        sides = after(sides, more)
+        y = mix(of_cores(order, range(1, core)), core, norm_gain.shape[1], sides, params, sums, more, short_rows, rank)
         y_blocks, _ = round_one(y)
         cells, rest = round_two(y_blocks, [])
         everything = jnp.concatenate([jnp.stack(list(y_blocks.values())), *rest])

time: 144 us -> 144 us (level)
  no operation moved by 1% of the time
where the time goes in v13:
time: 144 us
  starting transfers between devices  56.1 us (39%)
  waiting for transfers between devices  48.5 us (34%)
  Pallas kernels  36.3 us (25%)
  other arithmetic  2.33 us (2%)
    ppermute x38, starting transfers between devices, swap(): return lax.ppermute(value, 'dp', [(r, r ^ offset) for r in range(dp_count)])  42.1 us
    pallas_call x15, Pallas kernels, call(): pl.pallas_call(kernel, in_specs=specs, out_specs=in_vmem(len(outs)), out_...  36.3 us
    ppermute x38, waiting for transfers between devices, swap(): return lax.ppermute(value, 'dp', [(r, r ^ offset) for r in range(dp_count)])  35.4 us
    ppermute x8, starting transfers between devices, onward(): return lax.ppermute(value, ('section', 'dp'), pairs)  14 us
    ppermute x8, waiting for transfers between devices, onward(): return lax.ppermute(value, ('section', 'dp'), pairs)  13.2 us
  transfers between devices with their start and end apart: 46, of which 35 were waited for; matrix products, arithmetic and copies ran while one was open for 0% of the time, Pallas kernels for 13%

profile of v13, /device:TPU:0, one launch (start us, length us, event | category | flops | bytes accessed | tf_op | source)
XLA Modules:
  0.0 144.1 jit_solution(12783932265401267444)
XLA Ops:
  0.9 3.0 %collective-permute-start = (bf16[128,512]{1,0:T(8,128)(2,1)S(1)}, bf16[128,512]{1,0:T(8,128)(2,1)S(1)}, u32[]{:S(2)}, u32[]{:S(2)}) collective-permute-start(bf16[128,512]{1,0:T(8,128)(2,1)S(1)} %select_bitcast_fusion.own_ref), channel_id=1, source_target_pairs={{0,2},{1,3},{2,0},{3,1},{4,6},{5,7},{6,4},{7,5},{8,10},{9,11},{10,... | collective-permute-start | bytes 393224 | tf_op jit(solution)/shard_map/ppermute | solution.py:300
  5.5 2.6 %collective-permute-start.2 = (bf16[128,512]{1,0:T(8,128)(2,1)S(1)}, bf16[128,512]{1,0:T(8,128)(2,1)S(1)}, u32[]{:S(2)}, u32[]{:S(2)}) collective-permute-start(bf16[128,512]{1,0:T(8,128)(2,1)S(1)} %select_bitcast_fusion.own_ref), channel_id=1, source_target_pairs={{0,8},{1,9},{2,10},{3,11},{4,12},{5,13},{6,14},{7,15},{8,0},{9,1},... | collective-permute-start | bytes 393224 | tf_op jit(solution)/shard_map/ppermute | solution.py:300
  8.2 2.4 %collective-permute-done.1 = bf16[128,512]{1,0:T(8,128)(2,1)S(1)} collective-permute-done((bf16[128,512]{1,0:T(8,128)(2,1)S(1)}, bf16[128,512]{1,0:T(8,128)(2,1)S(1)}, u32[]{:S(2)}, u32[]{:S(2)}) %collective-permute-start.1) | collective-permute-done | bytes 131104 | tf_op jit(solution)/shard_map/ppermute | solution.py:300
  10.6 3.3 %collective-permute-done.2 = bf16[128,512]{1,0:T(8,128)(2,1)S(1)} collective-permute-done((bf16[128,512]{1,0:T(8,128)(2,1)S(1)}, bf16[128,512]{1,0:T(8,128)(2,1)S(1)}, u32[]{:S(2)}, u32[]{:S(2)}) %collective-permute-start.2) | collective-permute-done | bytes 131104 | tf_op jit(solution)/shard_map/ppermute | solution.py:300
  17.7 6.8 %project_load.1 = (bf16[3,256,1024]{2,1,0:T(8,128)(2,1)S(1)}, bf16[3,256,1024]{2,1,0:T(8,128)(2,1)S(1)}, bf16[3,256,1024]{2,1,0:T(8,128)(2,1)S(1)}, bf16[3,256,1...) custom-call(s32[2]{0:T(128)S(1)} %pad_add_fusion.rank_ref, ...), custom_call_target="tpu_custom_call" | custom-call | flops 402653184 | bytes 393216 | tf_op jit(solution)/shard_map/project_load/pallas_call | solution.py:207
  24.7 1.7 %project_more.3 = (f32[3,128,256]{2,1,0:T(8,128)S(1)}, f32[128,128]{1,0:T(8,128)S(1)}) custom-call(s32[2]{0:T(128)S(1)} %pad_add_fusion.rank_ref, bf16[4,128,512]{2,1,0:T(8,128)(2,1)S(1)} %pad_maximum_fusion.3.x_ref, f32[1,8192]{1,0:T(1,128)S(1)} %get-tuple-element.104.gain_ref.refs_1_, ...), custom_call_target="tpu_custom_call" | custom-call | flops 402653184 | bytes 393216 | tf_op jit(solution)/shard_map/project_more/pallas_call | solution.py:207
  27.3 4.9 %project_mix.3 = bf16[128,256]{1,0:T(8,128)(2,1)S(1)} custom-call(s32[2]{0:T(128)S(1)} %pad_add_fusion.rank_ref, bf16[8,128,512]{2,1,0:T(8,128)(2,1)S(1)} %collective-permute-done.6.refs_0_, f32[1,8192]{1,0:T(1,128)S(1)} %get-tuple-element.104.gain_ref.refs_1_, f32[3,128,256]{2,1,0:T(8,128)S(1)} %get-tuple-element.99.refs_2_, ...), custom_call_target="tpu_custom_call" | custom-call | flops 1610612736 | bytes 1572864 | tf_op jit(solution)/shard_map/project_mix/pallas_call | solution.py:207
  33.2 2.7 %collective-permute-start.9 = (bf16[128,256]{1,0:T(8,128)(2,1)S(1)}, bf16[128,256]{1,0:T(8,128)(2,1)S(1)}, u32[]{:S(2)}, u32[]{:S(2)}) collective-permute-start(bf16[128,256]{1,0:T(8,128)(2,1)S(1)} %project_mix.3), channel_id=1, source_target_pairs={{0,8},{1,9},{2,10},{3,11},{4,12},{5,13},{6,14},{7,15},{8,0},{9,1},... | collective-permute-start | bytes 196616 | tf_op jit(solution)/shard_map/ppermute | solution.py:300
  37.8 1.8 %collective-permute-done.9 = bf16[128,256]{1,0:T(8,128)(2,1)S(1)} collective-permute-done((bf16[128,256]{1,0:T(8,128)(2,1)S(1)}, bf16[128,256]{1,0:T(8,128)(2,1)S(1)}, u32[]{:S(2)}, u32[]{:S(2)}) %collective-permute-start.9) | collective-permute-done | bytes 65568 | tf_op jit(solution)/shard_map/ppermute | solution.py:300
  51.9 2.5 %collective-permute-start.16 = (bf16[128,512]{1,0:T(8,128)(2,1)S(1)}, bf16[128,512]{1,0:T(8,128)(2,1)S(1)}, u32[]{:S(2)}, u32[]{:S(2)}) collective-permute-start(bf16[128,512]{1,0:T(8,128)(2,1)S(1)} %get-tuple-element.126), channel_id=1, source_target_pairs={{0,24},{1,25},{2,26},{3,27},{4,28},{5,29},{6,30},{7,31},{8,16},{9,... | collective-permute-start | bytes 393224 | tf_op jit(solution)/shard_map/ppermute | solution.py:309
  55.9 4.2 %collective-permute-done.14.own_ref = bf16[128,512]{1,0:T(8,128)(2,1)S(1)} collective-permute-done((bf16[128,512]{1,0:T(8,128)(2,1)S(1)}, bf16[128,512]{1,0:T(8,128)(2,1)S(1)}, u32[]{:S(2)}, u32[]{:S(2)}) %collective-permute-start.14) | collective-permute-done | bytes 131104 | tf_op jit(solution)/shard_map/ppermute | solution.py:309
  63.3 2.0 %collective-permute-start.19 = (bf16[1,128,512]{2,1,0:T(8,128)(2,1)S(1)}, bf16[1,128,512]{2,1,0:T(8,128)(2,1)S(1)}, u32[]{:S(2)}, u32[]{:S(2)}) collective-permute-start(bf16[1,128,512]{2,1,0:T(8,128)(2,1)S(1)} %bitcast.77), channel_id=1, source_target_pairs={{0,6},{1,7},{2,4},{3,5},{4,2},{5,3},{6,0},{7,1},{8,14},{9,15},{10,... | collective-permute-start | bytes 393224 | tf_op jit(solution)/shard_map/ppermute | solution.py:300
  70.7 2.0 %project_more.4 = (f32[3,128,256]{2,1,0:T(8,128)S(1)}, f32[128,128]{1,0:T(8,128)S(1)}) custom-call(s32[2]{0:T(128)S(1)} %pad_add_fusion.rank_ref, bf16[5,128,512]{2,1,0:T(8,128)(2,1)S(1)} %pad_maximum_fusion.x_ref, f32[1,8192]{1,0:T(1,128)S(1)} %get-tuple-element.104.gain_ref.refs_1_, bf16[3,256,1024]{2,1,0:T(8,128)(2,1)S(1)} %get-tuple-element.105.refs_0_.refs_12_.refs_11_, ...), custom_call_target="tpu_custom_call" | custom-call | flops 503316480 | bytes 491520 | tf_op jit(solution)/shard_map/project_more/pallas_call | solution.py:207
  73.3 5.1 %project_mix.4 = bf16[128,256]{1,0:T(8,128)(2,1)S(1)} custom-call(s32[2]{0:T(128)S(1)} %pad_add_fusion.rank_ref, bf16[8,128,512]{2,1,0:T(8,128)(2,1)S(1)} %collective-permute-done.22.refs_0_, f32[1,8192]{1,0:T(1,128)S(1)} %get-tuple-element.104.gain_ref.refs_1_, f32[3,128,256]{2,1,0:T(8,128)S(1)} %get-tuple-element.135.refs_2_, ...), custom_call_target="tpu_custom_call" | custom-call | flops 1610612736 | bytes 1572864 | tf_op jit(solution)/shard_map/project_mix/pallas_call | solution.py:207
  83.9 2.8 %collective-permute-done.25 = bf16[128,256]{1,0:T(8,128)(2,1)S(1)} collective-permute-done((bf16[128,256]{1,0:T(8,128)(2,1)S(1)}, bf16[128,256]{1,0:T(8,128)(2,1)S(1)}, u32[]{:S(2)}, u32[]{:S(2)}) %collective-permute-start.25) | collective-permute-done | bytes 65568 | tf_op jit(solution)/shard_map/ppermute | solution.py:300
  88.5 1.8 %collective-permute-start.28 = (bf16[1,128,256]{2,1,0:T(8,128)(2,1)S(1)}, bf16[1,128,256]{2,1,0:T(8,128)(2,1)S(1)}, u32[]{:S(2)}, u32[]{:S(2)}) collective-permute-start(bf16[1,128,256]{2,1,0:T(8,128)(2,1)S(1)} %bitcast.103), channel_id=1, source_target_pairs={{0,4},{1,5},{2,6},{3,7},{4,0},{5,1},{6,2},{7,3},{8,12},{9,13},{10,... | collective-permute-start | bytes 196616 | tf_op jit(solution)/shard_map/ppermute | solution.py:300
  96.2 2.8 %collective-permute-start.30 = (bf16[128,512]{1,0:T(8,128)(2,1)S(1)}, bf16[128,512]{1,0:T(8,128)(2,1)S(1)}, u32[]{:S(2)}, u32[]{:S(2)}) collective-permute-start(bf16[128,512]{1,0:T(8,128)(2,1)S(1)} %get-tuple-element.153), channel_id=1, source_target_pairs={{0,16},{1,17},{2,18},{3,19},{4,20},{5,21},{6,22},{7,23},{8,24},{9,... | collective-permute-start | bytes 393224 | tf_op jit(solution)/shard_map/ppermute | solution.py:309
  99.3 2.7 %collective-permute-start.32 = (bf16[128,512]{1,0:T(8,128)(2,1)S(1)}, bf16[128,512]{1,0:T(8,128)(2,1)S(1)}, u32[]{:S(2)}, u32[]{:S(2)}) collective-permute-start(bf16[128,512]{1,0:T(8,128)(2,1)S(1)} %get-tuple-element.153), channel_id=1, source_target_pairs={{0,24},{1,25},{2,26},{3,27},{4,28},{5,29},{6,30},{7,31},{8,16},{9,... | collective-permute-start | bytes 393224 | tf_op jit(solution)/shard_map/ppermute | solution.py:309
  102.8 5.3 %collective-permute-done.30.own_ref = bf16[128,512]{1,0:T(8,128)(2,1)S(1)} collective-permute-done((bf16[128,512]{1,0:T(8,128)(2,1)S(1)}, bf16[128,512]{1,0:T(8,128)(2,1)S(1)}, u32[]{:S(2)}, u32[]{:S(2)}) %collective-permute-start.30) | collective-permute-done | bytes 131104 | tf_op jit(solution)/shard_map/ppermute | solution.py:309
  110.1 2.7 %collective-permute-start.35 = (bf16[1,128,512]{2,1,0:T(8,128)(2,1)S(1)}, bf16[1,128,512]{2,1,0:T(8,128)(2,1)S(1)}, u32[]{:S(2)}, u32[]{:S(2)}) collective-permute-start(bf16[1,128,512]{2,1,0:T(8,128)(2,1)S(1)} %bitcast.81), channel_id=1, source_target_pairs={{0,6},{1,7},{2,4},{3,5},{4,2},{5,3},{6,0},{7,1},{8,14},{9,15},{10,... | collective-permute-start | bytes 393224 | tf_op jit(solution)/shard_map/ppermute | solution.py:300
  118.1 2.0 %project_more.5 = (f32[3,128,256]{2,1,0:T(8,128)S(1)}, f32[128,128]{1,0:T(8,128)S(1)}) custom-call(s32[2]{0:T(128)S(1)} %pad_add_fusion.rank_ref, bf16[5,128,512]{2,1,0:T(8,128)(2,1)S(1)} %pad_maximum_fusion.1.x_ref, f32[1,8192]{1,0:T(1,128)S(1)} %get-tuple-element.104.gain_ref.refs_1_, ...), custom_call_target="tpu_custom_call" | custom-call | flops 503316480 | bytes 491520 | tf_op jit(solution)/shard_map/project_more/pallas_call | solution.py:207
  120.6 4.9 %project_mix.5 = bf16[128,256]{1,0:T(8,128)(2,1)S(1)} custom-call(s32[2]{0:T(128)S(1)} %pad_add_fusion.rank_ref, bf16[8,128,512]{2,1,0:T(8,128)(2,1)S(1)} %collective-permute-done.38.refs_0_, f32[1,8192]{1,0:T(1,128)S(1)} %get-tuple-element.104.gain_ref.refs_1_, f32[3,128,256]{2,1,0:T(8,128)S(1)} %get-tuple-element.162.refs_2_, ...), custom_call_target="tpu_custom_call" | custom-call | flops 1610612736 | bytes 1572864 | tf_op jit(solution)/shard_map/project_mix/pallas_call | solution.py:207
  129.9 2.1 %collective-permute-done.40 = bf16[128,256]{1,0:T(8,128)(2,1)S(1)} collective-permute-done((bf16[128,256]{1,0:T(8,128)(2,1)S(1)}, bf16[128,256]{1,0:T(8,128)(2,1)S(1)}, u32[]{:S(2)}, u32[]{:S(2)}) %collective-permute-start.40) | collective-permute-done | bytes 65568 | tf_op jit(solution)/shard_map/ppermute | solution.py:300
  131.9 2.0 %collective-permute-done.41 = bf16[128,256]{1,0:T(8,128)(2,1)S(1)} collective-permute-done((bf16[128,256]{1,0:T(8,128)(2,1)S(1)}, bf16[128,256]{1,0:T(8,128)(2,1)S(1)}, u32[]{:S(2)}, u32[]{:S(2)}) %collective-permute-start.41) | collective-permute-done | bytes 65568 | tf_op jit(solution)/shard_map/ppermute | solution.py:300
  (146 shorter events, 69.5 us)
Async XLA Ops:
  0.9 7.2 %collective-permute-start = (bf16[128,512]{1,0:T(8,128)(2,1)S(1)}, bf16[128,512]{1,0:T(8,128)(2,1)S(1)}, u32[]{:S(2)}, u32[]{:S(2)}) collective-permute-start(bf16[128,512]{1,0:T(8,128)(2,1)S(1)} %select_bitcast_fusion.own_ref), channel_id=1, source_target_pairs={{0,2},{1,3},{2,0},{3,1},{4,6},{5,7},{6,4},{7,5},{8,10},{9,11},{10,... | collective-permute-start | bytes 393224 | tf_op jit(solution)/shard_map/ppermute | solution.py:300
  3.9 6.7 %collective-permute-start.1 = (bf16[128,512]{1,0:T(8,128)(2,1)S(1)}, bf16[128,512]{1,0:T(8,128)(2,1)S(1)}, u32[]{:S(2)}, u32[]{:S(2)}) collective-permute-start(bf16[128,512]{1,0:T(8,128)(2,1)S(1)} %select_bitcast_fusion.own_ref), channel_id=1, source_target_pairs={{0,4},{1,5},{2,6},{3,7},{4,0},{5,1},{6,2},{7,3},{8,12},{9,13},{10,... | collective-permute-start | bytes 393224 | tf_op jit(solution)/shard_map/ppermute | solution.py:300
  5.5 8.4 %collective-permute-start.2 = (bf16[128,512]{1,0:T(8,128)(2,1)S(1)}, bf16[128,512]{1,0:T(8,128)(2,1)S(1)}, u32[]{:S(2)}, u32[]{:S(2)}) collective-permute-start(bf16[128,512]{1,0:T(8,128)(2,1)S(1)} %select_bitcast_fusion.own_ref), channel_id=1, source_target_pairs={{0,8},{1,9},{2,10},{3,11},{4,12},{5,13},{6,14},{7,15},{8,0},{9,1},... | collective-permute-start | bytes 393224 | tf_op jit(solution)/shard_map/ppermute | solution.py:300
  14.0 10.5 %collective-permute-start.3 = (bf16[2,128,512]{2,1,0:T(8,128)(2,1)S(1)}, bf16[2,128,512]{2,1,0:T(8,128)(2,1)S(1)}, u32[]{:S(2)}, u32[]{:S(2)}) collective-permute-start(bf16[2,128,512]{2,1,0:T(8,128)(2,1)S(1)} %pad_maximum_fusion.6), channel_id=1, source_target_pairs={{0,2},{1,3},{2,0},{3,1},{4,6},{5,7},{6,4},{7,5},{8,10},{9,11},{10,... | collective-permute-start | bytes 786440 | tf_op jit(solution)/shard_map/ppermute | solution.py:300
  14.6 9.9 %collective-permute-start.4 = (bf16[1,128,512]{2,1,0:T(8,128)(2,1)S(1)}, bf16[1,128,512]{2,1,0:T(8,128)(2,1)S(1)}, u32[]{:S(2)}, u32[]{:S(2)}) collective-permute-start(bf16[1,128,512]{2,1,0:T(8,128)(2,1)S(1)} %bitcast.88), channel_id=1, source_target_pairs={{0,6},{1,7},{2,4},{3,5},{4,2},{5,3},{6,0},{7,1},{8,14},{9,15},{10,... | collective-permute-start | bytes 393224 | tf_op jit(solution)/shard_map/ppermute | solution.py:300
  16.0 8.5 %collective-permute-start.5 = (bf16[1,128,512]{2,1,0:T(8,128)(2,1)S(1)}, bf16[1,128,512]{2,1,0:T(8,128)(2,1)S(1)}, u32[]{:S(2)}, u32[]{:S(2)}) collective-permute-start(bf16[1,128,512]{2,1,0:T(8,128)(2,1)S(1)} %bitcast.89), channel_id=1, source_target_pairs={{0,4},{1,5},{2,6},{3,7},{4,0},{5,1},{6,2},{7,3},{8,12},{9,13},{10,... | collective-permute-start | bytes 393224 | tf_op jit(solution)/shard_map/ppermute | solution.py:300
  33.2 6.4 %collective-permute-start.9 = (bf16[128,256]{1,0:T(8,128)(2,1)S(1)}, bf16[128,256]{1,0:T(8,128)(2,1)S(1)}, u32[]{:S(2)}, u32[]{:S(2)}) collective-permute-start(bf16[128,256]{1,0:T(8,128)(2,1)S(1)} %project_mix.3), channel_id=1, source_target_pairs={{0,8},{1,9},{2,10},{3,11},{4,12},{5,13},{6,14},{7,15},{8,0},{9,1},... | collective-permute-start | bytes 196616 | tf_op jit(solution)/shard_map/ppermute | solution.py:300
  41.2 5.2 %collective-permute-start.11 = (bf16[1,128,256]{2,1,0:T(8,128)(2,1)S(1)}, bf16[1,128,256]{2,1,0:T(8,128)(2,1)S(1)}, u32[]{:S(2)}, u32[]{:S(2)}) collective-permute-start(bf16[1,128,256]{2,1,0:T(8,128)(2,1)S(1)} %bitcast.99), channel_id=1, source_target_pairs={{0,6},{1,7},{2,4},{3,5},{4,2},{5,3},{6,0},{7,1},{8,14},{9,15},{10,... | collective-permute-start | bytes 196616 | tf_op jit(solution)/shard_map/ppermute | solution.py:300
  49.4 10.7 %collective-permute-start.14 = (bf16[128,512]{1,0:T(8,128)(2,1)S(1)}, bf16[128,512]{1,0:T(8,128)(2,1)S(1)}, u32[]{:S(2)}, u32[]{:S(2)}) collective-permute-start(bf16[128,512]{1,0:T(8,128)(2,1)S(1)} %get-tuple-element.126), channel_id=1, source_target_pairs={{0,16},{1,17},{2,18},{3,19},{4,20},{5,21},{6,22},{7,23},{8,24},{9,... | collective-permute-start | bytes 393224 | tf_op jit(solution)/shard_map/ppermute | solution.py:309
  51.0 9.1 %collective-permute-start.15 = (bf16[128,512]{1,0:T(8,128)(2,1)S(1)}, bf16[128,512]{1,0:T(8,128)(2,1)S(1)}, u32[]{:S(2)}, u32[]{:S(2)}) collective-permute-start(bf16[128,512]{1,0:T(8,128)(2,1)S(1)} %get-tuple-element.126), channel_id=1, source_target_pairs={{0,20},{1,21},{2,22},{3,23},{4,16},{5,17},{6,18},{7,19},{8,28},{9,... | collective-permute-start | bytes 393224 | tf_op jit(solution)/shard_map/ppermute | solution.py:309
  51.9 9.6 %collective-permute-start.16 = (bf16[128,512]{1,0:T(8,128)(2,1)S(1)}, bf16[128,512]{1,0:T(8,128)(2,1)S(1)}, u32[]{:S(2)}, u32[]{:S(2)}) collective-permute-start(bf16[128,512]{1,0:T(8,128)(2,1)S(1)} %get-tuple-element.126), channel_id=1, source_target_pairs={{0,24},{1,25},{2,26},{3,27},{4,28},{5,29},{6,30},{7,31},{8,16},{9,... | collective-permute-start | bytes 393224 | tf_op jit(solution)/shard_map/ppermute | solution.py:309
  54.4 7.1 %collective-permute-start.17 = (bf16[128,512]{1,0:T(8,128)(2,1)S(1)}, bf16[128,512]{1,0:T(8,128)(2,1)S(1)}, u32[]{:S(2)}, u32[]{:S(2)}) collective-permute-start(bf16[128,512]{1,0:T(8,128)(2,1)S(1)} %get-tuple-element.126), channel_id=1, source_target_pairs={{0,2},{1,3},{2,0},{3,1},{4,6},{5,7},{6,4},{7,5},{8,10},{9,11},{10,... | collective-permute-start | bytes 393224 | tf_op jit(solution)/shard_map/ppermute | solution.py:300
  61.6 8.9 %collective-permute-start.18 = (bf16[2,128,512]{2,1,0:T(8,128)(2,1)S(1)}, bf16[2,128,512]{2,1,0:T(8,128)(2,1)S(1)}, u32[]{:S(2)}, u32[]{:S(2)}) collective-permute-start(bf16[2,128,512]{2,1,0:T(8,128)(2,1)S(1)} %pad_maximum_fusion.7), channel_id=1, source_target_pairs={{0,2},{1,3},{2,0},{3,1},{4,6},{5,7},{6,4},{7,5},{8,10},{9,11},{10,... | collective-permute-start | bytes 786440 | tf_op jit(solution)/shard_map/ppermute | solution.py:300
  63.3 6.3 %collective-permute-start.19 = (bf16[1,128,512]{2,1,0:T(8,128)(2,1)S(1)}, bf16[1,128,512]{2,1,0:T(8,128)(2,1)S(1)}, u32[]{:S(2)}, u32[]{:S(2)}) collective-permute-start(bf16[1,128,512]{2,1,0:T(8,128)(2,1)S(1)} %bitcast.77), channel_id=1, source_target_pairs={{0,6},{1,7},{2,4},{3,5},{4,2},{5,3},{6,0},{7,1},{8,14},{9,15},{10,... | collective-permute-start | bytes 393224 | tf_op jit(solution)/shard_map/ppermute | solution.py:300
  80.8 5.9 %collective-permute-start.25 = (bf16[128,256]{1,0:T(8,128)(2,1)S(1)}, bf16[128,256]{1,0:T(8,128)(2,1)S(1)}, u32[]{:S(2)}, u32[]{:S(2)}) collective-permute-start(bf16[128,256]{1,0:T(8,128)(2,1)S(1)} %project_mix.4), channel_id=1, source_target_pairs={{0,8},{1,9},{2,10},{3,11},{4,12},{5,13},{6,14},{7,15},{8,0},{9,1},... | collective-permute-start | bytes 196616 | tf_op jit(solution)/shard_map/ppermute | solution.py:300
  87.7 5.2 %collective-permute-start.27 = (bf16[1,128,256]{2,1,0:T(8,128)(2,1)S(1)}, bf16[1,128,256]{2,1,0:T(8,128)(2,1)S(1)}, u32[]{:S(2)}, u32[]{:S(2)}) collective-permute-start(bf16[1,128,256]{2,1,0:T(8,128)(2,1)S(1)} %bitcast.102), channel_id=1, source_target_pairs={{0,6},{1,7},{2,4},{3,5},{4,2},{5,3},{6,0},{7,1},{8,14},{9,15},{10,... | collective-permute-start | bytes 196616 | tf_op jit(solution)/shard_map/ppermute | solution.py:300
  96.2 12.0 %collective-permute-start.30 = (bf16[128,512]{1,0:T(8,128)(2,1)S(1)}, bf16[128,512]{1,0:T(8,128)(2,1)S(1)}, u32[]{:S(2)}, u32[]{:S(2)}) collective-permute-start(bf16[128,512]{1,0:T(8,128)(2,1)S(1)} %get-tuple-element.153), channel_id=1, source_target_pairs={{0,16},{1,17},{2,18},{3,19},{4,20},{5,21},{6,22},{7,23},{8,24},{9,... | collective-permute-start | bytes 393224 | tf_op jit(solution)/shard_map/ppermute | solution.py:309
  99.0 9.1 %collective-permute-start.31 = (bf16[128,512]{1,0:T(8,128)(2,1)S(1)}, bf16[128,512]{1,0:T(8,128)(2,1)S(1)}, u32[]{:S(2)}, u32[]{:S(2)}) collective-permute-start(bf16[128,512]{1,0:T(8,128)(2,1)S(1)} %get-tuple-element.153), channel_id=1, source_target_pairs={{0,20},{1,21},{2,22},{3,23},{4,16},{5,17},{6,18},{7,19},{8,28},{9,... | collective-permute-start | bytes 393224 | tf_op jit(solution)/shard_map/ppermute | solution.py:309
  99.3 9.9 %collective-permute-start.32 = (bf16[128,512]{1,0:T(8,128)(2,1)S(1)}, bf16[128,512]{1,0:T(8,128)(2,1)S(1)}, u32[]{:S(2)}, u32[]{:S(2)}) collective-permute-start(bf16[128,512]{1,0:T(8,128)(2,1)S(1)} %get-tuple-element.153), channel_id=1, source_target_pairs={{0,24},{1,25},{2,26},{3,27},{4,28},{5,29},{6,30},{7,31},{8,16},{9,... | collective-permute-start | bytes 393224 | tf_op jit(solution)/shard_map/ppermute | solution.py:309
  101.9 7.2 %collective-permute-start.33 = (bf16[128,512]{1,0:T(8,128)(2,1)S(1)}, bf16[128,512]{1,0:T(8,128)(2,1)S(1)}, u32[]{:S(2)}, u32[]{:S(2)}) collective-permute-start(bf16[128,512]{1,0:T(8,128)(2,1)S(1)} %get-tuple-element.153), channel_id=1, source_target_pairs={{0,2},{1,3},{2,0},{3,1},{4,6},{5,7},{6,4},{7,5},{8,10},{9,11},{10,... | collective-permute-start | bytes 393224 | tf_op jit(solution)/shard_map/ppermute | solution.py:300
  109.2 8.6 %collective-permute-start.34 = (bf16[2,128,512]{2,1,0:T(8,128)(2,1)S(1)}, bf16[2,128,512]{2,1,0:T(8,128)(2,1)S(1)}, u32[]{:S(2)}, u32[]{:S(2)}) collective-permute-start(bf16[2,128,512]{2,1,0:T(8,128)(2,1)S(1)} %pad_maximum_fusion.8), channel_id=1, source_target_pairs={{0,2},{1,3},{2,0},{3,1},{4,6},{5,7},{6,4},{7,5},{8,10},{9,11},{10,... | collective-permute-start | bytes 786440 | tf_op jit(solution)/shard_map/ppermute | solution.py:300
  110.1 7.1 %collective-permute-start.35 = (bf16[1,128,512]{2,1,0:T(8,128)(2,1)S(1)}, bf16[1,128,512]{2,1,0:T(8,128)(2,1)S(1)}, u32[]{:S(2)}, u32[]{:S(2)}) collective-permute-start(bf16[1,128,512]{2,1,0:T(8,128)(2,1)S(1)} %bitcast.81), channel_id=1, source_target_pairs={{0,6},{1,7},{2,4},{3,5},{4,2},{5,3},{6,0},{7,1},{8,14},{9,15},{10,... | collective-permute-start | bytes 393224 | tf_op jit(solution)/shard_map/ppermute | solution.py:300
  127.6 6.3 %collective-permute-start.41 = (bf16[128,256]{1,0:T(8,128)(2,1)S(1)}, bf16[128,256]{1,0:T(8,128)(2,1)S(1)}, u32[]{:S(2)}, u32[]{:S(2)}) collective-permute-start(bf16[128,256]{1,0:T(8,128)(2,1)S(1)} %project_mix.5), channel_id=1, source_target_pairs={{0,8},{1,9},{2,10},{3,11},{4,12},{5,13},{6,14},{7,15},{8,0},{9,1},... | collective-permute-start | bytes 196616 | tf_op jit(solution)/shard_map/ppermute | solution.py:300
  135.1 5.2 %collective-permute-start.43 = (bf16[1,128,256]{2,1,0:T(8,128)(2,1)S(1)}, bf16[1,128,256]{2,1,0:T(8,128)(2,1)S(1)}, u32[]{:S(2)}, u32[]{:S(2)}) collective-permute-start(bf16[1,128,256]{2,1,0:T(8,128)(2,1)S(1)} %bitcast.105), channel_id=1, source_target_pairs={{0,6},{1,7},{2,4},{3,5},{4,2},{5,3},{6,0},{7,1},{8,14},{9,15},{10,... | collective-permute-start | bytes 196616 | tf_op jit(solution)/shard_map/ppermute | solution.py:300
  (25 other events, 113.9 us)

commit v14 on v13

--- a/solution.py
+++ b/solution.py
@@ -94,16 +94,17 @@
     for group in [small] + copies:
         for copy in group:
             copy.start()
-    for copy in small:
+    small[0].wait()
+
+    def ready(n):
+        for copy in copies[n]:
+            copy.wait()
+
+    project(blocks, core, lambda n: x_ref[n], lambda n: w_refs[n], rank_ref, gain_ref, acc_ref, sq_ref, None, ready)
+    for copy in small[1:]:
         copy.wait()
     lags = lax.broadcasted_iota(jnp.int32, long_ref.shape, 0).astype(jnp.float32)
     long_ref[...] = taps_ref[...].T * jnp.exp(-decay_ref[...] * lags)
-
-    def ready(n):
-        for copy in copies[n]:
-            copy.wait()
-
-    project(blocks, core, lambda n: x_ref[n], lambda n: w_refs[n], rank_ref, gain_ref, acc_ref, sq_ref, None, ready)
     for n in range(len(blocks), len(order)):
         ready(n)
 

time: 144 us -> 144 us (level)
  no operation moved by 1% of the time
where the time goes in v14:
time: 144 us
  starting transfers between devices  56.1 us (39%)
  waiting for transfers between devices  48.5 us (34%)
  Pallas kernels  35.9 us (25%)
  other arithmetic  2.33 us (2%)
    ppermute x38, starting transfers between devices, swap(): return lax.ppermute(value, 'dp', [(r, r ^ offset) for r in range(dp_count)])  42.1 us
    pallas_call x15, Pallas kernels, call(): pl.pallas_call(kernel, in_specs=specs, out_specs=in_vmem(len(outs)), out_...  35.9 us
    ppermute x38, waiting for transfers between devices, swap(): return lax.ppermute(value, 'dp', [(r, r ^ offset) for r in range(dp_count)])  35.3 us
    ppermute x8, starting transfers between devices, onward(): return lax.ppermute(value, ('section', 'dp'), pairs)  14 us
    ppermute x8, waiting for transfers between devices, onward(): return lax.ppermute(value, ('section', 'dp'), pairs)  13.2 us
  transfers between devices with their start and end apart: 46, of which 35 were waited for; matrix products, arithmetic and copies ran while one was open for 0% of the time, Pallas kernels for 13%

profile of v14, /device:TPU:0, one launch (start us, length us, event | category | flops | bytes accessed | tf_op | source)
XLA Modules:
  0.0 143.8 jit_solution(5313591465685641345)
XLA Ops:
  0.9 3.0 %collective-permute-start = (bf16[128,512]{1,0:T(8,128)(2,1)S(1)}, bf16[128,512]{1,0:T(8,128)(2,1)S(1)}, u32[]{:S(2)}, u32[]{:S(2)}) collective-permute-start(bf16[128,512]{1,0:T(8,128)(2,1)S(1)} %select_bitcast_fusion.own_ref), channel_id=1, source_target_pairs={{0,2},{1,3},{2,0},{3,1},{4,6},{5,7},{6,4},{7,5},{8,10},{9,11},{10,... | collective-permute-start | bytes 393224 | tf_op jit(solution)/shard_map/ppermute | solution.py:301
  5.5 2.6 %collective-permute-start.2 = (bf16[128,512]{1,0:T(8,128)(2,1)S(1)}, bf16[128,512]{1,0:T(8,128)(2,1)S(1)}, u32[]{:S(2)}, u32[]{:S(2)}) collective-permute-start(bf16[128,512]{1,0:T(8,128)(2,1)S(1)} %select_bitcast_fusion.own_ref), channel_id=1, source_target_pairs={{0,8},{1,9},{2,10},{3,11},{4,12},{5,13},{6,14},{7,15},{8,0},{9,1},... | collective-permute-start | bytes 393224 | tf_op jit(solution)/shard_map/ppermute | solution.py:301
  8.2 2.4 %collective-permute-done.1 = bf16[128,512]{1,0:T(8,128)(2,1)S(1)} collective-permute-done((bf16[128,512]{1,0:T(8,128)(2,1)S(1)}, bf16[128,512]{1,0:T(8,128)(2,1)S(1)}, u32[]{:S(2)}, u32[]{:S(2)}) %collective-permute-start.1) | collective-permute-done | bytes 131104 | tf_op jit(solution)/shard_map/ppermute | solution.py:301
  10.6 3.3 %collective-permute-done.2 = bf16[128,512]{1,0:T(8,128)(2,1)S(1)} collective-permute-done((bf16[128,512]{1,0:T(8,128)(2,1)S(1)}, bf16[128,512]{1,0:T(8,128)(2,1)S(1)}, u32[]{:S(2)}, u32[]{:S(2)}) %collective-permute-start.2) | collective-permute-done | bytes 131104 | tf_op jit(solution)/shard_map/ppermute | solution.py:301
  17.7 6.4 %project_load.1 = (bf16[3,256,1024]{2,1,0:T(8,128)(2,1)S(1)}, bf16[3,256,1024]{2,1,0:T(8,128)(2,1)S(1)}, bf16[3,256,1024]{2,1,0:T(8,128)(2,1)S(1)}, bf16[3,256,1...) custom-call(s32[2]{0:T(128)S(1)} %pad_add_fusion.rank_ref, ...), custom_call_target="tpu_custom_call" | custom-call | flops 402653184 | bytes 393216 | tf_op jit(solution)/shard_map/project_load/pallas_call | solution.py:208
  24.4 1.7 %project_more.3 = (f32[3,128,256]{2,1,0:T(8,128)S(1)}, f32[128,128]{1,0:T(8,128)S(1)}) custom-call(s32[2]{0:T(128)S(1)} %pad_add_fusion.rank_ref, bf16[4,128,512]{2,1,0:T(8,128)(2,1)S(1)} %pad_maximum_fusion.3.x_ref, f32[1,8192]{1,0:T(1,128)S(1)} %get-tuple-element.104.gain_ref.refs_1_, ...), custom_call_target="tpu_custom_call" | custom-call | flops 402653184 | bytes 393216 | tf_op jit(solution)/shard_map/project_more/pallas_call | solution.py:208
  26.9 4.9 %project_mix.3 = bf16[128,256]{1,0:T(8,128)(2,1)S(1)} custom-call(s32[2]{0:T(128)S(1)} %pad_add_fusion.rank_ref, bf16[8,128,512]{2,1,0:T(8,128)(2,1)S(1)} %collective-permute-done.6.refs_0_, f32[1,8192]{1,0:T(1,128)S(1)} %get-tuple-element.104.gain_ref.refs_1_, f32[3,128,256]{2,1,0:T(8,128)S(1)} %get-tuple-element.99.refs_2_, ...), custom_call_target="tpu_custom_call" | custom-call | flops 1610612736 | bytes 1572864 | tf_op jit(solution)/shard_map/project_mix/pallas_call | solution.py:208
  32.8 2.7 %collective-permute-start.9 = (bf16[128,256]{1,0:T(8,128)(2,1)S(1)}, bf16[128,256]{1,0:T(8,128)(2,1)S(1)}, u32[]{:S(2)}, u32[]{:S(2)}) collective-permute-start(bf16[128,256]{1,0:T(8,128)(2,1)S(1)} %project_mix.3), channel_id=1, source_target_pairs={{0,8},{1,9},{2,10},{3,11},{4,12},{5,13},{6,14},{7,15},{8,0},{9,1},... | collective-permute-start | bytes 196616 | tf_op jit(solution)/shard_map/ppermute | solution.py:301
  37.4 1.8 %collective-permute-done.9 = bf16[128,256]{1,0:T(8,128)(2,1)S(1)} collective-permute-done((bf16[128,256]{1,0:T(8,128)(2,1)S(1)}, bf16[128,256]{1,0:T(8,128)(2,1)S(1)}, u32[]{:S(2)}, u32[]{:S(2)}) %collective-permute-start.9) | collective-permute-done | bytes 65568 | tf_op jit(solution)/shard_map/ppermute | solution.py:301
  51.5 2.5 %collective-permute-start.16 = (bf16[128,512]{1,0:T(8,128)(2,1)S(1)}, bf16[128,512]{1,0:T(8,128)(2,1)S(1)}, u32[]{:S(2)}, u32[]{:S(2)}) collective-permute-start(bf16[128,512]{1,0:T(8,128)(2,1)S(1)} %get-tuple-element.126), channel_id=1, source_target_pairs={{0,24},{1,25},{2,26},{3,27},{4,28},{5,29},{6,30},{7,31},{8,16},{9,... | collective-permute-start | bytes 393224 | tf_op jit(solution)/shard_map/ppermute | solution.py:310
  55.5 4.2 %collective-permute-done.14.own_ref = bf16[128,512]{1,0:T(8,128)(2,1)S(1)} collective-permute-done((bf16[128,512]{1,0:T(8,128)(2,1)S(1)}, bf16[128,512]{1,0:T(8,128)(2,1)S(1)}, u32[]{:S(2)}, u32[]{:S(2)}) %collective-permute-start.14) | collective-permute-done | bytes 131104 | tf_op jit(solution)/shard_map/ppermute | solution.py:310
  62.9 2.0 %collective-permute-start.19 = (bf16[1,128,512]{2,1,0:T(8,128)(2,1)S(1)}, bf16[1,128,512]{2,1,0:T(8,128)(2,1)S(1)}, u32[]{:S(2)}, u32[]{:S(2)}) collective-permute-start(bf16[1,128,512]{2,1,0:T(8,128)(2,1)S(1)} %bitcast.77), channel_id=1, source_target_pairs={{0,6},{1,7},{2,4},{3,5},{4,2},{5,3},{6,0},{7,1},{8,14},{9,15},{10,... | collective-permute-start | bytes 393224 | tf_op jit(solution)/shard_map/ppermute | solution.py:301
  70.3 2.0 %project_more.4 = (f32[3,128,256]{2,1,0:T(8,128)S(1)}, f32[128,128]{1,0:T(8,128)S(1)}) custom-call(s32[2]{0:T(128)S(1)} %pad_add_fusion.rank_ref, bf16[5,128,512]{2,1,0:T(8,128)(2,1)S(1)} %pad_maximum_fusion.x_ref, f32[1,8192]{1,0:T(1,128)S(1)} %get-tuple-element.104.gain_ref.refs_1_, bf16[3,256,1024]{2,1,0:T(8,128)(2,1)S(1)} %get-tuple-element.105.refs_0_.refs_12_.refs_11_, ...), custom_call_target="tpu_custom_call" | custom-call | flops 503316480 | bytes 491520 | tf_op jit(solution)/shard_map/project_more/pallas_call | solution.py:208
  72.9 5.1 %project_mix.4 = bf16[128,256]{1,0:T(8,128)(2,1)S(1)} custom-call(s32[2]{0:T(128)S(1)} %pad_add_fusion.rank_ref, bf16[8,128,512]{2,1,0:T(8,128)(2,1)S(1)} %collective-permute-done.22.refs_0_, f32[1,8192]{1,0:T(1,128)S(1)} %get-tuple-element.104.gain_ref.refs_1_, f32[3,128,256]{2,1,0:T(8,128)S(1)} %get-tuple-element.135.refs_2_, ...), custom_call_target="tpu_custom_call" | custom-call | flops 1610612736 | bytes 1572864 | tf_op jit(solution)/shard_map/project_mix/pallas_call | solution.py:208
  83.5 2.8 %collective-permute-done.25 = bf16[128,256]{1,0:T(8,128)(2,1)S(1)} collective-permute-done((bf16[128,256]{1,0:T(8,128)(2,1)S(1)}, bf16[128,256]{1,0:T(8,128)(2,1)S(1)}, u32[]{:S(2)}, u32[]{:S(2)}) %collective-permute-start.25) | collective-permute-done | bytes 65568 | tf_op jit(solution)/shard_map/ppermute | solution.py:301
  88.0 1.9 %collective-permute-start.28 = (bf16[1,128,256]{2,1,0:T(8,128)(2,1)S(1)}, bf16[1,128,256]{2,1,0:T(8,128)(2,1)S(1)}, u32[]{:S(2)}, u32[]{:S(2)}) collective-permute-start(bf16[1,128,256]{2,1,0:T(8,128)(2,1)S(1)} %bitcast.103), channel_id=1, source_target_pairs={{0,4},{1,5},{2,6},{3,7},{4,0},{5,1},{6,2},{7,3},{8,12},{9,13},{10,... | collective-permute-start | bytes 196616 | tf_op jit(solution)/shard_map/ppermute | solution.py:301
  95.8 2.8 %collective-permute-start.30 = (bf16[128,512]{1,0:T(8,128)(2,1)S(1)}, bf16[128,512]{1,0:T(8,128)(2,1)S(1)}, u32[]{:S(2)}, u32[]{:S(2)}) collective-permute-start(bf16[128,512]{1,0:T(8,128)(2,1)S(1)} %get-tuple-element.153), channel_id=1, source_target_pairs={{0,16},{1,17},{2,18},{3,19},{4,20},{5,21},{6,22},{7,23},{8,24},{9,... | collective-permute-start | bytes 393224 | tf_op jit(solution)/shard_map/ppermute | solution.py:310
  98.9 2.7 %collective-permute-start.32 = (bf16[128,512]{1,0:T(8,128)(2,1)S(1)}, bf16[128,512]{1,0:T(8,128)(2,1)S(1)}, u32[]{:S(2)}, u32[]{:S(2)}) collective-permute-start(bf16[128,512]{1,0:T(8,128)(2,1)S(1)} %get-tuple-element.153), channel_id=1, source_target_pairs={{0,24},{1,25},{2,26},{3,27},{4,28},{5,29},{6,30},{7,31},{8,16},{9,... | collective-permute-start | bytes 393224 | tf_op jit(solution)/shard_map/ppermute | solution.py:310
  102.4 5.3 %collective-permute-done.30.own_ref = bf16[128,512]{1,0:T(8,128)(2,1)S(1)} collective-permute-done((bf16[128,512]{1,0:T(8,128)(2,1)S(1)}, bf16[128,512]{1,0:T(8,128)(2,1)S(1)}, u32[]{:S(2)}, u32[]{:S(2)}) %collective-permute-start.30) | collective-permute-done | bytes 131104 | tf_op jit(solution)/shard_map/ppermute | solution.py:310
  109.7 2.8 %collective-permute-start.35 = (bf16[1,128,512]{2,1,0:T(8,128)(2,1)S(1)}, bf16[1,128,512]{2,1,0:T(8,128)(2,1)S(1)}, u32[]{:S(2)}, u32[]{:S(2)}) collective-permute-start(bf16[1,128,512]{2,1,0:T(8,128)(2,1)S(1)} %bitcast.81), channel_id=1, source_target_pairs={{0,6},{1,7},{2,4},{3,5},{4,2},{5,3},{6,0},{7,1},{8,14},{9,15},{10,... | collective-permute-start | bytes 393224 | tf_op jit(solution)/shard_map/ppermute | solution.py:301
  117.7 2.0 %project_more.5 = (f32[3,128,256]{2,1,0:T(8,128)S(1)}, f32[128,128]{1,0:T(8,128)S(1)}) custom-call(s32[2]{0:T(128)S(1)} %pad_add_fusion.rank_ref, bf16[5,128,512]{2,1,0:T(8,128)(2,1)S(1)} %pad_maximum_fusion.1.x_ref, f32[1,8192]{1,0:T(1,128)S(1)} %get-tuple-element.104.gain_ref.refs_1_, ...), custom_call_target="tpu_custom_call" | custom-call | flops 503316480 | bytes 491520 | tf_op jit(solution)/shard_map/project_more/pallas_call | solution.py:208
  120.3 4.9 %project_mix.5 = bf16[128,256]{1,0:T(8,128)(2,1)S(1)} custom-call(s32[2]{0:T(128)S(1)} %pad_add_fusion.rank_ref, bf16[8,128,512]{2,1,0:T(8,128)(2,1)S(1)} %collective-permute-done.38.refs_0_, f32[1,8192]{1,0:T(1,128)S(1)} %get-tuple-element.104.gain_ref.refs_1_, f32[3,128,256]{2,1,0:T(8,128)S(1)} %get-tuple-element.162.refs_2_, ...), custom_call_target="tpu_custom_call" | custom-call | flops 1610612736 | bytes 1572864 | tf_op jit(solution)/shard_map/project_mix/pallas_call | solution.py:208
  129.5 2.0 %collective-permute-done.40 = bf16[128,256]{1,0:T(8,128)(2,1)S(1)} collective-permute-done((bf16[128,256]{1,0:T(8,128)(2,1)S(1)}, bf16[128,256]{1,0:T(8,128)(2,1)S(1)}, u32[]{:S(2)}, u32[]{:S(2)}) %collective-permute-start.40) | collective-permute-done | bytes 65568 | tf_op jit(solution)/shard_map/ppermute | solution.py:301
  131.5 2.0 %collective-permute-done.41 = bf16[128,256]{1,0:T(8,128)(2,1)S(1)} collective-permute-done((bf16[128,256]{1,0:T(8,128)(2,1)S(1)}, bf16[128,256]{1,0:T(8,128)(2,1)S(1)}, u32[]{:S(2)}, u32[]{:S(2)}) %collective-permute-start.41) | collective-permute-done | bytes 65568 | tf_op jit(solution)/shard_map/ppermute | solution.py:301
  (146 shorter events, 69.4 us)
Async XLA Ops:
  0.9 7.2 %collective-permute-start = (bf16[128,512]{1,0:T(8,128)(2,1)S(1)}, bf16[128,512]{1,0:T(8,128)(2,1)S(1)}, u32[]{:S(2)}, u32[]{:S(2)}) collective-permute-start(bf16[128,512]{1,0:T(8,128)(2,1)S(1)} %select_bitcast_fusion.own_ref), channel_id=1, source_target_pairs={{0,2},{1,3},{2,0},{3,1},{4,6},{5,7},{6,4},{7,5},{8,10},{9,11},{10,... | collective-permute-start | bytes 393224 | tf_op jit(solution)/shard_map/ppermute | solution.py:301
  3.9 6.7 %collective-permute-start.1 = (bf16[128,512]{1,0:T(8,128)(2,1)S(1)}, bf16[128,512]{1,0:T(8,128)(2,1)S(1)}, u32[]{:S(2)}, u32[]{:S(2)}) collective-permute-start(bf16[128,512]{1,0:T(8,128)(2,1)S(1)} %select_bitcast_fusion.own_ref), channel_id=1, source_target_pairs={{0,4},{1,5},{2,6},{3,7},{4,0},{5,1},{6,2},{7,3},{8,12},{9,13},{10,... | collective-permute-start | bytes 393224 | tf_op jit(solution)/shard_map/ppermute | solution.py:301
  5.5 8.4 %collective-permute-start.2 = (bf16[128,512]{1,0:T(8,128)(2,1)S(1)}, bf16[128,512]{1,0:T(8,128)(2,1)S(1)}, u32[]{:S(2)}, u32[]{:S(2)}) collective-permute-start(bf16[128,512]{1,0:T(8,128)(2,1)S(1)} %select_bitcast_fusion.own_ref), channel_id=1, source_target_pairs={{0,8},{1,9},{2,10},{3,11},{4,12},{5,13},{6,14},{7,15},{8,0},{9,1},... | collective-permute-start | bytes 393224 | tf_op jit(solution)/shard_map/ppermute | solution.py:301
  14.0 10.1 %collective-permute-start.3 = (bf16[2,128,512]{2,1,0:T(8,128)(2,1)S(1)}, bf16[2,128,512]{2,1,0:T(8,128)(2,1)S(1)}, u32[]{:S(2)}, u32[]{:S(2)}) collective-permute-start(bf16[2,128,512]{2,1,0:T(8,128)(2,1)S(1)} %pad_maximum_fusion.6), channel_id=1, source_target_pairs={{0,2},{1,3},{2,0},{3,1},{4,6},{5,7},{6,4},{7,5},{8,10},{9,11},{10,... | collective-permute-start | bytes 786440 | tf_op jit(solution)/shard_map/ppermute | solution.py:301
  14.6 9.5 %collective-permute-start.4 = (bf16[1,128,512]{2,1,0:T(8,128)(2,1)S(1)}, bf16[1,128,512]{2,1,0:T(8,128)(2,1)S(1)}, u32[]{:S(2)}, u32[]{:S(2)}) collective-permute-start(bf16[1,128,512]{2,1,0:T(8,128)(2,1)S(1)} %bitcast.88), channel_id=1, source_target_pairs={{0,6},{1,7},{2,4},{3,5},{4,2},{5,3},{6,0},{7,1},{8,14},{9,15},{10,... | collective-permute-start | bytes 393224 | tf_op jit(solution)/shard_map/ppermute | solution.py:301
  16.0 8.1 %collective-permute-start.5 = (bf16[1,128,512]{2,1,0:T(8,128)(2,1)S(1)}, bf16[1,128,512]{2,1,0:T(8,128)(2,1)S(1)}, u32[]{:S(2)}, u32[]{:S(2)}) collective-permute-start(bf16[1,128,512]{2,1,0:T(8,128)(2,1)S(1)} %bitcast.89), channel_id=1, source_target_pairs={{0,4},{1,5},{2,6},{3,7},{4,0},{5,1},{6,2},{7,3},{8,12},{9,13},{10,... | collective-permute-start | bytes 393224 | tf_op jit(solution)/shard_map/ppermute | solution.py:301
  32.8 6.4 %collective-permute-start.9 = (bf16[128,256]{1,0:T(8,128)(2,1)S(1)}, bf16[128,256]{1,0:T(8,128)(2,1)S(1)}, u32[]{:S(2)}, u32[]{:S(2)}) collective-permute-start(bf16[128,256]{1,0:T(8,128)(2,1)S(1)} %project_mix.3), channel_id=1, source_target_pairs={{0,8},{1,9},{2,10},{3,11},{4,12},{5,13},{6,14},{7,15},{8,0},{9,1},... | collective-permute-start | bytes 196616 | tf_op jit(solution)/shard_map/ppermute | solution.py:301
  40.8 5.2 %collective-permute-start.11 = (bf16[1,128,256]{2,1,0:T(8,128)(2,1)S(1)}, bf16[1,128,256]{2,1,0:T(8,128)(2,1)S(1)}, u32[]{:S(2)}, u32[]{:S(2)}) collective-permute-start(bf16[1,128,256]{2,1,0:T(8,128)(2,1)S(1)} %bitcast.99), channel_id=1, source_target_pairs={{0,6},{1,7},{2,4},{3,5},{4,2},{5,3},{6,0},{7,1},{8,14},{9,15},{10,... | collective-permute-start | bytes 196616 | tf_op jit(solution)/shard_map/ppermute | solution.py:301
  49.0 10.7 %collective-permute-start.14 = (bf16[128,512]{1,0:T(8,128)(2,1)S(1)}, bf16[128,512]{1,0:T(8,128)(2,1)S(1)}, u32[]{:S(2)}, u32[]{:S(2)}) collective-permute-start(bf16[128,512]{1,0:T(8,128)(2,1)S(1)} %get-tuple-element.126), channel_id=1, source_target_pairs={{0,16},{1,17},{2,18},{3,19},{4,20},{5,21},{6,22},{7,23},{8,24},{9,... | collective-permute-start | bytes 393224 | tf_op jit(solution)/shard_map/ppermute | solution.py:310
  50.6 9.1 %collective-permute-start.15 = (bf16[128,512]{1,0:T(8,128)(2,1)S(1)}, bf16[128,512]{1,0:T(8,128)(2,1)S(1)}, u32[]{:S(2)}, u32[]{:S(2)}) collective-permute-start(bf16[128,512]{1,0:T(8,128)(2,1)S(1)} %get-tuple-element.126), channel_id=1, source_target_pairs={{0,20},{1,21},{2,22},{3,23},{4,16},{5,17},{6,18},{7,19},{8,28},{9,... | collective-permute-start | bytes 393224 | tf_op jit(solution)/shard_map/ppermute | solution.py:310
  51.5 9.6 %collective-permute-start.16 = (bf16[128,512]{1,0:T(8,128)(2,1)S(1)}, bf16[128,512]{1,0:T(8,128)(2,1)S(1)}, u32[]{:S(2)}, u32[]{:S(2)}) collective-permute-start(bf16[128,512]{1,0:T(8,128)(2,1)S(1)} %get-tuple-element.126), channel_id=1, source_target_pairs={{0,24},{1,25},{2,26},{3,27},{4,28},{5,29},{6,30},{7,31},{8,16},{9,... | collective-permute-start | bytes 393224 | tf_op jit(solution)/shard_map/ppermute | solution.py:310
  54.0 7.1 %collective-permute-start.17 = (bf16[128,512]{1,0:T(8,128)(2,1)S(1)}, bf16[128,512]{1,0:T(8,128)(2,1)S(1)}, u32[]{:S(2)}, u32[]{:S(2)}) collective-permute-start(bf16[128,512]{1,0:T(8,128)(2,1)S(1)} %get-tuple-element.126), channel_id=1, source_target_pairs={{0,2},{1,3},{2,0},{3,1},{4,6},{5,7},{6,4},{7,5},{8,10},{9,11},{10,... | collective-permute-start | bytes 393224 | tf_op jit(solution)/shard_map/ppermute | solution.py:301
  61.2 8.9 %collective-permute-start.18 = (bf16[2,128,512]{2,1,0:T(8,128)(2,1)S(1)}, bf16[2,128,512]{2,1,0:T(8,128)(2,1)S(1)}, u32[]{:S(2)}, u32[]{:S(2)}) collective-permute-start(bf16[2,128,512]{2,1,0:T(8,128)(2,1)S(1)} %pad_maximum_fusion.7), channel_id=1, source_target_pairs={{0,2},{1,3},{2,0},{3,1},{4,6},{5,7},{6,4},{7,5},{8,10},{9,11},{10,... | collective-permute-start | bytes 786440 | tf_op jit(solution)/shard_map/ppermute | solution.py:301
  62.9 6.3 %collective-permute-start.19 = (bf16[1,128,512]{2,1,0:T(8,128)(2,1)S(1)}, bf16[1,128,512]{2,1,0:T(8,128)(2,1)S(1)}, u32[]{:S(2)}, u32[]{:S(2)}) collective-permute-start(bf16[1,128,512]{2,1,0:T(8,128)(2,1)S(1)} %bitcast.77), channel_id=1, source_target_pairs={{0,6},{1,7},{2,4},{3,5},{4,2},{5,3},{6,0},{7,1},{8,14},{9,15},{10,... | collective-permute-start | bytes 393224 | tf_op jit(solution)/shard_map/ppermute | solution.py:301
  80.4 5.9 %collective-permute-start.25 = (bf16[128,256]{1,0:T(8,128)(2,1)S(1)}, bf16[128,256]{1,0:T(8,128)(2,1)S(1)}, u32[]{:S(2)}, u32[]{:S(2)}) collective-permute-start(bf16[128,256]{1,0:T(8,128)(2,1)S(1)} %project_mix.4), channel_id=1, source_target_pairs={{0,8},{1,9},{2,10},{3,11},{4,12},{5,13},{6,14},{7,15},{8,0},{9,1},... | collective-permute-start | bytes 196616 | tf_op jit(solution)/shard_map/ppermute | solution.py:301
  87.3 5.2 %collective-permute-start.27 = (bf16[1,128,256]{2,1,0:T(8,128)(2,1)S(1)}, bf16[1,128,256]{2,1,0:T(8,128)(2,1)S(1)}, u32[]{:S(2)}, u32[]{:S(2)}) collective-permute-start(bf16[1,128,256]{2,1,0:T(8,128)(2,1)S(1)} %bitcast.102), channel_id=1, source_target_pairs={{0,6},{1,7},{2,4},{3,5},{4,2},{5,3},{6,0},{7,1},{8,14},{9,15},{10,... | collective-permute-start | bytes 196616 | tf_op jit(solution)/shard_map/ppermute | solution.py:301
  95.8 12.0 %collective-permute-start.30 = (bf16[128,512]{1,0:T(8,128)(2,1)S(1)}, bf16[128,512]{1,0:T(8,128)(2,1)S(1)}, u32[]{:S(2)}, u32[]{:S(2)}) collective-permute-start(bf16[128,512]{1,0:T(8,128)(2,1)S(1)} %get-tuple-element.153), channel_id=1, source_target_pairs={{0,16},{1,17},{2,18},{3,19},{4,20},{5,21},{6,22},{7,23},{8,24},{9,... | collective-permute-start | bytes 393224 | tf_op jit(solution)/shard_map/ppermute | solution.py:310
  98.6 9.1 %collective-permute-start.31 = (bf16[128,512]{1,0:T(8,128)(2,1)S(1)}, bf16[128,512]{1,0:T(8,128)(2,1)S(1)}, u32[]{:S(2)}, u32[]{:S(2)}) collective-permute-start(bf16[128,512]{1,0:T(8,128)(2,1)S(1)} %get-tuple-element.153), channel_id=1, source_target_pairs={{0,20},{1,21},{2,22},{3,23},{4,16},{5,17},{6,18},{7,19},{8,28},{9,... | collective-permute-start | bytes 393224 | tf_op jit(solution)/shard_map/ppermute | solution.py:310
  98.9 9.9 %collective-permute-start.32 = (bf16[128,512]{1,0:T(8,128)(2,1)S(1)}, bf16[128,512]{1,0:T(8,128)(2,1)S(1)}, u32[]{:S(2)}, u32[]{:S(2)}) collective-permute-start(bf16[128,512]{1,0:T(8,128)(2,1)S(1)} %get-tuple-element.153), channel_id=1, source_target_pairs={{0,24},{1,25},{2,26},{3,27},{4,28},{5,29},{6,30},{7,31},{8,16},{9,... | collective-permute-start | bytes 393224 | tf_op jit(solution)/shard_map/ppermute | solution.py:310
  101.5 7.2 %collective-permute-start.33 = (bf16[128,512]{1,0:T(8,128)(2,1)S(1)}, bf16[128,512]{1,0:T(8,128)(2,1)S(1)}, u32[]{:S(2)}, u32[]{:S(2)}) collective-permute-start(bf16[128,512]{1,0:T(8,128)(2,1)S(1)} %get-tuple-element.153), channel_id=1, source_target_pairs={{0,2},{1,3},{2,0},{3,1},{4,6},{5,7},{6,4},{7,5},{8,10},{9,11},{10,... | collective-permute-start | bytes 393224 | tf_op jit(solution)/shard_map/ppermute | solution.py:301
  108.9 8.6 %collective-permute-start.34 = (bf16[2,128,512]{2,1,0:T(8,128)(2,1)S(1)}, bf16[2,128,512]{2,1,0:T(8,128)(2,1)S(1)}, u32[]{:S(2)}, u32[]{:S(2)}) collective-permute-start(bf16[2,128,512]{2,1,0:T(8,128)(2,1)S(1)} %pad_maximum_fusion.8), channel_id=1, source_target_pairs={{0,2},{1,3},{2,0},{3,1},{4,6},{5,7},{6,4},{7,5},{8,10},{9,11},{10,... | collective-permute-start | bytes 786440 | tf_op jit(solution)/shard_map/ppermute | solution.py:301
  109.7 7.1 %collective-permute-start.35 = (bf16[1,128,512]{2,1,0:T(8,128)(2,1)S(1)}, bf16[1,128,512]{2,1,0:T(8,128)(2,1)S(1)}, u32[]{:S(2)}, u32[]{:S(2)}) collective-permute-start(bf16[1,128,512]{2,1,0:T(8,128)(2,1)S(1)} %bitcast.81), channel_id=1, source_target_pairs={{0,6},{1,7},{2,4},{3,5},{4,2},{5,3},{6,0},{7,1},{8,14},{9,15},{10,... | collective-permute-start | bytes 393224 | tf_op jit(solution)/shard_map/ppermute | solution.py:301
  127.2 6.3 %collective-permute-start.41 = (bf16[128,256]{1,0:T(8,128)(2,1)S(1)}, bf16[128,256]{1,0:T(8,128)(2,1)S(1)}, u32[]{:S(2)}, u32[]{:S(2)}) collective-permute-start(bf16[128,256]{1,0:T(8,128)(2,1)S(1)} %project_mix.5), channel_id=1, source_target_pairs={{0,8},{1,9},{2,10},{3,11},{4,12},{5,13},{6,14},{7,15},{8,0},{9,1},... | collective-permute-start | bytes 196616 | tf_op jit(solution)/shard_map/ppermute | solution.py:301
  134.8 5.2 %collective-permute-start.43 = (bf16[1,128,256]{2,1,0:T(8,128)(2,1)S(1)}, bf16[1,128,256]{2,1,0:T(8,128)(2,1)S(1)}, u32[]{:S(2)}, u32[]{:S(2)}) collective-permute-start(bf16[1,128,256]{2,1,0:T(8,128)(2,1)S(1)} %bitcast.105), channel_id=1, source_target_pairs={{0,6},{1,7},{2,4},{3,5},{4,2},{5,3},{6,0},{7,1},{8,14},{9,15},{10,... | collective-permute-start | bytes 196616 | tf_op jit(solution)/shard_map/ppermute | solution.py:301
  (25 other events, 113.9 us)
